TPU v7x, 32 devices: a whole 2x2x4 slice. The times are simulated.
32 devices in a mesh: dp: 4 (over y, x), dom: 8 (over z, core).
Axes of the slice: x: 2, y: 2, z: 4, core: 2. Of those that a mesh axis runs over, the one named last changes fastest.
Arguments:
- features: bfloat16 [4, 4096, 128], P('dp', 'dom'), may hold values from -6 to 6
- keep_masks: bfloat16 [4, 4, 4096], P('dp', None, 'dom'), may hold values from 0 to 1, as said below
- serve_ids: int32 [4, 8, 8, 1], P('dp', 'dom'), may hold values from 0 to 3, as said below
- col_slot: int32 [4, 32, 4], P('dp', 'dom'), may hold values from 0 to 11, as said below
- adj_blocks: bfloat16 [4, 32, 4, 128, 128], P('dp', 'dom'), may hold values from -0.25 to 0.25
- node_labels: int32 [4, 4096], P('dp', 'dom'), may hold values from 0 to 171
- labeled: int32 [4, 4096], P('dp', 'dom'), may hold values 0 or 1
- weight_in: bfloat16 [128, 1024], replicated, may hold values from -0.5 to 0.5
- bias_in: float32 [1024], replicated, may hold values from -3 to 3
- weight_out: bfloat16 [1024, 172], replicated, may hold values from -0.1875 to 0.1875
- bias_out: float32 [172], replicated, may hold values from -4 to 4
Outputs:
- grad_weight_in: float32 [128, 1024], replicated
- grad_bias_in: float32 [1024], replicated
- grad_weight_out: float32 [1024, 172], replicated
- grad_bias_out: float32 [172], replicated
Inputs may be any that keep to these rules, and one draw needn't show every extreme that they name: `serve_ids`: for each batch, sending device and receiving device: 1 distinct own tile numbers of the sender. `col_slot`: slots below 8 name received tiles; within one device's row tiles every such slot is named exactly once and each own tile slot exactly 2 times. `keep_masks`: values are 0 or 1.
All inputs are finite; a program needn't handle non-finite values. No bound on the sum of `labeled` on one device may be relied on, other than what follows from the above.
Results may differ from a plain program's by a relative error of at most 0.0015.
Values may be sent and summed in bfloat16 or wider, within the bound.
No kernel may reach another device: no remote copies, remote signals or barrier semaphores. Data moves between devices by JAX's collectives and lax.ppermute only.
A program may use at most 64 MiB of HBM per device.

v0:
```python
import jax
import jax.numpy as jnp
from jax import lax
from jax.sharding import PartitionSpec as P

ORDER = 2


KEEP_RATE = 0.5


def tile_products(block_vals, picked):
    return jnp.einsum("rjab,rjsbf->rsaf", block_vals, picked, preferred_element_type=jnp.float32)


def mlp_grads(xbar, node_labels, labeled, weight_in, bias_in, weight_out, bias_out, scale):
    row_tiles, samples, tile_size, feat_size = xbar.shape
    classes = weight_out.shape[1]
    node_rows = xbar.reshape(-1, feat_size)
    hidden_pre = jnp.dot(node_rows, weight_in, preferred_element_type=jnp.float32) + bias_in
    activation = jax.nn.silu(hidden_pre).astype(jnp.bfloat16)
    logits = jnp.dot(activation, weight_out, preferred_element_type=jnp.float32) + bias_out
    expo = jnp.exp(logits)
    prob = (expo / jnp.sum(expo, -1, keepdims=True)).reshape(row_tiles, samples, tile_size, classes)
    average = jnp.mean(prob, axis=1)
    squares = average * average
    sharp = squares / jnp.sum(squares, -1, keepdims=True)
    onehot = (
        node_labels.reshape(row_tiles, tile_size)[..., None] == jnp.arange(classes, dtype=jnp.int32)
    ).astype(jnp.float32)
    used = labeled.reshape(row_tiles, 1, tile_size, 1).astype(jnp.float32)
    push = 2.0 * (prob - sharp[:, None])
    inner = jnp.sum(push * prob, -1, keepdims=True)
    dlogits = (used * (prob - onehot[:, None]) + prob * (push - inner)) * scale
    dlogits = dlogits.reshape(-1, classes)
    dlog_b = dlogits.astype(jnp.bfloat16)
    grad_weight_out = jnp.dot(activation.T, dlog_b, preferred_element_type=jnp.float32)
    grad_bias_out = jnp.sum(dlogits, 0)
    dact = jnp.dot(dlog_b, weight_out.T, preferred_element_type=jnp.float32)
    sigma = jax.nn.sigmoid(hidden_pre)
    dpre = dact * sigma * (1.0 + hidden_pre * (1.0 - sigma))
    grad_bias_in = jnp.sum(dpre, 0)
    grad_weight_in = jnp.dot(
        node_rows.T, dpre.astype(jnp.bfloat16), preferred_element_type=jnp.float32
    )
    return (grad_weight_in, grad_bias_in, grad_weight_out, grad_bias_out)


def per_device(
    features,
    keep_masks,
    serve_ids,
    col_slot,
    adj_blocks,
    node_labels,
    labeled,
    weight_in,
    bias_in,
    weight_out,
    bias_out,
):
    tiles_dev = col_slot.shape[1]
    tile_size = adj_blocks.shape[-1]
    feat_size = features.shape[-1]
    samples = keep_masks.shape[1]
    dom_count = lax.axis_size("dom")
    capacity = serve_ids.shape[-1]
    send_ids = serve_ids[0, 0].reshape(-1)
    slot_ids = col_slot[0]
    block_vals = adj_blocks[0]
    own_tiles = features[0].reshape(tiles_dev, tile_size, feat_size)
    mask_tiles = keep_masks[0].reshape(samples, tiles_dev, tile_size).transpose(1, 0, 2)
    masked = mask_tiles[:, :, :, None] * own_tiles[:, None, :, :]
    outgoing = masked[send_ids].reshape(dom_count, capacity, samples, tile_size, feat_size)
    incoming = lax.all_to_all(outgoing, "dom", split_axis=0, concat_axis=0, tiled=True)
    pool = jnp.concatenate([incoming.reshape(-1, samples, tile_size, feat_size), masked], 0)
    picked = pool[slot_ids]
    result = tile_products(block_vals, picked)
    total = masked.astype(jnp.float32) + result
    current = result.astype(jnp.bfloat16)
    outgoing = current[send_ids].reshape(dom_count, capacity, samples, tile_size, feat_size)
    incoming = lax.all_to_all(outgoing, "dom", split_axis=0, concat_axis=0, tiled=True)
    pool = jnp.concatenate([incoming.reshape(-1, samples, tile_size, feat_size), current], 0)
    result = tile_products(block_vals, pool[slot_ids])
    total = total + result
    xbar = (total * (1.0 / ((ORDER + 1) * KEEP_RATE))).astype(jnp.bfloat16)
    scale = 1.0 / (samples * tiles_dev * tile_size)
    grad_w1, grad_b1, grad_w2, grad_b2 = mlp_grads(
        xbar, node_labels[0], labeled[0], weight_in, bias_in, weight_out, bias_out, scale
    )
    inside = lax.psum((grad_w1, grad_b1, grad_w2, grad_b2), "dom")
    grad_w1, grad_b1, grad_w2, grad_b2 = lax.psum(
        (inside[0], inside[1], inside[2], inside[3]), "dp"
    )
    return (grad_w1, grad_b1, grad_w2, grad_b2)


def solution(mesh):
    placed = (
        P("dp", "dom", None),
        P("dp", None, "dom"),
        P("dp", "dom", None, None),
        P("dp", "dom", None),
        P("dp", "dom", None, None, None),
        P("dp", "dom"),
        P("dp", "dom"),
        P(),
        P(),
        P(),
        P(),
    )
    return jax.shard_map(
        per_device, mesh=mesh, in_specs=placed, out_specs=(P(), P(), P(), P()), check_vma=False
    )
```

profile of v0, /device:TPU:0, one launch (start us, length us, event | category | flops | bytes accessed | tf_op | source)
XLA Modules:
  0.0 246.0 jit_solution(1435440240521743489)
XLA Ops:
  7.9 1.2 broadcast_multiply_fusion
  9.2 1.6 gather_fusion
  10.8 6.3 %all-to-all-start = ((bf16[8,1,4,128,128]{4,3,2,1,0:T(8,128)(2,1)}), bf16[8,1,4,128,128]{4,3,2,1,0:T(8,128)(2,1)S(1)}, u32[]{:S(2)}, u32[]{:S(2)}) async-start(bf16[8,1,4,128,128]{4,3,2,1,0:T(8,128)(2,1)} %bitcast.6), calls=%async_computation | async-start | bytes 2097152 | tf_op jit(solution)/shard_map/all_to_all | solution.py:75
  17.2 26.5 %all-to-all-done = bf16[8,1,4,128,128]{4,3,2,1,0:T(8,128)(2,1)S(1)} async-done(((bf16[8,1,4,128,128]{4,3,2,1,0:T(8,128)(2,1)}), bf16[8,1,4,128,128]{4,3,2,1,0:T(8,128)(2,1)S(1)}, u32[]{:S(2)}, u32[]{:S(2)}) %all-to-all-start) | async-done | bytes 1048608 | tf_op jit(solution)/shard_map/all_to_all | solution.py:75
  43.7 1.0 copy-done.3
  44.7 1.4 pad_maximum_fusion
  46.1 2.2 gather_fusion.1
  48.2 3.0 %fusion.16 = (bf16[4,4,128,128]{3,2,1,0:T(8,128)(2,1)S(1)}, f32[4,4,128,128]{3,2,1,0:T(8,128)}) fusion(bf16[4,4,4,128,128]{4,3,2,1,0:T(8,128)(2,1)} %bitcast.78, bf16[1,4,4,128,128]{4,3,2,1,0:T(8,128)(2,1)S(1)} %copy-done), kind=kOutput, calls=%fused_computation.39 | convolution fusion | flops 268697600 | bytes 4194304 | tf_op jit(solution)/shard_map/rjab,rjsbf->rsaf/dot_general | solution.py:13
  51.3 1.6 gather_fusion.2
  52.9 3.6 %all-to-all-start.1 = ((bf16[8,1,4,128,128]{4,3,2,1,0:T(8,128)(2,1)}), bf16[8,1,4,128,128]{4,3,2,1,0:T(8,128)(2,1)S(1)}, u32[]{:S(2)}, u32[]{:S(2)}) async-start(bf16[8,1,4,128,128]{4,3,2,1,0:T(8,128)(2,1)} %bitcast.18), calls=%async_computation.1 | async-start | bytes 2097152 | tf_op jit(solution)/shard_map/all_to_all | solution.py:82
  56.9 1.7 sub.36
  58.6 24.4 %all-to-all-done.1 = bf16[8,1,4,128,128]{4,3,2,1,0:T(8,128)(2,1)S(1)} async-done(((bf16[8,1,4,128,128]{4,3,2,1,0:T(8,128)(2,1)}), bf16[8,1,4,128,128]{4,3,2,1,0:T(8,128)(2,1)S(1)}, u32[]{:S(2)}, u32[]{:S(2)}) %all-to-all-start.1) | async-done | bytes 1048608 | tf_op jit(solution)/shard_map/all_to_all | solution.py:82
  83.9 1.4 pad_maximum_fusion.1
  85.3 2.2 gather_fusion.3
  87.5 2.5 fusion.5
  90.0 4.8 %multiply_convert_fusion = (bf16[2048,1024]{1,0:T(8,128)(2,1)S(1)}, f32[2048,1024]{1,0:T(8,128)}) fusion(f32[1024]{0:T(1024)S(1)} %copy-done.14, bf16[2048,128]{1,0:T(8,128)(2,1)S(1)} %bitcast.81, bf16[128,1024]{1,0:T(8,128)(2,1)S(1)} %copy-done.13), kind=kOutput, calls=%fused_computation.5 | convolution fusion | flops 549453824 | bytes 13373440 | tf_op jit(solution)/shard_map/dot_general | solution.py:20
  94.8 1.6 fusion.17
  97.0 2.1 reshape.121
  99.0 2.3 reduce_sum.55
  101.6 1.3 sub.38
  102.9 1.8 sub.39
  105.1 1.0 copy-done.1
  106.8 1.5 copy-done.17
  108.3 1.8 fusion.8
  110.1 6.6 %fusion.18 = (f32[1024]{0:T(1024)S(1)}, bf16[2048,1024]{1,0:T(8,128)(2,1)S(1)}) fusion(f32[2048,1024]{1,0:T(8,128)} %get-tuple-element.17, f32[1024]{0:T(1024)S(1)} %copy-done.14, bf16[1024,172]{0,1:T(8,128)(2,1)S(1)} %copy-done.12, bf16[2048,172]{0,1:T(8,128)(2,1)S(1)} %get-tuple-element.13), kind=kOutput, calls=%fused_computation.41 | convolution fusion | flops 744487936 | bytes 13647872 | tf_op jit(solution)/shard_map/dot_general | solution.py:39
  116.7 1.5 fusion
  118.3 58.8 %all-reduce.7.cloned.1.call-done = (f32[128,1024]{1,0:T(8,128)}, f32[1024,172]{0,1:T(8,128)}) async-done(((f32[128,1024]{1,0:T(8,128)}, f32[1024,172]{0,1:T(8,128)}), (f32[128,1024]{1,0:T(8,128)}, f32[1024,172]{0,1:T(8,128)})) %all-reduce.7.cloned.1.call-update) | async-done | bytes 1228816 | tf_op jit(solution)/shard_map/psum | solution.py:91
  177.2 13.9 %all-reduce = (f32[1024]{0:T(1024)S(1)}, f32[172]{0:T(256)S(1)}) all-reduce(f32[1024]{0:T(1024)S(1)} %get-tuple-element.20, f32[172]{0:T(256)S(1)} %get-tuple-element.12), channel_id=1, replica_groups=mesh['dp'=4,'dom'=8] {'dom'}, use_global_device_ids=true, to_apply=%region_7.8 | all-reduce | flops 1196 | bytes 9568 | tf_op jit(solution)/shard_map/psum | solution.py:91
  191.1 10.5 %all-reduce.2 = (f32[1024]{0:T(1024)}, f32[172]{0:T(256)}) all-reduce(f32[1024]{0:T(1024)S(1)} %get-tuple-element.4, f32[172]{0:T(256)S(1)} %get-tuple-element.5), channel_id=1, replica_groups=mesh['dp'=4,'dom'=8] {'dp'}, use_global_device_ids=true, to_apply=%region_8.9 | all-reduce | flops 1196 | bytes 9568 | tf_op jit(solution)/shard_map/psum | solution.py:92
  201.6 33.6 %all-reduce.9.cloned.1.call-done = (f32[128,1024]{1,0:T(8,128)}, f32[1024,172]{0,1:T(8,128)}) async-done(((f32[128,1024]{1,0:T(8,128)}, f32[1024,172]{0,1:T(8,128)}), (f32[128,1024]{1,0:T(8,128)}, f32[1024,172]{0,1:T(8,128)})) %all-reduce.9.cloned.1.call-update) | async-done | bytes 1228816 | tf_op jit(solution)/shard_map/psum | solution.py:92
  235.2 1.9 copy.30
  237.1 2.0 copy.31
  (51 shorter events, 4.1 us)
Async XLA Ops:
  7.2 41.0 %copy-start = (bf16[1,4,4,128,128]{4,3,2,1,0:T(8,128)(2,1)S(1)}, bf16[1,4,4,128,128]{4,3,2,1,0:T(8,128)(2,1)}, u32[]{:S(2)}) copy-start(bf16[1,4,4,128,128]{4,3,2,1,0:T(8,128)(2,1)} %param.15) | copy-start | bytes 1572868
  9.2 8.0 %copy-start.9 = (s32[1,4,4]{2,1,0:T(4,128)S(1)}, s32[1,4,4]{2,1,0:T(4,128)}, u32[]{:S(2)}) copy-start(s32[1,4,4]{2,1,0:T(4,128)} %param.14) | copy-start | bytes 196
  10.8 32.9 %all-to-all-start = ((bf16[8,1,4,128,128]{4,3,2,1,0:T(8,128)(2,1)}), bf16[8,1,4,128,128]{4,3,2,1,0:T(8,128)(2,1)S(1)}, u32[]{:S(2)}, u32[]{:S(2)}) async-start(bf16[8,1,4,128,128]{4,3,2,1,0:T(8,128)(2,1)} %bitcast.6), calls=%async_computation | async-start | bytes 2097152 | tf_op jit(solution)/shard_map/all_to_all | solution.py:75
  43.7 1.0 copy-start.3
  51.3 5.3 %copy-start.10 = (s32[1,512]{1,0:T(1,128)S(1)}, s32[1,512]{1,0:T(1,128)}, u32[]{:S(2)}) copy-start(s32[1,512]{1,0:T(1,128)} %param.17) | copy-start | bytes 6148
  51.3 5.3 %copy-start.8 = (s32[1,512]{1,0:T(1,128)S(1)}, s32[1,512]{1,0:T(1,128)}, u32[]{:S(2)}) copy-start(s32[1,512]{1,0:T(1,128)} %param.16) | copy-start | bytes 6148
  52.9 30.1 %all-to-all-start.1 = ((bf16[8,1,4,128,128]{4,3,2,1,0:T(8,128)(2,1)}), bf16[8,1,4,128,128]{4,3,2,1,0:T(8,128)(2,1)S(1)}, u32[]{:S(2)}, u32[]{:S(2)}) async-start(bf16[8,1,4,128,128]{4,3,2,1,0:T(8,128)(2,1)} %bitcast.18), calls=%async_computation.1 | async-start | bytes 2097152 | tf_op jit(solution)/shard_map/all_to_all | solution.py:82
  56.5 120.7 %all-reduce.7.cloned.1.call-start = ((), (), s32[]{:S(2)}) async-start(), calls=%async_computation.2 | async-start | bytes 2490368 | tf_op jit(solution)/shard_map/psum | solution.py:91
  83.0 1.0 copy-start.2
  85.3 2.2 copy-start.6
  85.3 2.2 copy-start.7
  87.5 2.5 %copy-start.13 = (bf16[128,1024]{1,0:T(8,128)(2,1)S(1)}, bf16[128,1024]{1,0:T(8,128)(2,1)}, u32[]{:S(2)}) copy-start(bf16[128,1024]{1,0:T(8,128)(2,1)} %param.18) | copy-start | bytes 786436
  87.5 2.5 %copy-start.14 = (f32[1024]{0:T(1024)S(1)}, f32[1024]{0:T(1024)}, u32[]{:S(2)}) copy-start(f32[1024]{0:T(1024)} %param.19) | copy-start | bytes 12292
  90.0 4.9 %copy-start.4 = (bf16[4,4,128,128]{3,2,1,0:T(8,128)(2,1)}, bf16[4,4,128,128]{3,2,1,0:T(8,128)(2,1)S(1)}, u32[]{:S(2)}) copy-start(bf16[4,4,128,128]{3,2,1,0:T(8,128)(2,1)S(1)} %fusion.5) | copy-start | bytes 1572868
  90.0 4.8 %copy-start.11 = (bf16[1024,172]{0,1:T(8,128)(2,1)S(1)}, bf16[1024,172]{0,1:T(8,128)(2,1)}, u32[]{:S(2)}) copy-start(bf16[1024,172]{0,1:T(8,128)(2,1)} %param.20) | copy-start | bytes 1056772
  90.0 4.8 %copy-start.15 = (f32[172]{0:T(256)S(1)}, f32[172]{0:T(256)}, u32[]{:S(2)}) copy-start(f32[172]{0:T(256)} %param.21) | copy-start | bytes 2068
  94.8 2.0 copy-start.16
  104.8 1.4 copy-start.1
  106.1 2.2 copy-start.17
  108.3 1.8 copy-start.12
  110.1 6.6 %copy-start.5 = (bf16[4,4,128,128]{3,2,1,0:T(8,128)(2,1)S(1)}, bf16[4,4,128,128]{3,2,1,0:T(8,128)(2,1)}, u32[]{:S(2)}) copy-start(bf16[4,4,128,128]{3,2,1,0:T(8,128)(2,1)} %copy-done.4) | copy-start | bytes 1572868
  118.3 116.9 %all-reduce.9.cloned.1.call-start = ((), (), s32[]{:S(2)}) async-start(), calls=%async_computation.3 | async-start | bytes 2490368 | tf_op jit(solution)/shard_map/psum | solution.py:92
Sparse Core Ops, SparseCore 0:
  118.4 58.7 all-reduce.6
  180.3 54.8 all-reduce.8
where the time goes:
time: 247 us; the launch traced here: 246 us
  waiting for transfers between devices  143 us (58%)
  blocking collectives  24.5 us (10%)
  local copies, waits for them, and re-layouts  23.7 us (10%)
  matrix products  21.8 us (9%)
  between operations  14.3 us (6%)
  starting transfers between devices  9.96 us (4%)
  other arithmetic  8.44 us (3%)
    psum x1, waiting for transfers between devices, per_device(): inside = lax.psum((grad_w1, grad_b1, grad_w2, grad_b2), 'dom')  58.8 us
    all_to_all x2, waiting for transfers between devices, per_device(): lax.all_to_all(outgoing, 'dom', split_axis=0, concat_axis=0, tiled=True)  50.9 us
    psum x1, waiting for transfers between devices, per_device(): lax.psum((inside[0], inside[1], inside[2], inside[3]), 'dp')  33.6 us
    psum x1, blocking collectives, per_device(): inside = lax.psum((grad_w1, grad_b1, grad_w2, grad_b2), 'dom')  13.9 us
    psum x1, blocking collectives, per_device(): lax.psum((inside[0], inside[1], inside[2], inside[3]), 'dp')  10.5 us
    all_to_all x2, starting transfers between devices, per_device(): lax.all_to_all(outgoing, 'dom', split_axis=0, concat_axis=0, tiled=True)  9.88 us
    unnamed x38, local copies, waits for them, and re-layouts  8.84 us
    dot_general x1, matrix products, mlp_grads(): dact = jnp.dot(dlog_b, weight_out.T, preferred_element_type=jnp.float32)  6.59 us
  transfers between devices with their start and end apart: 4, of which 4 were waited for; matrix products, arithmetic and copies ran while one was open for 1% of the time, Pallas kernels for 0%

commit v1 on v0

v1 whole, which is shorter than its diff:
```python
import functools

import jax
import jax.numpy as jnp
from jax import lax
from jax.experimental import pallas as pl
from jax.experimental.pallas import tpu as pltpu
from jax.sharding import PartitionSpec as P

ORDER = 2
KEEP_RATE = 0.5
XBAR_SCALE = 1.0 / ((ORDER + 1) * KEEP_RATE)
F32, BF16, I16, I32 = jnp.float32, jnp.bfloat16, jnp.int16, jnp.int32
VMEM_LIMIT = 50 * 1024 * 1024
SMEM = pl.BlockSpec(memory_space=pltpu.SMEM)
VMEM = pl.BlockSpec(memory_space=pltpu.VMEM)
CHUNK = 256
TAIL = 8


def call(kernel, outs, ins, scratch=(), n_smem=0):
    return pl.pallas_call(
        kernel,
        out_shape=outs,
        in_specs=[SMEM] * n_smem + [VMEM] * (len(ins) - n_smem),
        out_specs=jax.tree.map(lambda _: VMEM, outs),
        scratch_shapes=list(scratch),
        compiler_params=pltpu.CompilerParams(vmem_limit_bytes=VMEM_LIMIT),
    )(*ins)


def like(shape, dtype):
    return jax.ShapeDtypeStruct(shape, dtype)


def select_kernel(info, serve, feats, masks, *msgs):
    tile = feats.shape[1]
    samples = masks.shape[0]
    for k in range(1, len(msgs) + 1):
        t = serve[info[0] ^ k]
        out = msgs[k - 1]
        out[:tile, :] = feats[t]
        m = masks[:, pl.ds(pl.multiple_of(t * tile, tile), tile)]
        out[tile:, :] = jnp.concatenate([m, jnp.zeros((out.shape[0] - tile - samples, tile), BF16)], 0)


def pool_index(info, serve, slots, r, j, dom, nnz):
    q = slots[r * nnz + j]
    k = q ^ info[0]
    own = (dom - 1) + serve[info[0]]
    return jnp.where(q >= dom, q - 1, jnp.where(k == 0, own, k - 1))


def hop_rows(info, serve, slots, adj, pool, r, dom):
    nnz = adj.shape[1]
    lhs = jnp.concatenate([adj[r, j] for j in range(nnz)], 1)
    rhs = jnp.concatenate([pool[pool_index(info, serve, slots, r, j, dom, nnz)] for j in range(nnz)], 0)
    return jnp.dot(lhs, rhs, preferred_element_type=F32)


def hop1_kernel(dom, info, serve, slots, feats, masks, adj, *refs):
    msgs, (cur, total), outs, pool = refs[: dom - 1], refs[dom - 1 : dom + 1], refs[dom + 1 : -1], refs[-1]
    tiles, tile, feat = feats.shape
    samples = masks.shape[0]

    def put(at, f, m):
        cols = jnp.concatenate([m.astype(F32), jnp.zeros((8 - samples, tile), F32)], 0).T
        f = f.astype(F32)
        for s in range(samples):
            pool[at, :, s * feat : (s + 1) * feat] = (f * cols[:, s : s + 1]).astype(BF16)

    for k in range(dom - 1):
        put(k, msgs[k][:tile, :], msgs[k][tile : tile + samples, :])
    for t in range(tiles):
        put(dom - 1 + t, feats[t], masks[:, t * tile : (t + 1) * tile])
    for r in range(tiles):
        hop = hop_rows(info, serve, slots, adj, pool, r, dom)
        cur[r] = hop.astype(BF16)
        total[r] = hop + pool[dom - 1 + r].astype(F32)
    for k in range(1, dom):
        outs[k - 1][...] = cur[serve[info[0] ^ k]]


def mlp_kernel(dom, samples, classes, scale, info, serve, slots, adj, cur, total, code, w_in, b_in, w_out, w_out_t, b_out, *refs):
    recv = refs[: dom - 1]
    keep, send, pool, x_t, act, slope, dl, dl_t, dpre, acc, bias_acc, cls_acc = refs[dom - 1 :]
    tiles, tile, lanes = cur.shape
    feat = lanes // samples
    hidden = w_in.shape[1]
    wide = w_out.shape[1]
    rows = samples * tile
    nch = hidden // CHUNK
    for k in range(dom - 1):
        pool[k] = recv[k][...]
    for t in range(tiles):
        pool[dom - 1 + t] = cur[t]
    bias_acc[...] = jnp.zeros(bias_acc.shape, F32)
    cls_acc[...] = jnp.zeros(cls_acc.shape, F32)

    def one_tile(r, carry):
        hop = hop_rows(info, serve, slots, adj, pool, r, dom)
        xbar = ((total[r] + hop) * XBAR_SCALE).astype(BF16)
        base = pl.multiple_of(r * rows, rows)
        logits = []
        for s in range(samples):
            x = xbar[:, s * feat : (s + 1) * feat]
            x_t[:, pl.ds(base + s * tile, tile)] = x.T
            for n in range(nch):
                cols = slice(n * CHUNK, (n + 1) * CHUNK)
                pre = jnp.dot(x, w_in[:, cols], preferred_element_type=F32) + b_in[:, cols]
                den = 1.0 + jnp.exp(jnp.minimum(-pre, 87.0))
                g = pl.reciprocal(den, approx=True)
                g = g * (2.0 - den * g)
                silu = pre * g
                act[pl.ds(base + s * tile, tile), cols] = silu.astype(BF16)
                slope[s * tile : (s + 1) * tile, cols] = g + silu * (1.0 - g)
            logits.append(
                jnp.dot(act[pl.ds(base + s * tile, tile), :], w_out[...], preferred_element_type=F32) + b_out[...]
            )
        step = 32
        for c in range(0, tile, step):
            prob = []
            for s in range(samples):
                e = jnp.exp(logits[s][c : c + step])
                prob.append(e / jnp.sum(e, -1, keepdims=True))
            avg = sum(prob[1:], prob[0]) * (1.0 / samples)
            sq = avg * avg
            sharp = sq / jnp.sum(sq, -1, keepdims=True)
            label = code[r, c : c + step, :]
            hit = (lax.broadcasted_iota(I32, (step, wide), 1) == label).astype(F32)
            used = (label >= 0).astype(F32)
            part = jnp.zeros((step, wide), F32)
            for s in range(samples):
                p = prob[s]
                push = 2.0 * (p - sharp)
                inner = jnp.sum(push * p, -1, keepdims=True)
                d = (used * p - hit + p * (push - inner)) * scale
                part = part + d
                dl[s * tile + c : s * tile + c + step, :] = d.astype(BF16)
            cls_acc[...] += functools.reduce(lambda a, b: a + b, [part[i : i + 8] for i in range(0, step, 8)])
        for s in range(samples):
            d = dl[s * tile : (s + 1) * tile, :]
            dl_t[:, pl.ds(base + s * tile, tile)] = d.T[: dl_t.shape[0]]
            for n in range(nch):
                cols = slice(n * CHUNK, (n + 1) * CHUNK)
                dact = jnp.dot(d, w_out_t[:, cols], preferred_element_type=F32)
                dp = dact * slope[s * tile : (s + 1) * tile, cols]
                dpre[pl.ds(base + s * tile, tile), cols] = dp.astype(BF16)
                bias_acc[:, cols] += functools.reduce(lambda a, b: a + b, [dp[i : i + 8] for i in range(0, tile, 8)])
        return carry

    lax.fori_loop(0, tiles, one_tile, 0)
    lanes_out = acc.shape[2]
    wide_t = dl_t.shape[0]
    cls = jnp.sum(cls_acc[...], 0, keepdims=True)
    for n in range(nch):
        cols = slice(n * CHUNK, (n + 1) * CHUNK)
        g_in = jnp.dot(x_t[...], dpre[:, cols], preferred_element_type=F32)
        g_out = jnp.dot(dl_t[...], act[:, cols], preferred_element_type=F32)
        g_bias = jnp.sum(bias_acc[:, cols], 0, keepdims=True)
        for i in range(CHUNK // lanes_out):
            at = n * (CHUNK // lanes_out) + i
            part = slice(i * lanes_out, (i + 1) * lanes_out)
            acc[at, :feat, :] = g_in[:, part]
            acc[at, feat : feat + wide_t, :] = g_out[:, part]
            acc[at, feat + wide_t :, :] = jnp.concatenate(
                [g_bias[:, part]]
                + [cls[:, i * lanes_out : (i + 1) * lanes_out] for i in range(wide // lanes_out)]
                + [jnp.zeros((TAIL - 1 - wide // lanes_out, lanes_out), F32)],
                0,
            )
    for m in range(keep.shape[0]):
        pair = (info[1] ^ m) * 2
        keep[m] = acc[pair + info[2]]
        send[m] = acc[pair + 1 - info[2]]


def encode(x, feat, n_tail):
    body = x.shape[0] - TAIL
    parts = [x[:feat], x[feat:body]] + [x[body + i : body + i + 1] for i in range(n_tail)]
    ints, exps = [], []
    for p in parts:
        top = jnp.max(jnp.abs(p), 0, keepdims=True)
        e = jnp.floor(jnp.log2(jnp.maximum(top, 1e-30)))
        q = jnp.round(p * jnp.exp2(14.0 - e))
        ints.append(jnp.clip(q, -32767.0, 32767.0).astype(I32))
        exps.append(e.astype(I32))
    used = 2 * n_tail + 2
    last = ints[2:] + exps + [jnp.zeros((2 * TAIL - used, x.shape[1]), I32)]
    return jnp.concatenate(ints[:2] + [jnp.concatenate(last, 0)], 0).astype(I16)


def decode(ref, feat, n_tail):
    body = ref.shape[0] - 2 * TAIL
    v = ref[...].astype(I32).astype(F32)
    last = v[body:]
    scales = jnp.exp2(last[n_tail : 2 * n_tail + 2] - 14.0)
    tail = jnp.concatenate(
        [last[:n_tail] * scales[2:], jnp.zeros((TAIL - n_tail, v.shape[1]), F32)], 0
    )
    return jnp.concatenate([v[:feat] * scales[0:1], v[feat:body] * scales[1:2], tail], 0)


def pair_kernel(feat, n_tail, keep, recv, own, *msgs):
    own[...] = keep[0] + recv[0]
    for m in range(1, keep.shape[0]):
        msgs[m - 1][...] = encode(keep[m] + recv[m], feat, n_tail)


def scatter_kernel(feat, n_tail, own, *refs):
    total = own[...]
    for ref in refs[:-1]:
        total = total + decode(ref, feat, n_tail)
    refs[-1][...] = encode(total, feat, n_tail)


def tree_kernel(feat, n_tail, *refs):
    parts = [decode(ref, feat, n_tail) for ref in refs[:-1]]
    while len(parts) > 1:
        parts = [a + b for a, b in zip(parts[::2], parts[1::2])]
    refs[-1][...] = encode(parts[0], feat, n_tail)


def unpack_kernel(feat, n_tail, classes, info, *refs):
    pieces, (g_in, b_in, g_out, b_out) = refs[:-4], refs[-4:]
    lanes = pieces[0].shape[1]
    half = len(pieces) // 2
    body = pieces[0].shape[0] - 2 * TAIL
    for c in range(2):
        for m in range(half):
            at = (info[1] ^ m) * 2 + (info[2] ^ c)
            x = decode(pieces[c * half + m], feat, n_tail)
            where = pl.ds(pl.multiple_of(at * lanes, lanes), lanes)
            g_in[:, where] = x[:feat]
            g_out[:, where] = x[feat : feat + classes]
            b_in[:, where] = x[body : body + 1]

            @pl.when(at == 0)
            def _():
                for i in range(n_tail - 1):
                    b_out[:, i * lanes : (i + 1) * lanes] = x[body + 1 + i : body + 2 + i]


def xor_permute(x, axis, mask):
    return lax.ppermute(x, axis, [(i, i ^ mask) for i in range(lax.axis_size(axis))])


def bit_groups(axis, first):
    size, bit, groups = lax.axis_size(axis), first, []
    while (1 << bit) < size:
        groups.append([m << bit for m in (1, 2, 3) if (m << bit) < size])
        bit += 2
    return groups


def reduce_grads(keep, send, info, feat, n_tail, classes, hidden):
    count, rows, lanes = keep.shape
    coded = like((rows + TAIL, lanes), I16)
    recv = xor_permute(send, "dom", 1)
    own, *msgs = call(
        functools.partial(pair_kernel, feat, n_tail),
        [like((rows, lanes), F32)] + [coded] * (count - 1),
        [keep, recv],
    )
    msgs = [xor_permute(x, "dp", m + 1) for m, x in enumerate(msgs)]
    q = call(functools.partial(scatter_kernel, feat, n_tail), coded, [own] + msgs)
    for axis, groups in (("dom", bit_groups("dom", 1)), ("dp", bit_groups("dp", 2))):
        for masks in groups:
            got = [xor_permute(q, axis, m) for m in masks]
            q = call(functools.partial(tree_kernel, feat, n_tail), coded, [q] + got)
    pieces = [q] + [xor_permute(q, "dp", m) for m in range(1, count)]
    pieces = pieces + [xor_permute(x, "dom", 1) for x in pieces]
    return call(
        functools.partial(unpack_kernel, feat, n_tail, classes),
        [like((feat, hidden), F32), like((1, hidden), F32), like((classes, hidden), F32), like((1, (n_tail - 1) * lanes), F32)],
        [info] + pieces,
        n_smem=1,
    )


def per_device(
    features,
    keep_masks,
    serve_ids,
    col_slot,
    adj_blocks,
    node_labels,
    labeled,
    weight_in,
    bias_in,
    weight_out,
    bias_out,
):
    tiles, nnz = col_slot.shape[1:]
    tile = adj_blocks.shape[-1]
    feat = features.shape[-1]
    samples = keep_masks.shape[1]
    hidden, classes = weight_out.shape
    dom = lax.axis_size("dom")
    me = lax.axis_index("dom")
    info = jnp.stack([me, lax.axis_index("dp") & 3, me & 1]).astype(I32)
    serve = serve_ids.reshape(-1)
    slots = col_slot.reshape(-1)
    adj = adj_blocks[0]
    feats = features.reshape(tiles, tile, feat)
    masks = keep_masks[0]
    lanes = samples * feat
    wide = -(-classes // 128) * 128

    msgs = call(
        select_kernel, [like((tile + 16, feat), BF16)] * (dom - 1), [info, serve, feats, masks], n_smem=2
    )
    msgs = [xor_permute(x, "dom", k + 1) for k, x in enumerate(msgs)]
    cur, total, *outs = call(
        functools.partial(hop1_kernel, dom),
        [like((tiles, tile, lanes), BF16), like((tiles, tile, lanes), F32)] + [like((tile, lanes), BF16)] * (dom - 1),
        [info, serve, slots, feats, masks, adj] + msgs,
        [pltpu.VMEM((dom - 1 + tiles, tile, lanes), BF16)],
        n_smem=3,
    )
    outs = [xor_permute(x, "dom", k + 1) for k, x in enumerate(outs)]

    code = jnp.where(labeled != 0, node_labels, -1).reshape(tiles, tile, 1)
    w_out = jnp.pad(weight_out, ((0, 0), (0, wide - classes)))
    b_out = jnp.pad(bias_out, (0, wide - classes), constant_values=-1e30).reshape(1, wide)
    rows = samples * tile
    all_rows = rows * tiles
    wide_t = -(-classes // 16) * 16
    piece = (feat + wide_t + TAIL, 128)
    pieces = hidden // 128
    keep, send = call(
        functools.partial(mlp_kernel, dom, samples, classes, 1.0 / (samples * tiles * tile)),
        [like((pieces // 2,) + piece, F32)] * 2,
        [info, serve, slots, adj, cur, total, code, weight_in, bias_in.reshape(1, hidden), w_out, w_out.T, b_out] + outs,
        [
            pltpu.VMEM((dom - 1 + tiles, tile, lanes), BF16),
            pltpu.VMEM((feat, all_rows), BF16),
            pltpu.VMEM((all_rows, hidden), BF16),
            pltpu.VMEM((rows, hidden), F32),
            pltpu.VMEM((rows, wide), BF16),
            pltpu.VMEM((wide_t, all_rows), BF16),
            pltpu.VMEM((all_rows, hidden), BF16),
            pltpu.VMEM((pieces,) + piece, F32),
            pltpu.VMEM((8, hidden), F32),
            pltpu.VMEM((8, wide), F32),
        ],
        n_smem=3,
    )
    g_in, b_in, g_out, b_out = reduce_grads(keep, send, info, feat, 1 + wide // 128, classes, hidden)
    return g_in, b_in.reshape(hidden), g_out.T, b_out.reshape(-1)[:classes]


def solution(mesh):
    placed = (
        P("dp", "dom", None),
        P("dp", None, "dom"),
        P("dp", "dom", None, None),
        P("dp", "dom", None),
        P("dp", "dom", None, None, None),
        P("dp", "dom"),
        P("dp", "dom"),
        P(),
        P(),
        P(),
        P(),
    )
    return jax.shard_map(
        per_device, mesh=mesh, in_specs=placed, out_specs=(P(), P(), P(), P()), check_vma=False
    )
```

time: 247 us -> 92.8 us (0.38)
  waiting for transfers between devices: 143 us -> 36.8 us
  blocking collectives: 24.5 us -> 0 us
  matrix products: 21.8 us -> 0 us
  starting transfers between devices: 9.96 us -> 30.6 us
  Pallas kernels: 0 us -> 18.4 us
  local copies, waits for them, and re-layouts: 23.7 us -> 5.75 us
  between operations: 14.3 us -> 0.82 us
  other arithmetic: 8.44 us -> 0.08 us
    psum x2 -> x0, waiting for transfers between devices: 92.4 us -> none  [the longest x1 58.8 us: per_device(): inside = lax.psum((grad_w1, grad_b1, grad_w2, grad_b2), 'dom')]
    all_to_all x2 -> x0, waiting for transfers between devices: 50.9 us -> none  [per_device(): lax.all_to_all(outgoing, 'dom', split_axis=0, concat_axis=0, tiled=True)]
    ppermute x0 -> x28, waiting for transfers between devices: none -> 36.8 us  [xor_permute(): lax.ppermute(x, axis, [(i, i ^ mask) for i in range(lax.axis_size(axis))])]
    ppermute x0 -> x28, starting transfers between devices: none -> 30.6 us  [xor_permute(): lax.ppermute(x, axis, [(i, i ^ mask) for i in range(lax.axis_size(axis))])]
    psum x2 -> x0, blocking collectives: 24.5 us -> none  [the longest x1 13.9 us: per_device(): inside = lax.psum((grad_w1, grad_b1, grad_w2, grad_b2), 'dom')]
    dot_general x7 -> x0, matrix products: 21.8 us -> none  [the longest x1 6.59 us: mlp_grads(): dact = jnp.dot(dlog_b, weight_out.T, preferred_element_type=jnp.float32)]
    pallas_call x0 -> x7, Pallas kernels: none -> 18.4 us  [call(): pl.pallas_call(kernel, out_shape=outs, in_specs=[SMEM] * n_smem + [VMEM]...]
    all_to_all x2 -> x0, starting transfers between devices: 9.88 us -> none  [per_device(): lax.all_to_all(outgoing, 'dom', split_axis=0, concat_axis=0, tiled=True)]
  transfers between devices with their start and end apart: 4 -> 28, of which waited for: 4 -> 17; matrix products, arithmetic and copies ran while one was open for 1% -> 1% of each run, Pallas kernels for 0% -> 0%
where the time goes in v1:
time: 92.8 us; the launch traced here: 92.4 us
  waiting for transfers between devices  36.8 us (40%)
  starting transfers between devices  30.6 us (33%)
  Pallas kernels  18.4 us (20%)
  local copies, waits for them, and re-layouts  5.75 us (6%)
    ppermute x28, waiting for transfers between devices, xor_permute(): lax.ppermute(x, axis, [(i, i ^ mask) for i in range(lax.axis_size(axis))])  36.8 us
    ppermute x28, starting transfers between devices, xor_permute(): lax.ppermute(x, axis, [(i, i ^ mask) for i in range(lax.axis_size(axis))])  30.6 us
    pallas_call x7, Pallas kernels, call(): pl.pallas_call(kernel, out_shape=outs, in_specs=[SMEM] * n_smem + [VMEM]...  18.4 us
    unnamed x31, local copies, waits for them, and re-layouts  5.39 us
  transfers between devices with their start and end apart: 28, of which 17 were waited for; matrix products, arithmetic and copies ran while one was open for 1% of the time, Pallas kernels for 0%

profile of v1, /device:TPU:0, one launch (start us, length us, event | category | flops | bytes accessed | tf_op | source)
XLA Modules:
  0.0 92.4 jit_solution(3875354377552183364)
XLA Ops:
  1.4 0.9 copy-done.4
  3.4 2.6 %collective-permute-start.1 = (bf16[144,128]{1,0:T(8,128)(2,1)S(1)}, bf16[144,128]{1,0:T(8,128)(2,1)S(1)}, u32[]{:S(2)}, u32[]{:S(2)}) collective-permute-start(bf16[144,128]{1,0:T(8,128)(2,1)S(1)} %get-tuple-element.31), channel_id=1, source_target_pairs={{0,2},{1,3},{2,0},{3,1},{4,6},{5,7},{6,4},{7,5},{8,10},{9,11},{10,... | collective-permute-start | bytes 110600 | tf_op jit(solution)/shard_map/ppermute | solution.py:245
  6.1 2.8 %collective-permute-start.3 = (bf16[144,128]{1,0:T(8,128)(2,1)S(1)}, bf16[144,128]{1,0:T(8,128)(2,1)S(1)}, u32[]{:S(2)}, u32[]{:S(2)}) collective-permute-start(bf16[144,128]{1,0:T(8,128)(2,1)S(1)} %get-tuple-element.33), channel_id=1, source_target_pairs={{0,4},{1,5},{2,6},{3,7},{4,0},{5,1},{6,2},{7,3},{8,12},{9,13},{10,... | collective-permute-start | bytes 110600 | tf_op jit(solution)/shard_map/ppermute | solution.py:245
  8.9 3.6 %collective-permute-start.5 = (bf16[144,128]{1,0:T(8,128)(2,1)S(1)}, bf16[144,128]{1,0:T(8,128)(2,1)S(1)}, u32[]{:S(2)}, u32[]{:S(2)}) collective-permute-start(bf16[144,128]{1,0:T(8,128)(2,1)S(1)} %get-tuple-element.35), channel_id=1, source_target_pairs={{0,6},{1,7},{2,4},{3,5},{4,2},{5,3},{6,0},{7,1},{8,14},{9,15},{10,... | collective-permute-start | bytes 110600 | tf_op jit(solution)/shard_map/ppermute | solution.py:245
  13.3 2.1 %collective-permute-done.5.refs_5_ = bf16[144,128]{1,0:T(8,128)(2,1)S(1)} collective-permute-done((bf16[144,128]{1,0:T(8,128)(2,1)S(1)}, bf16[144,128]{1,0:T(8,128)(2,1)S(1)}, u32[]{:S(2)}, u32[]{:S(2)}) %collective-permute-start.5) | collective-permute-done | bytes 36896 | tf_op jit(solution)/shard_map/ppermute | solution.py:245
  15.4 2.3 %collective-permute-done.6.refs_6_ = bf16[144,128]{1,0:T(8,128)(2,1)S(1)} collective-permute-done((bf16[144,128]{1,0:T(8,128)(2,1)S(1)}, bf16[144,128]{1,0:T(8,128)(2,1)S(1)}, u32[]{:S(2)}, u32[]{:S(2)}) %collective-permute-start.6) | collective-permute-done | bytes 36896 | tf_op jit(solution)/shard_map/ppermute | solution.py:245
  17.7 1.0 %copy-done = bf16[1,4,4,128,128]{4,3,2,1,0:T(8,128)(2,1)S(1)} copy-done((bf16[1,4,4,128,128]{4,3,2,1,0:T(8,128)(2,1)S(1)}, bf16[1,4,4,128,128]{4,3,2,1,0:T(8,128)(2,1)}, u32[]{:S(2)}) %copy-start) | copy-done | bytes 524312
  18.7 1.7 %shard_map.139 = (bf16[4,128,512]{2,1,0:T(8,128)(2,1)S(1)}, f32[4,128,512]{2,1,0:T(8,128)S(1)}, bf16[128,512]{1,0:T(8,128)(2,1)S(1)}, bf16[128,512]{1,0:T(8,128)...) custom-call(s32[3]{0:T(128)S(1)} %pad_add_fusion.info, ...), custom_call_target="tpu_custom_call" | custom-call | tf_op jit(solution)/shard_map/pallas_call | solution.py:22
  20.5 1.0 %copy-done.2 = f32[4,128,512]{2,1,0:T(8,128)} copy-done((f32[4,128,512]{2,1,0:T(8,128)}, f32[4,128,512]{2,1,0:T(8,128)S(1)}, u32[]{:S(2)}) %copy-start.2) | copy-done | bytes 1048600
  21.6 1.7 %collective-permute-start.9 = (bf16[128,512]{1,0:T(8,128)(2,1)S(1)}, bf16[128,512]{1,0:T(8,128)(2,1)S(1)}, u32[]{:S(2)}, u32[]{:S(2)}) collective-permute-start(bf16[128,512]{1,0:T(8,128)(2,1)S(1)} %get-tuple-element.41), channel_id=1, source_target_pairs={{0,3},{1,2},{2,1},{3,0},{4,7},{5,6},{6,5},{7,4},{8,11},{9,10},{10,... | collective-permute-start | bytes 393224 | tf_op jit(solution)/shard_map/ppermute | solution.py:245
  23.3 1.3 %collective-permute-start.10 = (bf16[128,512]{1,0:T(8,128)(2,1)S(1)}, bf16[128,512]{1,0:T(8,128)(2,1)S(1)}, u32[]{:S(2)}, u32[]{:S(2)}) collective-permute-start(bf16[128,512]{1,0:T(8,128)(2,1)S(1)} %get-tuple-element.42), channel_id=1, source_target_pairs={{0,4},{1,5},{2,6},{3,7},{4,0},{5,1},{6,2},{7,3},{8,12},{9,13},{10,... | collective-permute-start | bytes 393224 | tf_op jit(solution)/shard_map/ppermute | solution.py:245
  24.6 1.4 %collective-permute-start.11 = (bf16[128,512]{1,0:T(8,128)(2,1)S(1)}, bf16[128,512]{1,0:T(8,128)(2,1)S(1)}, u32[]{:S(2)}, u32[]{:S(2)}) collective-permute-start(bf16[128,512]{1,0:T(8,128)(2,1)S(1)} %get-tuple-element.43), channel_id=1, source_target_pairs={{0,5},{1,4},{2,7},{3,6},{4,1},{5,0},{6,3},{7,2},{8,13},{9,12},{10,... | collective-permute-start | bytes 393224 | tf_op jit(solution)/shard_map/ppermute | solution.py:245
  26.0 0.9 %collective-permute-start.12 = (bf16[128,512]{1,0:T(8,128)(2,1)S(1)}, bf16[128,512]{1,0:T(8,128)(2,1)S(1)}, u32[]{:S(2)}, u32[]{:S(2)}) collective-permute-start(bf16[128,512]{1,0:T(8,128)(2,1)S(1)} %get-tuple-element.44), channel_id=1, source_target_pairs={{0,6},{1,7},{2,4},{3,5},{4,2},{5,3},{6,0},{7,1},{8,14},{9,15},{10,... | collective-permute-start | bytes 393224 | tf_op jit(solution)/shard_map/ppermute | solution.py:245
  27.0 4.7 %collective-permute-done.8.refs_1_ = bf16[128,512]{1,0:T(8,128)(2,1)S(1)} collective-permute-done((bf16[128,512]{1,0:T(8,128)(2,1)S(1)}, bf16[128,512]{1,0:T(8,128)(2,1)S(1)}, u32[]{:S(2)}, u32[]{:S(2)}) %collective-permute-start.8) | collective-permute-done | bytes 131104 | tf_op jit(solution)/shard_map/ppermute | solution.py:245
  33.3 10.5 %collective-permute-done.11.refs_4_ = bf16[128,512]{1,0:T(8,128)(2,1)S(1)} collective-permute-done((bf16[128,512]{1,0:T(8,128)(2,1)S(1)}, bf16[128,512]{1,0:T(8,128)(2,1)S(1)}, u32[]{:S(2)}, u32[]{:S(2)}) %collective-permute-start.11) | collective-permute-done | bytes 131104 | tf_op jit(solution)/shard_map/ppermute | solution.py:245
  43.8 13.9 %shard_map.140 = (f32[4,312,128]{2,1,0:T(8,128)}, f32[4,312,128]{2,1,0:T(8,128)}) custom-call(s32[3]{0:T(128)S(1)} %pad_add_fusion.info, s32[8]{0:T(128)S(1)} %bitcast.24, s32[16]{0:T(128)S(1)} %reshape.32.slots, bf16[4,4,128,128]{3,2,1,0:T(8,128)(2,1)S(1)} %bitcast.17, bf16[4,128,512]{2,1,0:T(8,128)(2,1)S(1)} %get-tuple-element.37.cur, ...), custom_call_target="tpu_custom_call" | custom-call | tf_op jit(solution)/shard_map/pallas_call | solution.py:22
  58.3 1.9 %collective-permute-done.14.recv = f32[4,312,128]{2,1,0:T(8,128)S(1)} collective-permute-done((f32[4,312,128]{2,1,0:T(8,128)}, f32[4,312,128]{2,1,0:T(8,128)S(1)}, u32[]{:S(2)}, u32[]{:S(2)}) %collective-permute-start.14) | collective-permute-done | bytes 639008 | tf_op jit(solution)/shard_map/ppermute | solution.py:245
  60.3 1.1 %copy-done.3 = f32[4,312,128]{2,1,0:T(8,128)S(1)} copy-done((f32[4,312,128]{2,1,0:T(8,128)S(1)}, f32[4,312,128]{2,1,0:T(8,128)}, u32[]{:S(2)}) %copy-start.3) | copy-done | bytes 639000
  61.5 1.6 %collective-permute-start.15 = (s16[320,128]{1,0:T(8,128)(2,1)S(1)}, s16[320,128]{1,0:T(8,128)(2,1)S(1)}, u32[]{:S(2)}, u32[]{:S(2)}) collective-permute-start(s16[320,128]{1,0:T(8,128)(2,1)S(1)} %get-tuple-element.49), channel_id=1, source_target_pairs={{0,8},{8,0},{16,24},{24,16},{1,9},{9,1},{17,25},{25,17},{2,10},{10... | collective-permute-start | bytes 245768 | tf_op jit(solution)/shard_map/ppermute | solution.py:245
  63.1 1.5 %collective-permute-start.16 = (s16[320,128]{1,0:T(8,128)(2,1)S(1)}, s16[320,128]{1,0:T(8,128)(2,1)S(1)}, u32[]{:S(2)}, u32[]{:S(2)}) collective-permute-start(s16[320,128]{1,0:T(8,128)(2,1)S(1)} %get-tuple-element.50), channel_id=1, source_target_pairs={{0,16},{8,24},{16,0},{24,8},{1,17},{9,25},{17,1},{25,9},{2,18},{10... | collective-permute-start | bytes 245768 | tf_op jit(solution)/shard_map/ppermute | solution.py:245
  65.1 1.2 %collective-permute-done.15.refs_0_ = s16[320,128]{1,0:T(8,128)(2,1)S(1)} collective-permute-done((s16[320,128]{1,0:T(8,128)(2,1)S(1)}, s16[320,128]{1,0:T(8,128)(2,1)S(1)}, u32[]{:S(2)}, u32[]{:S(2)}) %collective-permute-start.15) | collective-permute-done | bytes 81952 | tf_op jit(solution)/shard_map/ppermute | solution.py:245
  66.3 2.1 %collective-permute-done.16.refs_1_ = s16[320,128]{1,0:T(8,128)(2,1)S(1)} collective-permute-done((s16[320,128]{1,0:T(8,128)(2,1)S(1)}, s16[320,128]{1,0:T(8,128)(2,1)S(1)}, u32[]{:S(2)}, u32[]{:S(2)}) %collective-permute-start.16) | collective-permute-done | bytes 81952 | tf_op jit(solution)/shard_map/ppermute | solution.py:245
  68.3 1.6 %collective-permute-done.17.refs_2_ = s16[320,128]{1,0:T(8,128)(2,1)S(1)} collective-permute-done((s16[320,128]{1,0:T(8,128)(2,1)S(1)}, s16[320,128]{1,0:T(8,128)(2,1)S(1)}, u32[]{:S(2)}, u32[]{:S(2)}) %collective-permute-start.17) | collective-permute-done | bytes 81952 | tf_op jit(solution)/shard_map/ppermute | solution.py:245
  70.1 1.1 %collective-permute-start.20 = (s16[320,128]{1,0:T(8,128)(2,1)S(1)}, s16[320,128]{1,0:T(8,128)(2,1)S(1)}, u32[]{:S(2)}, u32[]{:S(2)}) collective-permute-start(s16[320,128]{1,0:T(8,128)(2,1)S(1)} %shard_map.142.refs_0_), channel_id=1, source_target_pairs={{0,6},{1,7},{2,4},{3,5},{4,2},{5,3},{6,0},{7,1},{8,14},{9,15},{10,... | collective-permute-start | bytes 245768 | tf_op jit(solution)/shard_map/ppermute | solution.py:245
  71.2 6.2 %collective-permute-start.19 = (s16[320,128]{1,0:T(8,128)(2,1)S(1)}, s16[320,128]{1,0:T(8,128)(2,1)S(1)}, u32[]{:S(2)}, u32[]{:S(2)}) collective-permute-start(s16[320,128]{1,0:T(8,128)(2,1)S(1)} %shard_map.142.refs_0_), channel_id=1, source_target_pairs={{0,4},{1,5},{2,6},{3,7},{4,0},{5,1},{6,2},{7,3},{8,12},{9,13},{10,... | collective-permute-start | bytes 245768 | tf_op jit(solution)/shard_map/ppermute | solution.py:245
  77.4 4.5 %collective-permute-done.19.refs_2_ = s16[320,128]{1,0:T(8,128)(2,1)S(1)} collective-permute-done((s16[320,128]{1,0:T(8,128)(2,1)S(1)}, s16[320,128]{1,0:T(8,128)(2,1)S(1)}, u32[]{:S(2)}, u32[]{:S(2)}) %collective-permute-start.19) | collective-permute-done | bytes 81952 | tf_op jit(solution)/shard_map/ppermute | solution.py:245
  81.9 0.8 collective-permute-done.18.refs_1_
  82.8 0.9 collective-permute-start.23
  83.7 1.2 %collective-permute-start.22 = (s16[320,128]{1,0:T(8,128)(2,1)S(1)}, s16[320,128]{1,0:T(8,128)(2,1)S(1)}, u32[]{:S(2)}, u32[]{:S(2)}) collective-permute-start(s16[320,128]{1,0:T(8,128)(2,1)S(1)} %shard_map.143.refs_0_), channel_id=1, source_target_pairs={{0,16},{8,24},{16,0},{24,8},{1,17},{9,25},{17,1},{25,9},{2,18},{10... | collective-permute-start | bytes 245768 | tf_op jit(solution)/shard_map/ppermute | solution.py:245
  84.9 1.4 %collective-permute-start.21 = (s16[320,128]{1,0:T(8,128)(2,1)S(1)}, s16[320,128]{1,0:T(8,128)(2,1)S(1)}, u32[]{:S(2)}, u32[]{:S(2)}) collective-permute-start(s16[320,128]{1,0:T(8,128)(2,1)S(1)} %shard_map.143.refs_0_), channel_id=1, source_target_pairs={{0,8},{8,0},{16,24},{24,16},{1,9},{9,1},{17,25},{25,17},{2,10},{10... | collective-permute-start | bytes 245768 | tf_op jit(solution)/shard_map/ppermute | solution.py:245
  86.4 2.0 %collective-permute-done.23.refs_3_ = s16[320,128]{1,0:T(8,128)(2,1)S(1)} collective-permute-done((s16[320,128]{1,0:T(8,128)(2,1)S(1)}, s16[320,128]{1,0:T(8,128)(2,1)S(1)}, u32[]{:S(2)}, u32[]{:S(2)}) %collective-permute-start.23) | collective-permute-done | bytes 81952 | tf_op jit(solution)/shard_map/ppermute | solution.py:245
  90.6 1.8 %shard_map.144 = (f32[128,1024]{1,0:T(8,128)}, f32[1,1024]{1,0:T(1,128)}, f32[172,1024]{1,0:T(8,128)}, f32[1,256]{1,0:T(1,128)}) custom-call(s32[3]{0:T(128)S(1)} %pad_add_fusion.info, s16[320,128]{1,0:T(8,128)(2,1)S(1)} %shard_map.143.refs_0_, s16[320,128]{1,0:T(8,128)(2,1)S(1)} %collective-permute-done.21.refs_1_, ...), custom_call_target="tpu_custom_call" | custom-call | tf_op jit(solution)/shard_map/pallas_call | solution.py:22
  (69 shorter events, 8.4 us)
Async XLA Ops:
  2.3 15.4 %copy-start.5 = (bf16[1,512,128]{2,1,0:T(8,128)(2,1)S(1)}, bf16[1,512,128]{2,1,0:T(8,128)(2,1)}, u32[]{:S(2)}) copy-start(bf16[1,512,128]{2,1,0:T(8,128)(2,1)} %param.11) | copy-start | bytes 393220
  2.9 6.0 %collective-permute-start = (bf16[144,128]{1,0:T(8,128)(2,1)S(1)}, bf16[144,128]{1,0:T(8,128)(2,1)S(1)}, u32[]{:S(2)}, u32[]{:S(2)}) collective-permute-start(bf16[144,128]{1,0:T(8,128)(2,1)S(1)} %get-tuple-element.30), channel_id=1, source_target_pairs={{0,1},{1,0},{2,3},{3,2},{4,5},{5,4},{6,7},{7,6},{8,9},{9,8},{10,11... | collective-permute-start | bytes 110600 | tf_op jit(solution)/shard_map/ppermute | solution.py:245
  3.4 9.1 %collective-permute-start.1 = (bf16[144,128]{1,0:T(8,128)(2,1)S(1)}, bf16[144,128]{1,0:T(8,128)(2,1)S(1)}, u32[]{:S(2)}, u32[]{:S(2)}) collective-permute-start(bf16[144,128]{1,0:T(8,128)(2,1)S(1)} %get-tuple-element.31), channel_id=1, source_target_pairs={{0,2},{1,3},{2,0},{3,1},{4,6},{5,7},{6,4},{7,5},{8,10},{9,11},{10,... | collective-permute-start | bytes 110600 | tf_op jit(solution)/shard_map/ppermute | solution.py:245
  6.0 6.6 %collective-permute-start.2 = (bf16[144,128]{1,0:T(8,128)(2,1)S(1)}, bf16[144,128]{1,0:T(8,128)(2,1)S(1)}, u32[]{:S(2)}, u32[]{:S(2)}) collective-permute-start(bf16[144,128]{1,0:T(8,128)(2,1)S(1)} %get-tuple-element.32), channel_id=1, source_target_pairs={{0,3},{1,2},{2,1},{3,0},{4,7},{5,6},{6,5},{7,4},{8,11},{9,10},{10,... | collective-permute-start | bytes 110600 | tf_op jit(solution)/shard_map/ppermute | solution.py:245
  6.1 6.6 %collective-permute-start.3 = (bf16[144,128]{1,0:T(8,128)(2,1)S(1)}, bf16[144,128]{1,0:T(8,128)(2,1)S(1)}, u32[]{:S(2)}, u32[]{:S(2)}) collective-permute-start(bf16[144,128]{1,0:T(8,128)(2,1)S(1)} %get-tuple-element.33), channel_id=1, source_target_pairs={{0,4},{1,5},{2,6},{3,7},{4,0},{5,1},{6,2},{7,3},{8,12},{9,13},{10,... | collective-permute-start | bytes 110600 | tf_op jit(solution)/shard_map/ppermute | solution.py:245
  8.9 4.4 %collective-permute-start.4 = (bf16[144,128]{1,0:T(8,128)(2,1)S(1)}, bf16[144,128]{1,0:T(8,128)(2,1)S(1)}, u32[]{:S(2)}, u32[]{:S(2)}) collective-permute-start(bf16[144,128]{1,0:T(8,128)(2,1)S(1)} %get-tuple-element.34), channel_id=1, source_target_pairs={{0,5},{1,4},{2,7},{3,6},{4,1},{5,0},{6,3},{7,2},{8,13},{9,12},{10,... | collective-permute-start | bytes 110600 | tf_op jit(solution)/shard_map/ppermute | solution.py:245
  8.9 6.6 %collective-permute-start.5 = (bf16[144,128]{1,0:T(8,128)(2,1)S(1)}, bf16[144,128]{1,0:T(8,128)(2,1)S(1)}, u32[]{:S(2)}, u32[]{:S(2)}) collective-permute-start(bf16[144,128]{1,0:T(8,128)(2,1)S(1)} %get-tuple-element.35), channel_id=1, source_target_pairs={{0,6},{1,7},{2,4},{3,5},{4,2},{5,3},{6,0},{7,1},{8,14},{9,15},{10,... | collective-permute-start | bytes 110600 | tf_op jit(solution)/shard_map/ppermute | solution.py:245
  12.5 5.2 %collective-permute-start.6 = (bf16[144,128]{1,0:T(8,128)(2,1)S(1)}, bf16[144,128]{1,0:T(8,128)(2,1)S(1)}, u32[]{:S(2)}, u32[]{:S(2)}) collective-permute-start(bf16[144,128]{1,0:T(8,128)(2,1)S(1)} %get-tuple-element.36), channel_id=1, source_target_pairs={{0,7},{1,6},{2,5},{3,4},{4,3},{5,2},{6,1},{7,0},{8,15},{9,14},{10,... | collective-permute-start | bytes 110600 | tf_op jit(solution)/shard_map/ppermute | solution.py:245
  18.7 13.1 %copy-start.10 = (bf16[1024,172]{0,1:T(8,128)(2,1)S(1)}, bf16[1024,172]{0,1:T(8,128)(2,1)}, u32[]{:S(2)}) copy-start(bf16[1024,172]{0,1:T(8,128)(2,1)} %param.20) | copy-start | bytes 1056772
  21.5 4.6 %collective-permute-start.7 = (bf16[128,512]{1,0:T(8,128)(2,1)S(1)}, bf16[128,512]{1,0:T(8,128)(2,1)S(1)}, u32[]{:S(2)}, u32[]{:S(2)}) collective-permute-start(bf16[128,512]{1,0:T(8,128)(2,1)S(1)} %get-tuple-element.39), channel_id=1, source_target_pairs={{0,1},{1,0},{2,3},{3,2},{4,5},{5,4},{6,7},{7,6},{8,9},{9,8},{10,11... | collective-permute-start | bytes 393224 | tf_op jit(solution)/shard_map/ppermute | solution.py:245
  21.6 10.0 %collective-permute-start.8 = (bf16[128,512]{1,0:T(8,128)(2,1)S(1)}, bf16[128,512]{1,0:T(8,128)(2,1)S(1)}, u32[]{:S(2)}, u32[]{:S(2)}) collective-permute-start(bf16[128,512]{1,0:T(8,128)(2,1)S(1)} %get-tuple-element.40), channel_id=1, source_target_pairs={{0,2},{1,3},{2,0},{3,1},{4,6},{5,7},{6,4},{7,5},{8,10},{9,11},{10,... | collective-permute-start | bytes 393224 | tf_op jit(solution)/shard_map/ppermute | solution.py:245
  21.6 11.6 %collective-permute-start.9 = (bf16[128,512]{1,0:T(8,128)(2,1)S(1)}, bf16[128,512]{1,0:T(8,128)(2,1)S(1)}, u32[]{:S(2)}, u32[]{:S(2)}) collective-permute-start(bf16[128,512]{1,0:T(8,128)(2,1)S(1)} %get-tuple-element.41), channel_id=1, source_target_pairs={{0,3},{1,2},{2,1},{3,0},{4,7},{5,6},{6,5},{7,4},{8,11},{9,10},{10,... | collective-permute-start | bytes 393224 | tf_op jit(solution)/shard_map/ppermute | solution.py:245
  23.3 9.9 %collective-permute-start.10 = (bf16[128,512]{1,0:T(8,128)(2,1)S(1)}, bf16[128,512]{1,0:T(8,128)(2,1)S(1)}, u32[]{:S(2)}, u32[]{:S(2)}) collective-permute-start(bf16[128,512]{1,0:T(8,128)(2,1)S(1)} %get-tuple-element.42), channel_id=1, source_target_pairs={{0,4},{1,5},{2,6},{3,7},{4,0},{5,1},{6,2},{7,3},{8,12},{9,13},{10,... | collective-permute-start | bytes 393224 | tf_op jit(solution)/shard_map/ppermute | solution.py:245
  24.6 19.1 %collective-permute-start.11 = (bf16[128,512]{1,0:T(8,128)(2,1)S(1)}, bf16[128,512]{1,0:T(8,128)(2,1)S(1)}, u32[]{:S(2)}, u32[]{:S(2)}) collective-permute-start(bf16[128,512]{1,0:T(8,128)(2,1)S(1)} %get-tuple-element.43), channel_id=1, source_target_pairs={{0,5},{1,4},{2,7},{3,6},{4,1},{5,0},{6,3},{7,2},{8,13},{9,12},{10,... | collective-permute-start | bytes 393224 | tf_op jit(solution)/shard_map/ppermute | solution.py:245
  26.0 17.7 %collective-permute-start.12 = (bf16[128,512]{1,0:T(8,128)(2,1)S(1)}, bf16[128,512]{1,0:T(8,128)(2,1)S(1)}, u32[]{:S(2)}, u32[]{:S(2)}) collective-permute-start(bf16[128,512]{1,0:T(8,128)(2,1)S(1)} %get-tuple-element.44), channel_id=1, source_target_pairs={{0,6},{1,7},{2,4},{3,5},{4,2},{5,3},{6,0},{7,1},{8,14},{9,15},{10,... | collective-permute-start | bytes 393224 | tf_op jit(solution)/shard_map/ppermute | solution.py:245
  31.6 12.1 %collective-permute-start.13 = (bf16[128,512]{1,0:T(8,128)(2,1)S(1)}, bf16[128,512]{1,0:T(8,128)(2,1)S(1)}, u32[]{:S(2)}, u32[]{:S(2)}) collective-permute-start(bf16[128,512]{1,0:T(8,128)(2,1)S(1)} %get-tuple-element.45), channel_id=1, source_target_pairs={{0,7},{1,6},{2,5},{3,4},{4,3},{5,2},{6,1},{7,0},{8,15},{9,14},{10,... | collective-permute-start | bytes 393224 | tf_op jit(solution)/shard_map/ppermute | solution.py:245
  32.6 11.1 %copy-start.1 = (bf16[1,4,4,128,128]{4,3,2,1,0:T(8,128)(2,1)S(1)}, bf16[1,4,4,128,128]{4,3,2,1,0:T(8,128)(2,1)}, u32[]{:S(2)}) copy-start(bf16[1,4,4,128,128]{4,3,2,1,0:T(8,128)(2,1)} %param.15) | copy-start | bytes 1572868
  32.6 11.1 %copy-start.6 = (bf16[128,1024]{1,0:T(8,128)(2,1)S(1)}, bf16[128,1024]{1,0:T(8,128)(2,1)}, u32[]{:S(2)}) copy-start(bf16[128,1024]{1,0:T(8,128)(2,1)} %w_in.1) | copy-start | bytes 786436
  57.7 2.6 %collective-permute-start.14 = (f32[4,312,128]{2,1,0:T(8,128)}, f32[4,312,128]{2,1,0:T(8,128)S(1)}, u32[]{:S(2)}, u32[]{:S(2)}) collective-permute-start(f32[4,312,128]{2,1,0:T(8,128)} %get-tuple-element.47), channel_id=1, source_target_pairs={{0,1},{1,0},{2,3},{3,2},{4,5},{5,4},{6,7},{7,6},{8,9},{9,8},{10,11... | collective-permute-start | bytes 1916936 | tf_op jit(solution)/shard_map/ppermute | solution.py:245
  61.5 4.8 %collective-permute-start.15 = (s16[320,128]{1,0:T(8,128)(2,1)S(1)}, s16[320,128]{1,0:T(8,128)(2,1)S(1)}, u32[]{:S(2)}, u32[]{:S(2)}) collective-permute-start(s16[320,128]{1,0:T(8,128)(2,1)S(1)} %get-tuple-element.49), channel_id=1, source_target_pairs={{0,8},{8,0},{16,24},{24,16},{1,9},{9,1},{17,25},{25,17},{2,10},{10... | collective-permute-start | bytes 245768 | tf_op jit(solution)/shard_map/ppermute | solution.py:245
  63.1 5.3 %collective-permute-start.16 = (s16[320,128]{1,0:T(8,128)(2,1)S(1)}, s16[320,128]{1,0:T(8,128)(2,1)S(1)}, u32[]{:S(2)}, u32[]{:S(2)}) collective-permute-start(s16[320,128]{1,0:T(8,128)(2,1)S(1)} %get-tuple-element.50), channel_id=1, source_target_pairs={{0,16},{8,24},{16,0},{24,8},{1,17},{9,25},{17,1},{25,9},{2,18},{10... | collective-permute-start | bytes 245768 | tf_op jit(solution)/shard_map/ppermute | solution.py:245
  64.6 5.3 %collective-permute-start.17 = (s16[320,128]{1,0:T(8,128)(2,1)S(1)}, s16[320,128]{1,0:T(8,128)(2,1)S(1)}, u32[]{:S(2)}, u32[]{:S(2)}) collective-permute-start(s16[320,128]{1,0:T(8,128)(2,1)S(1)} %get-tuple-element.51), channel_id=1, source_target_pairs={{0,24},{8,16},{16,8},{24,0},{1,25},{9,17},{17,9},{25,1},{2,26},{10... | collective-permute-start | bytes 245768 | tf_op jit(solution)/shard_map/ppermute | solution.py:245
  70.1 7.4 %collective-permute-start.20 = (s16[320,128]{1,0:T(8,128)(2,1)S(1)}, s16[320,128]{1,0:T(8,128)(2,1)S(1)}, u32[]{:S(2)}, u32[]{:S(2)}) collective-permute-start(s16[320,128]{1,0:T(8,128)(2,1)S(1)} %shard_map.142.refs_0_), channel_id=1, source_target_pairs={{0,6},{1,7},{2,4},{3,5},{4,2},{5,3},{6,0},{7,1},{8,14},{9,15},{10,... | collective-permute-start | bytes 245768 | tf_op jit(solution)/shard_map/ppermute | solution.py:245
  71.2 10.7 %collective-permute-start.19 = (s16[320,128]{1,0:T(8,128)(2,1)S(1)}, s16[320,128]{1,0:T(8,128)(2,1)S(1)}, u32[]{:S(2)}, u32[]{:S(2)}) collective-permute-start(s16[320,128]{1,0:T(8,128)(2,1)S(1)} %shard_map.142.refs_0_), channel_id=1, source_target_pairs={{0,4},{1,5},{2,6},{3,7},{4,0},{5,1},{6,2},{7,3},{8,12},{9,13},{10,... | collective-permute-start | bytes 245768 | tf_op jit(solution)/shard_map/ppermute | solution.py:245
  77.4 5.3 %collective-permute-start.18 = (s16[320,128]{1,0:T(8,128)(2,1)S(1)}, s16[320,128]{1,0:T(8,128)(2,1)S(1)}, u32[]{:S(2)}, u32[]{:S(2)}) collective-permute-start(s16[320,128]{1,0:T(8,128)(2,1)S(1)} %shard_map.142.refs_0_), channel_id=1, source_target_pairs={{0,2},{1,3},{2,0},{3,1},{4,6},{5,7},{6,4},{7,5},{8,10},{9,11},{10,... | collective-permute-start | bytes 245768 | tf_op jit(solution)/shard_map/ppermute | solution.py:245
  82.8 5.5 %collective-permute-start.23 = (s16[320,128]{1,0:T(8,128)(2,1)S(1)}, s16[320,128]{1,0:T(8,128)(2,1)S(1)}, u32[]{:S(2)}, u32[]{:S(2)}) collective-permute-start(s16[320,128]{1,0:T(8,128)(2,1)S(1)} %shard_map.143.refs_0_), channel_id=1, source_target_pairs={{0,24},{8,16},{16,8},{24,0},{1,25},{9,17},{17,9},{25,1},{2,26},{10... | collective-permute-start | bytes 245768 | tf_op jit(solution)/shard_map/ppermute | solution.py:245
  83.7 5.3 %collective-permute-start.22 = (s16[320,128]{1,0:T(8,128)(2,1)S(1)}, s16[320,128]{1,0:T(8,128)(2,1)S(1)}, u32[]{:S(2)}, u32[]{:S(2)}) collective-permute-start(s16[320,128]{1,0:T(8,128)(2,1)S(1)} %shard_map.143.refs_0_), channel_id=1, source_target_pairs={{0,16},{8,24},{16,0},{24,8},{1,17},{9,25},{17,1},{25,9},{2,18},{10... | collective-permute-start | bytes 245768 | tf_op jit(solution)/shard_map/ppermute | solution.py:245
  84.9 4.4 %collective-permute-start.21 = (s16[320,128]{1,0:T(8,128)(2,1)S(1)}, s16[320,128]{1,0:T(8,128)(2,1)S(1)}, u32[]{:S(2)}, u32[]{:S(2)}) collective-permute-start(s16[320,128]{1,0:T(8,128)(2,1)S(1)} %shard_map.143.refs_0_), channel_id=1, source_target_pairs={{0,8},{8,0},{16,24},{24,16},{1,9},{9,1},{17,25},{25,17},{2,10},{10... | collective-permute-start | bytes 245768 | tf_op jit(solution)/shard_map/ppermute | solution.py:245
  86.4 3.2 %collective-permute-start.24 = (s16[320,128]{1,0:T(8,128)(2,1)S(1)}, s16[320,128]{1,0:T(8,128)(2,1)S(1)}, u32[]{:S(2)}, u32[]{:S(2)}) collective-permute-start(s16[320,128]{1,0:T(8,128)(2,1)S(1)} %shard_map.143.refs_0_), channel_id=1, source_target_pairs={{0,1},{1,0},{2,3},{3,2},{4,5},{5,4},{6,7},{7,6},{8,9},{9,8},{10,11... | collective-permute-start | bytes 245768 | tf_op jit(solution)/shard_map/ppermute | solution.py:245
  88.3 1.3 %collective-permute-start.27 = (s16[320,128]{1,0:T(8,128)(2,1)S(1)}, s16[320,128]{1,0:T(8,128)(2,1)S(1)}, u32[]{:S(2)}, u32[]{:S(2)}) collective-permute-start(s16[320,128]{1,0:T(8,128)(2,1)S(1)} %collective-permute-done.23.refs_3_), channel_id=1, source_target_pairs={{0,1},{1,0},{2,3},{3,2},{4,5},{5,4},{6,7},{7,6},{8,9},{9,8},{10,11... | collective-permute-start | bytes 245768 | tf_op jit(solution)/shard_map/ppermute | solution.py:245
  89.1 1.3 %collective-permute-start.26 = (s16[320,128]{1,0:T(8,128)(2,1)S(1)}, s16[320,128]{1,0:T(8,128)(2,1)S(1)}, u32[]{:S(2)}, u32[]{:S(2)}) collective-permute-start(s16[320,128]{1,0:T(8,128)(2,1)S(1)} %collective-permute-done.22.refs_2_), channel_id=1, source_target_pairs={{0,1},{1,0},{2,3},{3,2},{4,5},{5,4},{6,7},{7,6},{8,9},{9,8},{10,11... | collective-permute-start | bytes 245768 | tf_op jit(solution)/shard_map/ppermute | solution.py:245
  89.4 1.3 %collective-permute-start.25 = (s16[320,128]{1,0:T(8,128)(2,1)S(1)}, s16[320,128]{1,0:T(8,128)(2,1)S(1)}, u32[]{:S(2)}, u32[]{:S(2)}) collective-permute-start(s16[320,128]{1,0:T(8,128)(2,1)S(1)} %collective-permute-done.21.refs_1_), channel_id=1, source_target_pairs={{0,1},{1,0},{2,3},{3,2},{4,5},{5,4},{6,7},{7,6},{8,9},{9,8},{10,11... | collective-permute-start | bytes 245768 | tf_op jit(solution)/shard_map/ppermute | solution.py:245
  (11 other events, 34.9 us)

commit v2 on v1

--- a/solution.py
+++ b/solution.py
@@ -11,21 +11,22 @@
 KEEP_RATE = 0.5
 XBAR_SCALE = 1.0 / ((ORDER + 1) * KEEP_RATE)
 F32, BF16, I16, I32 = jnp.float32, jnp.bfloat16, jnp.int16, jnp.int32
-VMEM_LIMIT = 50 * 1024 * 1024
+MIB = 1024 * 1024
 SMEM = pl.BlockSpec(memory_space=pltpu.SMEM)
 VMEM = pl.BlockSpec(memory_space=pltpu.VMEM)
+HBM = pl.BlockSpec(memory_space=pltpu.HBM)
 CHUNK = 256
 TAIL = 8
 
 
-def call(kernel, outs, ins, scratch=(), n_smem=0):
+def call(kernel, outs, ins, scratch=(), n_smem=0, n_hbm=0, vmem=8):
     return pl.pallas_call(
         kernel,
         out_shape=outs,
-        in_specs=[SMEM] * n_smem + [VMEM] * (len(ins) - n_smem),
+        in_specs=[SMEM] * n_smem + [HBM] * n_hbm + [VMEM] * (len(ins) - n_smem - n_hbm),
         out_specs=jax.tree.map(lambda _: VMEM, outs),
         scratch_shapes=list(scratch),
-        compiler_params=pltpu.CompilerParams(vmem_limit_bytes=VMEM_LIMIT),
+        compiler_params=pltpu.CompilerParams(vmem_limit_bytes=vmem * MIB),
     )(*ins)
 
 
@@ -33,15 +34,25 @@
     return jax.ShapeDtypeStruct(shape, dtype)
 
 
-def select_kernel(info, serve, feats, masks, *msgs):
+def select_kernel(info, serve, feats, masks, *refs):
+    msgs, (held, sem, mask_sem) = refs[:-3], refs[-3:]
     tile = feats.shape[1]
     samples = masks.shape[0]
-    for k in range(1, len(msgs) + 1):
-        t = serve[info[0] ^ k]
-        out = msgs[k - 1]
-        out[:tile, :] = feats[t]
-        m = masks[:, pl.ds(pl.multiple_of(t * tile, tile), tile)]
+    ids = [serve[info[0] ^ k] for k in range(1, len(msgs) + 1)]
+    copy = pltpu.make_async_copy(masks, held, mask_sem)
+    copy.start()
+    copies = [
+        pltpu.make_async_copy(feats.at[t], out.at[pl.ds(0, tile)], sem.at[i])
+        for i, (t, out) in enumerate(zip(ids, msgs))
+    ]
+    for c in copies:
+        c.start()
+    copy.wait()
+    for t, out in zip(ids, msgs):
+        m = held[:, pl.ds(pl.multiple_of(t * tile, tile), tile)]
         out[tile:, :] = jnp.concatenate([m, jnp.zeros((out.shape[0] - tile - samples, tile), BF16)], 0)
+    for c in copies:
+        c.wait()
 
 
 def pool_index(info, serve, slots, r, j, dom, nnz):
@@ -245,6 +256,11 @@
     return lax.ppermute(x, axis, [(i, i ^ mask) for i in range(lax.axis_size(axis))])
 
 
+def swap_all(blocks):
+    got = [xor_permute(blocks[k - 1], "dom", k) for k in range(len(blocks), 0, -1)]
+    return got[::-1]
+
+
 def bit_groups(axis, first):
     size, bit, groups = lax.axis_size(axis), first, []
     while (1 << bit) < size:
@@ -308,9 +324,14 @@
     wide = -(-classes // 128) * 128
 
     msgs = call(
-        select_kernel, [like((tile + 16, feat), BF16)] * (dom - 1), [info, serve, feats, masks], n_smem=2
-    )
-    msgs = [xor_permute(x, "dom", k + 1) for k, x in enumerate(msgs)]
+        select_kernel,
+        [like((tile + 16, feat), BF16)] * (dom - 1),
+        [info, serve, feats, masks],
+        [pltpu.VMEM(masks.shape, BF16), pltpu.SemaphoreType.DMA((dom - 1,)), pltpu.SemaphoreType.DMA],
+        n_smem=2,
+        n_hbm=2,
+    )
+    msgs = swap_all(msgs)
     cur, total, *outs = call(
         functools.partial(hop1_kernel, dom),
         [like((tiles, tile, lanes), BF16), like((tiles, tile, lanes), F32)] + [like((tile, lanes), BF16)] * (dom - 1),
@@ -318,7 +339,7 @@
         [pltpu.VMEM((dom - 1 + tiles, tile, lanes), BF16)],
         n_smem=3,
     )
-    outs = [xor_permute(x, "dom", k + 1) for k, x in enumerate(outs)]
+    outs = swap_all(outs)
 
     code = jnp.where(labeled != 0, node_labels, -1).reshape(tiles, tile, 1)
     w_out = jnp.pad(weight_out, ((0, 0), (0, wide - classes)))
@@ -345,6 +366,7 @@
             pltpu.VMEM((8, wide), F32),
         ],
         n_smem=3,
+        vmem=28,
     )
     g_in, b_in, g_out, b_out = reduce_grads(keep, send, info, feat, 1 + wide // 128, classes, hidden)
     return g_in, b_in.reshape(hidden), g_out.T, b_out.reshape(-1)[:classes]

time: 92.8 us -> 89.7 us (0.967)
  waiting for transfers between devices: 36.8 us -> 34.2 us
    ppermute x28, waiting for transfers between devices: 36.8 us -> 34.2 us  [xor_permute(): lax.ppermute(x, axis, [(i, i ^ mask) for i in range(lax.axis_size(axis))])]
    pad x1, local copies, waits for them, and re-layouts: 0.09 us -> 1.18 us  [per_device(): w_out = jnp.pad(weight_out, ((0, 0), (0, wide - classes)))]
    unnamed x31 -> x27, local copies, waits for them, and re-layouts: 5.39 us -> 4.64 us
  transfers between devices with their start and end apart: 28 -> 28, of which waited for: 17 -> 16; matrix products, arithmetic and copies ran while one was open for 1% -> 4% of each run, Pallas kernels for 0% -> 0%
where the time goes in v2:
time: 89.7 us; the launch traced here: 89.5 us
  waiting for transfers between devices  34.2 us (38%)
  starting transfers between devices  30.7 us (34%)
  Pallas kernels  17.6 us (20%)
  local copies, waits for them, and re-layouts  6.09 us (7%)
    ppermute x28, waiting for transfers between devices, xor_permute(): lax.ppermute(x, axis, [(i, i ^ mask) for i in range(lax.axis_size(axis))])  34.2 us
    ppermute x28, starting transfers between devices, xor_permute(): lax.ppermute(x, axis, [(i, i ^ mask) for i in range(lax.axis_size(axis))])  30.7 us
    pallas_call x7, Pallas kernels, call(): pl.pallas_call(kernel, out_shape=outs, in_specs=[SMEM] * n_smem + [HBM] *...  17.6 us
    unnamed x27, local copies, waits for them, and re-layouts  4.64 us
  transfers between devices with their start and end apart: 28, of which 16 were waited for; matrix products, arithmetic and copies ran while one was open for 4% of the time, Pallas kernels for 0%

profile of v2, /device:TPU:0, one launch (start us, length us, event | category | flops | bytes accessed | tf_op | source)
XLA Modules:
  0.0 89.5 jit_solution(16199127691892505262)
XLA Ops:
  1.4 0.9 %copy-done.2 = bf16[1,512,128]{2,1,0:T(8,128)(2,1)S(1)} copy-done((bf16[1,512,128]{2,1,0:T(8,128)(2,1)S(1)}, bf16[1,512,128]{2,1,0:T(8,128)(2,1)}, u32[]{:S(2)}) %copy-start.2) | copy-done | bytes 131096
  2.3 0.9 %shard_map.138 = (bf16[144,128]{1,0:T(8,128)(2,1)S(1)}, bf16[144,128]{1,0:T(8,128)(2,1)S(1)}, bf16[144,128]{1,0:T(8,128)(2,1)S(1)}, bf16[144,128]{1,0:T(8,128)(2...) custom-call(s32[3]{0:T(128)S(1)} %pad_add_fusion.info, ...), custom_call_target="tpu_custom_call" | custom-call | tf_op jit(solution)/shard_map/pallas_call | solution.py:23
  3.8 2.6 %collective-permute-start.1 = (bf16[144,128]{1,0:T(8,128)(2,1)S(1)}, bf16[144,128]{1,0:T(8,128)(2,1)S(1)}, u32[]{:S(2)}, u32[]{:S(2)}) collective-permute-start(bf16[144,128]{1,0:T(8,128)(2,1)S(1)} %get-tuple-element.31), channel_id=1, source_target_pairs={{0,2},{1,3},{2,0},{3,1},{4,6},{5,7},{6,4},{7,5},{8,10},{9,11},{10,... | collective-permute-start | bytes 110600 | tf_op jit(solution)/shard_map/ppermute | solution.py:256
  6.5 2.8 %collective-permute-start.3 = (bf16[144,128]{1,0:T(8,128)(2,1)S(1)}, bf16[144,128]{1,0:T(8,128)(2,1)S(1)}, u32[]{:S(2)}, u32[]{:S(2)}) collective-permute-start(bf16[144,128]{1,0:T(8,128)(2,1)S(1)} %get-tuple-element.33), channel_id=1, source_target_pairs={{0,4},{1,5},{2,6},{3,7},{4,0},{5,1},{6,2},{7,3},{8,12},{9,13},{10,... | collective-permute-start | bytes 110600 | tf_op jit(solution)/shard_map/ppermute | solution.py:256
  9.2 3.6 %collective-permute-start.5 = (bf16[144,128]{1,0:T(8,128)(2,1)S(1)}, bf16[144,128]{1,0:T(8,128)(2,1)S(1)}, u32[]{:S(2)}, u32[]{:S(2)}) collective-permute-start(bf16[144,128]{1,0:T(8,128)(2,1)S(1)} %get-tuple-element.35), channel_id=1, source_target_pairs={{0,6},{1,7},{2,4},{3,5},{4,2},{5,3},{6,0},{7,1},{8,14},{9,15},{10,... | collective-permute-start | bytes 110600 | tf_op jit(solution)/shard_map/ppermute | solution.py:256
  13.7 2.1 %collective-permute-done.5.refs_5_ = bf16[144,128]{1,0:T(8,128)(2,1)S(1)} collective-permute-done((bf16[144,128]{1,0:T(8,128)(2,1)S(1)}, bf16[144,128]{1,0:T(8,128)(2,1)S(1)}, u32[]{:S(2)}, u32[]{:S(2)}) %collective-permute-start.5) | collective-permute-done | bytes 36896 | tf_op jit(solution)/shard_map/ppermute | solution.py:256
  15.8 2.3 %collective-permute-done.6.refs_6_ = bf16[144,128]{1,0:T(8,128)(2,1)S(1)} collective-permute-done((bf16[144,128]{1,0:T(8,128)(2,1)S(1)}, bf16[144,128]{1,0:T(8,128)(2,1)S(1)}, u32[]{:S(2)}, u32[]{:S(2)}) %collective-permute-start.6) | collective-permute-done | bytes 36896 | tf_op jit(solution)/shard_map/ppermute | solution.py:256
  18.1 1.0 %copy-done = bf16[1,4,4,128,128]{4,3,2,1,0:T(8,128)(2,1)S(1)} copy-done((bf16[1,4,4,128,128]{4,3,2,1,0:T(8,128)(2,1)S(1)}, bf16[1,4,4,128,128]{4,3,2,1,0:T(8,128)(2,1)}, u32[]{:S(2)}) %copy-start) | copy-done | bytes 524312
  19.1 1.7 %shard_map.139 = (bf16[4,128,512]{2,1,0:T(8,128)(2,1)S(1)}, f32[4,128,512]{2,1,0:T(8,128)S(1)}, bf16[128,512]{1,0:T(8,128)(2,1)S(1)}, bf16[128,512]{1,0:T(8,128)...) custom-call(s32[3]{0:T(128)S(1)} %pad_add_fusion.info, ...), custom_call_target="tpu_custom_call" | custom-call | tf_op jit(solution)/shard_map/pallas_call | solution.py:23
  21.1 1.7 %collective-permute-start.9 = (bf16[128,512]{1,0:T(8,128)(2,1)S(1)}, bf16[128,512]{1,0:T(8,128)(2,1)S(1)}, u32[]{:S(2)}, u32[]{:S(2)}) collective-permute-start(bf16[128,512]{1,0:T(8,128)(2,1)S(1)} %get-tuple-element.41), channel_id=1, source_target_pairs={{0,3},{1,2},{2,1},{3,0},{4,7},{5,6},{6,5},{7,4},{8,11},{9,10},{10,... | collective-permute-start | bytes 393224 | tf_op jit(solution)/shard_map/ppermute | solution.py:256
  22.8 1.3 %collective-permute-start.10 = (bf16[128,512]{1,0:T(8,128)(2,1)S(1)}, bf16[128,512]{1,0:T(8,128)(2,1)S(1)}, u32[]{:S(2)}, u32[]{:S(2)}) collective-permute-start(bf16[128,512]{1,0:T(8,128)(2,1)S(1)} %get-tuple-element.42), channel_id=1, source_target_pairs={{0,4},{1,5},{2,6},{3,7},{4,0},{5,1},{6,2},{7,3},{8,12},{9,13},{10,... | collective-permute-start | bytes 393224 | tf_op jit(solution)/shard_map/ppermute | solution.py:256
  24.1 1.4 %collective-permute-start.11 = (bf16[128,512]{1,0:T(8,128)(2,1)S(1)}, bf16[128,512]{1,0:T(8,128)(2,1)S(1)}, u32[]{:S(2)}, u32[]{:S(2)}) collective-permute-start(bf16[128,512]{1,0:T(8,128)(2,1)S(1)} %get-tuple-element.43), channel_id=1, source_target_pairs={{0,5},{1,4},{2,7},{3,6},{4,1},{5,0},{6,3},{7,2},{8,13},{9,12},{10,... | collective-permute-start | bytes 393224 | tf_op jit(solution)/shard_map/ppermute | solution.py:256
  25.5 0.9 %collective-permute-start.12 = (bf16[128,512]{1,0:T(8,128)(2,1)S(1)}, bf16[128,512]{1,0:T(8,128)(2,1)S(1)}, u32[]{:S(2)}, u32[]{:S(2)}) collective-permute-start(bf16[128,512]{1,0:T(8,128)(2,1)S(1)} %get-tuple-element.44), channel_id=1, source_target_pairs={{0,6},{1,7},{2,4},{3,5},{4,2},{5,3},{6,0},{7,1},{8,14},{9,15},{10,... | collective-permute-start | bytes 393224 | tf_op jit(solution)/shard_map/ppermute | solution.py:256
  26.4 4.7 %collective-permute-done.8.refs_1_ = bf16[128,512]{1,0:T(8,128)(2,1)S(1)} collective-permute-done((bf16[128,512]{1,0:T(8,128)(2,1)S(1)}, bf16[128,512]{1,0:T(8,128)(2,1)S(1)}, u32[]{:S(2)}, u32[]{:S(2)}) %collective-permute-start.8) | collective-permute-done | bytes 131104 | tf_op jit(solution)/shard_map/ppermute | solution.py:256
  31.3 2.0 %copy.18 = bf16[1024,172]{1,0:T(8,128)(2,1)} copy(bf16[1024,172]{0,1:T(8,128)(2,1)} %param.20) | data formatting | bytes 704512
  33.3 1.2 %pad.8.clone.w_out = bf16[1024,256]{1,0:T(8,128)(2,1)S(1)} pad(bf16[1024,172]{1,0:T(8,128)(2,1)} %copy.18, bf16[]{:T(256)} %constant.19.clone.1), padding=0_0x0_84 | pad | bytes 876546 | tf_op jit(solution)/shard_map/jit(_pad)/pad | solution.py:345
  34.6 8.6 %collective-permute-done.11.refs_4_ = bf16[128,512]{1,0:T(8,128)(2,1)S(1)} collective-permute-done((bf16[128,512]{1,0:T(8,128)(2,1)S(1)}, bf16[128,512]{1,0:T(8,128)(2,1)S(1)}, u32[]{:S(2)}, u32[]{:S(2)}) %collective-permute-start.11) | collective-permute-done | bytes 131104 | tf_op jit(solution)/shard_map/ppermute | solution.py:256
  43.2 12.7 %shard_map.140 = (f32[4,312,128]{2,1,0:T(8,128)S(1)}, f32[4,312,128]{2,1,0:T(8,128)S(1)}) custom-call(s32[3]{0:T(128)S(1)} %pad_add_fusion.info, s32[8]{0:T(128)S(1)} %bitcast.24, s32[16]{0:T(128)S(1)} %reshape.32.slots, bf16[4,4,128,128]{3,2,1,0:T(8,128)(2,1)S(1)} %bitcast.17, bf16[4,128,512]{2,1,0:T(8,128)(2,1)S(1)} %get-tuple-element.37.cur, ...), custom_call_target="tpu_custom_call" | custom-call | tf_op jit(solution)/shard_map/pallas_call | solution.py:23
  56.6 1.7 %collective-permute-done.14.recv = f32[4,312,128]{2,1,0:T(8,128)S(1)} collective-permute-done((f32[4,312,128]{2,1,0:T(8,128)S(1)}, f32[4,312,128]{2,1,0:T(8,128)S(1)}, u32[]{:S(2)}, u32[]{:S(2)}) %collective-permute-start.14) | collective-permute-done | bytes 639008 | tf_op jit(solution)/shard_map/ppermute | solution.py:256
  58.5 1.6 %collective-permute-start.15 = (s16[320,128]{1,0:T(8,128)(2,1)S(1)}, s16[320,128]{1,0:T(8,128)(2,1)S(1)}, u32[]{:S(2)}, u32[]{:S(2)}) collective-permute-start(s16[320,128]{1,0:T(8,128)(2,1)S(1)} %get-tuple-element.49), channel_id=1, source_target_pairs={{0,8},{8,0},{16,24},{24,16},{1,9},{9,1},{17,25},{25,17},{2,10},{10... | collective-permute-start | bytes 245768 | tf_op jit(solution)/shard_map/ppermute | solution.py:256
  60.1 1.5 %collective-permute-start.16 = (s16[320,128]{1,0:T(8,128)(2,1)S(1)}, s16[320,128]{1,0:T(8,128)(2,1)S(1)}, u32[]{:S(2)}, u32[]{:S(2)}) collective-permute-start(s16[320,128]{1,0:T(8,128)(2,1)S(1)} %get-tuple-element.50), channel_id=1, source_target_pairs={{0,16},{8,24},{16,0},{24,8},{1,17},{9,25},{17,1},{25,9},{2,18},{10... | collective-permute-start | bytes 245768 | tf_op jit(solution)/shard_map/ppermute | solution.py:256
  62.1 1.2 %collective-permute-done.15.refs_0_ = s16[320,128]{1,0:T(8,128)(2,1)S(1)} collective-permute-done((s16[320,128]{1,0:T(8,128)(2,1)S(1)}, s16[320,128]{1,0:T(8,128)(2,1)S(1)}, u32[]{:S(2)}, u32[]{:S(2)}) %collective-permute-start.15) | collective-permute-done | bytes 81952 | tf_op jit(solution)/shard_map/ppermute | solution.py:256
  63.3 2.1 %collective-permute-done.16.refs_1_ = s16[320,128]{1,0:T(8,128)(2,1)S(1)} collective-permute-done((s16[320,128]{1,0:T(8,128)(2,1)S(1)}, s16[320,128]{1,0:T(8,128)(2,1)S(1)}, u32[]{:S(2)}, u32[]{:S(2)}) %collective-permute-start.16) | collective-permute-done | bytes 81952 | tf_op jit(solution)/shard_map/ppermute | solution.py:256
  65.4 1.6 %collective-permute-done.17.refs_2_ = s16[320,128]{1,0:T(8,128)(2,1)S(1)} collective-permute-done((s16[320,128]{1,0:T(8,128)(2,1)S(1)}, s16[320,128]{1,0:T(8,128)(2,1)S(1)}, u32[]{:S(2)}, u32[]{:S(2)}) %collective-permute-start.17) | collective-permute-done | bytes 81952 | tf_op jit(solution)/shard_map/ppermute | solution.py:256
  67.1 1.1 %collective-permute-start.20 = (s16[320,128]{1,0:T(8,128)(2,1)S(1)}, s16[320,128]{1,0:T(8,128)(2,1)S(1)}, u32[]{:S(2)}, u32[]{:S(2)}) collective-permute-start(s16[320,128]{1,0:T(8,128)(2,1)S(1)} %shard_map.142.refs_0_), channel_id=1, source_target_pairs={{0,6},{1,7},{2,4},{3,5},{4,2},{5,3},{6,0},{7,1},{8,14},{9,15},{10,... | collective-permute-start | bytes 245768 | tf_op jit(solution)/shard_map/ppermute | solution.py:256
  68.2 6.2 %collective-permute-start.19 = (s16[320,128]{1,0:T(8,128)(2,1)S(1)}, s16[320,128]{1,0:T(8,128)(2,1)S(1)}, u32[]{:S(2)}, u32[]{:S(2)}) collective-permute-start(s16[320,128]{1,0:T(8,128)(2,1)S(1)} %shard_map.142.refs_0_), channel_id=1, source_target_pairs={{0,4},{1,5},{2,6},{3,7},{4,0},{5,1},{6,2},{7,3},{8,12},{9,13},{10,... | collective-permute-start | bytes 245768 | tf_op jit(solution)/shard_map/ppermute | solution.py:256
  74.4 4.5 %collective-permute-done.19.refs_2_ = s16[320,128]{1,0:T(8,128)(2,1)S(1)} collective-permute-done((s16[320,128]{1,0:T(8,128)(2,1)S(1)}, s16[320,128]{1,0:T(8,128)(2,1)S(1)}, u32[]{:S(2)}, u32[]{:S(2)}) %collective-permute-start.19) | collective-permute-done | bytes 81952 | tf_op jit(solution)/shard_map/ppermute | solution.py:256
  79.8 0.9 %collective-permute-start.23 = (s16[320,128]{1,0:T(8,128)(2,1)S(1)}, s16[320,128]{1,0:T(8,128)(2,1)S(1)}, u32[]{:S(2)}, u32[]{:S(2)}) collective-permute-start(s16[320,128]{1,0:T(8,128)(2,1)S(1)} %shard_map.143.refs_0_), channel_id=1, source_target_pairs={{0,24},{8,16},{16,8},{24,0},{1,25},{9,17},{17,9},{25,1},{2,26},{10... | collective-permute-start | bytes 245768 | tf_op jit(solution)/shard_map/ppermute | solution.py:256
  80.7 1.2 %collective-permute-start.22 = (s16[320,128]{1,0:T(8,128)(2,1)S(1)}, s16[320,128]{1,0:T(8,128)(2,1)S(1)}, u32[]{:S(2)}, u32[]{:S(2)}) collective-permute-start(s16[320,128]{1,0:T(8,128)(2,1)S(1)} %shard_map.143.refs_0_), channel_id=1, source_target_pairs={{0,16},{8,24},{16,0},{24,8},{1,17},{9,25},{17,1},{25,9},{2,18},{10... | collective-permute-start | bytes 245768 | tf_op jit(solution)/shard_map/ppermute | solution.py:256
  81.9 1.4 %collective-permute-start.21 = (s16[320,128]{1,0:T(8,128)(2,1)S(1)}, s16[320,128]{1,0:T(8,128)(2,1)S(1)}, u32[]{:S(2)}, u32[]{:S(2)}) collective-permute-start(s16[320,128]{1,0:T(8,128)(2,1)S(1)} %shard_map.143.refs_0_), channel_id=1, source_target_pairs={{0,8},{8,0},{16,24},{24,16},{1,9},{9,1},{17,25},{25,17},{2,10},{10... | collective-permute-start | bytes 245768 | tf_op jit(solution)/shard_map/ppermute | solution.py:256
  83.4 2.0 %collective-permute-done.23.refs_3_ = s16[320,128]{1,0:T(8,128)(2,1)S(1)} collective-permute-done((s16[320,128]{1,0:T(8,128)(2,1)S(1)}, s16[320,128]{1,0:T(8,128)(2,1)S(1)}, u32[]{:S(2)}, u32[]{:S(2)}) %collective-permute-start.23) | collective-permute-done | bytes 81952 | tf_op jit(solution)/shard_map/ppermute | solution.py:256
  87.6 1.8 %shard_map.144 = (f32[128,1024]{1,0:T(8,128)}, f32[1,1024]{1,0:T(1,128)}, f32[172,1024]{1,0:T(8,128)}, f32[1,256]{1,0:T(1,128)}) custom-call(s32[3]{0:T(128)S(1)} %pad_add_fusion.info, s16[320,128]{1,0:T(8,128)(2,1)S(1)} %shard_map.143.refs_0_, s16[320,128]{1,0:T(8,128)(2,1)S(1)} %collective-permute-done.21.refs_1_, ...), custom_call_target="tpu_custom_call" | custom-call | tf_op jit(solution)/shard_map/pallas_call | solution.py:23
  (65 shorter events, 7.4 us)
Async XLA Ops:
  2.3 15.8 %copy-start.3 = (bf16[1,512,128]{2,1,0:T(8,128)(2,1)S(1)}, bf16[1,512,128]{2,1,0:T(8,128)(2,1)}, u32[]{:S(2)}) copy-start(bf16[1,512,128]{2,1,0:T(8,128)(2,1)} %param.11) | copy-start | bytes 393220
  3.2 6.0 %collective-permute-start = (bf16[144,128]{1,0:T(8,128)(2,1)S(1)}, bf16[144,128]{1,0:T(8,128)(2,1)S(1)}, u32[]{:S(2)}, u32[]{:S(2)}) collective-permute-start(bf16[144,128]{1,0:T(8,128)(2,1)S(1)} %get-tuple-element.30), channel_id=1, source_target_pairs={{0,1},{1,0},{2,3},{3,2},{4,5},{5,4},{6,7},{7,6},{8,9},{9,8},{10,11... | collective-permute-start | bytes 110600 | tf_op jit(solution)/shard_map/ppermute | solution.py:256
  3.8 9.1 %collective-permute-start.1 = (bf16[144,128]{1,0:T(8,128)(2,1)S(1)}, bf16[144,128]{1,0:T(8,128)(2,1)S(1)}, u32[]{:S(2)}, u32[]{:S(2)}) collective-permute-start(bf16[144,128]{1,0:T(8,128)(2,1)S(1)} %get-tuple-element.31), channel_id=1, source_target_pairs={{0,2},{1,3},{2,0},{3,1},{4,6},{5,7},{6,4},{7,5},{8,10},{9,11},{10,... | collective-permute-start | bytes 110600 | tf_op jit(solution)/shard_map/ppermute | solution.py:256
  6.4 6.6 %collective-permute-start.2 = (bf16[144,128]{1,0:T(8,128)(2,1)S(1)}, bf16[144,128]{1,0:T(8,128)(2,1)S(1)}, u32[]{:S(2)}, u32[]{:S(2)}) collective-permute-start(bf16[144,128]{1,0:T(8,128)(2,1)S(1)} %get-tuple-element.32), channel_id=1, source_target_pairs={{0,3},{1,2},{2,1},{3,0},{4,7},{5,6},{6,5},{7,4},{8,11},{9,10},{10,... | collective-permute-start | bytes 110600 | tf_op jit(solution)/shard_map/ppermute | solution.py:256
  6.5 6.6 %collective-permute-start.3 = (bf16[144,128]{1,0:T(8,128)(2,1)S(1)}, bf16[144,128]{1,0:T(8,128)(2,1)S(1)}, u32[]{:S(2)}, u32[]{:S(2)}) collective-permute-start(bf16[144,128]{1,0:T(8,128)(2,1)S(1)} %get-tuple-element.33), channel_id=1, source_target_pairs={{0,4},{1,5},{2,6},{3,7},{4,0},{5,1},{6,2},{7,3},{8,12},{9,13},{10,... | collective-permute-start | bytes 110600 | tf_op jit(solution)/shard_map/ppermute | solution.py:256
  9.2 4.4 %collective-permute-start.4 = (bf16[144,128]{1,0:T(8,128)(2,1)S(1)}, bf16[144,128]{1,0:T(8,128)(2,1)S(1)}, u32[]{:S(2)}, u32[]{:S(2)}) collective-permute-start(bf16[144,128]{1,0:T(8,128)(2,1)S(1)} %get-tuple-element.34), channel_id=1, source_target_pairs={{0,5},{1,4},{2,7},{3,6},{4,1},{5,0},{6,3},{7,2},{8,13},{9,12},{10,... | collective-permute-start | bytes 110600 | tf_op jit(solution)/shard_map/ppermute | solution.py:256
  9.2 6.6 %collective-permute-start.5 = (bf16[144,128]{1,0:T(8,128)(2,1)S(1)}, bf16[144,128]{1,0:T(8,128)(2,1)S(1)}, u32[]{:S(2)}, u32[]{:S(2)}) collective-permute-start(bf16[144,128]{1,0:T(8,128)(2,1)S(1)} %get-tuple-element.35), channel_id=1, source_target_pairs={{0,6},{1,7},{2,4},{3,5},{4,2},{5,3},{6,0},{7,1},{8,14},{9,15},{10,... | collective-permute-start | bytes 110600 | tf_op jit(solution)/shard_map/ppermute | solution.py:256
  12.8 5.2 %collective-permute-start.6 = (bf16[144,128]{1,0:T(8,128)(2,1)S(1)}, bf16[144,128]{1,0:T(8,128)(2,1)S(1)}, u32[]{:S(2)}, u32[]{:S(2)}) collective-permute-start(bf16[144,128]{1,0:T(8,128)(2,1)S(1)} %get-tuple-element.36), channel_id=1, source_target_pairs={{0,7},{1,6},{2,5},{3,4},{4,3},{5,2},{6,1},{7,0},{8,15},{9,14},{10,... | collective-permute-start | bytes 110600 | tf_op jit(solution)/shard_map/ppermute | solution.py:256
  20.8 4.6 %collective-permute-start.7 = (bf16[128,512]{1,0:T(8,128)(2,1)S(1)}, bf16[128,512]{1,0:T(8,128)(2,1)S(1)}, u32[]{:S(2)}, u32[]{:S(2)}) collective-permute-start(bf16[128,512]{1,0:T(8,128)(2,1)S(1)} %get-tuple-element.39), channel_id=1, source_target_pairs={{0,1},{1,0},{2,3},{3,2},{4,5},{5,4},{6,7},{7,6},{8,9},{9,8},{10,11... | collective-permute-start | bytes 393224 | tf_op jit(solution)/shard_map/ppermute | solution.py:256
  21.1 10.0 %collective-permute-start.8 = (bf16[128,512]{1,0:T(8,128)(2,1)S(1)}, bf16[128,512]{1,0:T(8,128)(2,1)S(1)}, u32[]{:S(2)}, u32[]{:S(2)}) collective-permute-start(bf16[128,512]{1,0:T(8,128)(2,1)S(1)} %get-tuple-element.40), channel_id=1, source_target_pairs={{0,2},{1,3},{2,0},{3,1},{4,6},{5,7},{6,4},{7,5},{8,10},{9,11},{10,... | collective-permute-start | bytes 393224 | tf_op jit(solution)/shard_map/ppermute | solution.py:256
  21.1 13.5 %collective-permute-start.9 = (bf16[128,512]{1,0:T(8,128)(2,1)S(1)}, bf16[128,512]{1,0:T(8,128)(2,1)S(1)}, u32[]{:S(2)}, u32[]{:S(2)}) collective-permute-start(bf16[128,512]{1,0:T(8,128)(2,1)S(1)} %get-tuple-element.41), channel_id=1, source_target_pairs={{0,3},{1,2},{2,1},{3,0},{4,7},{5,6},{6,5},{7,4},{8,11},{9,10},{10,... | collective-permute-start | bytes 393224 | tf_op jit(solution)/shard_map/ppermute | solution.py:256
  22.8 11.8 %collective-permute-start.10 = (bf16[128,512]{1,0:T(8,128)(2,1)S(1)}, bf16[128,512]{1,0:T(8,128)(2,1)S(1)}, u32[]{:S(2)}, u32[]{:S(2)}) collective-permute-start(bf16[128,512]{1,0:T(8,128)(2,1)S(1)} %get-tuple-element.42), channel_id=1, source_target_pairs={{0,4},{1,5},{2,6},{3,7},{4,0},{5,1},{6,2},{7,3},{8,12},{9,13},{10,... | collective-permute-start | bytes 393224 | tf_op jit(solution)/shard_map/ppermute | solution.py:256
  24.1 19.1 %collective-permute-start.11 = (bf16[128,512]{1,0:T(8,128)(2,1)S(1)}, bf16[128,512]{1,0:T(8,128)(2,1)S(1)}, u32[]{:S(2)}, u32[]{:S(2)}) collective-permute-start(bf16[128,512]{1,0:T(8,128)(2,1)S(1)} %get-tuple-element.43), channel_id=1, source_target_pairs={{0,5},{1,4},{2,7},{3,6},{4,1},{5,0},{6,3},{7,2},{8,13},{9,12},{10,... | collective-permute-start | bytes 393224 | tf_op jit(solution)/shard_map/ppermute | solution.py:256
  25.5 17.7 %collective-permute-start.12 = (bf16[128,512]{1,0:T(8,128)(2,1)S(1)}, bf16[128,512]{1,0:T(8,128)(2,1)S(1)}, u32[]{:S(2)}, u32[]{:S(2)}) collective-permute-start(bf16[128,512]{1,0:T(8,128)(2,1)S(1)} %get-tuple-element.44), channel_id=1, source_target_pairs={{0,6},{1,7},{2,4},{3,5},{4,2},{5,3},{6,0},{7,1},{8,14},{9,15},{10,... | collective-permute-start | bytes 393224 | tf_op jit(solution)/shard_map/ppermute | solution.py:256
  31.1 12.1 %collective-permute-start.13 = (bf16[128,512]{1,0:T(8,128)(2,1)S(1)}, bf16[128,512]{1,0:T(8,128)(2,1)S(1)}, u32[]{:S(2)}, u32[]{:S(2)}) collective-permute-start(bf16[128,512]{1,0:T(8,128)(2,1)S(1)} %get-tuple-element.45), channel_id=1, source_target_pairs={{0,7},{1,6},{2,5},{3,4},{4,3},{5,2},{6,1},{7,0},{8,15},{9,14},{10,... | collective-permute-start | bytes 393224 | tf_op jit(solution)/shard_map/ppermute | solution.py:256
  34.5 8.7 %copy-start.1 = (bf16[1,4,4,128,128]{4,3,2,1,0:T(8,128)(2,1)S(1)}, bf16[1,4,4,128,128]{4,3,2,1,0:T(8,128)(2,1)}, u32[]{:S(2)}) copy-start(bf16[1,4,4,128,128]{4,3,2,1,0:T(8,128)(2,1)} %param.15) | copy-start | bytes 1572868
  34.5 8.7 %copy-start.4 = (bf16[128,1024]{1,0:T(8,128)(2,1)S(1)}, bf16[128,1024]{1,0:T(8,128)(2,1)}, u32[]{:S(2)}) copy-start(bf16[128,1024]{1,0:T(8,128)(2,1)} %w_in.1) | copy-start | bytes 786436
  34.5 8.7 %copy-start.7 = (f32[1024]{0:T(1024)S(1)}, f32[1024]{0:T(1024)}, u32[]{:S(2)}) copy-start(f32[1024]{0:T(1024)} %param.19) | copy-start | bytes 12292
  55.9 2.5 %collective-permute-start.14 = (f32[4,312,128]{2,1,0:T(8,128)S(1)}, f32[4,312,128]{2,1,0:T(8,128)S(1)}, u32[]{:S(2)}, u32[]{:S(2)}) collective-permute-start(f32[4,312,128]{2,1,0:T(8,128)S(1)} %get-tuple-element.47), channel_id=1, source_target_pairs={{0,1},{1,0},{2,3},{3,2},{4,5},{5,4},{6,7},{7,6},{8,9},{9,8},{10,11... | collective-permute-start | bytes 1916936 | tf_op jit(solution)/shard_map/ppermute | solution.py:256
  58.5 4.8 %collective-permute-start.15 = (s16[320,128]{1,0:T(8,128)(2,1)S(1)}, s16[320,128]{1,0:T(8,128)(2,1)S(1)}, u32[]{:S(2)}, u32[]{:S(2)}) collective-permute-start(s16[320,128]{1,0:T(8,128)(2,1)S(1)} %get-tuple-element.49), channel_id=1, source_target_pairs={{0,8},{8,0},{16,24},{24,16},{1,9},{9,1},{17,25},{25,17},{2,10},{10... | collective-permute-start | bytes 245768 | tf_op jit(solution)/shard_map/ppermute | solution.py:256
  60.1 5.3 %collective-permute-start.16 = (s16[320,128]{1,0:T(8,128)(2,1)S(1)}, s16[320,128]{1,0:T(8,128)(2,1)S(1)}, u32[]{:S(2)}, u32[]{:S(2)}) collective-permute-start(s16[320,128]{1,0:T(8,128)(2,1)S(1)} %get-tuple-element.50), channel_id=1, source_target_pairs={{0,16},{8,24},{16,0},{24,8},{1,17},{9,25},{17,1},{25,9},{2,18},{10... | collective-permute-start | bytes 245768 | tf_op jit(solution)/shard_map/ppermute | solution.py:256
  61.6 5.3 %collective-permute-start.17 = (s16[320,128]{1,0:T(8,128)(2,1)S(1)}, s16[320,128]{1,0:T(8,128)(2,1)S(1)}, u32[]{:S(2)}, u32[]{:S(2)}) collective-permute-start(s16[320,128]{1,0:T(8,128)(2,1)S(1)} %get-tuple-element.51), channel_id=1, source_target_pairs={{0,24},{8,16},{16,8},{24,0},{1,25},{9,17},{17,9},{25,1},{2,26},{10... | collective-permute-start | bytes 245768 | tf_op jit(solution)/shard_map/ppermute | solution.py:256
  67.1 7.3 %collective-permute-start.20 = (s16[320,128]{1,0:T(8,128)(2,1)S(1)}, s16[320,128]{1,0:T(8,128)(2,1)S(1)}, u32[]{:S(2)}, u32[]{:S(2)}) collective-permute-start(s16[320,128]{1,0:T(8,128)(2,1)S(1)} %shard_map.142.refs_0_), channel_id=1, source_target_pairs={{0,6},{1,7},{2,4},{3,5},{4,2},{5,3},{6,0},{7,1},{8,14},{9,15},{10,... | collective-permute-start | bytes 245768 | tf_op jit(solution)/shard_map/ppermute | solution.py:256
  68.2 10.7 %collective-permute-start.19 = (s16[320,128]{1,0:T(8,128)(2,1)S(1)}, s16[320,128]{1,0:T(8,128)(2,1)S(1)}, u32[]{:S(2)}, u32[]{:S(2)}) collective-permute-start(s16[320,128]{1,0:T(8,128)(2,1)S(1)} %shard_map.142.refs_0_), channel_id=1, source_target_pairs={{0,4},{1,5},{2,6},{3,7},{4,0},{5,1},{6,2},{7,3},{8,12},{9,13},{10,... | collective-permute-start | bytes 245768 | tf_op jit(solution)/shard_map/ppermute | solution.py:256
  74.4 5.3 %collective-permute-start.18 = (s16[320,128]{1,0:T(8,128)(2,1)S(1)}, s16[320,128]{1,0:T(8,128)(2,1)S(1)}, u32[]{:S(2)}, u32[]{:S(2)}) collective-permute-start(s16[320,128]{1,0:T(8,128)(2,1)S(1)} %shard_map.142.refs_0_), channel_id=1, source_target_pairs={{0,2},{1,3},{2,0},{3,1},{4,6},{5,7},{6,4},{7,5},{8,10},{9,11},{10,... | collective-permute-start | bytes 245768 | tf_op jit(solution)/shard_map/ppermute | solution.py:256
  79.8 5.5 %collective-permute-start.23 = (s16[320,128]{1,0:T(8,128)(2,1)S(1)}, s16[320,128]{1,0:T(8,128)(2,1)S(1)}, u32[]{:S(2)}, u32[]{:S(2)}) collective-permute-start(s16[320,128]{1,0:T(8,128)(2,1)S(1)} %shard_map.143.refs_0_), channel_id=1, source_target_pairs={{0,24},{8,16},{16,8},{24,0},{1,25},{9,17},{17,9},{25,1},{2,26},{10... | collective-permute-start | bytes 245768 | tf_op jit(solution)/shard_map/ppermute | solution.py:256
  80.7 5.3 %collective-permute-start.22 = (s16[320,128]{1,0:T(8,128)(2,1)S(1)}, s16[320,128]{1,0:T(8,128)(2,1)S(1)}, u32[]{:S(2)}, u32[]{:S(2)}) collective-permute-start(s16[320,128]{1,0:T(8,128)(2,1)S(1)} %shard_map.143.refs_0_), channel_id=1, source_target_pairs={{0,16},{8,24},{16,0},{24,8},{1,17},{9,25},{17,1},{25,9},{2,18},{10... | collective-permute-start | bytes 245768 | tf_op jit(solution)/shard_map/ppermute | solution.py:256
  81.9 4.4 %collective-permute-start.21 = (s16[320,128]{1,0:T(8,128)(2,1)S(1)}, s16[320,128]{1,0:T(8,128)(2,1)S(1)}, u32[]{:S(2)}, u32[]{:S(2)}) collective-permute-start(s16[320,128]{1,0:T(8,128)(2,1)S(1)} %shard_map.143.refs_0_), channel_id=1, source_target_pairs={{0,8},{8,0},{16,24},{24,16},{1,9},{9,1},{17,25},{25,17},{2,10},{10... | collective-permute-start | bytes 245768 | tf_op jit(solution)/shard_map/ppermute | solution.py:256
  83.4 3.2 %collective-permute-start.24 = (s16[320,128]{1,0:T(8,128)(2,1)S(1)}, s16[320,128]{1,0:T(8,128)(2,1)S(1)}, u32[]{:S(2)}, u32[]{:S(2)}) collective-permute-start(s16[320,128]{1,0:T(8,128)(2,1)S(1)} %shard_map.143.refs_0_), channel_id=1, source_target_pairs={{0,1},{1,0},{2,3},{3,2},{4,5},{5,4},{6,7},{7,6},{8,9},{9,8},{10,11... | collective-permute-start | bytes 245768 | tf_op jit(solution)/shard_map/ppermute | solution.py:256
  85.3 1.3 %collective-permute-start.27 = (s16[320,128]{1,0:T(8,128)(2,1)S(1)}, s16[320,128]{1,0:T(8,128)(2,1)S(1)}, u32[]{:S(2)}, u32[]{:S(2)}) collective-permute-start(s16[320,128]{1,0:T(8,128)(2,1)S(1)} %collective-permute-done.23.refs_3_), channel_id=1, source_target_pairs={{0,1},{1,0},{2,3},{3,2},{4,5},{5,4},{6,7},{7,6},{8,9},{9,8},{10,11... | collective-permute-start | bytes 245768 | tf_op jit(solution)/shard_map/ppermute | solution.py:256
  86.1 1.3 %collective-permute-start.26 = (s16[320,128]{1,0:T(8,128)(2,1)S(1)}, s16[320,128]{1,0:T(8,128)(2,1)S(1)}, u32[]{:S(2)}, u32[]{:S(2)}) collective-permute-start(s16[320,128]{1,0:T(8,128)(2,1)S(1)} %collective-permute-done.22.refs_2_), channel_id=1, source_target_pairs={{0,1},{1,0},{2,3},{3,2},{4,5},{5,4},{6,7},{7,6},{8,9},{9,8},{10,11... | collective-permute-start | bytes 245768 | tf_op jit(solution)/shard_map/ppermute | solution.py:256
  86.4 1.3 %collective-permute-start.25 = (s16[320,128]{1,0:T(8,128)(2,1)S(1)}, s16[320,128]{1,0:T(8,128)(2,1)S(1)}, u32[]{:S(2)}, u32[]{:S(2)}) collective-permute-start(s16[320,128]{1,0:T(8,128)(2,1)S(1)} %collective-permute-done.21.refs_1_), channel_id=1, source_target_pairs={{0,1},{1,0},{2,3},{3,2},{4,5},{5,4},{6,7},{7,6},{8,9},{9,8},{10,11... | collective-permute-start | bytes 245768 | tf_op jit(solution)/shard_map/ppermute | solution.py:256
  (9 other events, 24.3 us)

commit v3 on v1

v3 whole, which is shorter than its diff:
```python
import functools

import jax
import jax.numpy as jnp
from jax import lax
from jax.experimental import pallas as pl
from jax.experimental.pallas import tpu as pltpu
from jax.sharding import PartitionSpec as P

ORDER = 2
KEEP_RATE = 0.5
XBAR_SCALE = 1.0 / ((ORDER + 1) * KEEP_RATE)
F32, BF16, I16, I32 = jnp.float32, jnp.bfloat16, jnp.int16, jnp.int32
MIB = 1024 * 1024
SMEM = pl.BlockSpec(memory_space=pltpu.SMEM)
VMEM = pl.BlockSpec(memory_space=pltpu.VMEM)
HBM = pl.BlockSpec(memory_space=pltpu.HBM)
CHUNK = 256
BATCH = 1
TAIL = 8


def call(kernel, outs, ins, scratch=(), n_smem=0, n_hbm=0, vmem=8):
    return pl.pallas_call(
        kernel,
        out_shape=outs,
        in_specs=[SMEM] * n_smem + [HBM] * n_hbm + [VMEM] * (len(ins) - n_smem - n_hbm),
        out_specs=jax.tree.map(lambda _: VMEM, outs),
        scratch_shapes=list(scratch),
        compiler_params=pltpu.CompilerParams(vmem_limit_bytes=vmem * MIB),
    )(*ins)


def like(shape, dtype):
    return jax.ShapeDtypeStruct(shape, dtype)


def partners(dom):
    tops = [1 << b for b in reversed(range((dom - 1).bit_length()))]
    return [k for odd in (0, 1) for top in tops for k in range(top, 2 * top) if k % 2 == odd]


def select_kernel(info, feats, masks, *msgs):
    tile = feats.shape[1]
    samples = masks.shape[0]
    for i, k in enumerate(partners(len(msgs) + 1)):
        t = info[3 + (info[0] ^ k)]
        out = msgs[i]
        out[:tile, :] = feats[t]
        m = masks[:, pl.ds(pl.multiple_of(t * tile, tile), tile)]
        out[tile:, :] = jnp.concatenate([m, jnp.zeros((out.shape[0] - tile - samples, tile), BF16)], 0)


def masked_tile(f, m, put):
    samples, tile = m.shape
    cols = jnp.concatenate([m.astype(F32), jnp.zeros((8 - samples, tile), F32)], 0).T
    f = f.astype(F32)
    for s in range(samples):
        put(s, (f * cols[:, s : s + 1]).astype(BF16))


def layout_kernel(after, feats, masks, adj, lhs, own):
    tiles, tile, feat = feats.shape
    for t in range(tiles):
        lhs[t] = jnp.concatenate([adj[t, j] for j in range(adj.shape[1])], 1)

        def put(s, x):
            own[t, :, s * feat : (s + 1) * feat] = x

        masked_tile(feats[t], masks[:, t * tile : (t + 1) * tile], put)


def pool_index(info, slots, r, j, dom, nnz):
    q = slots[r * nnz + j]
    k = q ^ info[0]
    own = (dom - 1) + info[3 + info[0]]
    return jnp.where(q >= dom, q - 1, jnp.where(k == 0, own, k - 1))


def hop_rows(info, slots, lhs, pool, r, dom):
    nnz = lhs.shape[2] // lhs.shape[1]
    rhs = jnp.concatenate([pool[pool_index(info, slots, r, j, dom, nnz)] for j in range(nnz)], 0)
    return jnp.dot(lhs[r], rhs, preferred_element_type=F32)


def hop1_kernel(dom, samples, info, slots, lhs, own, *refs):
    msgs, (cur, total), outs, pool = refs[: dom - 1], refs[dom - 1 : dom + 1], refs[dom + 1 : -1], refs[-1]
    tiles, tile, lanes = own.shape
    feat = lanes // samples
    for i, k in enumerate(partners(dom)):

        def put(s, x):
            pool[k - 1, :, s * feat : (s + 1) * feat] = x

        masked_tile(msgs[i][:tile, :], msgs[i][tile : tile + samples, :], put)
    for t in range(tiles):
        pool[dom - 1 + t] = own[t]
    for r in range(tiles):
        hop = hop_rows(info, slots, lhs, pool, r, dom)
        cur[r] = hop.astype(BF16)
        total[r] = hop + own[r].astype(F32)
    for i, k in enumerate(partners(dom)):
        outs[i][...] = cur[info[3 + (info[0] ^ k)]]


def mlp_kernel(dom, samples, classes, scale, info, slots, lhs, cur, total, code, w_in, b_in, w_out, w_out_t, b_out, *refs):
    recv = refs[: dom - 1]
    keep, send, pool, x_t, act, slope, prob, dl, dl_t, dpre, acc, bias_acc, cls_acc = refs[dom - 1 :]
    tiles, tile, lanes = cur.shape
    feat = lanes // samples
    hidden = w_in.shape[1]
    wide = w_out.shape[1]
    rows = samples * tile
    nch = hidden // CHUNK
    for i, k in enumerate(partners(dom)):
        pool[k - 1] = recv[i][...]
    for t in range(tiles):
        pool[dom - 1 + t] = cur[t]
    bias_acc[...] = jnp.zeros(bias_acc.shape, F32)
    cls_acc[...] = jnp.zeros(cls_acc.shape, F32)

    def one_tile(r, carry):
        hop = hop_rows(info, slots, lhs, pool, r, dom)
        xbar = ((total[r] + hop) * XBAR_SCALE).astype(BF16)
        base = pl.multiple_of(r * rows, rows)
        for s in range(samples):
            x_t[:, pl.ds(base + s * tile, tile)] = xbar[:, s * feat : (s + 1) * feat].T
        for s in range(0, samples, BATCH):
            x = jnp.concatenate([xbar[:, i * feat : (i + 1) * feat] for i in range(s, s + BATCH)], 0)
            here = pl.ds(base + s * tile, BATCH * tile)
            there = slice(s * tile, (s + BATCH) * tile)
            for n in range(nch):
                cols = slice(n * CHUNK, (n + 1) * CHUNK)
                half = jnp.dot(x, w_in[:, cols], preferred_element_type=F32) + b_in[:, cols]
                t = jnp.tanh(half)
                up = 1.0 + t
                silu = half * up
                act[here, cols] = silu.astype(BF16)
                slope[there, cols] = up + silu * (1.0 - t)
            logits = jnp.dot(act[here, :], w_out[...], preferred_element_type=F32) + b_out[...]
            e = jnp.exp(logits)
            prob[there, :] = e * (1.0 / jnp.sum(e, -1, keepdims=True))
        step = 32
        for c in range(0, tile, step):
            probs = [prob[s * tile + c : s * tile + c + step, :] for s in range(samples)]
            avg = sum(probs[1:], probs[0]) * (1.0 / samples)
            sq = avg * avg
            sharp = sq * (1.0 / jnp.sum(sq, -1, keepdims=True))
            label = code[r, c : c + step, :]
            hit = jnp.where(lax.broadcasted_iota(I32, (step, wide), 1) == label, scale, 0.0)
            used = jnp.where(label >= 0, scale, 0.0)
            part = jnp.zeros((step, wide), F32)
            for s, p in enumerate(probs):
                off = p - sharp
                inner = jnp.sum(off * p, -1, keepdims=True)
                d = p * ((2.0 * scale) * (off - inner) + used) - hit
                part = part + d
                dl[s * tile + c : s * tile + c + step, :] = d.astype(BF16)
            cls_acc[...] += functools.reduce(lambda a, b: a + b, [part[i : i + 8] for i in range(0, step, 8)])
        for s in range(samples):
            d = dl[s * tile : (s + 1) * tile, :]
            dl_t[:, pl.ds(base + s * tile, tile)] = d.T[: dl_t.shape[0]]
            for n in range(nch):
                cols = slice(n * CHUNK, (n + 1) * CHUNK)
                dact = jnp.dot(d, w_out_t[:, cols], preferred_element_type=F32)
                dp = dact * slope[s * tile : (s + 1) * tile, cols]
                dpre[pl.ds(base + s * tile, tile), cols] = dp.astype(BF16)
                bias_acc[:, cols] += functools.reduce(lambda a, b: a + b, [dp[i : i + 8] for i in range(0, tile, 8)])
        return carry

    lax.fori_loop(0, tiles, one_tile, 0)
    lanes_out = acc.shape[2]
    wide_t = dl_t.shape[0]
    cls = jnp.sum(cls_acc[...], 0, keepdims=True)
    for n in range(nch):
        cols = slice(n * CHUNK, (n + 1) * CHUNK)
        g_in = jnp.dot(x_t[...], dpre[:, cols], preferred_element_type=F32)
        g_out = jnp.dot(dl_t[...], act[:, cols], preferred_element_type=F32)
        g_bias = jnp.sum(bias_acc[:, cols], 0, keepdims=True)
        for i in range(CHUNK // lanes_out):
            at = n * (CHUNK // lanes_out) + i
            part = slice(i * lanes_out, (i + 1) * lanes_out)
            acc[at, :feat, :] = g_in[:, part]
            acc[at, feat : feat + wide_t, :] = g_out[:, part]
            acc[at, feat + wide_t :, :] = jnp.concatenate(
                [g_bias[:, part]]
                + [cls[:, i * lanes_out : (i + 1) * lanes_out] for i in range(wide // lanes_out)]
                + [jnp.zeros((TAIL - 1 - wide // lanes_out, lanes_out), F32)],
                0,
            )
    for m in range(keep.shape[0]):
        pair = (info[1] ^ m) * 2
        keep[m] = acc[pair + info[2]]
        send[m] = acc[pair + 1 - info[2]]


def mlp_call(dom, samples, tiles, tile, feat, hidden, classes, wide, ins):
    lanes = samples * feat
    rows = samples * tile
    all_rows = rows * tiles
    wide_t = -(-classes // 16) * 16
    piece = (feat + wide_t + TAIL, 128)
    pieces = hidden // 128
    return call(
        functools.partial(mlp_kernel, dom, samples, classes, 1.0 / (samples * tiles * tile)),
        [like((pieces // 2,) + piece, F32)] * 2,
        list(ins),
        [
            pltpu.VMEM((dom - 1 + tiles, tile, lanes), BF16),
            pltpu.VMEM((feat, all_rows), BF16),
            pltpu.VMEM((all_rows, hidden), BF16),
            pltpu.VMEM((rows, hidden), F32),
            pltpu.VMEM((rows, wide), F32),
            pltpu.VMEM((rows, wide), BF16),
            pltpu.VMEM((wide_t, all_rows), BF16),
            pltpu.VMEM((all_rows, hidden), BF16),
            pltpu.VMEM((pieces,) + piece, F32),
            pltpu.VMEM((8, hidden), F32),
            pltpu.VMEM((8, wide), F32),
        ],
        n_smem=2,
        vmem=28,
    )


def encode(x, feat, n_tail):
    body = x.shape[0] - TAIL
    parts = [x[:feat], x[feat:body]] + [x[body + i : body + i + 1] for i in range(n_tail)]
    ints, exps = [], []
    for p in parts:
        top = jnp.max(jnp.abs(p), 0, keepdims=True)
        e = jnp.floor(jnp.log2(jnp.maximum(top, 1e-30)))
        q = jnp.round(p * jnp.exp2(14.0 - e))
        ints.append(jnp.clip(q, -32767.0, 32767.0).astype(I32))
        exps.append(e.astype(I32))
    used = 2 * n_tail + 2
    last = ints[2:] + exps + [jnp.zeros((2 * TAIL - used, x.shape[1]), I32)]
    return jnp.concatenate(ints[:2] + [jnp.concatenate(last, 0)], 0).astype(I16)


def decode(ref, feat, n_tail):
    body = ref.shape[0] - 2 * TAIL
    v = ref[...].astype(I32).astype(F32)
    last = v[body:]
    scales = jnp.exp2(last[n_tail : 2 * n_tail + 2] - 14.0)
    tail = jnp.concatenate(
        [last[:n_tail] * scales[2:], jnp.zeros((TAIL - n_tail, v.shape[1]), F32)], 0
    )
    return jnp.concatenate([v[:feat] * scales[0:1], v[feat:body] * scales[1:2], tail], 0)


def pair_kernel(feat, n_tail, keep, recv, own, *msgs):
    own[...] = keep[0] + recv[0]
    for m in range(1, keep.shape[0]):
        msgs[m - 1][...] = encode(keep[m] + recv[m], feat, n_tail)


def scatter_kernel(feat, n_tail, n_out, own, *refs):
    total = own[...]
    msgs, outs = refs[: -n_out], refs[-n_out:]
    for ref in msgs:
        total = total + decode(ref, feat, n_tail)
    q = encode(total, feat, n_tail)
    for ref in outs:
        ref[...] = q


def tree_kernel(feat, n_tail, order, *refs):
    n_in = len(order) + 1
    parts = [decode(refs[i], feat, n_tail) for i in [n_in - 1] + [order.index(m) for m in range(len(order))]]
    while len(parts) > 1:
        parts = [a + b for a, b in zip(parts[::2], parts[1::2])]
    q = encode(parts[0], feat, n_tail)
    for ref in refs[n_in:]:
        ref[...] = q


def unpack_kernel(feat, n_tail, classes, info, *refs):
    pieces, (g_in, b_in, g_out, b_out) = refs[:-4], refs[-4:]
    lanes = pieces[0].shape[1]
    half = len(pieces) // 2
    body = pieces[0].shape[0] - 2 * TAIL
    for c in range(2):
        for m in range(half):
            at = (info[1] ^ m) * 2 + (info[2] ^ c)
            x = decode(pieces[c * half + m], feat, n_tail)
            where = pl.ds(pl.multiple_of(at * lanes, lanes), lanes)
            g_in[:, where] = x[:feat]
            g_out[:, where] = x[feat : feat + classes]
            b_in[:, where] = x[body : body + 1]

            @pl.when(at == 0)
            def _():
                for i in range(n_tail - 1):
                    b_out[:, i * lanes : (i + 1) * lanes] = x[body + 1 + i : body + 2 + i]


def xor_permute(x, axis, mask):
    return lax.ppermute(x, axis, [(i, i ^ mask) for i in range(lax.axis_size(axis))])


def swap_all(blocks):
    return [xor_permute(x, "dom", k) for k, x in zip(partners(len(blocks) + 1), blocks)]


def bit_groups(axis, first):
    size, bit, groups = lax.axis_size(axis), first, []
    while (1 << bit) < size:
        groups.append([m << bit for m in (1, 2, 3) if (m << bit) < size])
        bit += 2
    return groups


def reduce_grads(keep, send, info, feat, n_tail, classes, hidden):
    count, rows, lanes = keep.shape
    coded = like((rows + TAIL, lanes), I16)
    recv = xor_permute(send, "dom", 1)
    own, *msgs = call(
        functools.partial(pair_kernel, feat, n_tail),
        [like((rows, lanes), F32)] + [coded] * (count - 1),
        [keep, recv],
    )
    msgs = [xor_permute(x, "dp", m + 1) for m, x in enumerate(msgs)]
    groups = [("dom", masks) for masks in bit_groups("dom", 1)] + [("dp", masks) for masks in bit_groups("dp", 2)]
    qs = call(functools.partial(scatter_kernel, feat, n_tail, 4), [coded] * 4, [own] + msgs)
    for axis, masks in groups:
        order = [m for m in (1, 2, 0) if m < len(masks)]
        got = [xor_permute(qs[i + 1], axis, masks[m]) for i, m in enumerate(order)]
        qs = call(functools.partial(tree_kernel, feat, n_tail, order), [coded] * 4, got + [qs[0]])
    pieces = [qs[0]] + [xor_permute(qs[m], "dp", m) for m in range(1, count)]
    pieces = pieces + [xor_permute(x, "dom", 1) for x in pieces]
    return call(
        functools.partial(unpack_kernel, feat, n_tail, classes),
        [like((feat, hidden), F32), like((1, hidden), F32), like((classes, hidden), F32), like((1, (n_tail - 1) * lanes), F32)],
        [info] + pieces,
        n_smem=1,
    )


def per_device(
    features,
    keep_masks,
    serve_ids,
    col_slot,
    adj_blocks,
    node_labels,
    labeled,
    weight_in,
    bias_in,
    weight_out,
    bias_out,
):
    tiles, nnz = col_slot.shape[1:]
    tile = adj_blocks.shape[-1]
    feat = features.shape[-1]
    samples = keep_masks.shape[1]
    hidden, classes = weight_out.shape
    dom = lax.axis_size("dom")
    me = lax.axis_index("dom")
    place = jnp.stack([me, lax.axis_index("dp") & 3, me & 1]).astype(I32)
    info = jnp.concatenate([place, serve_ids.reshape(-1)])
    slots = col_slot.reshape(-1)
    adj = adj_blocks[0]
    feats = features.reshape(tiles, tile, feat)
    masks = keep_masks[0]
    lanes = samples * feat
    wide = -(-classes // 128) * 128

    msgs = call(
        select_kernel,
        [like((tile + 16, feat), BF16)] * (dom - 1),
        [info, feats, masks],
        n_smem=1,
    )
    lhs, own = call(
        layout_kernel,
        [like((tiles, tile, nnz * tile), BF16), like((tiles, tile, lanes), BF16)],
        [msgs[-1], feats, masks, adj],
        n_hbm=1,
    )
    msgs = swap_all(msgs)
    cur, total, *outs = call(
        functools.partial(hop1_kernel, dom, samples),
        [like((tiles, tile, lanes), BF16), like((tiles, tile, lanes), F32)] + [like((tile, lanes), BF16)] * (dom - 1),
        [info, slots, lhs, own] + msgs,
        [pltpu.VMEM((dom - 1 + tiles, tile, lanes), BF16)],
        n_smem=2,
    )
    outs = swap_all(outs)

    code = jnp.where(labeled != 0, node_labels, -1).reshape(tiles, tile, 1)
    w_out = jnp.pad(weight_out, ((0, 0), (0, wide - classes)))
    b_out = jnp.pad(bias_out, (0, wide - classes), constant_values=-1e30).reshape(1, wide)
    keep, send = mlp_call(
        dom, samples, tiles, tile, feat, hidden, classes, wide,
        [info, slots, lhs, cur, total, code, 0.5 * weight_in, 0.5 * bias_in.reshape(1, hidden), w_out, 0.5 * w_out.T, b_out] + outs,
    )
    g_in, b_in, g_out, b_out = reduce_grads(keep, send, info, feat, 1 + wide // 128, classes, hidden)
    return g_in, b_in.reshape(hidden), g_out.T, b_out.reshape(-1)[:classes]


def solution(mesh):
    placed = (
        P("dp", "dom", None),
        P("dp", None, "dom"),
        P("dp", "dom", None, None),
        P("dp", "dom", None),
        P("dp", "dom", None, None, None),
        P("dp", "dom"),
        P("dp", "dom"),
        P(),
        P(),
        P(),
        P(),
    )
    return jax.shard_map(
        per_device, mesh=mesh, in_specs=placed, out_specs=(P(), P(), P(), P()), check_vma=False
    )
```

time: 92.8 us -> 84.9 us (0.915)
  waiting for transfers between devices: 36.8 us -> 30.4 us
  Pallas kernels: 18.4 us -> 16.2 us
  other arithmetic: 0.08 us -> 1.88 us
    ppermute x28, waiting for transfers between devices: 36.8 us -> 30.4 us  [xor_permute(): lax.ppermute(x, axis, [(i, i ^ mask) for i in range(lax.axis_size(axis))])]
    pallas_call x7 -> x8, Pallas kernels: 18.4 us -> 16.2 us  [call(): pl.pallas_call(kernel, out_shape=outs, in_specs=[SMEM] * n_smem + [HBM] *...]
    unnamed x31 -> x23, local copies, waits for them, and re-layouts: 5.39 us -> 4.21 us
    pad x1, local copies, waits for them, and re-layouts: 0.09 us -> 1.18 us  [per_device(): w_out = jnp.pad(weight_out, ((0, 0), (0, wide - classes)))]
    mul x0 -> x3, other arithmetic: none -> 1.09 us  [the longest x1 1.01 us: per_device(): 0.5 * weight_in]
  transfers between devices with their start and end apart: 28 -> 28, of which waited for: 17 -> 16; matrix products, arithmetic and copies ran while one was open for 1% -> 5% of each run, Pallas kernels for 0% -> 0%
where the time goes in v3:
time: 84.9 us; the launch traced here: 84.7 us
  waiting for transfers between devices  30.4 us (36%)
  starting transfers between devices  29.8 us (35%)
  Pallas kernels  16.2 us (19%)
  local copies, waits for them, and re-layouts  5.62 us (7%)
  other arithmetic  1.88 us (2%)
    ppermute x28, waiting for transfers between devices, xor_permute(): lax.ppermute(x, axis, [(i, i ^ mask) for i in range(lax.axis_size(axis))])  30.4 us
    ppermute x28, starting transfers between devices, xor_permute(): lax.ppermute(x, axis, [(i, i ^ mask) for i in range(lax.axis_size(axis))])  29.8 us
    pallas_call x8, Pallas kernels, call(): pl.pallas_call(kernel, out_shape=outs, in_specs=[SMEM] * n_smem + [HBM] *...  16.2 us
    unnamed x23, local copies, waits for them, and re-layouts  4.21 us
  transfers between devices with their start and end apart: 28, of which 16 were waited for; matrix products, arithmetic and copies ran while one was open for 5% of the time, Pallas kernels for 0%

profile of v3, /device:TPU:0, one launch (start us, length us, event | category | flops | bytes accessed | tf_op | source)
XLA Modules:
  0.0 84.7 jit_solution(4135096972401445693)
XLA Ops:
  1.4 0.9 %copy-done.1 = bf16[1,512,128]{2,1,0:T(8,128)(2,1)S(1)} copy-done((bf16[1,512,128]{2,1,0:T(8,128)(2,1)S(1)}, bf16[1,512,128]{2,1,0:T(8,128)(2,1)}, u32[]{:S(2)}) %copy-start.1) | copy-done | bytes 131096
  3.6 4.1 %collective-permute-start = (bf16[144,128]{1,0:T(8,128)(2,1)S(1)}, bf16[144,128]{1,0:T(8,128)(2,1)S(1)}, u32[]{:S(2)}, u32[]{:S(2)}) collective-permute-start(bf16[144,128]{1,0:T(8,128)(2,1)S(1)} %get-tuple-element.43), channel_id=1, source_target_pairs={{0,4},{1,5},{2,6},{3,7},{4,0},{5,1},{6,2},{7,3},{8,12},{9,13},{10,... | collective-permute-start | bytes 110600 | tf_op jit(solution)/shard_map/ppermute | solution.py:299
  7.7 1.3 %collective-permute-start.1 = (bf16[144,128]{1,0:T(8,128)(2,1)S(1)}, bf16[144,128]{1,0:T(8,128)(2,1)S(1)}, u32[]{:S(2)}, u32[]{:S(2)}) collective-permute-start(bf16[144,128]{1,0:T(8,128)(2,1)S(1)} %get-tuple-element.44), channel_id=1, source_target_pairs={{0,6},{1,7},{2,4},{3,5},{4,2},{5,3},{6,0},{7,1},{8,14},{9,15},{10,... | collective-permute-start | bytes 110600 | tf_op jit(solution)/shard_map/ppermute | solution.py:299
  9.3 1.4 %collective-permute-start.3 = (bf16[144,128]{1,0:T(8,128)(2,1)S(1)}, bf16[144,128]{1,0:T(8,128)(2,1)S(1)}, u32[]{:S(2)}, u32[]{:S(2)}) collective-permute-start(bf16[144,128]{1,0:T(8,128)(2,1)S(1)} %get-tuple-element.46), channel_id=1, source_target_pairs={{0,5},{1,4},{2,7},{3,6},{4,1},{5,0},{6,3},{7,2},{8,13},{9,12},{10,... | collective-permute-start | bytes 110600 | tf_op jit(solution)/shard_map/ppermute | solution.py:299
  10.7 2.5 %collective-permute-start.4 = (bf16[144,128]{1,0:T(8,128)(2,1)S(1)}, bf16[144,128]{1,0:T(8,128)(2,1)S(1)}, u32[]{:S(2)}, u32[]{:S(2)}) collective-permute-start(bf16[144,128]{1,0:T(8,128)(2,1)S(1)} %get-tuple-element.47), channel_id=1, source_target_pairs={{0,7},{1,6},{2,5},{3,4},{4,3},{5,2},{6,1},{7,0},{8,15},{9,14},{10,... | collective-permute-start | bytes 110600 | tf_op jit(solution)/shard_map/ppermute | solution.py:299
  13.5 1.0 %broadcast_multiply_fusion.w_in = bf16[128,1024]{1,0:T(8,128)(2,1)S(1)} fusion(bf16[128,1024]{1,0:T(8,128)(2,1)} %param.18), kind=kLoop, calls=%fused_computation.1 | loop fusion | flops 131072 | bytes 524288 | tf_op jit(solution)/shard_map/mul | solution.py:396
  16.7 2.3 %shard_map.140 = (bf16[4,128,512]{2,1,0:T(8,128)(2,1)S(1)}, f32[4,128,512]{2,1,0:T(8,128)S(1)}, bf16[128,512]{1,0:T(8,128)(2,1)S(1)}, bf16[128,512]{1,0:T(8,128)...) custom-call(s32[11]{0:T(128)S(1)} %pad_add_fusion.info, ...), custom_call_target="tpu_custom_call" | custom-call | tf_op jit(solution)/shard_map/pallas_call | solution.py:24
  19.0 1.7 %collective-permute-start.7 = (bf16[128,512]{1,0:T(8,128)(2,1)S(1)}, bf16[128,512]{1,0:T(8,128)(2,1)S(1)}, u32[]{:S(2)}, u32[]{:S(2)}) collective-permute-start(bf16[128,512]{1,0:T(8,128)(2,1)S(1)} %get-tuple-element.51), channel_id=1, source_target_pairs={{0,4},{1,5},{2,6},{3,7},{4,0},{5,1},{6,2},{7,3},{8,12},{9,13},{10,... | collective-permute-start | bytes 393224 | tf_op jit(solution)/shard_map/ppermute | solution.py:299
  20.7 1.3 %collective-permute-start.8 = (bf16[128,512]{1,0:T(8,128)(2,1)S(1)}, bf16[128,512]{1,0:T(8,128)(2,1)S(1)}, u32[]{:S(2)}, u32[]{:S(2)}) collective-permute-start(bf16[128,512]{1,0:T(8,128)(2,1)S(1)} %get-tuple-element.52), channel_id=1, source_target_pairs={{0,6},{1,7},{2,4},{3,5},{4,2},{5,3},{6,0},{7,1},{8,14},{9,15},{10,... | collective-permute-start | bytes 393224 | tf_op jit(solution)/shard_map/ppermute | solution.py:299
  22.5 1.5 %collective-permute-start.10 = (bf16[128,512]{1,0:T(8,128)(2,1)}, bf16[128,512]{1,0:T(8,128)(2,1)S(1)}, u32[]{:S(2)}, u32[]{:S(2)}) collective-permute-start(bf16[128,512]{1,0:T(8,128)(2,1)} %get-tuple-element.54), channel_id=1, source_target_pairs={{0,5},{1,4},{2,7},{3,6},{4,1},{5,0},{6,3},{7,2},{8,13},{9,12},{10,... | collective-permute-start | bytes 393224 | tf_op jit(solution)/shard_map/ppermute | solution.py:299
  23.9 2.3 %collective-permute-start.11 = (bf16[128,512]{1,0:T(8,128)(2,1)}, bf16[128,512]{1,0:T(8,128)(2,1)S(1)}, u32[]{:S(2)}, u32[]{:S(2)}) collective-permute-start(bf16[128,512]{1,0:T(8,128)(2,1)} %get-tuple-element.55), channel_id=1, source_target_pairs={{0,7},{1,6},{2,5},{3,4},{4,3},{5,2},{6,1},{7,0},{8,15},{9,14},{10,... | collective-permute-start | bytes 393224 | tf_op jit(solution)/shard_map/ppermute | solution.py:299
  26.2 5.6 %collective-permute-done.7.refs_0_ = bf16[128,512]{1,0:T(8,128)(2,1)S(1)} collective-permute-done((bf16[128,512]{1,0:T(8,128)(2,1)S(1)}, bf16[128,512]{1,0:T(8,128)(2,1)S(1)}, u32[]{:S(2)}, u32[]{:S(2)}) %collective-permute-start.7) | collective-permute-done | bytes 131104 | tf_op jit(solution)/shard_map/ppermute | solution.py:299
  32.0 2.0 %copy.18 = bf16[1024,172]{1,0:T(8,128)(2,1)} copy(bf16[1024,172]{0,1:T(8,128)(2,1)} %param.20) | data formatting | bytes 704512
  34.0 1.2 %pad.8.clone.w_out = bf16[1024,256]{1,0:T(8,128)(2,1)S(1)} pad(bf16[1024,172]{1,0:T(8,128)(2,1)} %copy.18, bf16[]{:T(256)} %constant.24.clone.1), padding=0_0x0_84 | pad | bytes 876546 | tf_op jit(solution)/shard_map/jit(_pad)/pad | solution.py:392
  35.3 7.2 %collective-permute-done.10.refs_3_ = bf16[128,512]{1,0:T(8,128)(2,1)S(1)} collective-permute-done((bf16[128,512]{1,0:T(8,128)(2,1)}, bf16[128,512]{1,0:T(8,128)(2,1)S(1)}, u32[]{:S(2)}, u32[]{:S(2)}) %collective-permute-start.10) | collective-permute-done | bytes 131104 | tf_op jit(solution)/shard_map/ppermute | solution.py:299
  42.5 10.7 %shard_map.141 = (f32[4,312,128]{2,1,0:T(8,128)S(1)}, f32[4,312,128]{2,1,0:T(8,128)S(1)}) custom-call(s32[11]{0:T(128)S(1)} %pad_add_fusion.info, s32[16]{0:T(128)S(1)} %reshape.31.slots, bf16[4,128,512]{2,1,0:T(8,128)(2,1)S(1)} %get-tuple-element.41.lhs, bf16[4,128,512]{2,1,0:T(8,128)(2,1)S(1)} %get-tuple-element.49.cur, ...), custom_call_target="tpu_custom_call" | custom-call | tf_op jit(solution)/shard_map/pallas_call | solution.py:24
  53.3 2.0 %collective-permute-done.14.recv = f32[4,312,128]{2,1,0:T(8,128)S(1)} collective-permute-done((f32[4,312,128]{2,1,0:T(8,128)S(1)}, f32[4,312,128]{2,1,0:T(8,128)S(1)}, u32[]{:S(2)}, u32[]{:S(2)}) %collective-permute-start.14) | collective-permute-done | bytes 639008 | tf_op jit(solution)/shard_map/ppermute | solution.py:299
  55.5 1.6 %collective-permute-start.15 = (s16[320,128]{1,0:T(8,128)(2,1)S(1)}, s16[320,128]{1,0:T(8,128)(2,1)S(1)}, u32[]{:S(2)}, u32[]{:S(2)}) collective-permute-start(s16[320,128]{1,0:T(8,128)(2,1)S(1)} %get-tuple-element.61), channel_id=1, source_target_pairs={{0,8},{8,0},{16,24},{24,16},{1,9},{9,1},{17,25},{25,17},{2,10},{10... | collective-permute-start | bytes 245768 | tf_op jit(solution)/shard_map/ppermute | solution.py:299
  57.1 1.5 %collective-permute-start.16 = (s16[320,128]{1,0:T(8,128)(2,1)S(1)}, s16[320,128]{1,0:T(8,128)(2,1)S(1)}, u32[]{:S(2)}, u32[]{:S(2)}) collective-permute-start(s16[320,128]{1,0:T(8,128)(2,1)S(1)} %get-tuple-element.62), channel_id=1, source_target_pairs={{0,16},{8,24},{16,0},{24,8},{1,17},{9,25},{17,1},{25,9},{2,18},{10... | collective-permute-start | bytes 245768 | tf_op jit(solution)/shard_map/ppermute | solution.py:299
  59.1 1.0 %collective-permute-done.15.refs_0_ = s16[320,128]{1,0:T(8,128)(2,1)S(1)} collective-permute-done((s16[320,128]{1,0:T(8,128)(2,1)S(1)}, s16[320,128]{1,0:T(8,128)(2,1)S(1)}, u32[]{:S(2)}, u32[]{:S(2)}) %collective-permute-start.15) | collective-permute-done | bytes 81952 | tf_op jit(solution)/shard_map/ppermute | solution.py:299
  60.1 2.3 %collective-permute-done.16.refs_1_ = s16[320,128]{1,0:T(8,128)(2,1)S(1)} collective-permute-done((s16[320,128]{1,0:T(8,128)(2,1)S(1)}, s16[320,128]{1,0:T(8,128)(2,1)S(1)}, u32[]{:S(2)}, u32[]{:S(2)}) %collective-permute-start.16) | collective-permute-done | bytes 81952 | tf_op jit(solution)/shard_map/ppermute | solution.py:299
  62.3 1.6 %collective-permute-done.17.refs_2_ = s16[320,128]{1,0:T(8,128)(2,1)S(1)} collective-permute-done((s16[320,128]{1,0:T(8,128)(2,1)S(1)}, s16[320,128]{1,0:T(8,128)(2,1)S(1)}, u32[]{:S(2)}, u32[]{:S(2)}) %collective-permute-start.17) | collective-permute-done | bytes 81952 | tf_op jit(solution)/shard_map/ppermute | solution.py:299
  64.1 3.3 %collective-permute-start.18 = (s16[320,128]{1,0:T(8,128)(2,1)S(1)}, s16[320,128]{1,0:T(8,128)(2,1)S(1)}, u32[]{:S(2)}, u32[]{:S(2)}) collective-permute-start(s16[320,128]{1,0:T(8,128)(2,1)S(1)} %get-tuple-element.64), channel_id=1, source_target_pairs={{0,4},{1,5},{2,6},{3,7},{4,0},{5,1},{6,2},{7,3},{8,12},{9,13},{10,... | collective-permute-start | bytes 245768 | tf_op jit(solution)/shard_map/ppermute | solution.py:299
  67.4 2.4 %collective-permute-start.19 = (s16[320,128]{1,0:T(8,128)(2,1)S(1)}, s16[320,128]{1,0:T(8,128)(2,1)S(1)}, u32[]{:S(2)}, u32[]{:S(2)}) collective-permute-start(s16[320,128]{1,0:T(8,128)(2,1)S(1)} %get-tuple-element.65), channel_id=1, source_target_pairs={{0,6},{1,7},{2,4},{3,5},{4,2},{5,3},{6,0},{7,1},{8,14},{9,15},{10,... | collective-permute-start | bytes 245768 | tf_op jit(solution)/shard_map/ppermute | solution.py:299
  69.8 1.8 %collective-permute-done.18.refs_0_ = s16[320,128]{1,0:T(8,128)(2,1)S(1)} collective-permute-done((s16[320,128]{1,0:T(8,128)(2,1)S(1)}, s16[320,128]{1,0:T(8,128)(2,1)S(1)}, u32[]{:S(2)}, u32[]{:S(2)}) %collective-permute-start.18) | collective-permute-done | bytes 81952 | tf_op jit(solution)/shard_map/ppermute | solution.py:299
  71.6 2.2 %collective-permute-done.19.refs_1_ = s16[320,128]{1,0:T(8,128)(2,1)S(1)} collective-permute-done((s16[320,128]{1,0:T(8,128)(2,1)S(1)}, s16[320,128]{1,0:T(8,128)(2,1)S(1)}, u32[]{:S(2)}, u32[]{:S(2)}) %collective-permute-start.19) | collective-permute-done | bytes 81952 | tf_op jit(solution)/shard_map/ppermute | solution.py:299
  74.8 1.0 %collective-permute-start.21 = (s16[320,128]{1,0:T(8,128)(2,1)S(1)}, s16[320,128]{1,0:T(8,128)(2,1)S(1)}, u32[]{:S(2)}, u32[]{:S(2)}) collective-permute-start(s16[320,128]{1,0:T(8,128)(2,1)S(1)} %get-tuple-element.69), channel_id=1, source_target_pairs={{0,8},{8,0},{16,24},{24,16},{1,9},{9,1},{17,25},{25,17},{2,10},{10... | collective-permute-start | bytes 245768 | tf_op jit(solution)/shard_map/ppermute | solution.py:299
  76.2 2.1 %collective-permute-start.23 = (s16[320,128]{1,0:T(8,128)(2,1)S(1)}, s16[320,128]{1,0:T(8,128)(2,1)S(1)}, u32[]{:S(2)}, u32[]{:S(2)}) collective-permute-start(s16[320,128]{1,0:T(8,128)(2,1)S(1)} %get-tuple-element.71), channel_id=1, source_target_pairs={{0,24},{8,16},{16,8},{24,0},{1,25},{9,17},{17,9},{25,1},{2,26},{10... | collective-permute-start | bytes 245768 | tf_op jit(solution)/shard_map/ppermute | solution.py:299
  78.3 0.9 %collective-permute-done.21.refs_1_ = s16[320,128]{1,0:T(8,128)(2,1)S(1)} collective-permute-done((s16[320,128]{1,0:T(8,128)(2,1)S(1)}, s16[320,128]{1,0:T(8,128)(2,1)S(1)}, u32[]{:S(2)}, u32[]{:S(2)}) %collective-permute-start.21) | collective-permute-done | bytes 81952 | tf_op jit(solution)/shard_map/ppermute | solution.py:299
  80.2 1.4 %collective-permute-done.23.refs_3_ = s16[320,128]{1,0:T(8,128)(2,1)S(1)} collective-permute-done((s16[320,128]{1,0:T(8,128)(2,1)S(1)}, s16[320,128]{1,0:T(8,128)(2,1)S(1)}, u32[]{:S(2)}, u32[]{:S(2)}) %collective-permute-start.23) | collective-permute-done | bytes 81952 | tf_op jit(solution)/shard_map/ppermute | solution.py:299
  81.6 1.3 %collective-permute-done.27.refs_7_ = s16[320,128]{1,0:T(8,128)(2,1)S(1)} collective-permute-done((s16[320,128]{1,0:T(8,128)(2,1)S(1)}, s16[320,128]{1,0:T(8,128)(2,1)S(1)}, u32[]{:S(2)}, u32[]{:S(2)}) %collective-permute-start.27) | collective-permute-done | bytes 81952 | tf_op jit(solution)/shard_map/ppermute | solution.py:299
  82.9 1.8 %shard_map.145 = (f32[128,1024]{1,0:T(8,128)}, f32[1,1024]{1,0:T(1,128)}, f32[172,1024]{1,0:T(8,128)}, f32[1,256]{1,0:T(1,128)}) custom-call(s32[11]{0:T(128)S(1)} %pad_add_fusion.info, s16[320,128]{1,0:T(8,128)(2,1)S(1)} %get-tuple-element.68.refs_0_, s16[320,128]{1,0:T(8,128)(2,1)S(1)} %collective-permute-done.21.refs_1_, ...), custom_call_target="tpu_custom_call" | custom-call | tf_op jit(solution)/shard_map/pallas_call | solution.py:24
  (64 shorter events, 8.8 us)
Async XLA Ops:
  0.6 14.0 %copy-start = (bf16[1,4,4,128,128]{4,3,2,1,0:T(8,128)(2,1)S(1)}, bf16[1,4,4,128,128]{4,3,2,1,0:T(8,128)(2,1)}, u32[]{:S(2)}) copy-start(bf16[1,4,4,128,128]{4,3,2,1,0:T(8,128)(2,1)} %param.15) | copy-start | bytes 1572868
  3.6 9.6 %collective-permute-start = (bf16[144,128]{1,0:T(8,128)(2,1)S(1)}, bf16[144,128]{1,0:T(8,128)(2,1)S(1)}, u32[]{:S(2)}, u32[]{:S(2)}) collective-permute-start(bf16[144,128]{1,0:T(8,128)(2,1)S(1)} %get-tuple-element.43), channel_id=1, source_target_pairs={{0,4},{1,5},{2,6},{3,7},{4,0},{5,1},{6,2},{7,3},{8,12},{9,13},{10,... | collective-permute-start | bytes 110600 | tf_op jit(solution)/shard_map/ppermute | solution.py:299
  7.7 5.8 %collective-permute-start.1 = (bf16[144,128]{1,0:T(8,128)(2,1)S(1)}, bf16[144,128]{1,0:T(8,128)(2,1)S(1)}, u32[]{:S(2)}, u32[]{:S(2)}) collective-permute-start(bf16[144,128]{1,0:T(8,128)(2,1)S(1)} %get-tuple-element.44), channel_id=1, source_target_pairs={{0,6},{1,7},{2,4},{3,5},{4,2},{5,3},{6,0},{7,1},{8,14},{9,15},{10,... | collective-permute-start | bytes 110600 | tf_op jit(solution)/shard_map/ppermute | solution.py:299
  9.1 6.5 %collective-permute-start.2 = (bf16[144,128]{1,0:T(8,128)(2,1)S(1)}, bf16[144,128]{1,0:T(8,128)(2,1)S(1)}, u32[]{:S(2)}, u32[]{:S(2)}) collective-permute-start(bf16[144,128]{1,0:T(8,128)(2,1)S(1)} %get-tuple-element.45), channel_id=1, source_target_pairs={{0,2},{1,3},{2,0},{3,1},{4,6},{5,7},{6,4},{7,5},{8,10},{9,11},{10,... | collective-permute-start | bytes 110600 | tf_op jit(solution)/shard_map/ppermute | solution.py:299
  9.3 6.3 %collective-permute-start.3 = (bf16[144,128]{1,0:T(8,128)(2,1)S(1)}, bf16[144,128]{1,0:T(8,128)(2,1)S(1)}, u32[]{:S(2)}, u32[]{:S(2)}) collective-permute-start(bf16[144,128]{1,0:T(8,128)(2,1)S(1)} %get-tuple-element.46), channel_id=1, source_target_pairs={{0,5},{1,4},{2,7},{3,6},{4,1},{5,0},{6,3},{7,2},{8,13},{9,12},{10,... | collective-permute-start | bytes 110600 | tf_op jit(solution)/shard_map/ppermute | solution.py:299
  10.7 5.2 %collective-permute-start.4 = (bf16[144,128]{1,0:T(8,128)(2,1)S(1)}, bf16[144,128]{1,0:T(8,128)(2,1)S(1)}, u32[]{:S(2)}, u32[]{:S(2)}) collective-permute-start(bf16[144,128]{1,0:T(8,128)(2,1)S(1)} %get-tuple-element.47), channel_id=1, source_target_pairs={{0,7},{1,6},{2,5},{3,4},{4,3},{5,2},{6,1},{7,0},{8,15},{9,14},{10,... | collective-permute-start | bytes 110600 | tf_op jit(solution)/shard_map/ppermute | solution.py:299
  13.2 3.5 %collective-permute-start.5 = (bf16[144,128]{1,0:T(8,128)(2,1)S(1)}, bf16[144,128]{1,0:T(8,128)(2,1)S(1)}, u32[]{:S(2)}, u32[]{:S(2)}) collective-permute-start(bf16[144,128]{1,0:T(8,128)(2,1)S(1)} %get-tuple-element.48), channel_id=1, source_target_pairs={{0,3},{1,2},{2,1},{3,0},{4,7},{5,6},{6,5},{7,4},{8,11},{9,10},{10,... | collective-permute-start | bytes 110600 | tf_op jit(solution)/shard_map/ppermute | solution.py:299
  13.5 3.2 %collective-permute-start.6 = (bf16[144,128]{1,0:T(8,128)(2,1)S(1)}, bf16[144,128]{1,0:T(8,128)(2,1)S(1)}, u32[]{:S(2)}, u32[]{:S(2)}) collective-permute-start(bf16[144,128]{1,0:T(8,128)(2,1)S(1)} %get-tuple-element.40.after), channel_id=1, source_target_pairs={{0,1},{1,0},{2,3},{3,2},{4,5},{5,4},{6,7},{7,6},{8,9},{9,8},{10,11... | collective-permute-start | bytes 110600 | tf_op jit(solution)/shard_map/ppermute | solution.py:299
  16.7 5.4 %copy-start.6 = (f32[1024]{0:T(1024)S(1)}, f32[1024]{0:T(1024)}, u32[]{:S(2)}) copy-start(f32[1024]{0:T(1024)} %param.19) | copy-start | bytes 12292
  19.0 12.8 %collective-permute-start.7 = (bf16[128,512]{1,0:T(8,128)(2,1)S(1)}, bf16[128,512]{1,0:T(8,128)(2,1)S(1)}, u32[]{:S(2)}, u32[]{:S(2)}) collective-permute-start(bf16[128,512]{1,0:T(8,128)(2,1)S(1)} %get-tuple-element.51), channel_id=1, source_target_pairs={{0,4},{1,5},{2,6},{3,7},{4,0},{5,1},{6,2},{7,3},{8,12},{9,13},{10,... | collective-permute-start | bytes 393224 | tf_op jit(solution)/shard_map/ppermute | solution.py:299
  20.7 11.1 %collective-permute-start.8 = (bf16[128,512]{1,0:T(8,128)(2,1)S(1)}, bf16[128,512]{1,0:T(8,128)(2,1)S(1)}, u32[]{:S(2)}, u32[]{:S(2)}) collective-permute-start(bf16[128,512]{1,0:T(8,128)(2,1)S(1)} %get-tuple-element.52), channel_id=1, source_target_pairs={{0,6},{1,7},{2,4},{3,5},{4,2},{5,3},{6,0},{7,1},{8,14},{9,15},{10,... | collective-permute-start | bytes 393224 | tf_op jit(solution)/shard_map/ppermute | solution.py:299
  22.1 13.2 %collective-permute-start.9 = (bf16[128,512]{1,0:T(8,128)(2,1)}, bf16[128,512]{1,0:T(8,128)(2,1)S(1)}, u32[]{:S(2)}, u32[]{:S(2)}) collective-permute-start(bf16[128,512]{1,0:T(8,128)(2,1)} %get-tuple-element.53), channel_id=1, source_target_pairs={{0,2},{1,3},{2,0},{3,1},{4,6},{5,7},{6,4},{7,5},{8,10},{9,11},{10,... | collective-permute-start | bytes 393224 | tf_op jit(solution)/shard_map/ppermute | solution.py:299
  22.5 20.0 %collective-permute-start.10 = (bf16[128,512]{1,0:T(8,128)(2,1)}, bf16[128,512]{1,0:T(8,128)(2,1)S(1)}, u32[]{:S(2)}, u32[]{:S(2)}) collective-permute-start(bf16[128,512]{1,0:T(8,128)(2,1)} %get-tuple-element.54), channel_id=1, source_target_pairs={{0,5},{1,4},{2,7},{3,6},{4,1},{5,0},{6,3},{7,2},{8,13},{9,12},{10,... | collective-permute-start | bytes 393224 | tf_op jit(solution)/shard_map/ppermute | solution.py:299
  23.9 7.9 %copy-start.8 = (s32[1,512]{1,0:T(1,128)S(1)}, s32[1,512]{1,0:T(1,128)}, u32[]{:S(2)}) copy-start(s32[1,512]{1,0:T(1,128)} %param.17) | copy-start | bytes 6148
  23.9 7.9 %copy-start.7 = (s32[1,512]{1,0:T(1,128)S(1)}, s32[1,512]{1,0:T(1,128)}, u32[]{:S(2)}) copy-start(s32[1,512]{1,0:T(1,128)} %param.16) | copy-start | bytes 6148
  23.9 18.5 %collective-permute-start.11 = (bf16[128,512]{1,0:T(8,128)(2,1)}, bf16[128,512]{1,0:T(8,128)(2,1)S(1)}, u32[]{:S(2)}, u32[]{:S(2)}) collective-permute-start(bf16[128,512]{1,0:T(8,128)(2,1)} %get-tuple-element.55), channel_id=1, source_target_pairs={{0,7},{1,6},{2,5},{3,4},{4,3},{5,2},{6,1},{7,0},{8,15},{9,14},{10,... | collective-permute-start | bytes 393224 | tf_op jit(solution)/shard_map/ppermute | solution.py:299
  31.8 10.7 %collective-permute-start.12 = (bf16[128,512]{1,0:T(8,128)(2,1)}, bf16[128,512]{1,0:T(8,128)(2,1)S(1)}, u32[]{:S(2)}, u32[]{:S(2)}) collective-permute-start(bf16[128,512]{1,0:T(8,128)(2,1)} %get-tuple-element.56), channel_id=1, source_target_pairs={{0,3},{1,2},{2,1},{3,0},{4,7},{5,6},{6,5},{7,4},{8,11},{9,10},{10,... | collective-permute-start | bytes 393224 | tf_op jit(solution)/shard_map/ppermute | solution.py:299
  31.8 10.7 %collective-permute-start.13 = (bf16[128,512]{1,0:T(8,128)(2,1)}, bf16[128,512]{1,0:T(8,128)(2,1)S(1)}, u32[]{:S(2)}, u32[]{:S(2)}) collective-permute-start(bf16[128,512]{1,0:T(8,128)(2,1)} %get-tuple-element.57), channel_id=1, source_target_pairs={{0,1},{1,0},{2,3},{3,2},{4,5},{5,4},{6,7},{7,6},{8,9},{9,8},{10,11... | collective-permute-start | bytes 393224 | tf_op jit(solution)/shard_map/ppermute | solution.py:299
  53.2 2.1 %collective-permute-start.14 = (f32[4,312,128]{2,1,0:T(8,128)S(1)}, f32[4,312,128]{2,1,0:T(8,128)S(1)}, u32[]{:S(2)}, u32[]{:S(2)}) collective-permute-start(f32[4,312,128]{2,1,0:T(8,128)S(1)} %get-tuple-element.59), channel_id=1, source_target_pairs={{0,1},{1,0},{2,3},{3,2},{4,5},{5,4},{6,7},{7,6},{8,9},{9,8},{10,11... | collective-permute-start | bytes 1916936 | tf_op jit(solution)/shard_map/ppermute | solution.py:299
  55.5 4.6 %collective-permute-start.15 = (s16[320,128]{1,0:T(8,128)(2,1)S(1)}, s16[320,128]{1,0:T(8,128)(2,1)S(1)}, u32[]{:S(2)}, u32[]{:S(2)}) collective-permute-start(s16[320,128]{1,0:T(8,128)(2,1)S(1)} %get-tuple-element.61), channel_id=1, source_target_pairs={{0,8},{8,0},{16,24},{24,16},{1,9},{9,1},{17,25},{25,17},{2,10},{10... | collective-permute-start | bytes 245768 | tf_op jit(solution)/shard_map/ppermute | solution.py:299
  57.1 5.3 %collective-permute-start.16 = (s16[320,128]{1,0:T(8,128)(2,1)S(1)}, s16[320,128]{1,0:T(8,128)(2,1)S(1)}, u32[]{:S(2)}, u32[]{:S(2)}) collective-permute-start(s16[320,128]{1,0:T(8,128)(2,1)S(1)} %get-tuple-element.62), channel_id=1, source_target_pairs={{0,16},{8,24},{16,0},{24,8},{1,17},{9,25},{17,1},{25,9},{2,18},{10... | collective-permute-start | bytes 245768 | tf_op jit(solution)/shard_map/ppermute | solution.py:299
  58.6 5.3 %collective-permute-start.17 = (s16[320,128]{1,0:T(8,128)(2,1)S(1)}, s16[320,128]{1,0:T(8,128)(2,1)S(1)}, u32[]{:S(2)}, u32[]{:S(2)}) collective-permute-start(s16[320,128]{1,0:T(8,128)(2,1)S(1)} %get-tuple-element.63), channel_id=1, source_target_pairs={{0,24},{8,16},{16,8},{24,0},{1,25},{9,17},{17,9},{25,1},{2,26},{10... | collective-permute-start | bytes 245768 | tf_op jit(solution)/shard_map/ppermute | solution.py:299
  64.1 7.5 %collective-permute-start.18 = (s16[320,128]{1,0:T(8,128)(2,1)S(1)}, s16[320,128]{1,0:T(8,128)(2,1)S(1)}, u32[]{:S(2)}, u32[]{:S(2)}) collective-permute-start(s16[320,128]{1,0:T(8,128)(2,1)S(1)} %get-tuple-element.64), channel_id=1, source_target_pairs={{0,4},{1,5},{2,6},{3,7},{4,0},{5,1},{6,2},{7,3},{8,12},{9,13},{10,... | collective-permute-start | bytes 245768 | tf_op jit(solution)/shard_map/ppermute | solution.py:299
  67.4 6.4 %collective-permute-start.19 = (s16[320,128]{1,0:T(8,128)(2,1)S(1)}, s16[320,128]{1,0:T(8,128)(2,1)S(1)}, u32[]{:S(2)}, u32[]{:S(2)}) collective-permute-start(s16[320,128]{1,0:T(8,128)(2,1)S(1)} %get-tuple-element.65), channel_id=1, source_target_pairs={{0,6},{1,7},{2,4},{3,5},{4,2},{5,3},{6,0},{7,1},{8,14},{9,15},{10,... | collective-permute-start | bytes 245768 | tf_op jit(solution)/shard_map/ppermute | solution.py:299
  69.8 4.8 %collective-permute-start.20 = (s16[320,128]{1,0:T(8,128)(2,1)S(1)}, s16[320,128]{1,0:T(8,128)(2,1)S(1)}, u32[]{:S(2)}, u32[]{:S(2)}) collective-permute-start(s16[320,128]{1,0:T(8,128)(2,1)S(1)} %get-tuple-element.66), channel_id=1, source_target_pairs={{0,2},{1,3},{2,0},{3,1},{4,6},{5,7},{6,4},{7,5},{8,10},{9,11},{10,... | collective-permute-start | bytes 245768 | tf_op jit(solution)/shard_map/ppermute | solution.py:299
  74.8 4.5 %collective-permute-start.21 = (s16[320,128]{1,0:T(8,128)(2,1)S(1)}, s16[320,128]{1,0:T(8,128)(2,1)S(1)}, u32[]{:S(2)}, u32[]{:S(2)}) collective-permute-start(s16[320,128]{1,0:T(8,128)(2,1)S(1)} %get-tuple-element.69), channel_id=1, source_target_pairs={{0,8},{8,0},{16,24},{24,16},{1,9},{9,1},{17,25},{25,17},{2,10},{10... | collective-permute-start | bytes 245768 | tf_op jit(solution)/shard_map/ppermute | solution.py:299
  75.7 4.4 %collective-permute-start.22 = (s16[320,128]{1,0:T(8,128)(2,1)S(1)}, s16[320,128]{1,0:T(8,128)(2,1)S(1)}, u32[]{:S(2)}, u32[]{:S(2)}) collective-permute-start(s16[320,128]{1,0:T(8,128)(2,1)S(1)} %get-tuple-element.70), channel_id=1, source_target_pairs={{0,16},{8,24},{16,0},{24,8},{1,17},{9,25},{17,1},{25,9},{2,18},{10... | collective-permute-start | bytes 245768 | tf_op jit(solution)/shard_map/ppermute | solution.py:299
  76.2 5.3 %collective-permute-start.23 = (s16[320,128]{1,0:T(8,128)(2,1)S(1)}, s16[320,128]{1,0:T(8,128)(2,1)S(1)}, u32[]{:S(2)}, u32[]{:S(2)}) collective-permute-start(s16[320,128]{1,0:T(8,128)(2,1)S(1)} %get-tuple-element.71), channel_id=1, source_target_pairs={{0,24},{8,16},{16,8},{24,0},{1,25},{9,17},{17,9},{25,1},{2,26},{10... | collective-permute-start | bytes 245768 | tf_op jit(solution)/shard_map/ppermute | solution.py:299
  78.3 3.3 %collective-permute-start.24 = (s16[320,128]{1,0:T(8,128)(2,1)S(1)}, s16[320,128]{1,0:T(8,128)(2,1)S(1)}, u32[]{:S(2)}, u32[]{:S(2)}) collective-permute-start(s16[320,128]{1,0:T(8,128)(2,1)S(1)} %get-tuple-element.68.refs_0_), channel_id=1, source_target_pairs={{0,1},{1,0},{2,3},{3,2},{4,5},{5,4},{6,7},{7,6},{8,9},{9,8},{10,11... | collective-permute-start | bytes 245768 | tf_op jit(solution)/shard_map/ppermute | solution.py:299
  79.3 2.3 %collective-permute-start.25 = (s16[320,128]{1,0:T(8,128)(2,1)S(1)}, s16[320,128]{1,0:T(8,128)(2,1)S(1)}, u32[]{:S(2)}, u32[]{:S(2)}) collective-permute-start(s16[320,128]{1,0:T(8,128)(2,1)S(1)} %collective-permute-done.21.refs_1_), channel_id=1, source_target_pairs={{0,1},{1,0},{2,3},{3,2},{4,5},{5,4},{6,7},{7,6},{8,9},{9,8},{10,11... | collective-permute-start | bytes 245768 | tf_op jit(solution)/shard_map/ppermute | solution.py:299
  80.2 1.4 %collective-permute-start.26 = (s16[320,128]{1,0:T(8,128)(2,1)S(1)}, s16[320,128]{1,0:T(8,128)(2,1)S(1)}, u32[]{:S(2)}, u32[]{:S(2)}) collective-permute-start(s16[320,128]{1,0:T(8,128)(2,1)S(1)} %collective-permute-done.22.refs_2_), channel_id=1, source_target_pairs={{0,1},{1,0},{2,3},{3,2},{4,5},{5,4},{6,7},{7,6},{8,9},{9,8},{10,11... | collective-permute-start | bytes 245768 | tf_op jit(solution)/shard_map/ppermute | solution.py:299
  81.6 1.3 %collective-permute-start.27 = (s16[320,128]{1,0:T(8,128)(2,1)S(1)}, s16[320,128]{1,0:T(8,128)(2,1)S(1)}, u32[]{:S(2)}, u32[]{:S(2)}) collective-permute-start(s16[320,128]{1,0:T(8,128)(2,1)S(1)} %collective-permute-done.23.refs_3_), channel_id=1, source_target_pairs={{0,1},{1,0},{2,3},{3,2},{4,5},{5,4},{6,7},{7,6},{8,9},{9,8},{10,11... | collective-permute-start | bytes 245768 | tf_op jit(solution)/shard_map/ppermute | solution.py:299
  (7 other events, 7.6 us)

commit v4 on v3

--- a/solution.py
+++ b/solution.py
@@ -14,17 +14,16 @@
 MIB = 1024 * 1024
 SMEM = pl.BlockSpec(memory_space=pltpu.SMEM)
 VMEM = pl.BlockSpec(memory_space=pltpu.VMEM)
-HBM = pl.BlockSpec(memory_space=pltpu.HBM)
 CHUNK = 256
-BATCH = 1
+BATCH = 2
 TAIL = 8
 
 
-def call(kernel, outs, ins, scratch=(), n_smem=0, n_hbm=0, vmem=8):
+def call(kernel, outs, ins, scratch=(), n_smem=0, vmem=8):
     return pl.pallas_call(
         kernel,
         out_shape=outs,
-        in_specs=[SMEM] * n_smem + [HBM] * n_hbm + [VMEM] * (len(ins) - n_smem - n_hbm),
+        in_specs=[SMEM] * n_smem + [VMEM] * (len(ins) - n_smem),
         out_specs=jax.tree.map(lambda _: VMEM, outs),
         scratch_shapes=list(scratch),
         compiler_params=pltpu.CompilerParams(vmem_limit_bytes=vmem * MIB),
@@ -40,7 +39,10 @@
     return [k for odd in (0, 1) for top in tops for k in range(top, 2 * top) if k % 2 == odd]
 
 
-def select_kernel(info, feats, masks, *msgs):
+def select_kernel(info, feats, masks, *refs):
+    msgs = refs[:-2]
+    refs[-2][...] = feats[...]
+    refs[-1][...] = masks[...]
     tile = feats.shape[1]
     samples = masks.shape[0]
     for i, k in enumerate(partners(len(msgs) + 1)):
@@ -59,7 +61,7 @@
         put(s, (f * cols[:, s : s + 1]).astype(BF16))
 
 
-def layout_kernel(after, feats, masks, adj, lhs, own):
+def layout_kernel(feats, masks, adj, lhs, own):
     tiles, tile, feat = feats.shape
     for t in range(tiles):
         lhs[t] = jnp.concatenate([adj[t, j] for j in range(adj.shape[1])], 1)
@@ -103,12 +105,16 @@
         outs[i][...] = cur[info[3 + (info[0] ^ k)]]
 
 
-def mlp_kernel(dom, samples, classes, scale, info, slots, lhs, cur, total, code, w_in, b_in, w_out, w_out_t, b_out, *refs):
+def fold(x):
+    return functools.reduce(lambda a, b: a + b, [x[i : i + 8] for i in range(0, x.shape[0], 8)])
+
+
+def mlp_kernel(dom, samples, scale, info, slots, lhs, cur, total, code, half_w, half_b, w_out, half_w_t, b_out, *refs):
     recv = refs[: dom - 1]
-    keep, send, pool, x_t, act, slope, prob, dl, dl_t, dpre, acc, bias_acc, cls_acc = refs[dom - 1 :]
+    send, x_t, act, dl_t, dpre, bias_acc, cls_acc, pool, slope, prob, dl = refs[dom - 1 :]
     tiles, tile, lanes = cur.shape
     feat = lanes // samples
-    hidden = w_in.shape[1]
+    hidden = half_w.shape[1]
     wide = w_out.shape[1]
     rows = samples * tile
     nch = hidden // CHUNK
@@ -119,30 +125,34 @@
     bias_acc[...] = jnp.zeros(bias_acc.shape, F32)
     cls_acc[...] = jnp.zeros(cls_acc.shape, F32)
 
-    def one_tile(r, carry):
+    def forward(r):
         hop = hop_rows(info, slots, lhs, pool, r, dom)
         xbar = ((total[r] + hop) * XBAR_SCALE).astype(BF16)
-        base = pl.multiple_of(r * rows, rows)
+        base = r * rows
         for s in range(samples):
-            x_t[:, pl.ds(base + s * tile, tile)] = xbar[:, s * feat : (s + 1) * feat].T
-        for s in range(0, samples, BATCH):
-            x = jnp.concatenate([xbar[:, i * feat : (i + 1) * feat] for i in range(s, s + BATCH)], 0)
-            here = pl.ds(base + s * tile, BATCH * tile)
-            there = slice(s * tile, (s + BATCH) * tile)
+            x_t[:, base + s * tile : base + (s + 1) * tile] = xbar[:, s * feat : (s + 1) * feat].T
+        batch = BATCH if samples % BATCH == 0 else 1
+        for s in range(0, samples, batch):
+            x = jnp.concatenate([xbar[:, i * feat : (i + 1) * feat] for i in range(s, s + batch)], 0)
+            here = slice(base + s * tile, base + (s + batch) * tile)
             for n in range(nch):
                 cols = slice(n * CHUNK, (n + 1) * CHUNK)
-                half = jnp.dot(x, w_in[:, cols], preferred_element_type=F32) + b_in[:, cols]
-                t = jnp.tanh(half)
+                h = jnp.dot(x, half_w[:, cols], preferred_element_type=F32) + half_b[:, cols]
+                t = jnp.tanh(h)
                 up = 1.0 + t
-                silu = half * up
+                silu = h * up
                 act[here, cols] = silu.astype(BF16)
-                slope[there, cols] = up + silu * (1.0 - t)
+                slope[here, cols] = up + silu * (1.0 - t)
             logits = jnp.dot(act[here, :], w_out[...], preferred_element_type=F32) + b_out[...]
             e = jnp.exp(logits)
-            prob[there, :] = e * (1.0 / jnp.sum(e, -1, keepdims=True))
+            prob[here, :] = e * (1.0 / jnp.sum(e, -1, keepdims=True))
+
+    def backward(r):
+        base = r * rows
         step = 32
         for c in range(0, tile, step):
-            probs = [prob[s * tile + c : s * tile + c + step, :] for s in range(samples)]
+            at = [slice(base + s * tile + c, base + s * tile + c + step) for s in range(samples)]
+            probs = [prob[one, :] for one in at]
             avg = sum(probs[1:], probs[0]) * (1.0 / samples)
             sq = avg * avg
             sharp = sq * (1.0 / jnp.sum(sq, -1, keepdims=True))
@@ -150,77 +160,61 @@
             hit = jnp.where(lax.broadcasted_iota(I32, (step, wide), 1) == label, scale, 0.0)
             used = jnp.where(label >= 0, scale, 0.0)
             part = jnp.zeros((step, wide), F32)
-            for s, p in enumerate(probs):
+            for one, p in zip(at, probs):
                 off = p - sharp
                 inner = jnp.sum(off * p, -1, keepdims=True)
                 d = p * ((2.0 * scale) * (off - inner) + used) - hit
                 part = part + d
-                dl[s * tile + c : s * tile + c + step, :] = d.astype(BF16)
-            cls_acc[...] += functools.reduce(lambda a, b: a + b, [part[i : i + 8] for i in range(0, step, 8)])
+                dl[one, :] = d.astype(BF16)
+            cls_acc[...] += fold(part)
         for s in range(samples):
-            d = dl[s * tile : (s + 1) * tile, :]
-            dl_t[:, pl.ds(base + s * tile, tile)] = d.T[: dl_t.shape[0]]
+            here = slice(base + s * tile, base + (s + 1) * tile)
+            d = dl[here, :]
+            dl_t[:, here] = d.T[: dl_t.shape[0]]
             for n in range(nch):
                 cols = slice(n * CHUNK, (n + 1) * CHUNK)
-                dact = jnp.dot(d, w_out_t[:, cols], preferred_element_type=F32)
-                dp = dact * slope[s * tile : (s + 1) * tile, cols]
-                dpre[pl.ds(base + s * tile, tile), cols] = dp.astype(BF16)
-                bias_acc[:, cols] += functools.reduce(lambda a, b: a + b, [dp[i : i + 8] for i in range(0, tile, 8)])
-        return carry
-
-    lax.fori_loop(0, tiles, one_tile, 0)
-    lanes_out = acc.shape[2]
-    wide_t = dl_t.shape[0]
+                dp = jnp.dot(d, half_w_t[:, cols], preferred_element_type=F32) * slope[here, cols]
+                dpre[here, cols] = dp.astype(BF16)
+                bias_acc[:, cols] += fold(dp)
+
+    forward(0)
+    for r in range(1, tiles):
+        forward(r)
+        backward(r - 1)
+    backward(tiles - 1)
+    half_pieces(1 - info[2], x_t, act, dl_t, dpre, bias_acc, cls_acc, lambda m: info[1] ^ m, send)
+
+
+def half_pieces(core, x_t, act, dl_t, dpre, bias_acc, cls_acc, place, out):
+    feat, wide_t = x_t.shape[0], dl_t.shape[0]
+    half = act.shape[1] // 2
+    wide = cls_acc.shape[1]
+    lanes = out.shape[2]
+    start = pl.multiple_of(core * half, half)
+    chunk = min(CHUNK, half)
+    each = chunk // lanes
     cls = jnp.sum(cls_acc[...], 0, keepdims=True)
-    for n in range(nch):
-        cols = slice(n * CHUNK, (n + 1) * CHUNK)
+    first = place(0)
+    for n in range(half // chunk):
+        cols = pl.ds(start + n * chunk, chunk)
         g_in = jnp.dot(x_t[...], dpre[:, cols], preferred_element_type=F32)
         g_out = jnp.dot(dl_t[...], act[:, cols], preferred_element_type=F32)
         g_bias = jnp.sum(bias_acc[:, cols], 0, keepdims=True)
-        for i in range(CHUNK // lanes_out):
-            at = n * (CHUNK // lanes_out) + i
-            part = slice(i * lanes_out, (i + 1) * lanes_out)
-            acc[at, :feat, :] = g_in[:, part]
-            acc[at, feat : feat + wide_t, :] = g_out[:, part]
-            acc[at, feat + wide_t :, :] = jnp.concatenate(
+        for i in range(each):
+            at = (n * each + i) ^ first
+            part = slice(i * lanes, (i + 1) * lanes)
+            out[at, :feat, :] = g_in[:, part]
+            out[at, feat : feat + wide_t, :] = g_out[:, part]
+            out[at, feat + wide_t :, :] = jnp.concatenate(
                 [g_bias[:, part]]
-                + [cls[:, i * lanes_out : (i + 1) * lanes_out] for i in range(wide // lanes_out)]
-                + [jnp.zeros((TAIL - 1 - wide // lanes_out, lanes_out), F32)],
+                + [cls[:, j * lanes : (j + 1) * lanes] for j in range(wide // lanes)]
+                + [jnp.zeros((TAIL - 1 - wide // lanes, lanes), F32)],
                 0,
             )
-    for m in range(keep.shape[0]):
-        pair = (info[1] ^ m) * 2
-        keep[m] = acc[pair + info[2]]
-        send[m] = acc[pair + 1 - info[2]]
-
-
-def mlp_call(dom, samples, tiles, tile, feat, hidden, classes, wide, ins):
-    lanes = samples * feat
-    rows = samples * tile
-    all_rows = rows * tiles
-    wide_t = -(-classes // 16) * 16
-    piece = (feat + wide_t + TAIL, 128)
-    pieces = hidden // 128
-    return call(
-        functools.partial(mlp_kernel, dom, samples, classes, 1.0 / (samples * tiles * tile)),
-        [like((pieces // 2,) + piece, F32)] * 2,
-        list(ins),
-        [
-            pltpu.VMEM((dom - 1 + tiles, tile, lanes), BF16),
-            pltpu.VMEM((feat, all_rows), BF16),
-            pltpu.VMEM((all_rows, hidden), BF16),
-            pltpu.VMEM((rows, hidden), F32),
-            pltpu.VMEM((rows, wide), F32),
-            pltpu.VMEM((rows, wide), BF16),
-            pltpu.VMEM((wide_t, all_rows), BF16),
-            pltpu.VMEM((all_rows, hidden), BF16),
-            pltpu.VMEM((pieces,) + piece, F32),
-            pltpu.VMEM((8, hidden), F32),
-            pltpu.VMEM((8, wide), F32),
-        ],
-        n_smem=2,
-        vmem=28,
-    )
+
+
+def keep_kernel(info, x_t, act, dl_t, dpre, bias_acc, cls_acc, keep):
+    half_pieces(info[2], x_t, act, dl_t, dpre, bias_acc, cls_acc, lambda m: info[1] ^ m, keep)
 
 
 def encode(x, feat, n_tail):
@@ -282,7 +276,7 @@
     body = pieces[0].shape[0] - 2 * TAIL
     for c in range(2):
         for m in range(half):
-            at = (info[1] ^ m) * 2 + (info[2] ^ c)
+            at = (info[2] ^ c) * half + (info[1] ^ m)
             x = decode(pieces[c * half + m], feat, n_tail)
             where = pl.ds(pl.multiple_of(at * lanes, lanes), lanes)
             g_in[:, where] = x[:feat]
@@ -311,10 +305,9 @@
     return groups
 
 
-def reduce_grads(keep, send, info, feat, n_tail, classes, hidden):
+def reduce_grads(keep, recv, info, feat, n_tail, classes, hidden):
     count, rows, lanes = keep.shape
     coded = like((rows + TAIL, lanes), I16)
-    recv = xor_permute(send, "dom", 1)
     own, *msgs = call(
         functools.partial(pair_kernel, feat, n_tail),
         [like((rows, lanes), F32)] + [coded] * (count - 1),
@@ -366,17 +359,16 @@
     lanes = samples * feat
     wide = -(-classes // 128) * 128
 
-    msgs = call(
+    *msgs, feats, masks = call(
         select_kernel,
-        [like((tile + 16, feat), BF16)] * (dom - 1),
+        [like((tile + 16, feat), BF16)] * (dom - 1) + [like(feats.shape, BF16), like(masks.shape, BF16)],
         [info, feats, masks],
         n_smem=1,
     )
     lhs, own = call(
         layout_kernel,
         [like((tiles, tile, nnz * tile), BF16), like((tiles, tile, lanes), BF16)],
-        [msgs[-1], feats, masks, adj],
-        n_hbm=1,
+        [feats, masks, adj],
     )
     msgs = swap_all(msgs)
     cur, total, *outs = call(
@@ -391,11 +383,35 @@
     code = jnp.where(labeled != 0, node_labels, -1).reshape(tiles, tile, 1)
     w_out = jnp.pad(weight_out, ((0, 0), (0, wide - classes)))
     b_out = jnp.pad(bias_out, (0, wide - classes), constant_values=-1e30).reshape(1, wide)
-    keep, send = mlp_call(
-        dom, samples, tiles, tile, feat, hidden, classes, wide,
-        [info, slots, lhs, cur, total, code, 0.5 * weight_in, 0.5 * bias_in.reshape(1, hidden), w_out, 0.5 * w_out.T, b_out] + outs,
-    )
-    g_in, b_in, g_out, b_out = reduce_grads(keep, send, info, feat, 1 + wide // 128, classes, hidden)
+    rows = samples * tile * tiles
+    wide_t = -(-classes // 16) * 16
+    half = like((hidden // 256, feat + wide_t + TAIL, 128), F32)
+    send, *held = call(
+        functools.partial(mlp_kernel, dom, samples, 1.0 / (samples * tiles * tile)),
+        [
+            half,
+            like((feat, rows), BF16),
+            like((rows, hidden), BF16),
+            like((wide_t, rows), BF16),
+            like((rows, hidden), BF16),
+            like((8, hidden), F32),
+            like((8, wide), F32),
+        ],
+        [info, slots, lhs, cur, total, code, 0.5 * weight_in, 0.5 * bias_in.reshape(1, hidden)]
+        + [w_out, 0.5 * w_out.T, b_out]
+        + outs,
+        [
+            pltpu.VMEM((dom - 1 + tiles, tile, lanes), BF16),
+            pltpu.VMEM((rows, hidden), F32),
+            pltpu.VMEM((rows, wide), F32),
+            pltpu.VMEM((rows, wide), BF16),
+        ],
+        n_smem=2,
+        vmem=24,
+    )
+    recv = xor_permute(send, "dom", 1)
+    keep = call(keep_kernel, half, [info] + held, n_smem=1)
+    g_in, b_in, g_out, b_out = reduce_grads(keep, recv, info, feat, 1 + wide // 128, classes, hidden)
     return g_in, b_in.reshape(hidden), g_out.T, b_out.reshape(-1)[:classes]
 
 

time: 84.9 us -> 84.2 us (level)
  waiting for transfers between devices: 30.4 us -> 25 us
  other arithmetic: 1.88 us -> 4.16 us
  local copies, waits for them, and re-layouts: 5.62 us -> 7.35 us
  starting transfers between devices: 29.8 us -> 31.3 us
  Pallas kernels: 16.2 us -> 15.2 us
    ppermute x28, waiting for transfers between devices: 30.4 us -> 25 us  [xor_permute(): lax.ppermute(x, axis, [(i, i ^ mask) for i in range(lax.axis_size(axis))])]
    ppermute x28, starting transfers between devices: 29.8 us -> 31.3 us  [xor_permute(): lax.ppermute(x, axis, [(i, i ^ mask) for i in range(lax.axis_size(axis))])]
    pallas_call x8 -> x9, Pallas kernels: 16.2 us -> 15.2 us  [call(): pl.pallas_call(kernel, out_shape=outs, in_specs=[SMEM] * n_smem + [VMEM]...]
    mul x1, other arithmetic: 0.07 us -> 1.06 us  [per_device(): 0.5 * w_out.T]
    unnamed x23 -> x7, local copies, waits for them, and re-layouts: 4.21 us -> 4.62 us
  transfers between devices with their start and end apart: 28 -> 28, of which waited for: 16 -> 15; matrix products, arithmetic and copies ran while one was open for 5% -> 10% of each run, Pallas kernels for 0% -> 2%
where the time goes in v4:
time: 84.2 us; the launch traced here: 83.7 us
  starting transfers between devices  31.3 us (37%)
  waiting for transfers between devices  25 us (30%)
  Pallas kernels  15.2 us (18%)
  local copies, waits for them, and re-layouts  7.35 us (9%)
  other arithmetic  4.16 us (5%)
    ppermute x28, starting transfers between devices, xor_permute(): lax.ppermute(x, axis, [(i, i ^ mask) for i in range(lax.axis_size(axis))])  31.3 us
    ppermute x28, waiting for transfers between devices, xor_permute(): lax.ppermute(x, axis, [(i, i ^ mask) for i in range(lax.axis_size(axis))])  25 us
    pallas_call x9, Pallas kernels, call(): pl.pallas_call(kernel, out_shape=outs, in_specs=[SMEM] * n_smem + [VMEM]...  15.2 us
    unnamed x7, local copies, waits for them, and re-layouts  4.62 us
  transfers between devices with their start and end apart: 28, of which 15 were waited for; matrix products, arithmetic and copies ran while one was open for 10% of the time, Pallas kernels for 2%

profile of v4, /device:TPU:0, one launch (start us, length us, event | category | flops | bytes accessed | tf_op | source)
XLA Modules:
  0.0 83.7 jit_solution(16083834317594220149)
XLA Ops:
  3.5 4.1 %collective-permute-start = (bf16[144,128]{1,0:T(8,128)(2,1)S(1)}, bf16[144,128]{1,0:T(8,128)(2,1)S(1)}, u32[]{:S(2)}, u32[]{:S(2)}) collective-permute-start(bf16[144,128]{1,0:T(8,128)(2,1)S(1)} %get-tuple-element.51), channel_id=1, source_target_pairs={{0,4},{1,5},{2,6},{3,7},{4,0},{5,1},{6,2},{7,3},{8,12},{9,13},{10,... | collective-permute-start | bytes 110600 | tf_op jit(solution)/shard_map/ppermute | solution.py:293
  7.6 1.3 %collective-permute-start.1 = (bf16[144,128]{1,0:T(8,128)(2,1)S(1)}, bf16[144,128]{1,0:T(8,128)(2,1)S(1)}, u32[]{:S(2)}, u32[]{:S(2)}) collective-permute-start(bf16[144,128]{1,0:T(8,128)(2,1)S(1)} %get-tuple-element.52), channel_id=1, source_target_pairs={{0,6},{1,7},{2,4},{3,5},{4,2},{5,3},{6,0},{7,1},{8,14},{9,15},{10,... | collective-permute-start | bytes 110600 | tf_op jit(solution)/shard_map/ppermute | solution.py:293
  9.2 1.4 %collective-permute-start.3 = (bf16[144,128]{1,0:T(8,128)(2,1)S(1)}, bf16[144,128]{1,0:T(8,128)(2,1)S(1)}, u32[]{:S(2)}, u32[]{:S(2)}) collective-permute-start(bf16[144,128]{1,0:T(8,128)(2,1)S(1)} %get-tuple-element.54), channel_id=1, source_target_pairs={{0,5},{1,4},{2,7},{3,6},{4,1},{5,0},{6,3},{7,2},{8,13},{9,12},{10,... | collective-permute-start | bytes 110600 | tf_op jit(solution)/shard_map/ppermute | solution.py:293
  10.6 2.5 %collective-permute-start.4 = (bf16[144,128]{1,0:T(8,128)(2,1)S(1)}, bf16[144,128]{1,0:T(8,128)(2,1)S(1)}, u32[]{:S(2)}, u32[]{:S(2)}) collective-permute-start(bf16[144,128]{1,0:T(8,128)(2,1)S(1)} %get-tuple-element.55), channel_id=1, source_target_pairs={{0,7},{1,6},{2,5},{3,4},{4,3},{5,2},{6,1},{7,0},{8,15},{9,14},{10,... | collective-permute-start | bytes 110600 | tf_op jit(solution)/shard_map/ppermute | solution.py:293
  13.4 1.0 %broadcast_multiply_fusion.half_w = bf16[128,1024]{1,0:T(8,128)(2,1)S(1)} fusion(bf16[128,1024]{1,0:T(8,128)(2,1)} %param.18), kind=kLoop, calls=%fused_computation.1 | loop fusion | flops 131072 | bytes 524288 | tf_op jit(solution)/shard_map/mul | solution.py:400
  15.2 1.0 %copy-done = bf16[1,4,4,128,128]{4,3,2,1,0:T(8,128)(2,1)S(1)} copy-done((bf16[1,4,4,128,128]{4,3,2,1,0:T(8,128)(2,1)S(1)}, bf16[1,4,4,128,128]{4,3,2,1,0:T(8,128)(2,1)}, u32[]{:S(2)}) %copy-start) | copy-done | bytes 524312
  16.6 2.3 %shard_map.140 = (bf16[4,128,512]{2,1,0:T(8,128)(2,1)S(1)}, f32[4,128,512]{2,1,0:T(8,128)S(1)}, bf16[128,512]{1,0:T(8,128)(2,1)S(1)}, bf16[128,512]{1,0:T(8,128)...) custom-call(s32[11]{0:T(128)S(1)} %pad_add_fusion.info, ...), custom_call_target="tpu_custom_call" | custom-call | tf_op jit(solution)/shard_map/pallas_call | solution.py:23
  18.9 2.8 %collective-permute-start.7 = (bf16[128,512]{1,0:T(8,128)(2,1)S(1)}, bf16[128,512]{1,0:T(8,128)(2,1)S(1)}, u32[]{:S(2)}, u32[]{:S(2)}) collective-permute-start(bf16[128,512]{1,0:T(8,128)(2,1)S(1)} %get-tuple-element.60), channel_id=1, source_target_pairs={{0,4},{1,5},{2,6},{3,7},{4,0},{5,1},{6,2},{7,3},{8,12},{9,13},{10,... | collective-permute-start | bytes 393224 | tf_op jit(solution)/shard_map/ppermute | solution.py:293
  21.7 1.3 %collective-permute-start.8 = (bf16[128,512]{1,0:T(8,128)(2,1)S(1)}, bf16[128,512]{1,0:T(8,128)(2,1)S(1)}, u32[]{:S(2)}, u32[]{:S(2)}) collective-permute-start(bf16[128,512]{1,0:T(8,128)(2,1)S(1)} %get-tuple-element.61), channel_id=1, source_target_pairs={{0,6},{1,7},{2,4},{3,5},{4,2},{5,3},{6,0},{7,1},{8,14},{9,15},{10,... | collective-permute-start | bytes 393224 | tf_op jit(solution)/shard_map/ppermute | solution.py:293
  23.8 1.8 %collective-permute-start.10 = (bf16[128,512]{1,0:T(8,128)(2,1)}, bf16[128,512]{1,0:T(8,128)(2,1)S(1)}, u32[]{:S(2)}, u32[]{:S(2)}) collective-permute-start(bf16[128,512]{1,0:T(8,128)(2,1)} %get-tuple-element.63), channel_id=1, source_target_pairs={{0,5},{1,4},{2,7},{3,6},{4,1},{5,0},{6,3},{7,2},{8,13},{9,12},{10,... | collective-permute-start | bytes 393224 | tf_op jit(solution)/shard_map/ppermute | solution.py:293
  25.6 2.3 %collective-permute-start.11 = (bf16[128,512]{1,0:T(8,128)(2,1)}, bf16[128,512]{1,0:T(8,128)(2,1)S(1)}, u32[]{:S(2)}, u32[]{:S(2)}) collective-permute-start(bf16[128,512]{1,0:T(8,128)(2,1)} %get-tuple-element.64), channel_id=1, source_target_pairs={{0,7},{1,6},{2,5},{3,4},{4,3},{5,2},{6,1},{7,0},{8,15},{9,14},{10,... | collective-permute-start | bytes 393224 | tf_op jit(solution)/shard_map/ppermute | solution.py:293
  27.9 4.3 %collective-permute-done.7.refs_0_ = bf16[128,512]{1,0:T(8,128)(2,1)S(1)} collective-permute-done((bf16[128,512]{1,0:T(8,128)(2,1)S(1)}, bf16[128,512]{1,0:T(8,128)(2,1)S(1)}, u32[]{:S(2)}, u32[]{:S(2)}) %collective-permute-start.7) | collective-permute-done | bytes 131104 | tf_op jit(solution)/shard_map/ppermute | solution.py:293
  33.0 2.0 %copy.18 = bf16[1024,172]{1,0:T(8,128)(2,1)} copy(bf16[1024,172]{0,1:T(8,128)(2,1)} %param.20) | data formatting | bytes 704512
  35.7 1.1 %pad.8.clone.w_out = bf16[1024,256]{1,0:T(8,128)(2,1)S(1)} pad(bf16[1024,172]{1,0:T(8,128)(2,1)} %copy.18, bf16[]{:T(256)} %constant.24.clone.1), padding=0_0x0_84 | pad | bytes 876546 | tf_op jit(solution)/shard_map/jit(_pad)/pad | solution.py:384
  36.8 1.1 %multiply_bitcast_fusion.half_w_t = bf16[256,1024]{1,0:T(8,128)(2,1)S(1)} fusion(bf16[1024,172]{0,1:T(8,128)(2,1)} %param.20), kind=kLoop, calls=%fused_computation | loop fusion | flops 1048576 | bytes 876544 | tf_op jit(solution)/shard_map/mul | solution.py:401
  37.9 4.8 %collective-permute-done.10.refs_3_ = bf16[128,512]{1,0:T(8,128)(2,1)S(1)} collective-permute-done((bf16[128,512]{1,0:T(8,128)(2,1)}, bf16[128,512]{1,0:T(8,128)(2,1)S(1)}, u32[]{:S(2)}, u32[]{:S(2)}) %collective-permute-start.10) | collective-permute-done | bytes 131104 | tf_op jit(solution)/shard_map/ppermute | solution.py:293
  43.0 8.3 %shard_map.141 = (f32[4,312,128]{2,1,0:T(8,128)S(1)}, bf16[128,2048]{1,0:T(8,128)(2,1)S(1)}, bf16[2048,1024]{1,0:T(8,128)(2,1)S(1)}, bf16[176,2048]{1,0:T(8,128)...) custom-call(s32[11]{0:T(128)S(1)} %pad_add_fusion.info, ...), custom_call_target="tpu_custom_call" | custom-call | tf_op jit(solution)/shard_map/pallas_call | solution.py:23
  51.4 1.4 %shard_map.142.keep = f32[4,312,128]{2,1,0:T(8,128)S(1)} custom-call(s32[11]{0:T(128)S(1)} %pad_add_fusion.info, bf16[128,2048]{1,0:T(8,128)(2,1)S(1)} %get-tuple-element.67.x_t, bf16[2048,1024]{1,0:T(8,128)(2,1)S(1)} %get-tuple-element.68.act, bf16[176,2048]{1,0:T(8,128)(2,1)S(1)} %get-tuple-element.69.dl_t, bf16[2048,1024]{1,0:T(8,128)(2,1)S(1)} %get-tuple-element.70.dpre, ...), custom_call_target="tpu_custom_call" | custom-call | tf_op jit(solution)/shard_map/pallas_call | solution.py:23
  53.6 1.6 %collective-permute-start.15 = (s16[320,128]{1,0:T(8,128)(2,1)S(1)}, s16[320,128]{1,0:T(8,128)(2,1)S(1)}, u32[]{:S(2)}, u32[]{:S(2)}) collective-permute-start(s16[320,128]{1,0:T(8,128)(2,1)S(1)} %get-tuple-element.75), channel_id=1, source_target_pairs={{0,8},{8,0},{16,24},{24,16},{1,9},{9,1},{17,25},{25,17},{2,10},{10... | collective-permute-start | bytes 245768 | tf_op jit(solution)/shard_map/ppermute | solution.py:293
  55.2 1.5 %collective-permute-start.16 = (s16[320,128]{1,0:T(8,128)(2,1)S(1)}, s16[320,128]{1,0:T(8,128)(2,1)S(1)}, u32[]{:S(2)}, u32[]{:S(2)}) collective-permute-start(s16[320,128]{1,0:T(8,128)(2,1)S(1)} %get-tuple-element.76), channel_id=1, source_target_pairs={{0,16},{8,24},{16,0},{24,8},{1,17},{9,25},{17,1},{25,9},{2,18},{10... | collective-permute-start | bytes 245768 | tf_op jit(solution)/shard_map/ppermute | solution.py:293
  57.2 1.0 %collective-permute-done.15.refs_0_ = s16[320,128]{1,0:T(8,128)(2,1)S(1)} collective-permute-done((s16[320,128]{1,0:T(8,128)(2,1)S(1)}, s16[320,128]{1,0:T(8,128)(2,1)S(1)}, u32[]{:S(2)}, u32[]{:S(2)}) %collective-permute-start.15) | collective-permute-done | bytes 81952 | tf_op jit(solution)/shard_map/ppermute | solution.py:293
  58.1 2.3 %collective-permute-done.16.refs_1_ = s16[320,128]{1,0:T(8,128)(2,1)S(1)} collective-permute-done((s16[320,128]{1,0:T(8,128)(2,1)S(1)}, s16[320,128]{1,0:T(8,128)(2,1)S(1)}, u32[]{:S(2)}, u32[]{:S(2)}) %collective-permute-start.16) | collective-permute-done | bytes 81952 | tf_op jit(solution)/shard_map/ppermute | solution.py:293
  60.4 1.6 %collective-permute-done.17.refs_2_ = s16[320,128]{1,0:T(8,128)(2,1)S(1)} collective-permute-done((s16[320,128]{1,0:T(8,128)(2,1)S(1)}, s16[320,128]{1,0:T(8,128)(2,1)S(1)}, u32[]{:S(2)}, u32[]{:S(2)}) %collective-permute-start.17) | collective-permute-done | bytes 81952 | tf_op jit(solution)/shard_map/ppermute | solution.py:293
  62.2 5.0 %collective-permute-start.18 = (s16[320,128]{1,0:T(8,128)(2,1)S(1)}, s16[320,128]{1,0:T(8,128)(2,1)S(1)}, u32[]{:S(2)}, u32[]{:S(2)}) collective-permute-start(s16[320,128]{1,0:T(8,128)(2,1)S(1)} %get-tuple-element.78), channel_id=1, source_target_pairs={{0,4},{1,5},{2,6},{3,7},{4,0},{5,1},{6,2},{7,3},{8,12},{9,13},{10,... | collective-permute-start | bytes 245768 | tf_op jit(solution)/shard_map/ppermute | solution.py:293
  67.2 1.2 %collective-permute-start.19 = (s16[320,128]{1,0:T(8,128)(2,1)S(1)}, s16[320,128]{1,0:T(8,128)(2,1)S(1)}, u32[]{:S(2)}, u32[]{:S(2)}) collective-permute-start(s16[320,128]{1,0:T(8,128)(2,1)S(1)} %get-tuple-element.79), channel_id=1, source_target_pairs={{0,6},{1,7},{2,4},{3,5},{4,2},{5,3},{6,0},{7,1},{8,14},{9,15},{10,... | collective-permute-start | bytes 245768 | tf_op jit(solution)/shard_map/ppermute | solution.py:293
  68.4 3.6 %collective-permute-done.18.refs_0_ = s16[320,128]{1,0:T(8,128)(2,1)S(1)} collective-permute-done((s16[320,128]{1,0:T(8,128)(2,1)S(1)}, s16[320,128]{1,0:T(8,128)(2,1)S(1)}, u32[]{:S(2)}, u32[]{:S(2)}) %collective-permute-start.18) | collective-permute-done | bytes 81952 | tf_op jit(solution)/shard_map/ppermute | solution.py:293
  71.9 1.7 %collective-permute-done.19.refs_1_ = s16[320,128]{1,0:T(8,128)(2,1)S(1)} collective-permute-done((s16[320,128]{1,0:T(8,128)(2,1)S(1)}, s16[320,128]{1,0:T(8,128)(2,1)S(1)}, u32[]{:S(2)}, u32[]{:S(2)}) %collective-permute-start.19) | collective-permute-done | bytes 81952 | tf_op jit(solution)/shard_map/ppermute | solution.py:293
  75.3 2.1 %collective-permute-start.23 = (s16[320,128]{1,0:T(8,128)(2,1)S(1)}, s16[320,128]{1,0:T(8,128)(2,1)S(1)}, u32[]{:S(2)}, u32[]{:S(2)}) collective-permute-start(s16[320,128]{1,0:T(8,128)(2,1)S(1)} %get-tuple-element.85), channel_id=1, source_target_pairs={{0,24},{8,16},{16,8},{24,0},{1,25},{9,17},{17,9},{25,1},{2,26},{10... | collective-permute-start | bytes 245768 | tf_op jit(solution)/shard_map/ppermute | solution.py:293
  77.4 0.9 %collective-permute-done.21.refs_1_ = s16[320,128]{1,0:T(8,128)(2,1)S(1)} collective-permute-done((s16[320,128]{1,0:T(8,128)(2,1)S(1)}, s16[320,128]{1,0:T(8,128)(2,1)S(1)}, u32[]{:S(2)}, u32[]{:S(2)}) %collective-permute-start.21) | collective-permute-done | bytes 81952 | tf_op jit(solution)/shard_map/ppermute | solution.py:293
  79.2 1.5 %collective-permute-done.23.refs_3_ = s16[320,128]{1,0:T(8,128)(2,1)S(1)} collective-permute-done((s16[320,128]{1,0:T(8,128)(2,1)S(1)}, s16[320,128]{1,0:T(8,128)(2,1)S(1)}, u32[]{:S(2)}, u32[]{:S(2)}) %collective-permute-start.23) | collective-permute-done | bytes 81952 | tf_op jit(solution)/shard_map/ppermute | solution.py:293
  80.7 1.3 %collective-permute-done.27.refs_7_ = s16[320,128]{1,0:T(8,128)(2,1)S(1)} collective-permute-done((s16[320,128]{1,0:T(8,128)(2,1)S(1)}, s16[320,128]{1,0:T(8,128)(2,1)S(1)}, u32[]{:S(2)}, u32[]{:S(2)}) %collective-permute-start.27) | collective-permute-done | bytes 81952 | tf_op jit(solution)/shard_map/ppermute | solution.py:293
  81.9 1.8 %shard_map.146 = (f32[128,1024]{1,0:T(8,128)}, f32[1,1024]{1,0:T(1,128)}, f32[172,1024]{1,0:T(8,128)}, f32[1,256]{1,0:T(1,128)}) custom-call(s32[11]{0:T(128)S(1)} %pad_add_fusion.info, s16[320,128]{1,0:T(8,128)(2,1)S(1)} %get-tuple-element.82.refs_0_, s16[320,128]{1,0:T(8,128)(2,1)S(1)} %collective-permute-done.21.refs_1_, ...), custom_call_target="tpu_custom_call" | custom-call | tf_op jit(solution)/shard_map/pallas_call | solution.py:23
  (49 shorter events, 11.1 us)
Async XLA Ops:
  1.4 0.9 %copy-start.1 = (bf16[1,512,128]{2,1,0:T(8,128)(2,1)S(1)}, bf16[1,512,128]{2,1,0:T(8,128)(2,1)}, u32[]{:S(2)}) copy-start(bf16[1,512,128]{2,1,0:T(8,128)(2,1)} %param.11) | copy-start | bytes 393220
  2.3 0.7 copy-start.2
  3.5 9.6 %collective-permute-start = (bf16[144,128]{1,0:T(8,128)(2,1)S(1)}, bf16[144,128]{1,0:T(8,128)(2,1)S(1)}, u32[]{:S(2)}, u32[]{:S(2)}) collective-permute-start(bf16[144,128]{1,0:T(8,128)(2,1)S(1)} %get-tuple-element.51), channel_id=1, source_target_pairs={{0,4},{1,5},{2,6},{3,7},{4,0},{5,1},{6,2},{7,3},{8,12},{9,13},{10,... | collective-permute-start | bytes 110600 | tf_op jit(solution)/shard_map/ppermute | solution.py:293
  7.6 5.8 %collective-permute-start.1 = (bf16[144,128]{1,0:T(8,128)(2,1)S(1)}, bf16[144,128]{1,0:T(8,128)(2,1)S(1)}, u32[]{:S(2)}, u32[]{:S(2)}) collective-permute-start(bf16[144,128]{1,0:T(8,128)(2,1)S(1)} %get-tuple-element.52), channel_id=1, source_target_pairs={{0,6},{1,7},{2,4},{3,5},{4,2},{5,3},{6,0},{7,1},{8,14},{9,15},{10,... | collective-permute-start | bytes 110600 | tf_op jit(solution)/shard_map/ppermute | solution.py:293
  9.0 7.6 %collective-permute-start.2 = (bf16[144,128]{1,0:T(8,128)(2,1)S(1)}, bf16[144,128]{1,0:T(8,128)(2,1)S(1)}, u32[]{:S(2)}, u32[]{:S(2)}) collective-permute-start(bf16[144,128]{1,0:T(8,128)(2,1)S(1)} %get-tuple-element.53), channel_id=1, source_target_pairs={{0,2},{1,3},{2,0},{3,1},{4,6},{5,7},{6,4},{7,5},{8,10},{9,11},{10,... | collective-permute-start | bytes 110600 | tf_op jit(solution)/shard_map/ppermute | solution.py:293
  9.2 7.3 %collective-permute-start.3 = (bf16[144,128]{1,0:T(8,128)(2,1)S(1)}, bf16[144,128]{1,0:T(8,128)(2,1)S(1)}, u32[]{:S(2)}, u32[]{:S(2)}) collective-permute-start(bf16[144,128]{1,0:T(8,128)(2,1)S(1)} %get-tuple-element.54), channel_id=1, source_target_pairs={{0,5},{1,4},{2,7},{3,6},{4,1},{5,0},{6,3},{7,2},{8,13},{9,12},{10,... | collective-permute-start | bytes 110600 | tf_op jit(solution)/shard_map/ppermute | solution.py:293
  10.6 5.9 %collective-permute-start.4 = (bf16[144,128]{1,0:T(8,128)(2,1)S(1)}, bf16[144,128]{1,0:T(8,128)(2,1)S(1)}, u32[]{:S(2)}, u32[]{:S(2)}) collective-permute-start(bf16[144,128]{1,0:T(8,128)(2,1)S(1)} %get-tuple-element.55), channel_id=1, source_target_pairs={{0,7},{1,6},{2,5},{3,4},{4,3},{5,2},{6,1},{7,0},{8,15},{9,14},{10,... | collective-permute-start | bytes 110600 | tf_op jit(solution)/shard_map/ppermute | solution.py:293
  13.1 3.5 %collective-permute-start.5 = (bf16[144,128]{1,0:T(8,128)(2,1)S(1)}, bf16[144,128]{1,0:T(8,128)(2,1)S(1)}, u32[]{:S(2)}, u32[]{:S(2)}) collective-permute-start(bf16[144,128]{1,0:T(8,128)(2,1)S(1)} %get-tuple-element.56), channel_id=1, source_target_pairs={{0,3},{1,2},{2,1},{3,0},{4,7},{5,6},{6,5},{7,4},{8,11},{9,10},{10,... | collective-permute-start | bytes 110600 | tf_op jit(solution)/shard_map/ppermute | solution.py:293
  13.4 3.2 %collective-permute-start.6 = (bf16[144,128]{1,0:T(8,128)(2,1)S(1)}, bf16[144,128]{1,0:T(8,128)(2,1)S(1)}, u32[]{:S(2)}, u32[]{:S(2)}) collective-permute-start(bf16[144,128]{1,0:T(8,128)(2,1)S(1)} %get-tuple-element.57), channel_id=1, source_target_pairs={{0,1},{1,0},{2,3},{3,2},{4,5},{5,4},{6,7},{7,6},{8,9},{9,8},{10,11... | collective-permute-start | bytes 110600 | tf_op jit(solution)/shard_map/ppermute | solution.py:293
  15.2 1.0 %copy-start = (bf16[1,4,4,128,128]{4,3,2,1,0:T(8,128)(2,1)S(1)}, bf16[1,4,4,128,128]{4,3,2,1,0:T(8,128)(2,1)}, u32[]{:S(2)}) copy-start(bf16[1,4,4,128,128]{4,3,2,1,0:T(8,128)(2,1)} %param.15) | copy-start | bytes 1572868
  18.9 13.3 %collective-permute-start.7 = (bf16[128,512]{1,0:T(8,128)(2,1)S(1)}, bf16[128,512]{1,0:T(8,128)(2,1)S(1)}, u32[]{:S(2)}, u32[]{:S(2)}) collective-permute-start(bf16[128,512]{1,0:T(8,128)(2,1)S(1)} %get-tuple-element.60), channel_id=1, source_target_pairs={{0,4},{1,5},{2,6},{3,7},{4,0},{5,1},{6,2},{7,3},{8,12},{9,13},{10,... | collective-permute-start | bytes 393224 | tf_op jit(solution)/shard_map/ppermute | solution.py:293
  21.7 10.4 %collective-permute-start.8 = (bf16[128,512]{1,0:T(8,128)(2,1)S(1)}, bf16[128,512]{1,0:T(8,128)(2,1)S(1)}, u32[]{:S(2)}, u32[]{:S(2)}) collective-permute-start(bf16[128,512]{1,0:T(8,128)(2,1)S(1)} %get-tuple-element.61), channel_id=1, source_target_pairs={{0,6},{1,7},{2,4},{3,5},{4,2},{5,3},{6,0},{7,1},{8,14},{9,15},{10,... | collective-permute-start | bytes 393224 | tf_op jit(solution)/shard_map/ppermute | solution.py:293
  23.8 14.1 %collective-permute-start.9 = (bf16[128,512]{1,0:T(8,128)(2,1)}, bf16[128,512]{1,0:T(8,128)(2,1)S(1)}, u32[]{:S(2)}, u32[]{:S(2)}) collective-permute-start(bf16[128,512]{1,0:T(8,128)(2,1)} %get-tuple-element.62), channel_id=1, source_target_pairs={{0,2},{1,3},{2,0},{3,1},{4,6},{5,7},{6,4},{7,5},{8,10},{9,11},{10,... | collective-permute-start | bytes 393224 | tf_op jit(solution)/shard_map/ppermute | solution.py:293
  23.8 18.9 %collective-permute-start.10 = (bf16[128,512]{1,0:T(8,128)(2,1)}, bf16[128,512]{1,0:T(8,128)(2,1)S(1)}, u32[]{:S(2)}, u32[]{:S(2)}) collective-permute-start(bf16[128,512]{1,0:T(8,128)(2,1)} %get-tuple-element.63), channel_id=1, source_target_pairs={{0,5},{1,4},{2,7},{3,6},{4,1},{5,0},{6,3},{7,2},{8,13},{9,12},{10,... | collective-permute-start | bytes 393224 | tf_op jit(solution)/shard_map/ppermute | solution.py:293
  25.6 17.1 %collective-permute-start.11 = (bf16[128,512]{1,0:T(8,128)(2,1)}, bf16[128,512]{1,0:T(8,128)(2,1)S(1)}, u32[]{:S(2)}, u32[]{:S(2)}) collective-permute-start(bf16[128,512]{1,0:T(8,128)(2,1)} %get-tuple-element.64), channel_id=1, source_target_pairs={{0,7},{1,6},{2,5},{3,4},{4,3},{5,2},{6,1},{7,0},{8,15},{9,14},{10,... | collective-permute-start | bytes 393224 | tf_op jit(solution)/shard_map/ppermute | solution.py:293
  32.2 10.8 %collective-permute-start.12 = (bf16[128,512]{1,0:T(8,128)(2,1)}, bf16[128,512]{1,0:T(8,128)(2,1)S(1)}, u32[]{:S(2)}, u32[]{:S(2)}) collective-permute-start(bf16[128,512]{1,0:T(8,128)(2,1)} %get-tuple-element.65), channel_id=1, source_target_pairs={{0,3},{1,2},{2,1},{3,0},{4,7},{5,6},{6,5},{7,4},{8,11},{9,10},{10,... | collective-permute-start | bytes 393224 | tf_op jit(solution)/shard_map/ppermute | solution.py:293
  32.2 10.8 %collective-permute-start.13 = (bf16[128,512]{1,0:T(8,128)(2,1)}, bf16[128,512]{1,0:T(8,128)(2,1)S(1)}, u32[]{:S(2)}, u32[]{:S(2)}) collective-permute-start(bf16[128,512]{1,0:T(8,128)(2,1)} %get-tuple-element.66), channel_id=1, source_target_pairs={{0,1},{1,0},{2,3},{3,2},{4,5},{5,4},{6,7},{7,6},{8,9},{9,8},{10,11... | collective-permute-start | bytes 393224 | tf_op jit(solution)/shard_map/ppermute | solution.py:293
  51.3 2.1 %collective-permute-start.14 = (f32[4,312,128]{2,1,0:T(8,128)S(1)}, f32[4,312,128]{2,1,0:T(8,128)S(1)}, u32[]{:S(2)}, u32[]{:S(2)}) collective-permute-start(f32[4,312,128]{2,1,0:T(8,128)S(1)} %get-tuple-element.73), channel_id=1, source_target_pairs={{0,1},{1,0},{2,3},{3,2},{4,5},{5,4},{6,7},{7,6},{8,9},{9,8},{10,11... | collective-permute-start | bytes 1916936 | tf_op jit(solution)/shard_map/ppermute | solution.py:293
  53.6 4.6 %collective-permute-start.15 = (s16[320,128]{1,0:T(8,128)(2,1)S(1)}, s16[320,128]{1,0:T(8,128)(2,1)S(1)}, u32[]{:S(2)}, u32[]{:S(2)}) collective-permute-start(s16[320,128]{1,0:T(8,128)(2,1)S(1)} %get-tuple-element.75), channel_id=1, source_target_pairs={{0,8},{8,0},{16,24},{24,16},{1,9},{9,1},{17,25},{25,17},{2,10},{10... | collective-permute-start | bytes 245768 | tf_op jit(solution)/shard_map/ppermute | solution.py:293
  55.2 5.2 %collective-permute-start.16 = (s16[320,128]{1,0:T(8,128)(2,1)S(1)}, s16[320,128]{1,0:T(8,128)(2,1)S(1)}, u32[]{:S(2)}, u32[]{:S(2)}) collective-permute-start(s16[320,128]{1,0:T(8,128)(2,1)S(1)} %get-tuple-element.76), channel_id=1, source_target_pairs={{0,16},{8,24},{16,0},{24,8},{1,17},{9,25},{17,1},{25,9},{2,18},{10... | collective-permute-start | bytes 245768 | tf_op jit(solution)/shard_map/ppermute | solution.py:293
  56.7 5.3 %collective-permute-start.17 = (s16[320,128]{1,0:T(8,128)(2,1)S(1)}, s16[320,128]{1,0:T(8,128)(2,1)S(1)}, u32[]{:S(2)}, u32[]{:S(2)}) collective-permute-start(s16[320,128]{1,0:T(8,128)(2,1)S(1)} %get-tuple-element.77), channel_id=1, source_target_pairs={{0,24},{8,16},{16,8},{24,0},{1,25},{9,17},{17,9},{25,1},{2,26},{10... | collective-permute-start | bytes 245768 | tf_op jit(solution)/shard_map/ppermute | solution.py:293
  62.2 9.8 %collective-permute-start.18 = (s16[320,128]{1,0:T(8,128)(2,1)S(1)}, s16[320,128]{1,0:T(8,128)(2,1)S(1)}, u32[]{:S(2)}, u32[]{:S(2)}) collective-permute-start(s16[320,128]{1,0:T(8,128)(2,1)S(1)} %get-tuple-element.78), channel_id=1, source_target_pairs={{0,4},{1,5},{2,6},{3,7},{4,0},{5,1},{6,2},{7,3},{8,12},{9,13},{10,... | collective-permute-start | bytes 245768 | tf_op jit(solution)/shard_map/ppermute | solution.py:293
  67.2 6.5 %collective-permute-start.19 = (s16[320,128]{1,0:T(8,128)(2,1)S(1)}, s16[320,128]{1,0:T(8,128)(2,1)S(1)}, u32[]{:S(2)}, u32[]{:S(2)}) collective-permute-start(s16[320,128]{1,0:T(8,128)(2,1)S(1)} %get-tuple-element.79), channel_id=1, source_target_pairs={{0,6},{1,7},{2,4},{3,5},{4,2},{5,3},{6,0},{7,1},{8,14},{9,15},{10,... | collective-permute-start | bytes 245768 | tf_op jit(solution)/shard_map/ppermute | solution.py:293
  68.4 5.3 %collective-permute-start.20 = (s16[320,128]{1,0:T(8,128)(2,1)S(1)}, s16[320,128]{1,0:T(8,128)(2,1)S(1)}, u32[]{:S(2)}, u32[]{:S(2)}) collective-permute-start(s16[320,128]{1,0:T(8,128)(2,1)S(1)} %get-tuple-element.80), channel_id=1, source_target_pairs={{0,2},{1,3},{2,0},{3,1},{4,6},{5,7},{6,4},{7,5},{8,10},{9,11},{10,... | collective-permute-start | bytes 245768 | tf_op jit(solution)/shard_map/ppermute | solution.py:293
  73.8 4.5 %collective-permute-start.21 = (s16[320,128]{1,0:T(8,128)(2,1)S(1)}, s16[320,128]{1,0:T(8,128)(2,1)S(1)}, u32[]{:S(2)}, u32[]{:S(2)}) collective-permute-start(s16[320,128]{1,0:T(8,128)(2,1)S(1)} %get-tuple-element.83), channel_id=1, source_target_pairs={{0,8},{8,0},{16,24},{24,16},{1,9},{9,1},{17,25},{25,17},{2,10},{10... | collective-permute-start | bytes 245768 | tf_op jit(solution)/shard_map/ppermute | solution.py:293
  74.7 4.4 %collective-permute-start.22 = (s16[320,128]{1,0:T(8,128)(2,1)S(1)}, s16[320,128]{1,0:T(8,128)(2,1)S(1)}, u32[]{:S(2)}, u32[]{:S(2)}) collective-permute-start(s16[320,128]{1,0:T(8,128)(2,1)S(1)} %get-tuple-element.84), channel_id=1, source_target_pairs={{0,16},{8,24},{16,0},{24,8},{1,17},{9,25},{17,1},{25,9},{2,18},{10... | collective-permute-start | bytes 245768 | tf_op jit(solution)/shard_map/ppermute | solution.py:293
  75.3 5.3 %collective-permute-start.23 = (s16[320,128]{1,0:T(8,128)(2,1)S(1)}, s16[320,128]{1,0:T(8,128)(2,1)S(1)}, u32[]{:S(2)}, u32[]{:S(2)}) collective-permute-start(s16[320,128]{1,0:T(8,128)(2,1)S(1)} %get-tuple-element.85), channel_id=1, source_target_pairs={{0,24},{8,16},{16,8},{24,0},{1,25},{9,17},{17,9},{25,1},{2,26},{10... | collective-permute-start | bytes 245768 | tf_op jit(solution)/shard_map/ppermute | solution.py:293
  77.4 3.3 %collective-permute-start.24 = (s16[320,128]{1,0:T(8,128)(2,1)S(1)}, s16[320,128]{1,0:T(8,128)(2,1)S(1)}, u32[]{:S(2)}, u32[]{:S(2)}) collective-permute-start(s16[320,128]{1,0:T(8,128)(2,1)S(1)} %get-tuple-element.82.refs_0_), channel_id=1, source_target_pairs={{0,1},{1,0},{2,3},{3,2},{4,5},{5,4},{6,7},{7,6},{8,9},{9,8},{10,11... | collective-permute-start | bytes 245768 | tf_op jit(solution)/shard_map/ppermute | solution.py:293
  78.3 2.3 %collective-permute-start.25 = (s16[320,128]{1,0:T(8,128)(2,1)S(1)}, s16[320,128]{1,0:T(8,128)(2,1)S(1)}, u32[]{:S(2)}, u32[]{:S(2)}) collective-permute-start(s16[320,128]{1,0:T(8,128)(2,1)S(1)} %collective-permute-done.21.refs_1_), channel_id=1, source_target_pairs={{0,1},{1,0},{2,3},{3,2},{4,5},{5,4},{6,7},{7,6},{8,9},{9,8},{10,11... | collective-permute-start | bytes 245768 | tf_op jit(solution)/shard_map/ppermute | solution.py:293
  79.2 1.5 %collective-permute-start.26 = (s16[320,128]{1,0:T(8,128)(2,1)S(1)}, s16[320,128]{1,0:T(8,128)(2,1)S(1)}, u32[]{:S(2)}, u32[]{:S(2)}) collective-permute-start(s16[320,128]{1,0:T(8,128)(2,1)S(1)} %collective-permute-done.22.refs_2_), channel_id=1, source_target_pairs={{0,1},{1,0},{2,3},{3,2},{4,5},{5,4},{6,7},{7,6},{8,9},{9,8},{10,11... | collective-permute-start | bytes 245768 | tf_op jit(solution)/shard_map/ppermute | solution.py:293
  80.7 1.3 %collective-permute-start.27 = (s16[320,128]{1,0:T(8,128)(2,1)S(1)}, s16[320,128]{1,0:T(8,128)(2,1)S(1)}, u32[]{:S(2)}, u32[]{:S(2)}) collective-permute-start(s16[320,128]{1,0:T(8,128)(2,1)S(1)} %collective-permute-done.23.refs_3_), channel_id=1, source_target_pairs={{0,1},{1,0},{2,3},{3,2},{4,5},{5,4},{6,7},{7,6},{8,9},{9,8},{10,11... | collective-permute-start | bytes 245768 | tf_op jit(solution)/shard_map/ppermute | solution.py:293

commit v5 on v4

--- a/solution.py
+++ b/solution.py
@@ -16,6 +16,7 @@
 VMEM = pl.BlockSpec(memory_space=pltpu.VMEM)
 CHUNK = 256
 BATCH = 2
+LATE = 4
 TAIL = 8
 
 
@@ -61,7 +62,8 @@
         put(s, (f * cols[:, s : s + 1]).astype(BF16))
 
 
-def layout_kernel(feats, masks, adj, lhs, own):
+def layout_kernel(feats, masks, adj, slots, lhs, own, same_slots):
+    same_slots[...] = slots[...]
     tiles, tile, feat = feats.shape
     for t in range(tiles):
         lhs[t] = jnp.concatenate([adj[t, j] for j in range(adj.shape[1])], 1)
@@ -73,7 +75,7 @@
 
 
 def pool_index(info, slots, r, j, dom, nnz):
-    q = slots[r * nnz + j]
+    q = slots[r, j]
     k = q ^ info[0]
     own = (dom - 1) + info[3 + info[0]]
     return jnp.where(q >= dom, q - 1, jnp.where(k == 0, own, k - 1))
@@ -107,6 +109,24 @@
 
 def fold(x):
     return functools.reduce(lambda a, b: a + b, [x[i : i + 8] for i in range(0, x.shape[0], 8)])
+
+
+def prepare_kernel(
+    w_in, b_in, w_out_t, b_out, labels, labeled, block, half_w, half_b, wide_w, half_w_t, wide_b, code, same_block
+):
+    same_block[...] = block[...]
+    classes, hidden = w_out_t.shape
+    wide = wide_w.shape[1]
+    half_w[...] = w_in[...] * jnp.asarray(0.5, BF16)
+    half_b[...] = b_in[...] * 0.5
+    padded = jnp.concatenate([w_out_t[...], jnp.zeros((wide - classes, hidden), BF16)], 0)
+    half_w_t[...] = padded * jnp.asarray(0.5, BF16)
+    wide_w[...] = padded.T
+    wide_b[...] = jnp.concatenate([b_out[...], jnp.full((1, wide - classes), -1e30, F32)], 1)
+    tiles, tile = labels.shape
+    rows = jnp.where(labeled[...] != 0, labels[...], -1).astype(F32)
+    rows = jnp.concatenate([rows, jnp.zeros((-tiles % 8, tile), F32)], 0)
+    code[...] = rows.T.astype(I32)
 
 
 def mlp_kernel(dom, samples, scale, info, slots, lhs, cur, total, code, half_w, half_b, w_out, half_w_t, b_out, *refs):
@@ -156,7 +176,7 @@
             avg = sum(probs[1:], probs[0]) * (1.0 / samples)
             sq = avg * avg
             sharp = sq * (1.0 / jnp.sum(sq, -1, keepdims=True))
-            label = code[r, c : c + step, :]
+            label = code[c : c + step, r : r + 1]
             hit = jnp.where(lax.broadcasted_iota(I32, (step, wide), 1) == label, scale, 0.0)
             used = jnp.where(label >= 0, scale, 0.0)
             part = jnp.zeros((step, wide), F32)
@@ -352,7 +372,6 @@
     me = lax.axis_index("dom")
     place = jnp.stack([me, lax.axis_index("dp") & 3, me & 1]).astype(I32)
     info = jnp.concatenate([place, serve_ids.reshape(-1)])
-    slots = col_slot.reshape(-1)
     adj = adj_blocks[0]
     feats = features.reshape(tiles, tile, feat)
     masks = keep_masks[0]
@@ -365,10 +384,10 @@
         [info, feats, masks],
         n_smem=1,
     )
-    lhs, own = call(
+    lhs, own, slots = call(
         layout_kernel,
-        [like((tiles, tile, nnz * tile), BF16), like((tiles, tile, lanes), BF16)],
-        [feats, masks, adj],
+        [like((tiles, tile, nnz * tile), BF16), like((tiles, tile, lanes), BF16), like((tiles, nnz), I32)],
+        [feats, masks, adj, col_slot[0]],
     )
     msgs = swap_all(msgs)
     cur, total, *outs = call(
@@ -378,11 +397,22 @@
         [pltpu.VMEM((dom - 1 + tiles, tile, lanes), BF16)],
         n_smem=2,
     )
+    late = min(LATE, dom - 2)
+    half_w, half_b, w_out, half_w_t, b_out, code, outs[late] = call(
+        prepare_kernel,
+        [
+            like((feat, hidden), BF16),
+            like((1, hidden), F32),
+            like((hidden, wide), BF16),
+            like((wide, hidden), BF16),
+            like((1, wide), F32),
+            like((tile, -(-tiles // 8) * 8), I32),
+            like(outs[late].shape, BF16),
+        ],
+        [weight_in, bias_in.reshape(1, hidden), weight_out.T, bias_out.reshape(1, classes)]
+        + [node_labels.reshape(tiles, tile), labeled.reshape(tiles, tile), outs[late]],
+    )
     outs = swap_all(outs)
-
-    code = jnp.where(labeled != 0, node_labels, -1).reshape(tiles, tile, 1)
-    w_out = jnp.pad(weight_out, ((0, 0), (0, wide - classes)))
-    b_out = jnp.pad(bias_out, (0, wide - classes), constant_values=-1e30).reshape(1, wide)
     rows = samples * tile * tiles
     wide_t = -(-classes // 16) * 16
     half = like((hidden // 256, feat + wide_t + TAIL, 128), F32)
@@ -397,9 +427,7 @@
             like((8, hidden), F32),
             like((8, wide), F32),
         ],
-        [info, slots, lhs, cur, total, code, 0.5 * weight_in, 0.5 * bias_in.reshape(1, hidden)]
-        + [w_out, 0.5 * w_out.T, b_out]
-        + outs,
+        [info, slots, lhs, cur, total, code, half_w, half_b, w_out, half_w_t, b_out] + outs,
         [
             pltpu.VMEM((dom - 1 + tiles, tile, lanes), BF16),
             pltpu.VMEM((rows, hidden), F32),

time: 84.2 us -> 81.8 us (0.971)
  other arithmetic: 4.16 us -> 0.73 us
  starting transfers between devices: 31.3 us -> 33.2 us
    unnamed x7 -> x20, local copies, waits for them, and re-layouts: 4.62 us -> 7.97 us
    mul x3 -> x0, other arithmetic: 2.72 us -> none  [the longest x1 1.06 us: per_device(): 0.5 * w_out.T]
    ppermute x28, starting transfers between devices: 31.3 us -> 33.2 us  [xor_permute(): lax.ppermute(x, axis, [(i, i ^ mask) for i in range(lax.axis_size(axis))])]
    pad x2 -> x0, local copies, waits for them, and re-layouts: 1.81 us -> none  [the longest x1 1.13 us: per_device(): w_out = jnp.pad(weight_out, ((0, 0), (0, wide - classes)))]
    reshape x2 -> x0, local copies, waits for them, and re-layouts: 0.91 us -> none  [the longest x1 0.77 us: per_device(): slots = col_slot.reshape(-1)]
    pallas_call x9 -> x10, Pallas kernels: 15.2 us -> 14.6 us  [call(): pl.pallas_call(kernel, out_shape=outs, in_specs=[SMEM] * n_smem + [VMEM]...]
  transfers between devices with their start and end apart: 28 -> 28, of which waited for: 15 -> 16; matrix products, arithmetic and copies ran while one was open for 10% -> 0% of each run, Pallas kernels for 2% -> 2%
where the time goes in v5:
time: 81.8 us; the launch traced here: 81.5 us
  starting transfers between devices  33.2 us (41%)
  waiting for transfers between devices  24.2 us (30%)
  Pallas kernels  14.6 us (18%)
  local copies, waits for them, and re-layouts  7.97 us (10%)
    ppermute x28, starting transfers between devices, xor_permute(): lax.ppermute(x, axis, [(i, i ^ mask) for i in range(lax.axis_size(axis))])  33.2 us
    ppermute x28, waiting for transfers between devices, xor_permute(): lax.ppermute(x, axis, [(i, i ^ mask) for i in range(lax.axis_size(axis))])  24.2 us
    pallas_call x10, Pallas kernels, call(): pl.pallas_call(kernel, out_shape=outs, in_specs=[SMEM] * n_smem + [VMEM]...  14.6 us
    unnamed x20, local copies, waits for them, and re-layouts  7.97 us
  transfers between devices with their start and end apart: 28, of which 16 were waited for; matrix products, arithmetic and copies ran while one was open for 0% of the time, Pallas kernels for 2%

profile of v5, /device:TPU:0, one launch (start us, length us, event | category | flops | bytes accessed | tf_op | source)
XLA Modules:
  0.0 81.5 jit_solution(8772923075874379415)
XLA Ops:
  1.4 0.9 %copy-done.3 = bf16[1,512,128]{2,1,0:T(8,128)(2,1)S(1)} copy-done((bf16[1,512,128]{2,1,0:T(8,128)(2,1)S(1)}, bf16[1,512,128]{2,1,0:T(8,128)(2,1)}, u32[]{:S(2)}) %copy-start.3) | copy-done | bytes 131096
  3.5 4.1 %collective-permute-start = (bf16[144,128]{1,0:T(8,128)(2,1)S(1)}, bf16[144,128]{1,0:T(8,128)(2,1)S(1)}, u32[]{:S(2)}, u32[]{:S(2)}) collective-permute-start(bf16[144,128]{1,0:T(8,128)(2,1)S(1)} %get-tuple-element.60), channel_id=1, source_target_pairs={{0,4},{1,5},{2,6},{3,7},{4,0},{5,1},{6,2},{7,3},{8,12},{9,13},{10,... | collective-permute-start | bytes 110600 | tf_op jit(solution)/shard_map/ppermute | solution.py:313
  7.6 1.3 %collective-permute-start.1 = (bf16[144,128]{1,0:T(8,128)(2,1)S(1)}, bf16[144,128]{1,0:T(8,128)(2,1)S(1)}, u32[]{:S(2)}, u32[]{:S(2)}) collective-permute-start(bf16[144,128]{1,0:T(8,128)(2,1)S(1)} %get-tuple-element.61), channel_id=1, source_target_pairs={{0,6},{1,7},{2,4},{3,5},{4,2},{5,3},{6,0},{7,1},{8,14},{9,15},{10,... | collective-permute-start | bytes 110600 | tf_op jit(solution)/shard_map/ppermute | solution.py:313
  9.2 1.4 %collective-permute-start.3 = (bf16[144,128]{1,0:T(8,128)(2,1)S(1)}, bf16[144,128]{1,0:T(8,128)(2,1)S(1)}, u32[]{:S(2)}, u32[]{:S(2)}) collective-permute-start(bf16[144,128]{1,0:T(8,128)(2,1)S(1)} %get-tuple-element.63), channel_id=1, source_target_pairs={{0,5},{1,4},{2,7},{3,6},{4,1},{5,0},{6,3},{7,2},{8,13},{9,12},{10,... | collective-permute-start | bytes 110600 | tf_op jit(solution)/shard_map/ppermute | solution.py:313
  10.6 2.5 %collective-permute-start.4 = (bf16[144,128]{1,0:T(8,128)(2,1)S(1)}, bf16[144,128]{1,0:T(8,128)(2,1)S(1)}, u32[]{:S(2)}, u32[]{:S(2)}) collective-permute-start(bf16[144,128]{1,0:T(8,128)(2,1)S(1)} %get-tuple-element.64), channel_id=1, source_target_pairs={{0,7},{1,6},{2,5},{3,4},{4,3},{5,2},{6,1},{7,0},{8,15},{9,14},{10,... | collective-permute-start | bytes 110600 | tf_op jit(solution)/shard_map/ppermute | solution.py:313
  13.4 1.0 %copy-done = bf16[1,4,4,128,128]{4,3,2,1,0:T(8,128)(2,1)S(1)} copy-done((bf16[1,4,4,128,128]{4,3,2,1,0:T(8,128)(2,1)S(1)}, bf16[1,4,4,128,128]{4,3,2,1,0:T(8,128)(2,1)}, u32[]{:S(2)}) %copy-start) | copy-done | bytes 524312
  16.6 1.5 %shard_map.140 = (bf16[4,128,512]{2,1,0:T(8,128)(2,1)S(1)}, f32[4,128,512]{2,1,0:T(8,128)S(1)}, bf16[128,512]{1,0:T(8,128)(2,1)S(1)}, bf16[128,512]{1,0:T(8,128)...) custom-call(s32[11]{0:T(128)S(1)} %pad_add_fusion.info, ...), custom_call_target="tpu_custom_call" | custom-call | tf_op jit(solution)/shard_map/pallas_call | solution.py:24
  18.2 1.8 %collective-permute-start.7 = (bf16[128,512]{1,0:T(8,128)(2,1)S(1)}, bf16[128,512]{1,0:T(8,128)(2,1)S(1)}, u32[]{:S(2)}, u32[]{:S(2)}) collective-permute-start(bf16[128,512]{1,0:T(8,128)(2,1)S(1)} %get-tuple-element.76), channel_id=1, source_target_pairs={{0,4},{1,5},{2,6},{3,7},{4,0},{5,1},{6,2},{7,3},{8,12},{9,13},{10,... | collective-permute-start | bytes 393224 | tf_op jit(solution)/shard_map/ppermute | solution.py:313
  20.0 1.3 %collective-permute-start.8 = (bf16[128,512]{1,0:T(8,128)(2,1)S(1)}, bf16[128,512]{1,0:T(8,128)(2,1)S(1)}, u32[]{:S(2)}, u32[]{:S(2)}) collective-permute-start(bf16[128,512]{1,0:T(8,128)(2,1)S(1)} %get-tuple-element.77), channel_id=1, source_target_pairs={{0,6},{1,7},{2,4},{3,5},{4,2},{5,3},{6,0},{7,1},{8,14},{9,15},{10,... | collective-permute-start | bytes 393224 | tf_op jit(solution)/shard_map/ppermute | solution.py:313
  21.7 1.4 %collective-permute-start.10 = (bf16[128,512]{1,0:T(8,128)(2,1)S(1)}, bf16[128,512]{1,0:T(8,128)(2,1)S(1)}, u32[]{:S(2)}, u32[]{:S(2)}) collective-permute-start(bf16[128,512]{1,0:T(8,128)(2,1)S(1)} %get-tuple-element.79), channel_id=1, source_target_pairs={{0,5},{1,4},{2,7},{3,6},{4,1},{5,0},{6,3},{7,2},{8,13},{9,12},{10,... | collective-permute-start | bytes 393224 | tf_op jit(solution)/shard_map/ppermute | solution.py:313
  23.1 1.5 %collective-permute-start.12 = (bf16[128,512]{1,0:T(8,128)(2,1)S(1)}, bf16[128,512]{1,0:T(8,128)(2,1)S(1)}, u32[]{:S(2)}, u32[]{:S(2)}) collective-permute-start(bf16[128,512]{1,0:T(8,128)(2,1)S(1)} %get-tuple-element.81), channel_id=1, source_target_pairs={{0,3},{1,2},{2,1},{3,0},{4,7},{5,6},{6,5},{7,4},{8,11},{9,10},{10,... | collective-permute-start | bytes 393224 | tf_op jit(solution)/shard_map/ppermute | solution.py:313
  24.6 1.0 %copy-done.1 = bf16[1024,172]{0,1:T(8,128)(2,1)S(1)} copy-done((bf16[1024,172]{0,1:T(8,128)(2,1)S(1)}, bf16[1024,172]{0,1:T(8,128)(2,1)}, u32[]{:S(2)}) %copy-start.1) | copy-done | bytes 352280
  25.6 0.9 %copy-done.2 = bf16[128,1024]{1,0:T(8,128)(2,1)S(1)} copy-done((bf16[128,1024]{1,0:T(8,128)(2,1)S(1)}, bf16[128,1024]{1,0:T(8,128)(2,1)}, u32[]{:S(2)}) %copy-start.2) | copy-done | bytes 262168
  29.6 1.5 %collective-permute-done.7.refs_0_ = bf16[128,512]{1,0:T(8,128)(2,1)S(1)} collective-permute-done((bf16[128,512]{1,0:T(8,128)(2,1)S(1)}, bf16[128,512]{1,0:T(8,128)(2,1)S(1)}, u32[]{:S(2)}, u32[]{:S(2)}) %collective-permute-start.7) | collective-permute-done | bytes 131104 | tf_op jit(solution)/shard_map/ppermute | solution.py:313
  31.1 4.1 %collective-permute-start.11 = (bf16[128,512]{1,0:T(8,128)(2,1)S(1)}, bf16[128,512]{1,0:T(8,128)(2,1)S(1)}, u32[]{:S(2)}, u32[]{:S(2)}) collective-permute-start(bf16[128,512]{1,0:T(8,128)(2,1)S(1)} %get-tuple-element.80), channel_id=1, source_target_pairs={{0,7},{1,6},{2,5},{3,4},{4,3},{5,2},{6,1},{7,0},{8,15},{9,14},{10,... | collective-permute-start | bytes 393224 | tf_op jit(solution)/shard_map/ppermute | solution.py:313
  35.1 6.4 %collective-permute-done.10.refs_3_ = bf16[128,512]{1,0:T(8,128)(2,1)S(1)} collective-permute-done((bf16[128,512]{1,0:T(8,128)(2,1)S(1)}, bf16[128,512]{1,0:T(8,128)(2,1)S(1)}, u32[]{:S(2)}, u32[]{:S(2)}) %collective-permute-start.10) | collective-permute-done | bytes 131104 | tf_op jit(solution)/shard_map/ppermute | solution.py:313
  41.6 8.2 %shard_map.142 = (f32[4,312,128]{2,1,0:T(8,128)S(1)}, bf16[128,2048]{1,0:T(8,128)(2,1)S(1)}, bf16[2048,1024]{1,0:T(8,128)(2,1)S(1)}, bf16[176,2048]{1,0:T(8,128)...) custom-call(s32[11]{0:T(128)S(1)} %pad_add_fusion.info, ...), custom_call_target="tpu_custom_call" | custom-call | tf_op jit(solution)/shard_map/pallas_call | solution.py:24
  50.0 1.5 %shard_map.143.keep = f32[4,312,128]{2,1,0:T(8,128)S(1)} custom-call(s32[11]{0:T(128)S(1)} %pad_add_fusion.info, bf16[128,2048]{1,0:T(8,128)(2,1)S(1)} %get-tuple-element.83.x_t, bf16[2048,1024]{1,0:T(8,128)(2,1)S(1)} %get-tuple-element.84.act, bf16[176,2048]{1,0:T(8,128)(2,1)S(1)} %get-tuple-element.85.dl_t, bf16[2048,1024]{1,0:T(8,128)(2,1)S(1)} %get-tuple-element.86.dpre, ...), custom_call_target="tpu_custom_call" | custom-call | tf_op jit(solution)/shard_map/pallas_call | solution.py:24
  52.2 1.6 %collective-permute-start.15 = (s16[320,128]{1,0:T(8,128)(2,1)S(1)}, s16[320,128]{1,0:T(8,128)(2,1)S(1)}, u32[]{:S(2)}, u32[]{:S(2)}) collective-permute-start(s16[320,128]{1,0:T(8,128)(2,1)S(1)} %get-tuple-element.91), channel_id=1, source_target_pairs={{0,8},{8,0},{16,24},{24,16},{1,9},{9,1},{17,25},{25,17},{2,10},{10... | collective-permute-start | bytes 245768 | tf_op jit(solution)/shard_map/ppermute | solution.py:313
  53.7 1.5 %collective-permute-start.16 = (s16[320,128]{1,0:T(8,128)(2,1)S(1)}, s16[320,128]{1,0:T(8,128)(2,1)S(1)}, u32[]{:S(2)}, u32[]{:S(2)}) collective-permute-start(s16[320,128]{1,0:T(8,128)(2,1)S(1)} %get-tuple-element.92), channel_id=1, source_target_pairs={{0,16},{8,24},{16,0},{24,8},{1,17},{9,25},{17,1},{25,9},{2,18},{10... | collective-permute-start | bytes 245768 | tf_op jit(solution)/shard_map/ppermute | solution.py:313
  55.7 1.0 %collective-permute-done.15.refs_0_ = s16[320,128]{1,0:T(8,128)(2,1)S(1)} collective-permute-done((s16[320,128]{1,0:T(8,128)(2,1)S(1)}, s16[320,128]{1,0:T(8,128)(2,1)S(1)}, u32[]{:S(2)}, u32[]{:S(2)}) %collective-permute-start.15) | collective-permute-done | bytes 81952 | tf_op jit(solution)/shard_map/ppermute | solution.py:313
  56.7 2.3 %collective-permute-done.16.refs_1_ = s16[320,128]{1,0:T(8,128)(2,1)S(1)} collective-permute-done((s16[320,128]{1,0:T(8,128)(2,1)S(1)}, s16[320,128]{1,0:T(8,128)(2,1)S(1)}, u32[]{:S(2)}, u32[]{:S(2)}) %collective-permute-start.16) | collective-permute-done | bytes 81952 | tf_op jit(solution)/shard_map/ppermute | solution.py:313
  59.0 1.6 %collective-permute-done.17.refs_2_ = s16[320,128]{1,0:T(8,128)(2,1)S(1)} collective-permute-done((s16[320,128]{1,0:T(8,128)(2,1)S(1)}, s16[320,128]{1,0:T(8,128)(2,1)S(1)}, u32[]{:S(2)}, u32[]{:S(2)}) %collective-permute-start.17) | collective-permute-done | bytes 81952 | tf_op jit(solution)/shard_map/ppermute | solution.py:313
  60.7 3.3 %collective-permute-start.18 = (s16[320,128]{1,0:T(8,128)(2,1)S(1)}, s16[320,128]{1,0:T(8,128)(2,1)S(1)}, u32[]{:S(2)}, u32[]{:S(2)}) collective-permute-start(s16[320,128]{1,0:T(8,128)(2,1)S(1)} %get-tuple-element.94), channel_id=1, source_target_pairs={{0,4},{1,5},{2,6},{3,7},{4,0},{5,1},{6,2},{7,3},{8,12},{9,13},{10,... | collective-permute-start | bytes 245768 | tf_op jit(solution)/shard_map/ppermute | solution.py:313
  64.0 2.5 %collective-permute-start.19 = (s16[320,128]{1,0:T(8,128)(2,1)S(1)}, s16[320,128]{1,0:T(8,128)(2,1)S(1)}, u32[]{:S(2)}, u32[]{:S(2)}) collective-permute-start(s16[320,128]{1,0:T(8,128)(2,1)S(1)} %get-tuple-element.95), channel_id=1, source_target_pairs={{0,6},{1,7},{2,4},{3,5},{4,2},{5,3},{6,0},{7,1},{8,14},{9,15},{10,... | collective-permute-start | bytes 245768 | tf_op jit(solution)/shard_map/ppermute | solution.py:313
  66.5 1.8 %collective-permute-done.18.refs_0_ = s16[320,128]{1,0:T(8,128)(2,1)S(1)} collective-permute-done((s16[320,128]{1,0:T(8,128)(2,1)S(1)}, s16[320,128]{1,0:T(8,128)(2,1)S(1)}, u32[]{:S(2)}, u32[]{:S(2)}) %collective-permute-start.18) | collective-permute-done | bytes 81952 | tf_op jit(solution)/shard_map/ppermute | solution.py:313
  68.3 2.1 %collective-permute-done.19.refs_1_ = s16[320,128]{1,0:T(8,128)(2,1)S(1)} collective-permute-done((s16[320,128]{1,0:T(8,128)(2,1)S(1)}, s16[320,128]{1,0:T(8,128)(2,1)S(1)}, u32[]{:S(2)}, u32[]{:S(2)}) %collective-permute-start.19) | collective-permute-done | bytes 81952 | tf_op jit(solution)/shard_map/ppermute | solution.py:313
  73.1 1.8 %collective-permute-start.23 = (s16[320,128]{1,0:T(8,128)(2,1)S(1)}, s16[320,128]{1,0:T(8,128)(2,1)S(1)}, u32[]{:S(2)}, u32[]{:S(2)}) collective-permute-start(s16[320,128]{1,0:T(8,128)(2,1)S(1)} %get-tuple-element.101), channel_id=1, source_target_pairs={{0,24},{8,16},{16,8},{24,0},{1,25},{9,17},{17,9},{25,1},{2,26},{10... | collective-permute-start | bytes 245768 | tf_op jit(solution)/shard_map/ppermute | solution.py:313
  75.0 0.9 %collective-permute-done.21.refs_1_ = s16[320,128]{1,0:T(8,128)(2,1)S(1)} collective-permute-done((s16[320,128]{1,0:T(8,128)(2,1)S(1)}, s16[320,128]{1,0:T(8,128)(2,1)S(1)}, u32[]{:S(2)}, u32[]{:S(2)}) %collective-permute-start.21) | collective-permute-done | bytes 81952 | tf_op jit(solution)/shard_map/ppermute | solution.py:313
  76.7 1.7 %collective-permute-done.23.refs_3_ = s16[320,128]{1,0:T(8,128)(2,1)S(1)} collective-permute-done((s16[320,128]{1,0:T(8,128)(2,1)S(1)}, s16[320,128]{1,0:T(8,128)(2,1)S(1)}, u32[]{:S(2)}, u32[]{:S(2)}) %collective-permute-start.23) | collective-permute-done | bytes 81952 | tf_op jit(solution)/shard_map/ppermute | solution.py:313
  78.5 1.3 %collective-permute-done.27.refs_7_ = s16[320,128]{1,0:T(8,128)(2,1)S(1)} collective-permute-done((s16[320,128]{1,0:T(8,128)(2,1)S(1)}, s16[320,128]{1,0:T(8,128)(2,1)S(1)}, u32[]{:S(2)}, u32[]{:S(2)}) %collective-permute-start.27) | collective-permute-done | bytes 81952 | tf_op jit(solution)/shard_map/ppermute | solution.py:313
  79.7 1.8 %shard_map.147 = (f32[128,1024]{1,0:T(8,128)}, f32[1,1024]{1,0:T(1,128)}, f32[172,1024]{1,0:T(8,128)}, f32[1,256]{1,0:T(1,128)}) custom-call(s32[11]{0:T(128)S(1)} %pad_add_fusion.info, s16[320,128]{1,0:T(8,128)(2,1)S(1)} %get-tuple-element.98.refs_0_, s16[320,128]{1,0:T(8,128)(2,1)S(1)} %collective-permute-done.21.refs_1_, ...), custom_call_target="tpu_custom_call" | custom-call | tf_op jit(solution)/shard_map/pallas_call | solution.py:24
  (55 shorter events, 13.1 us)
Async XLA Ops:
  1.4 0.9 %copy-start.3 = (bf16[1,512,128]{2,1,0:T(8,128)(2,1)S(1)}, bf16[1,512,128]{2,1,0:T(8,128)(2,1)}, u32[]{:S(2)}) copy-start(bf16[1,512,128]{2,1,0:T(8,128)(2,1)} %param.11) | copy-start | bytes 393220
  3.5 9.6 %collective-permute-start = (bf16[144,128]{1,0:T(8,128)(2,1)S(1)}, bf16[144,128]{1,0:T(8,128)(2,1)S(1)}, u32[]{:S(2)}, u32[]{:S(2)}) collective-permute-start(bf16[144,128]{1,0:T(8,128)(2,1)S(1)} %get-tuple-element.60), channel_id=1, source_target_pairs={{0,4},{1,5},{2,6},{3,7},{4,0},{5,1},{6,2},{7,3},{8,12},{9,13},{10,... | collective-permute-start | bytes 110600 | tf_op jit(solution)/shard_map/ppermute | solution.py:313
  7.6 5.8 %collective-permute-start.1 = (bf16[144,128]{1,0:T(8,128)(2,1)S(1)}, bf16[144,128]{1,0:T(8,128)(2,1)S(1)}, u32[]{:S(2)}, u32[]{:S(2)}) collective-permute-start(bf16[144,128]{1,0:T(8,128)(2,1)S(1)} %get-tuple-element.61), channel_id=1, source_target_pairs={{0,6},{1,7},{2,4},{3,5},{4,2},{5,3},{6,0},{7,1},{8,14},{9,15},{10,... | collective-permute-start | bytes 110600 | tf_op jit(solution)/shard_map/ppermute | solution.py:313
  9.0 6.5 %collective-permute-start.2 = (bf16[144,128]{1,0:T(8,128)(2,1)S(1)}, bf16[144,128]{1,0:T(8,128)(2,1)S(1)}, u32[]{:S(2)}, u32[]{:S(2)}) collective-permute-start(bf16[144,128]{1,0:T(8,128)(2,1)S(1)} %get-tuple-element.62), channel_id=1, source_target_pairs={{0,2},{1,3},{2,0},{3,1},{4,6},{5,7},{6,4},{7,5},{8,10},{9,11},{10,... | collective-permute-start | bytes 110600 | tf_op jit(solution)/shard_map/ppermute | solution.py:313
  9.2 6.3 %collective-permute-start.3 = (bf16[144,128]{1,0:T(8,128)(2,1)S(1)}, bf16[144,128]{1,0:T(8,128)(2,1)S(1)}, u32[]{:S(2)}, u32[]{:S(2)}) collective-permute-start(bf16[144,128]{1,0:T(8,128)(2,1)S(1)} %get-tuple-element.63), channel_id=1, source_target_pairs={{0,5},{1,4},{2,7},{3,6},{4,1},{5,0},{6,3},{7,2},{8,13},{9,12},{10,... | collective-permute-start | bytes 110600 | tf_op jit(solution)/shard_map/ppermute | solution.py:313
  10.6 5.2 %collective-permute-start.4 = (bf16[144,128]{1,0:T(8,128)(2,1)S(1)}, bf16[144,128]{1,0:T(8,128)(2,1)S(1)}, u32[]{:S(2)}, u32[]{:S(2)}) collective-permute-start(bf16[144,128]{1,0:T(8,128)(2,1)S(1)} %get-tuple-element.64), channel_id=1, source_target_pairs={{0,7},{1,6},{2,5},{3,4},{4,3},{5,2},{6,1},{7,0},{8,15},{9,14},{10,... | collective-permute-start | bytes 110600 | tf_op jit(solution)/shard_map/ppermute | solution.py:313
  13.1 3.5 %collective-permute-start.5 = (bf16[144,128]{1,0:T(8,128)(2,1)S(1)}, bf16[144,128]{1,0:T(8,128)(2,1)S(1)}, u32[]{:S(2)}, u32[]{:S(2)}) collective-permute-start(bf16[144,128]{1,0:T(8,128)(2,1)S(1)} %get-tuple-element.65), channel_id=1, source_target_pairs={{0,3},{1,2},{2,1},{3,0},{4,7},{5,6},{6,5},{7,4},{8,11},{9,10},{10,... | collective-permute-start | bytes 110600 | tf_op jit(solution)/shard_map/ppermute | solution.py:313
  13.4 3.2 %collective-permute-start.6 = (bf16[144,128]{1,0:T(8,128)(2,1)S(1)}, bf16[144,128]{1,0:T(8,128)(2,1)S(1)}, u32[]{:S(2)}, u32[]{:S(2)}) collective-permute-start(bf16[144,128]{1,0:T(8,128)(2,1)S(1)} %get-tuple-element.66), channel_id=1, source_target_pairs={{0,1},{1,0},{2,3},{3,2},{4,5},{5,4},{6,7},{7,6},{8,9},{9,8},{10,11... | collective-permute-start | bytes 110600 | tf_op jit(solution)/shard_map/ppermute | solution.py:313
  13.4 1.0 %copy-start = (bf16[1,4,4,128,128]{4,3,2,1,0:T(8,128)(2,1)S(1)}, bf16[1,4,4,128,128]{4,3,2,1,0:T(8,128)(2,1)}, u32[]{:S(2)}) copy-start(bf16[1,4,4,128,128]{4,3,2,1,0:T(8,128)(2,1)} %param.15) | copy-start | bytes 1572868
  18.2 12.9 %collective-permute-start.7 = (bf16[128,512]{1,0:T(8,128)(2,1)S(1)}, bf16[128,512]{1,0:T(8,128)(2,1)S(1)}, u32[]{:S(2)}, u32[]{:S(2)}) collective-permute-start(bf16[128,512]{1,0:T(8,128)(2,1)S(1)} %get-tuple-element.76), channel_id=1, source_target_pairs={{0,4},{1,5},{2,6},{3,7},{4,0},{5,1},{6,2},{7,3},{8,12},{9,13},{10,... | collective-permute-start | bytes 393224 | tf_op jit(solution)/shard_map/ppermute | solution.py:313
  20.0 11.1 %collective-permute-start.8 = (bf16[128,512]{1,0:T(8,128)(2,1)S(1)}, bf16[128,512]{1,0:T(8,128)(2,1)S(1)}, u32[]{:S(2)}, u32[]{:S(2)}) collective-permute-start(bf16[128,512]{1,0:T(8,128)(2,1)S(1)} %get-tuple-element.77), channel_id=1, source_target_pairs={{0,6},{1,7},{2,4},{3,5},{4,2},{5,3},{6,0},{7,1},{8,14},{9,15},{10,... | collective-permute-start | bytes 393224 | tf_op jit(solution)/shard_map/ppermute | solution.py:313
  21.3 13.8 %collective-permute-start.9 = (bf16[128,512]{1,0:T(8,128)(2,1)S(1)}, bf16[128,512]{1,0:T(8,128)(2,1)S(1)}, u32[]{:S(2)}, u32[]{:S(2)}) collective-permute-start(bf16[128,512]{1,0:T(8,128)(2,1)S(1)} %get-tuple-element.78), channel_id=1, source_target_pairs={{0,2},{1,3},{2,0},{3,1},{4,6},{5,7},{6,4},{7,5},{8,10},{9,11},{10,... | collective-permute-start | bytes 393224 | tf_op jit(solution)/shard_map/ppermute | solution.py:313
  21.7 19.9 %collective-permute-start.10 = (bf16[128,512]{1,0:T(8,128)(2,1)S(1)}, bf16[128,512]{1,0:T(8,128)(2,1)S(1)}, u32[]{:S(2)}, u32[]{:S(2)}) collective-permute-start(bf16[128,512]{1,0:T(8,128)(2,1)S(1)} %get-tuple-element.79), channel_id=1, source_target_pairs={{0,5},{1,4},{2,7},{3,6},{4,1},{5,0},{6,3},{7,2},{8,13},{9,12},{10,... | collective-permute-start | bytes 393224 | tf_op jit(solution)/shard_map/ppermute | solution.py:313
  23.1 18.4 %collective-permute-start.12 = (bf16[128,512]{1,0:T(8,128)(2,1)S(1)}, bf16[128,512]{1,0:T(8,128)(2,1)S(1)}, u32[]{:S(2)}, u32[]{:S(2)}) collective-permute-start(bf16[128,512]{1,0:T(8,128)(2,1)S(1)} %get-tuple-element.81), channel_id=1, source_target_pairs={{0,3},{1,2},{2,1},{3,0},{4,7},{5,6},{6,5},{7,4},{8,11},{9,10},{10,... | collective-permute-start | bytes 393224 | tf_op jit(solution)/shard_map/ppermute | solution.py:313
  24.6 1.0 %copy-start.1 = (bf16[1024,172]{0,1:T(8,128)(2,1)S(1)}, bf16[1024,172]{0,1:T(8,128)(2,1)}, u32[]{:S(2)}) copy-start(bf16[1024,172]{0,1:T(8,128)(2,1)} %param.20) | copy-start | bytes 1056772
  25.6 0.9 %copy-start.2 = (bf16[128,1024]{1,0:T(8,128)(2,1)S(1)}, bf16[128,1024]{1,0:T(8,128)(2,1)}, u32[]{:S(2)}) copy-start(bf16[128,1024]{1,0:T(8,128)(2,1)} %w_in.1) | copy-start | bytes 786436
  31.0 10.6 %collective-permute-start.13 = (bf16[128,512]{1,0:T(8,128)(2,1)S(1)}, bf16[128,512]{1,0:T(8,128)(2,1)S(1)}, u32[]{:S(2)}, u32[]{:S(2)}) collective-permute-start(bf16[128,512]{1,0:T(8,128)(2,1)S(1)} %get-tuple-element.82), channel_id=1, source_target_pairs={{0,1},{1,0},{2,3},{3,2},{4,5},{5,4},{6,7},{7,6},{8,9},{9,8},{10,11... | collective-permute-start | bytes 393224 | tf_op jit(solution)/shard_map/ppermute | solution.py:313
  31.1 10.5 %collective-permute-start.11 = (bf16[128,512]{1,0:T(8,128)(2,1)S(1)}, bf16[128,512]{1,0:T(8,128)(2,1)S(1)}, u32[]{:S(2)}, u32[]{:S(2)}) collective-permute-start(bf16[128,512]{1,0:T(8,128)(2,1)S(1)} %get-tuple-element.80), channel_id=1, source_target_pairs={{0,7},{1,6},{2,5},{3,4},{4,3},{5,2},{6,1},{7,0},{8,15},{9,14},{10,... | collective-permute-start | bytes 393224 | tf_op jit(solution)/shard_map/ppermute | solution.py:313
  49.9 2.1 %collective-permute-start.14 = (f32[4,312,128]{2,1,0:T(8,128)S(1)}, f32[4,312,128]{2,1,0:T(8,128)S(1)}, u32[]{:S(2)}, u32[]{:S(2)}) collective-permute-start(f32[4,312,128]{2,1,0:T(8,128)S(1)} %get-tuple-element.89), channel_id=1, source_target_pairs={{0,1},{1,0},{2,3},{3,2},{4,5},{5,4},{6,7},{7,6},{8,9},{9,8},{10,11... | collective-permute-start | bytes 1916936 | tf_op jit(solution)/shard_map/ppermute | solution.py:313
  52.2 4.6 %collective-permute-start.15 = (s16[320,128]{1,0:T(8,128)(2,1)S(1)}, s16[320,128]{1,0:T(8,128)(2,1)S(1)}, u32[]{:S(2)}, u32[]{:S(2)}) collective-permute-start(s16[320,128]{1,0:T(8,128)(2,1)S(1)} %get-tuple-element.91), channel_id=1, source_target_pairs={{0,8},{8,0},{16,24},{24,16},{1,9},{9,1},{17,25},{25,17},{2,10},{10... | collective-permute-start | bytes 245768 | tf_op jit(solution)/shard_map/ppermute | solution.py:313
  53.7 5.3 %collective-permute-start.16 = (s16[320,128]{1,0:T(8,128)(2,1)S(1)}, s16[320,128]{1,0:T(8,128)(2,1)S(1)}, u32[]{:S(2)}, u32[]{:S(2)}) collective-permute-start(s16[320,128]{1,0:T(8,128)(2,1)S(1)} %get-tuple-element.92), channel_id=1, source_target_pairs={{0,16},{8,24},{16,0},{24,8},{1,17},{9,25},{17,1},{25,9},{2,18},{10... | collective-permute-start | bytes 245768 | tf_op jit(solution)/shard_map/ppermute | solution.py:313
  55.2 5.3 %collective-permute-start.17 = (s16[320,128]{1,0:T(8,128)(2,1)S(1)}, s16[320,128]{1,0:T(8,128)(2,1)S(1)}, u32[]{:S(2)}, u32[]{:S(2)}) collective-permute-start(s16[320,128]{1,0:T(8,128)(2,1)S(1)} %get-tuple-element.93), channel_id=1, source_target_pairs={{0,24},{8,16},{16,8},{24,0},{1,25},{9,17},{17,9},{25,1},{2,26},{10... | collective-permute-start | bytes 245768 | tf_op jit(solution)/shard_map/ppermute | solution.py:313
  60.7 7.6 %collective-permute-start.18 = (s16[320,128]{1,0:T(8,128)(2,1)S(1)}, s16[320,128]{1,0:T(8,128)(2,1)S(1)}, u32[]{:S(2)}, u32[]{:S(2)}) collective-permute-start(s16[320,128]{1,0:T(8,128)(2,1)S(1)} %get-tuple-element.94), channel_id=1, source_target_pairs={{0,4},{1,5},{2,6},{3,7},{4,0},{5,1},{6,2},{7,3},{8,12},{9,13},{10,... | collective-permute-start | bytes 245768 | tf_op jit(solution)/shard_map/ppermute | solution.py:313
  64.0 6.4 %collective-permute-start.19 = (s16[320,128]{1,0:T(8,128)(2,1)S(1)}, s16[320,128]{1,0:T(8,128)(2,1)S(1)}, u32[]{:S(2)}, u32[]{:S(2)}) collective-permute-start(s16[320,128]{1,0:T(8,128)(2,1)S(1)} %get-tuple-element.95), channel_id=1, source_target_pairs={{0,6},{1,7},{2,4},{3,5},{4,2},{5,3},{6,0},{7,1},{8,14},{9,15},{10,... | collective-permute-start | bytes 245768 | tf_op jit(solution)/shard_map/ppermute | solution.py:313
  66.5 4.7 %collective-permute-start.20 = (s16[320,128]{1,0:T(8,128)(2,1)S(1)}, s16[320,128]{1,0:T(8,128)(2,1)S(1)}, u32[]{:S(2)}, u32[]{:S(2)}) collective-permute-start(s16[320,128]{1,0:T(8,128)(2,1)S(1)} %get-tuple-element.96), channel_id=1, source_target_pairs={{0,2},{1,3},{2,0},{3,1},{4,6},{5,7},{6,4},{7,5},{8,10},{9,11},{10,... | collective-permute-start | bytes 245768 | tf_op jit(solution)/shard_map/ppermute | solution.py:313
  71.4 4.5 %collective-permute-start.21 = (s16[320,128]{1,0:T(8,128)(2,1)S(1)}, s16[320,128]{1,0:T(8,128)(2,1)S(1)}, u32[]{:S(2)}, u32[]{:S(2)}) collective-permute-start(s16[320,128]{1,0:T(8,128)(2,1)S(1)} %get-tuple-element.99), channel_id=1, source_target_pairs={{0,8},{8,0},{16,24},{24,16},{1,9},{9,1},{17,25},{25,17},{2,10},{10... | collective-permute-start | bytes 245768 | tf_op jit(solution)/shard_map/ppermute | solution.py:313
  72.3 4.4 %collective-permute-start.22 = (s16[320,128]{1,0:T(8,128)(2,1)S(1)}, s16[320,128]{1,0:T(8,128)(2,1)S(1)}, u32[]{:S(2)}, u32[]{:S(2)}) collective-permute-start(s16[320,128]{1,0:T(8,128)(2,1)S(1)} %get-tuple-element.100), channel_id=1, source_target_pairs={{0,16},{8,24},{16,0},{24,8},{1,17},{9,25},{17,1},{25,9},{2,18},{10... | collective-permute-start | bytes 245768 | tf_op jit(solution)/shard_map/ppermute | solution.py:313
  73.1 5.3 %collective-permute-start.23 = (s16[320,128]{1,0:T(8,128)(2,1)S(1)}, s16[320,128]{1,0:T(8,128)(2,1)S(1)}, u32[]{:S(2)}, u32[]{:S(2)}) collective-permute-start(s16[320,128]{1,0:T(8,128)(2,1)S(1)} %get-tuple-element.101), channel_id=1, source_target_pairs={{0,24},{8,16},{16,8},{24,0},{1,25},{9,17},{17,9},{25,1},{2,26},{10... | collective-permute-start | bytes 245768 | tf_op jit(solution)/shard_map/ppermute | solution.py:313
  75.0 3.5 %collective-permute-start.24 = (s16[320,128]{1,0:T(8,128)(2,1)S(1)}, s16[320,128]{1,0:T(8,128)(2,1)S(1)}, u32[]{:S(2)}, u32[]{:S(2)}) collective-permute-start(s16[320,128]{1,0:T(8,128)(2,1)S(1)} %get-tuple-element.98.refs_0_), channel_id=1, source_target_pairs={{0,1},{1,0},{2,3},{3,2},{4,5},{5,4},{6,7},{7,6},{8,9},{9,8},{10,11... | collective-permute-start | bytes 245768 | tf_op jit(solution)/shard_map/ppermute | solution.py:313
  75.9 2.6 %collective-permute-start.25 = (s16[320,128]{1,0:T(8,128)(2,1)S(1)}, s16[320,128]{1,0:T(8,128)(2,1)S(1)}, u32[]{:S(2)}, u32[]{:S(2)}) collective-permute-start(s16[320,128]{1,0:T(8,128)(2,1)S(1)} %collective-permute-done.21.refs_1_), channel_id=1, source_target_pairs={{0,1},{1,0},{2,3},{3,2},{4,5},{5,4},{6,7},{7,6},{8,9},{9,8},{10,11... | collective-permute-start | bytes 245768 | tf_op jit(solution)/shard_map/ppermute | solution.py:313
  76.7 1.7 %collective-permute-start.26 = (s16[320,128]{1,0:T(8,128)(2,1)S(1)}, s16[320,128]{1,0:T(8,128)(2,1)S(1)}, u32[]{:S(2)}, u32[]{:S(2)}) collective-permute-start(s16[320,128]{1,0:T(8,128)(2,1)S(1)} %collective-permute-done.22.refs_2_), channel_id=1, source_target_pairs={{0,1},{1,0},{2,3},{3,2},{4,5},{5,4},{6,7},{7,6},{8,9},{9,8},{10,11... | collective-permute-start | bytes 245768 | tf_op jit(solution)/shard_map/ppermute | solution.py:313
  78.5 1.3 %collective-permute-start.27 = (s16[320,128]{1,0:T(8,128)(2,1)S(1)}, s16[320,128]{1,0:T(8,128)(2,1)S(1)}, u32[]{:S(2)}, u32[]{:S(2)}) collective-permute-start(s16[320,128]{1,0:T(8,128)(2,1)S(1)} %collective-permute-done.23.refs_3_), channel_id=1, source_target_pairs={{0,1},{1,0},{2,3},{3,2},{4,5},{5,4},{6,7},{7,6},{8,9},{9,8},{10,11... | collective-permute-start | bytes 245768 | tf_op jit(solution)/shard_map/ppermute | solution.py:313
  (6 other events, 4.1 us)

commit v6 on v5

--- a/solution.py
+++ b/solution.py
@@ -40,18 +40,11 @@
     return [k for odd in (0, 1) for top in tops for k in range(top, 2 * top) if k % 2 == odd]
 
 
-def select_kernel(info, feats, masks, *refs):
-    msgs = refs[:-2]
-    refs[-2][...] = feats[...]
-    refs[-1][...] = masks[...]
-    tile = feats.shape[1]
-    samples = masks.shape[0]
+def select_kernel(info, tiles, *refs):
+    msgs = refs[:-1]
+    refs[-1][...] = tiles[...]
     for i, k in enumerate(partners(len(msgs) + 1)):
-        t = info[3 + (info[0] ^ k)]
-        out = msgs[i]
-        out[:tile, :] = feats[t]
-        m = masks[:, pl.ds(pl.multiple_of(t * tile, tile), tile)]
-        out[tile:, :] = jnp.concatenate([m, jnp.zeros((out.shape[0] - tile - samples, tile), BF16)], 0)
+        msgs[i][...] = tiles[info[3 + (info[0] ^ k)]]
 
 
 def masked_tile(f, m, put):
@@ -62,16 +55,17 @@
         put(s, (f * cols[:, s : s + 1]).astype(BF16))
 
 
-def layout_kernel(feats, masks, adj, slots, lhs, own, same_slots):
+def layout_kernel(samples, both, adj, slots, lhs, own, same_slots):
     same_slots[...] = slots[...]
-    tiles, tile, feat = feats.shape
+    tiles, tile, lanes = own.shape
+    feat = lanes // samples
     for t in range(tiles):
         lhs[t] = jnp.concatenate([adj[t, j] for j in range(adj.shape[1])], 1)
 
         def put(s, x):
             own[t, :, s * feat : (s + 1) * feat] = x
 
-        masked_tile(feats[t], masks[:, t * tile : (t + 1) * tile], put)
+        masked_tile(both[t, :tile, :], both[t, tile : tile + samples, :], put)
 
 
 def pool_index(info, slots, r, j, dom, nnz):
@@ -295,9 +289,9 @@
     half = len(pieces) // 2
     body = pieces[0].shape[0] - 2 * TAIL
     for c in range(2):
-        for m in range(half):
+        for i, m in enumerate((0,) + (3, 1, 2)):
             at = (info[2] ^ c) * half + (info[1] ^ m)
-            x = decode(pieces[c * half + m], feat, n_tail)
+            x = decode(pieces[c * half + i], feat, n_tail)
             where = pl.ds(pl.multiple_of(at * lanes, lanes), lanes)
             g_in[:, where] = x[:feat]
             g_out[:, where] = x[feat : feat + classes]
@@ -305,8 +299,8 @@
 
             @pl.when(at == 0)
             def _():
-                for i in range(n_tail - 1):
-                    b_out[:, i * lanes : (i + 1) * lanes] = x[body + 1 + i : body + 2 + i]
+                for j in range(n_tail - 1):
+                    b_out[:, j * lanes : (j + 1) * lanes] = x[body + 1 + j : body + 2 + j]
 
 
 def xor_permute(x, axis, mask):
@@ -337,10 +331,10 @@
     groups = [("dom", masks) for masks in bit_groups("dom", 1)] + [("dp", masks) for masks in bit_groups("dp", 2)]
     qs = call(functools.partial(scatter_kernel, feat, n_tail, 4), [coded] * 4, [own] + msgs)
     for axis, masks in groups:
-        order = [m for m in (1, 2, 0) if m < len(masks)]
+        order = [m for m in (1, 0, 2) if m < len(masks)]
         got = [xor_permute(qs[i + 1], axis, masks[m]) for i, m in enumerate(order)]
         qs = call(functools.partial(tree_kernel, feat, n_tail, order), [coded] * 4, got + [qs[0]])
-    pieces = [qs[0]] + [xor_permute(qs[m], "dp", m) for m in range(1, count)]
+    pieces = [qs[0]] + [xor_permute(qs[i + 1], "dp", m) for i, m in enumerate((3, 1, 2))]
     pieces = pieces + [xor_permute(x, "dom", 1) for x in pieces]
     return call(
         functools.partial(unpack_kernel, feat, n_tail, classes),
@@ -378,16 +372,15 @@
     lanes = samples * feat
     wide = -(-classes // 128) * 128
 
-    *msgs, feats, masks = call(
-        select_kernel,
-        [like((tile + 16, feat), BF16)] * (dom - 1) + [like(feats.shape, BF16), like(masks.shape, BF16)],
-        [info, feats, masks],
-        n_smem=1,
+    rows = jnp.pad(masks.reshape(samples, tiles, tile).transpose(1, 0, 2), ((0, 0), (0, 16 - samples), (0, 0)))
+    both = jnp.concatenate([feats, rows], 1)
+    *msgs, both = call(
+        select_kernel, [like((tile + 16, feat), BF16)] * (dom - 1) + [like(both.shape, BF16)], [info, both], n_smem=1
     )
     lhs, own, slots = call(
-        layout_kernel,
+        functools.partial(layout_kernel, samples),
         [like((tiles, tile, nnz * tile), BF16), like((tiles, tile, lanes), BF16), like((tiles, nnz), I32)],
-        [feats, masks, adj, col_slot[0]],
+        [both, adj, col_slot[0]],
     )
     msgs = swap_all(msgs)
     cur, total, *outs = call(

time: 81.8 us -> 80.6 us (0.985)
  local copies, waits for them, and re-layouts: 7.97 us -> 6.38 us
  waiting for transfers between devices: 24.2 us -> 23.2 us
  other arithmetic: 0.73 us -> 1.67 us
    unnamed x20 -> x16, local copies, waits for them, and re-layouts: 7.97 us -> 6.38 us
    ppermute x28, waiting for transfers between devices: 24.2 us -> 23.2 us  [xor_permute(): lax.ppermute(x, axis, [(i, i ^ mask) for i in range(lax.axis_size(axis))])]
    concatenate x0 -> x1, other arithmetic: none -> 0.93 us  [per_device(): both = jnp.concatenate([feats, rows], 1)]
  transfers between devices with their start and end apart: 28 -> 28, of which waited for: 16 -> 16; matrix products, arithmetic and copies ran while one was open for 0% -> 0% of each run, Pallas kernels for 2% -> 3%
where the time goes in v6:
time: 80.6 us; the launch traced here: 80.2 us
  starting transfers between devices  33.6 us (42%)
  waiting for transfers between devices  23.2 us (29%)
  Pallas kernels  14.6 us (18%)
  local copies, waits for them, and re-layouts  6.38 us (8%)
  other arithmetic  1.67 us (2%)
    ppermute x28, starting transfers between devices, xor_permute(): lax.ppermute(x, axis, [(i, i ^ mask) for i in range(lax.axis_size(axis))])  33.6 us
    ppermute x28, waiting for transfers between devices, xor_permute(): lax.ppermute(x, axis, [(i, i ^ mask) for i in range(lax.axis_size(axis))])  23.2 us
    pallas_call x10, Pallas kernels, call(): pl.pallas_call(kernel, out_shape=outs, in_specs=[SMEM] * n_smem + [VMEM]...  14.6 us
    unnamed x16, local copies, waits for them, and re-layouts  6.38 us
  transfers between devices with their start and end apart: 28, of which 16 were waited for; matrix products, arithmetic and copies ran while one was open for 0% of the time, Pallas kernels for 3%

profile of v6, /device:TPU:0, one launch (start us, length us, event | category | flops | bytes accessed | tf_op | source)
XLA Modules:
  0.0 80.2 jit_solution(12749135659973293666)
XLA Ops:
  0.6 0.9 %fusion.1.tiles = bf16[4,144,128]{2,1,0:T(8,128)(2,1)S(1)} fusion(bf16[4,4,128]{2,1,0:T(4,128)(2,1)} %bitcast.27, bf16[4,128,128]{2,1,0:T(8,128)(2,1)} %bitcast.26), kind=kLoop, calls=%fused_computation.2 | loop fusion | flops 442368 | bytes 282624 | tf_op jit(solution)/shard_map/concatenate | solution.py:376
  2.9 4.1 %collective-permute-start = (bf16[144,128]{1,0:T(8,128)(2,1)S(1)}, bf16[144,128]{1,0:T(8,128)(2,1)S(1)}, u32[]{:S(2)}, u32[]{:S(2)}) collective-permute-start(bf16[144,128]{1,0:T(8,128)(2,1)S(1)} %get-tuple-element.58), channel_id=1, source_target_pairs={{0,4},{1,5},{2,6},{3,7},{4,0},{5,1},{6,2},{7,3},{8,12},{9,13},{10,... | collective-permute-start | bytes 110600 | tf_op jit(solution)/shard_map/ppermute | solution.py:307
  7.0 1.3 %collective-permute-start.1 = (bf16[144,128]{1,0:T(8,128)(2,1)S(1)}, bf16[144,128]{1,0:T(8,128)(2,1)S(1)}, u32[]{:S(2)}, u32[]{:S(2)}) collective-permute-start(bf16[144,128]{1,0:T(8,128)(2,1)S(1)} %get-tuple-element.59), channel_id=1, source_target_pairs={{0,6},{1,7},{2,4},{3,5},{4,2},{5,3},{6,0},{7,1},{8,14},{9,15},{10,... | collective-permute-start | bytes 110600 | tf_op jit(solution)/shard_map/ppermute | solution.py:307
  8.6 1.4 %collective-permute-start.3 = (bf16[144,128]{1,0:T(8,128)(2,1)S(1)}, bf16[144,128]{1,0:T(8,128)(2,1)S(1)}, u32[]{:S(2)}, u32[]{:S(2)}) collective-permute-start(bf16[144,128]{1,0:T(8,128)(2,1)S(1)} %get-tuple-element.61), channel_id=1, source_target_pairs={{0,5},{1,4},{2,7},{3,6},{4,1},{5,0},{6,3},{7,2},{8,13},{9,12},{10,... | collective-permute-start | bytes 110600 | tf_op jit(solution)/shard_map/ppermute | solution.py:307
  10.0 2.5 %collective-permute-start.4 = (bf16[144,128]{1,0:T(8,128)(2,1)S(1)}, bf16[144,128]{1,0:T(8,128)(2,1)S(1)}, u32[]{:S(2)}, u32[]{:S(2)}) collective-permute-start(bf16[144,128]{1,0:T(8,128)(2,1)S(1)} %get-tuple-element.62), channel_id=1, source_target_pairs={{0,7},{1,6},{2,5},{3,4},{4,3},{5,2},{6,1},{7,0},{8,15},{9,14},{10,... | collective-permute-start | bytes 110600 | tf_op jit(solution)/shard_map/ppermute | solution.py:307
  12.8 1.0 %copy-done = bf16[1,4,4,128,128]{4,3,2,1,0:T(8,128)(2,1)S(1)} copy-done((bf16[1,4,4,128,128]{4,3,2,1,0:T(8,128)(2,1)S(1)}, bf16[1,4,4,128,128]{4,3,2,1,0:T(8,128)(2,1)}, u32[]{:S(2)}) %copy-start) | copy-done | bytes 524312
  16.0 1.5 %shard_map.140 = (bf16[4,128,512]{2,1,0:T(8,128)(2,1)S(1)}, f32[4,128,512]{2,1,0:T(8,128)S(1)}, bf16[128,512]{1,0:T(8,128)(2,1)S(1)}, bf16[128,512]{1,0:T(8,128)...) custom-call(s32[11]{0:T(128)S(1)} %pad_add_fusion.info, ...), custom_call_target="tpu_custom_call" | custom-call | tf_op jit(solution)/shard_map/pallas_call | solution.py:24
  17.5 1.8 %collective-permute-start.7 = (bf16[128,512]{1,0:T(8,128)(2,1)S(1)}, bf16[128,512]{1,0:T(8,128)(2,1)S(1)}, u32[]{:S(2)}, u32[]{:S(2)}) collective-permute-start(bf16[128,512]{1,0:T(8,128)(2,1)S(1)} %get-tuple-element.74), channel_id=1, source_target_pairs={{0,4},{1,5},{2,6},{3,7},{4,0},{5,1},{6,2},{7,3},{8,12},{9,13},{10,... | collective-permute-start | bytes 393224 | tf_op jit(solution)/shard_map/ppermute | solution.py:307
  19.3 1.3 %collective-permute-start.8 = (bf16[128,512]{1,0:T(8,128)(2,1)S(1)}, bf16[128,512]{1,0:T(8,128)(2,1)S(1)}, u32[]{:S(2)}, u32[]{:S(2)}) collective-permute-start(bf16[128,512]{1,0:T(8,128)(2,1)S(1)} %get-tuple-element.75), channel_id=1, source_target_pairs={{0,6},{1,7},{2,4},{3,5},{4,2},{5,3},{6,0},{7,1},{8,14},{9,15},{10,... | collective-permute-start | bytes 393224 | tf_op jit(solution)/shard_map/ppermute | solution.py:307
  21.1 1.4 %collective-permute-start.10 = (bf16[128,512]{1,0:T(8,128)(2,1)S(1)}, bf16[128,512]{1,0:T(8,128)(2,1)S(1)}, u32[]{:S(2)}, u32[]{:S(2)}) collective-permute-start(bf16[128,512]{1,0:T(8,128)(2,1)S(1)} %get-tuple-element.77), channel_id=1, source_target_pairs={{0,5},{1,4},{2,7},{3,6},{4,1},{5,0},{6,3},{7,2},{8,13},{9,12},{10,... | collective-permute-start | bytes 393224 | tf_op jit(solution)/shard_map/ppermute | solution.py:307
  22.5 1.5 %collective-permute-start.12 = (bf16[128,512]{1,0:T(8,128)(2,1)S(1)}, bf16[128,512]{1,0:T(8,128)(2,1)S(1)}, u32[]{:S(2)}, u32[]{:S(2)}) collective-permute-start(bf16[128,512]{1,0:T(8,128)(2,1)S(1)} %get-tuple-element.79), channel_id=1, source_target_pairs={{0,3},{1,2},{2,1},{3,0},{4,7},{5,6},{6,5},{7,4},{8,11},{9,10},{10,... | collective-permute-start | bytes 393224 | tf_op jit(solution)/shard_map/ppermute | solution.py:307
  24.0 1.0 %copy-done.1 = bf16[1024,172]{0,1:T(8,128)(2,1)S(1)} copy-done((bf16[1024,172]{0,1:T(8,128)(2,1)S(1)}, bf16[1024,172]{0,1:T(8,128)(2,1)}, u32[]{:S(2)}) %copy-start.1) | copy-done | bytes 352280
  25.0 0.9 %copy-done.2 = bf16[128,1024]{1,0:T(8,128)(2,1)S(1)} copy-done((bf16[128,1024]{1,0:T(8,128)(2,1)S(1)}, bf16[128,1024]{1,0:T(8,128)(2,1)}, u32[]{:S(2)}) %copy-start.2) | copy-done | bytes 262168
  28.9 1.5 %collective-permute-done.7.refs_0_ = bf16[128,512]{1,0:T(8,128)(2,1)S(1)} collective-permute-done((bf16[128,512]{1,0:T(8,128)(2,1)S(1)}, bf16[128,512]{1,0:T(8,128)(2,1)S(1)}, u32[]{:S(2)}, u32[]{:S(2)}) %collective-permute-start.7) | collective-permute-done | bytes 131104 | tf_op jit(solution)/shard_map/ppermute | solution.py:307
  30.4 4.1 %collective-permute-start.11 = (bf16[128,512]{1,0:T(8,128)(2,1)S(1)}, bf16[128,512]{1,0:T(8,128)(2,1)S(1)}, u32[]{:S(2)}, u32[]{:S(2)}) collective-permute-start(bf16[128,512]{1,0:T(8,128)(2,1)S(1)} %get-tuple-element.78), channel_id=1, source_target_pairs={{0,7},{1,6},{2,5},{3,4},{4,3},{5,2},{6,1},{7,0},{8,15},{9,14},{10,... | collective-permute-start | bytes 393224 | tf_op jit(solution)/shard_map/ppermute | solution.py:307
  34.5 6.4 %collective-permute-done.10.refs_3_ = bf16[128,512]{1,0:T(8,128)(2,1)S(1)} collective-permute-done((bf16[128,512]{1,0:T(8,128)(2,1)S(1)}, bf16[128,512]{1,0:T(8,128)(2,1)S(1)}, u32[]{:S(2)}, u32[]{:S(2)}) %collective-permute-start.10) | collective-permute-done | bytes 131104 | tf_op jit(solution)/shard_map/ppermute | solution.py:307
  41.0 8.2 %shard_map.142 = (f32[4,312,128]{2,1,0:T(8,128)S(1)}, bf16[128,2048]{1,0:T(8,128)(2,1)S(1)}, bf16[2048,1024]{1,0:T(8,128)(2,1)S(1)}, bf16[176,2048]{1,0:T(8,128)...) custom-call(s32[11]{0:T(128)S(1)} %pad_add_fusion.info, ...), custom_call_target="tpu_custom_call" | custom-call | tf_op jit(solution)/shard_map/pallas_call | solution.py:24
  49.4 1.5 %shard_map.143.keep = f32[4,312,128]{2,1,0:T(8,128)S(1)} custom-call(s32[11]{0:T(128)S(1)} %pad_add_fusion.info, bf16[128,2048]{1,0:T(8,128)(2,1)S(1)} %get-tuple-element.81.x_t, bf16[2048,1024]{1,0:T(8,128)(2,1)S(1)} %get-tuple-element.82.act, bf16[176,2048]{1,0:T(8,128)(2,1)S(1)} %get-tuple-element.83.dl_t, bf16[2048,1024]{1,0:T(8,128)(2,1)S(1)} %get-tuple-element.84.dpre, ...), custom_call_target="tpu_custom_call" | custom-call | tf_op jit(solution)/shard_map/pallas_call | solution.py:24
  51.5 1.6 %collective-permute-start.15 = (s16[320,128]{1,0:T(8,128)(2,1)S(1)}, s16[320,128]{1,0:T(8,128)(2,1)S(1)}, u32[]{:S(2)}, u32[]{:S(2)}) collective-permute-start(s16[320,128]{1,0:T(8,128)(2,1)S(1)} %get-tuple-element.89), channel_id=1, source_target_pairs={{0,8},{8,0},{16,24},{24,16},{1,9},{9,1},{17,25},{25,17},{2,10},{10... | collective-permute-start | bytes 245768 | tf_op jit(solution)/shard_map/ppermute | solution.py:307
  53.1 1.5 %collective-permute-start.16 = (s16[320,128]{1,0:T(8,128)(2,1)S(1)}, s16[320,128]{1,0:T(8,128)(2,1)S(1)}, u32[]{:S(2)}, u32[]{:S(2)}) collective-permute-start(s16[320,128]{1,0:T(8,128)(2,1)S(1)} %get-tuple-element.90), channel_id=1, source_target_pairs={{0,16},{8,24},{16,0},{24,8},{1,17},{9,25},{17,1},{25,9},{2,18},{10... | collective-permute-start | bytes 245768 | tf_op jit(solution)/shard_map/ppermute | solution.py:307
  55.1 1.0 %collective-permute-done.15.refs_0_ = s16[320,128]{1,0:T(8,128)(2,1)S(1)} collective-permute-done((s16[320,128]{1,0:T(8,128)(2,1)S(1)}, s16[320,128]{1,0:T(8,128)(2,1)S(1)}, u32[]{:S(2)}, u32[]{:S(2)}) %collective-permute-start.15) | collective-permute-done | bytes 81952 | tf_op jit(solution)/shard_map/ppermute | solution.py:307
  56.1 2.3 %collective-permute-done.16.refs_1_ = s16[320,128]{1,0:T(8,128)(2,1)S(1)} collective-permute-done((s16[320,128]{1,0:T(8,128)(2,1)S(1)}, s16[320,128]{1,0:T(8,128)(2,1)S(1)}, u32[]{:S(2)}, u32[]{:S(2)}) %collective-permute-start.16) | collective-permute-done | bytes 81952 | tf_op jit(solution)/shard_map/ppermute | solution.py:307
  58.3 1.6 %collective-permute-done.17.refs_2_ = s16[320,128]{1,0:T(8,128)(2,1)S(1)} collective-permute-done((s16[320,128]{1,0:T(8,128)(2,1)S(1)}, s16[320,128]{1,0:T(8,128)(2,1)S(1)}, u32[]{:S(2)}, u32[]{:S(2)}) %collective-permute-start.17) | collective-permute-done | bytes 81952 | tf_op jit(solution)/shard_map/ppermute | solution.py:307
  60.1 3.3 %collective-permute-start.18 = (s16[320,128]{1,0:T(8,128)(2,1)S(1)}, s16[320,128]{1,0:T(8,128)(2,1)S(1)}, u32[]{:S(2)}, u32[]{:S(2)}) collective-permute-start(s16[320,128]{1,0:T(8,128)(2,1)S(1)} %get-tuple-element.92), channel_id=1, source_target_pairs={{0,4},{1,5},{2,6},{3,7},{4,0},{5,1},{6,2},{7,3},{8,12},{9,13},{10,... | collective-permute-start | bytes 245768 | tf_op jit(solution)/shard_map/ppermute | solution.py:307
  63.6 2.3 %collective-permute-start.20 = (s16[320,128]{1,0:T(8,128)(2,1)S(1)}, s16[320,128]{1,0:T(8,128)(2,1)S(1)}, u32[]{:S(2)}, u32[]{:S(2)}) collective-permute-start(s16[320,128]{1,0:T(8,128)(2,1)S(1)} %get-tuple-element.94), channel_id=1, source_target_pairs={{0,6},{1,7},{2,4},{3,5},{4,2},{5,3},{6,0},{7,1},{8,14},{9,15},{10,... | collective-permute-start | bytes 245768 | tf_op jit(solution)/shard_map/ppermute | solution.py:307
  65.9 3.3 %collective-permute-done.18.refs_0_ = s16[320,128]{1,0:T(8,128)(2,1)S(1)} collective-permute-done((s16[320,128]{1,0:T(8,128)(2,1)S(1)}, s16[320,128]{1,0:T(8,128)(2,1)S(1)}, u32[]{:S(2)}, u32[]{:S(2)}) %collective-permute-start.18) | collective-permute-done | bytes 81952 | tf_op jit(solution)/shard_map/ppermute | solution.py:307
  69.2 1.1 %collective-permute-done.20.refs_2_ = s16[320,128]{1,0:T(8,128)(2,1)S(1)} collective-permute-done((s16[320,128]{1,0:T(8,128)(2,1)S(1)}, s16[320,128]{1,0:T(8,128)(2,1)S(1)}, u32[]{:S(2)}, u32[]{:S(2)}) %collective-permute-start.20) | collective-permute-done | bytes 81952 | tf_op jit(solution)/shard_map/ppermute | solution.py:307
  71.3 1.4 %collective-permute-start.22 = (s16[320,128]{1,0:T(8,128)(2,1)S(1)}, s16[320,128]{1,0:T(8,128)(2,1)S(1)}, u32[]{:S(2)}, u32[]{:S(2)}) collective-permute-start(s16[320,128]{1,0:T(8,128)(2,1)S(1)} %get-tuple-element.98), channel_id=1, source_target_pairs={{0,8},{8,0},{16,24},{24,16},{1,9},{9,1},{17,25},{25,17},{2,10},{10... | collective-permute-start | bytes 245768 | tf_op jit(solution)/shard_map/ppermute | solution.py:307
  72.7 1.3 %collective-permute-start.23 = (s16[320,128]{1,0:T(8,128)(2,1)S(1)}, s16[320,128]{1,0:T(8,128)(2,1)S(1)}, u32[]{:S(2)}, u32[]{:S(2)}) collective-permute-start(s16[320,128]{1,0:T(8,128)(2,1)S(1)} %get-tuple-element.99), channel_id=1, source_target_pairs={{0,16},{8,24},{16,0},{24,8},{1,17},{9,25},{17,1},{25,9},{2,18},{10... | collective-permute-start | bytes 245768 | tf_op jit(solution)/shard_map/ppermute | solution.py:307
  74.0 1.8 %collective-permute-done.21.refs_1_ = s16[320,128]{1,0:T(8,128)(2,1)S(1)} collective-permute-done((s16[320,128]{1,0:T(8,128)(2,1)S(1)}, s16[320,128]{1,0:T(8,128)(2,1)S(1)}, u32[]{:S(2)}, u32[]{:S(2)}) %collective-permute-start.21) | collective-permute-done | bytes 81952 | tf_op jit(solution)/shard_map/ppermute | solution.py:307
  77.3 1.1 %collective-permute-done.27.refs_7_ = s16[320,128]{1,0:T(8,128)(2,1)S(1)} collective-permute-done((s16[320,128]{1,0:T(8,128)(2,1)S(1)}, s16[320,128]{1,0:T(8,128)(2,1)S(1)}, u32[]{:S(2)}, u32[]{:S(2)}) %collective-permute-start.27) | collective-permute-done | bytes 81952 | tf_op jit(solution)/shard_map/ppermute | solution.py:307
  78.4 1.8 %shard_map.147 = (f32[128,1024]{1,0:T(8,128)}, f32[1,1024]{1,0:T(1,128)}, f32[172,1024]{1,0:T(8,128)}, f32[1,256]{1,0:T(1,128)}) custom-call(s32[11]{0:T(128)S(1)} %pad_add_fusion.info, s16[320,128]{1,0:T(8,128)(2,1)S(1)} %get-tuple-element.96.refs_0_, s16[320,128]{1,0:T(8,128)(2,1)S(1)} %collective-permute-done.21.refs_1_, ...), custom_call_target="tpu_custom_call" | custom-call | tf_op jit(solution)/shard_map/pallas_call | solution.py:24
  (52 shorter events, 11.5 us)
Async XLA Ops:
  2.9 9.6 %collective-permute-start = (bf16[144,128]{1,0:T(8,128)(2,1)S(1)}, bf16[144,128]{1,0:T(8,128)(2,1)S(1)}, u32[]{:S(2)}, u32[]{:S(2)}) collective-permute-start(bf16[144,128]{1,0:T(8,128)(2,1)S(1)} %get-tuple-element.58), channel_id=1, source_target_pairs={{0,4},{1,5},{2,6},{3,7},{4,0},{5,1},{6,2},{7,3},{8,12},{9,13},{10,... | collective-permute-start | bytes 110600 | tf_op jit(solution)/shard_map/ppermute | solution.py:307
  7.0 5.8 %collective-permute-start.1 = (bf16[144,128]{1,0:T(8,128)(2,1)S(1)}, bf16[144,128]{1,0:T(8,128)(2,1)S(1)}, u32[]{:S(2)}, u32[]{:S(2)}) collective-permute-start(bf16[144,128]{1,0:T(8,128)(2,1)S(1)} %get-tuple-element.59), channel_id=1, source_target_pairs={{0,6},{1,7},{2,4},{3,5},{4,2},{5,3},{6,0},{7,1},{8,14},{9,15},{10,... | collective-permute-start | bytes 110600 | tf_op jit(solution)/shard_map/ppermute | solution.py:307
  8.3 6.5 %collective-permute-start.2 = (bf16[144,128]{1,0:T(8,128)(2,1)S(1)}, bf16[144,128]{1,0:T(8,128)(2,1)S(1)}, u32[]{:S(2)}, u32[]{:S(2)}) collective-permute-start(bf16[144,128]{1,0:T(8,128)(2,1)S(1)} %get-tuple-element.60), channel_id=1, source_target_pairs={{0,2},{1,3},{2,0},{3,1},{4,6},{5,7},{6,4},{7,5},{8,10},{9,11},{10,... | collective-permute-start | bytes 110600 | tf_op jit(solution)/shard_map/ppermute | solution.py:307
  8.6 6.3 %collective-permute-start.3 = (bf16[144,128]{1,0:T(8,128)(2,1)S(1)}, bf16[144,128]{1,0:T(8,128)(2,1)S(1)}, u32[]{:S(2)}, u32[]{:S(2)}) collective-permute-start(bf16[144,128]{1,0:T(8,128)(2,1)S(1)} %get-tuple-element.61), channel_id=1, source_target_pairs={{0,5},{1,4},{2,7},{3,6},{4,1},{5,0},{6,3},{7,2},{8,13},{9,12},{10,... | collective-permute-start | bytes 110600 | tf_op jit(solution)/shard_map/ppermute | solution.py:307
  10.0 5.2 %collective-permute-start.4 = (bf16[144,128]{1,0:T(8,128)(2,1)S(1)}, bf16[144,128]{1,0:T(8,128)(2,1)S(1)}, u32[]{:S(2)}, u32[]{:S(2)}) collective-permute-start(bf16[144,128]{1,0:T(8,128)(2,1)S(1)} %get-tuple-element.62), channel_id=1, source_target_pairs={{0,7},{1,6},{2,5},{3,4},{4,3},{5,2},{6,1},{7,0},{8,15},{9,14},{10,... | collective-permute-start | bytes 110600 | tf_op jit(solution)/shard_map/ppermute | solution.py:307
  12.4 3.5 %collective-permute-start.5 = (bf16[144,128]{1,0:T(8,128)(2,1)S(1)}, bf16[144,128]{1,0:T(8,128)(2,1)S(1)}, u32[]{:S(2)}, u32[]{:S(2)}) collective-permute-start(bf16[144,128]{1,0:T(8,128)(2,1)S(1)} %get-tuple-element.63), channel_id=1, source_target_pairs={{0,3},{1,2},{2,1},{3,0},{4,7},{5,6},{6,5},{7,4},{8,11},{9,10},{10,... | collective-permute-start | bytes 110600 | tf_op jit(solution)/shard_map/ppermute | solution.py:307
  12.8 3.2 %collective-permute-start.6 = (bf16[144,128]{1,0:T(8,128)(2,1)S(1)}, bf16[144,128]{1,0:T(8,128)(2,1)S(1)}, u32[]{:S(2)}, u32[]{:S(2)}) collective-permute-start(bf16[144,128]{1,0:T(8,128)(2,1)S(1)} %get-tuple-element.64), channel_id=1, source_target_pairs={{0,1},{1,0},{2,3},{3,2},{4,5},{5,4},{6,7},{7,6},{8,9},{9,8},{10,11... | collective-permute-start | bytes 110600 | tf_op jit(solution)/shard_map/ppermute | solution.py:307
  12.8 1.0 %copy-start = (bf16[1,4,4,128,128]{4,3,2,1,0:T(8,128)(2,1)S(1)}, bf16[1,4,4,128,128]{4,3,2,1,0:T(8,128)(2,1)}, u32[]{:S(2)}) copy-start(bf16[1,4,4,128,128]{4,3,2,1,0:T(8,128)(2,1)} %param.15) | copy-start | bytes 1572868
  17.5 12.9 %collective-permute-start.7 = (bf16[128,512]{1,0:T(8,128)(2,1)S(1)}, bf16[128,512]{1,0:T(8,128)(2,1)S(1)}, u32[]{:S(2)}, u32[]{:S(2)}) collective-permute-start(bf16[128,512]{1,0:T(8,128)(2,1)S(1)} %get-tuple-element.74), channel_id=1, source_target_pairs={{0,4},{1,5},{2,6},{3,7},{4,0},{5,1},{6,2},{7,3},{8,12},{9,13},{10,... | collective-permute-start | bytes 393224 | tf_op jit(solution)/shard_map/ppermute | solution.py:307
  19.3 11.1 %collective-permute-start.8 = (bf16[128,512]{1,0:T(8,128)(2,1)S(1)}, bf16[128,512]{1,0:T(8,128)(2,1)S(1)}, u32[]{:S(2)}, u32[]{:S(2)}) collective-permute-start(bf16[128,512]{1,0:T(8,128)(2,1)S(1)} %get-tuple-element.75), channel_id=1, source_target_pairs={{0,6},{1,7},{2,4},{3,5},{4,2},{5,3},{6,0},{7,1},{8,14},{9,15},{10,... | collective-permute-start | bytes 393224 | tf_op jit(solution)/shard_map/ppermute | solution.py:307
  20.7 13.8 %collective-permute-start.9 = (bf16[128,512]{1,0:T(8,128)(2,1)S(1)}, bf16[128,512]{1,0:T(8,128)(2,1)S(1)}, u32[]{:S(2)}, u32[]{:S(2)}) collective-permute-start(bf16[128,512]{1,0:T(8,128)(2,1)S(1)} %get-tuple-element.76), channel_id=1, source_target_pairs={{0,2},{1,3},{2,0},{3,1},{4,6},{5,7},{6,4},{7,5},{8,10},{9,11},{10,... | collective-permute-start | bytes 393224 | tf_op jit(solution)/shard_map/ppermute | solution.py:307
  21.1 19.9 %collective-permute-start.10 = (bf16[128,512]{1,0:T(8,128)(2,1)S(1)}, bf16[128,512]{1,0:T(8,128)(2,1)S(1)}, u32[]{:S(2)}, u32[]{:S(2)}) collective-permute-start(bf16[128,512]{1,0:T(8,128)(2,1)S(1)} %get-tuple-element.77), channel_id=1, source_target_pairs={{0,5},{1,4},{2,7},{3,6},{4,1},{5,0},{6,3},{7,2},{8,13},{9,12},{10,... | collective-permute-start | bytes 393224 | tf_op jit(solution)/shard_map/ppermute | solution.py:307
  22.5 18.4 %collective-permute-start.12 = (bf16[128,512]{1,0:T(8,128)(2,1)S(1)}, bf16[128,512]{1,0:T(8,128)(2,1)S(1)}, u32[]{:S(2)}, u32[]{:S(2)}) collective-permute-start(bf16[128,512]{1,0:T(8,128)(2,1)S(1)} %get-tuple-element.79), channel_id=1, source_target_pairs={{0,3},{1,2},{2,1},{3,0},{4,7},{5,6},{6,5},{7,4},{8,11},{9,10},{10,... | collective-permute-start | bytes 393224 | tf_op jit(solution)/shard_map/ppermute | solution.py:307
  24.0 1.0 %copy-start.1 = (bf16[1024,172]{0,1:T(8,128)(2,1)S(1)}, bf16[1024,172]{0,1:T(8,128)(2,1)}, u32[]{:S(2)}) copy-start(bf16[1024,172]{0,1:T(8,128)(2,1)} %param.20) | copy-start | bytes 1056772
  25.0 0.9 %copy-start.2 = (bf16[128,1024]{1,0:T(8,128)(2,1)S(1)}, bf16[128,1024]{1,0:T(8,128)(2,1)}, u32[]{:S(2)}) copy-start(bf16[128,1024]{1,0:T(8,128)(2,1)} %w_in.1) | copy-start | bytes 786436
  25.9 0.7 copy-start.3
  30.4 10.6 %collective-permute-start.13 = (bf16[128,512]{1,0:T(8,128)(2,1)S(1)}, bf16[128,512]{1,0:T(8,128)(2,1)S(1)}, u32[]{:S(2)}, u32[]{:S(2)}) collective-permute-start(bf16[128,512]{1,0:T(8,128)(2,1)S(1)} %get-tuple-element.80), channel_id=1, source_target_pairs={{0,1},{1,0},{2,3},{3,2},{4,5},{5,4},{6,7},{7,6},{8,9},{9,8},{10,11... | collective-permute-start | bytes 393224 | tf_op jit(solution)/shard_map/ppermute | solution.py:307
  30.4 10.5 %collective-permute-start.11 = (bf16[128,512]{1,0:T(8,128)(2,1)S(1)}, bf16[128,512]{1,0:T(8,128)(2,1)S(1)}, u32[]{:S(2)}, u32[]{:S(2)}) collective-permute-start(bf16[128,512]{1,0:T(8,128)(2,1)S(1)} %get-tuple-element.78), channel_id=1, source_target_pairs={{0,7},{1,6},{2,5},{3,4},{4,3},{5,2},{6,1},{7,0},{8,15},{9,14},{10,... | collective-permute-start | bytes 393224 | tf_op jit(solution)/shard_map/ppermute | solution.py:307
  49.2 2.1 %collective-permute-start.14 = (f32[4,312,128]{2,1,0:T(8,128)S(1)}, f32[4,312,128]{2,1,0:T(8,128)S(1)}, u32[]{:S(2)}, u32[]{:S(2)}) collective-permute-start(f32[4,312,128]{2,1,0:T(8,128)S(1)} %get-tuple-element.87), channel_id=1, source_target_pairs={{0,1},{1,0},{2,3},{3,2},{4,5},{5,4},{6,7},{7,6},{8,9},{9,8},{10,11... | collective-permute-start | bytes 1916936 | tf_op jit(solution)/shard_map/ppermute | solution.py:307
  51.5 4.6 %collective-permute-start.15 = (s16[320,128]{1,0:T(8,128)(2,1)S(1)}, s16[320,128]{1,0:T(8,128)(2,1)S(1)}, u32[]{:S(2)}, u32[]{:S(2)}) collective-permute-start(s16[320,128]{1,0:T(8,128)(2,1)S(1)} %get-tuple-element.89), channel_id=1, source_target_pairs={{0,8},{8,0},{16,24},{24,16},{1,9},{9,1},{17,25},{25,17},{2,10},{10... | collective-permute-start | bytes 245768 | tf_op jit(solution)/shard_map/ppermute | solution.py:307
  53.1 5.3 %collective-permute-start.16 = (s16[320,128]{1,0:T(8,128)(2,1)S(1)}, s16[320,128]{1,0:T(8,128)(2,1)S(1)}, u32[]{:S(2)}, u32[]{:S(2)}) collective-permute-start(s16[320,128]{1,0:T(8,128)(2,1)S(1)} %get-tuple-element.90), channel_id=1, source_target_pairs={{0,16},{8,24},{16,0},{24,8},{1,17},{9,25},{17,1},{25,9},{2,18},{10... | collective-permute-start | bytes 245768 | tf_op jit(solution)/shard_map/ppermute | solution.py:307
  54.6 5.3 %collective-permute-start.17 = (s16[320,128]{1,0:T(8,128)(2,1)S(1)}, s16[320,128]{1,0:T(8,128)(2,1)S(1)}, u32[]{:S(2)}, u32[]{:S(2)}) collective-permute-start(s16[320,128]{1,0:T(8,128)(2,1)S(1)} %get-tuple-element.91), channel_id=1, source_target_pairs={{0,24},{8,16},{16,8},{24,0},{1,25},{9,17},{17,9},{25,1},{2,26},{10... | collective-permute-start | bytes 245768 | tf_op jit(solution)/shard_map/ppermute | solution.py:307
  60.1 9.1 %collective-permute-start.18 = (s16[320,128]{1,0:T(8,128)(2,1)S(1)}, s16[320,128]{1,0:T(8,128)(2,1)S(1)}, u32[]{:S(2)}, u32[]{:S(2)}) collective-permute-start(s16[320,128]{1,0:T(8,128)(2,1)S(1)} %get-tuple-element.92), channel_id=1, source_target_pairs={{0,4},{1,5},{2,6},{3,7},{4,0},{5,1},{6,2},{7,3},{8,12},{9,13},{10,... | collective-permute-start | bytes 245768 | tf_op jit(solution)/shard_map/ppermute | solution.py:307
  63.4 5.8 %collective-permute-start.19 = (s16[320,128]{1,0:T(8,128)(2,1)S(1)}, s16[320,128]{1,0:T(8,128)(2,1)S(1)}, u32[]{:S(2)}, u32[]{:S(2)}) collective-permute-start(s16[320,128]{1,0:T(8,128)(2,1)S(1)} %get-tuple-element.93), channel_id=1, source_target_pairs={{0,2},{1,3},{2,0},{3,1},{4,6},{5,7},{6,4},{7,5},{8,10},{9,11},{10,... | collective-permute-start | bytes 245768 | tf_op jit(solution)/shard_map/ppermute | solution.py:307
  63.6 6.7 %collective-permute-start.20 = (s16[320,128]{1,0:T(8,128)(2,1)S(1)}, s16[320,128]{1,0:T(8,128)(2,1)S(1)}, u32[]{:S(2)}, u32[]{:S(2)}) collective-permute-start(s16[320,128]{1,0:T(8,128)(2,1)S(1)} %get-tuple-element.94), channel_id=1, source_target_pairs={{0,6},{1,7},{2,4},{3,5},{4,2},{5,3},{6,0},{7,1},{8,14},{9,15},{10,... | collective-permute-start | bytes 245768 | tf_op jit(solution)/shard_map/ppermute | solution.py:307
  70.4 5.4 %collective-permute-start.21 = (s16[320,128]{1,0:T(8,128)(2,1)S(1)}, s16[320,128]{1,0:T(8,128)(2,1)S(1)}, u32[]{:S(2)}, u32[]{:S(2)}) collective-permute-start(s16[320,128]{1,0:T(8,128)(2,1)S(1)} %get-tuple-element.97), channel_id=1, source_target_pairs={{0,24},{8,16},{16,8},{24,0},{1,25},{9,17},{17,9},{25,1},{2,26},{10... | collective-permute-start | bytes 245768 | tf_op jit(solution)/shard_map/ppermute | solution.py:307
  71.3 4.6 %collective-permute-start.22 = (s16[320,128]{1,0:T(8,128)(2,1)S(1)}, s16[320,128]{1,0:T(8,128)(2,1)S(1)}, u32[]{:S(2)}, u32[]{:S(2)}) collective-permute-start(s16[320,128]{1,0:T(8,128)(2,1)S(1)} %get-tuple-element.98), channel_id=1, source_target_pairs={{0,8},{8,0},{16,24},{24,16},{1,9},{9,1},{17,25},{25,17},{2,10},{10... | collective-permute-start | bytes 245768 | tf_op jit(solution)/shard_map/ppermute | solution.py:307
  72.7 4.4 %collective-permute-start.23 = (s16[320,128]{1,0:T(8,128)(2,1)S(1)}, s16[320,128]{1,0:T(8,128)(2,1)S(1)}, u32[]{:S(2)}, u32[]{:S(2)}) collective-permute-start(s16[320,128]{1,0:T(8,128)(2,1)S(1)} %get-tuple-element.99), channel_id=1, source_target_pairs={{0,16},{8,24},{16,0},{24,8},{1,17},{9,25},{17,1},{25,9},{2,18},{10... | collective-permute-start | bytes 245768 | tf_op jit(solution)/shard_map/ppermute | solution.py:307
  74.0 3.2 %collective-permute-start.24 = (s16[320,128]{1,0:T(8,128)(2,1)S(1)}, s16[320,128]{1,0:T(8,128)(2,1)S(1)}, u32[]{:S(2)}, u32[]{:S(2)}) collective-permute-start(s16[320,128]{1,0:T(8,128)(2,1)S(1)} %get-tuple-element.96.refs_0_), channel_id=1, source_target_pairs={{0,1},{1,0},{2,3},{3,2},{4,5},{5,4},{6,7},{7,6},{8,9},{9,8},{10,11... | collective-permute-start | bytes 245768 | tf_op jit(solution)/shard_map/ppermute | solution.py:307
  75.8 1.3 %collective-permute-start.25 = (s16[320,128]{1,0:T(8,128)(2,1)S(1)}, s16[320,128]{1,0:T(8,128)(2,1)S(1)}, u32[]{:S(2)}, u32[]{:S(2)}) collective-permute-start(s16[320,128]{1,0:T(8,128)(2,1)S(1)} %collective-permute-done.21.refs_1_), channel_id=1, source_target_pairs={{0,1},{1,0},{2,3},{3,2},{4,5},{5,4},{6,7},{7,6},{8,9},{9,8},{10,11... | collective-permute-start | bytes 245768 | tf_op jit(solution)/shard_map/ppermute | solution.py:307
  76.0 1.3 %collective-permute-start.26 = (s16[320,128]{1,0:T(8,128)(2,1)S(1)}, s16[320,128]{1,0:T(8,128)(2,1)S(1)}, u32[]{:S(2)}, u32[]{:S(2)}) collective-permute-start(s16[320,128]{1,0:T(8,128)(2,1)S(1)} %collective-permute-done.22.refs_2_), channel_id=1, source_target_pairs={{0,1},{1,0},{2,3},{3,2},{4,5},{5,4},{6,7},{7,6},{8,9},{9,8},{10,11... | collective-permute-start | bytes 245768 | tf_op jit(solution)/shard_map/ppermute | solution.py:307
  77.1 1.3 %collective-permute-start.27 = (s16[320,128]{1,0:T(8,128)(2,1)S(1)}, s16[320,128]{1,0:T(8,128)(2,1)S(1)}, u32[]{:S(2)}, u32[]{:S(2)}) collective-permute-start(s16[320,128]{1,0:T(8,128)(2,1)S(1)} %collective-permute-done.23.refs_3_), channel_id=1, source_target_pairs={{0,1},{1,0},{2,3},{3,2},{4,5},{5,4},{6,7},{7,6},{8,9},{9,8},{10,11... | collective-permute-start | bytes 245768 | tf_op jit(solution)/shard_map/ppermute | solution.py:307
  (4 other events, 2.7 us)

commit v7 on v6

--- a/solution.py
+++ b/solution.py
@@ -15,7 +15,8 @@
 SMEM = pl.BlockSpec(memory_space=pltpu.SMEM)
 VMEM = pl.BlockSpec(memory_space=pltpu.VMEM)
 CHUNK = 256
-BATCH = 2
+AHEAD = 2
+BATCH = 4
 LATE = 4
 TAIL = 8
 
@@ -35,15 +36,22 @@
     return jax.ShapeDtypeStruct(shape, dtype)
 
 
+def tops(dom):
+    return [1 << b for b in reversed(range((dom - 1).bit_length()))]
+
+
 def partners(dom):
-    tops = [1 << b for b in reversed(range((dom - 1).bit_length()))]
-    return [k for odd in (0, 1) for top in tops for k in range(top, 2 * top) if k % 2 == odd]
+    return [k for odd in (0, 1) for top in tops(dom) for k in range(top, 2 * top) if k % 2 == odd]
+
+
+def partners_1(dom):
+    return [k for top in tops(dom) for odd in (0, 1) for k in range(top, 2 * top) if k % 2 == odd]
 
 
 def select_kernel(info, tiles, *refs):
     msgs = refs[:-1]
     refs[-1][...] = tiles[...]
-    for i, k in enumerate(partners(len(msgs) + 1)):
+    for i, k in enumerate(partners_1(len(msgs) + 1)):
         msgs[i][...] = tiles[info[3 + (info[0] ^ k)]]
 
 
@@ -85,7 +93,7 @@
     msgs, (cur, total), outs, pool = refs[: dom - 1], refs[dom - 1 : dom + 1], refs[dom + 1 : -1], refs[-1]
     tiles, tile, lanes = own.shape
     feat = lanes // samples
-    for i, k in enumerate(partners(dom)):
+    for i, k in enumerate(partners_1(dom)):
 
         def put(s, x):
             pool[k - 1, :, s * feat : (s + 1) * feat] = x
@@ -191,11 +199,11 @@
                 dpre[here, cols] = dp.astype(BF16)
                 bias_acc[:, cols] += fold(dp)
 
-    forward(0)
-    for r in range(1, tiles):
-        forward(r)
-        backward(r - 1)
-    backward(tiles - 1)
+    for r in range(tiles + AHEAD):
+        if r < tiles:
+            forward(r)
+        if r >= AHEAD:
+            backward(r - AHEAD)
     half_pieces(1 - info[2], x_t, act, dl_t, dpre, bias_acc, cls_acc, lambda m: info[1] ^ m, send)
 
 
@@ -382,7 +390,7 @@
         [like((tiles, tile, nnz * tile), BF16), like((tiles, tile, lanes), BF16), like((tiles, nnz), I32)],
         [both, adj, col_slot[0]],
     )
-    msgs = swap_all(msgs)
+    msgs = [xor_permute(x, "dom", k) for k, x in zip(partners_1(dom), msgs)]
     cur, total, *outs = call(
         functools.partial(hop1_kernel, dom, samples),
         [like((tiles, tile, lanes), BF16), like((tiles, tile, lanes), F32)] + [like((tile, lanes), BF16)] * (dom - 1),

time: 80.6 us -> 80.3 us (level)
  starting transfers between devices: 33.6 us -> 30.6 us
  waiting for transfers between devices: 23.2 us -> 25.9 us
    ppermute x28, starting transfers between devices: 33.6 us -> 30.6 us  [xor_permute(): lax.ppermute(x, axis, [(i, i ^ mask) for i in range(lax.axis_size(axis))])]
    ppermute x28, waiting for transfers between devices: 23.2 us -> 25.9 us  [xor_permute(): lax.ppermute(x, axis, [(i, i ^ mask) for i in range(lax.axis_size(axis))])]
where the time goes in v7:
time: 80.3 us; the launch traced here: 80 us
  starting transfers between devices  30.6 us (38%)
  waiting for transfers between devices  25.9 us (32%)
  Pallas kernels  14.6 us (18%)
  local copies, waits for them, and re-layouts  6.38 us (8%)
  other arithmetic  1.67 us (2%)
    ppermute x28, starting transfers between devices, xor_permute(): lax.ppermute(x, axis, [(i, i ^ mask) for i in range(lax.axis_size(axis))])  30.6 us
    ppermute x28, waiting for transfers between devices, xor_permute(): lax.ppermute(x, axis, [(i, i ^ mask) for i in range(lax.axis_size(axis))])  25.9 us
    pallas_call x10, Pallas kernels, call(): pl.pallas_call(kernel, out_shape=outs, in_specs=[SMEM] * n_smem + [VMEM]...  14.6 us
    unnamed x16, local copies, waits for them, and re-layouts  6.38 us
  transfers between devices with their start and end apart: 28, of which 16 were waited for; matrix products, arithmetic and copies ran while one was open for 0% of the time, Pallas kernels for 3%

profile of v7, /device:TPU:0, one launch (start us, length us, event | category | flops | bytes accessed | tf_op | source)
XLA Modules:
  0.0 80.0 jit_solution(9556346348645387189)
XLA Ops:
  0.6 0.9 %fusion.1.tiles = bf16[4,144,128]{2,1,0:T(8,128)(2,1)S(1)} fusion(bf16[4,4,128]{2,1,0:T(4,128)(2,1)} %bitcast.27, bf16[4,128,128]{2,1,0:T(8,128)(2,1)} %bitcast.26), kind=kLoop, calls=%fused_computation.2 | loop fusion | flops 442368 | bytes 282624 | tf_op jit(solution)/shard_map/concatenate | solution.py:384
  2.9 4.1 %collective-permute-start = (bf16[144,128]{1,0:T(8,128)(2,1)S(1)}, bf16[144,128]{1,0:T(8,128)(2,1)S(1)}, u32[]{:S(2)}, u32[]{:S(2)}) collective-permute-start(bf16[144,128]{1,0:T(8,128)(2,1)S(1)} %get-tuple-element.58), channel_id=1, source_target_pairs={{0,4},{1,5},{2,6},{3,7},{4,0},{5,1},{6,2},{7,3},{8,12},{9,13},{10,... | collective-permute-start | bytes 110600 | tf_op jit(solution)/shard_map/ppermute | solution.py:315
  7.0 1.3 %collective-permute-start.1 = (bf16[144,128]{1,0:T(8,128)(2,1)S(1)}, bf16[144,128]{1,0:T(8,128)(2,1)S(1)}, u32[]{:S(2)}, u32[]{:S(2)}) collective-permute-start(bf16[144,128]{1,0:T(8,128)(2,1)S(1)} %get-tuple-element.59), channel_id=1, source_target_pairs={{0,6},{1,7},{2,4},{3,5},{4,2},{5,3},{6,0},{7,1},{8,14},{9,15},{10,... | collective-permute-start | bytes 110600 | tf_op jit(solution)/shard_map/ppermute | solution.py:315
  8.9 1.7 %collective-permute-start.3 = (bf16[144,128]{1,0:T(8,128)(2,1)S(1)}, bf16[144,128]{1,0:T(8,128)(2,1)S(1)}, u32[]{:S(2)}, u32[]{:S(2)}) collective-permute-start(bf16[144,128]{1,0:T(8,128)(2,1)S(1)} %get-tuple-element.61), channel_id=1, source_target_pairs={{0,7},{1,6},{2,5},{3,4},{4,3},{5,2},{6,1},{7,0},{8,15},{9,14},{10,... | collective-permute-start | bytes 110600 | tf_op jit(solution)/shard_map/ppermute | solution.py:315
  12.8 1.0 %copy-done = bf16[1,4,4,128,128]{4,3,2,1,0:T(8,128)(2,1)S(1)} copy-done((bf16[1,4,4,128,128]{4,3,2,1,0:T(8,128)(2,1)S(1)}, bf16[1,4,4,128,128]{4,3,2,1,0:T(8,128)(2,1)}, u32[]{:S(2)}) %copy-start) | copy-done | bytes 524312
  15.2 1.0 %collective-permute-done.5.refs_5_ = bf16[144,128]{1,0:T(8,128)(2,1)S(1)} collective-permute-done((bf16[144,128]{1,0:T(8,128)(2,1)S(1)}, bf16[144,128]{1,0:T(8,128)(2,1)S(1)}, u32[]{:S(2)}, u32[]{:S(2)}) %collective-permute-start.5) | collective-permute-done | bytes 36896 | tf_op jit(solution)/shard_map/ppermute | solution.py:315
  16.2 1.5 %shard_map.140 = (bf16[4,128,512]{2,1,0:T(8,128)(2,1)S(1)}, f32[4,128,512]{2,1,0:T(8,128)S(1)}, bf16[128,512]{1,0:T(8,128)(2,1)S(1)}, bf16[128,512]{1,0:T(8,128)...) custom-call(s32[11]{0:T(128)S(1)} %pad_add_fusion.info, ...), custom_call_target="tpu_custom_call" | custom-call | tf_op jit(solution)/shard_map/pallas_call | solution.py:25
  17.8 1.4 %collective-permute-start.7 = (bf16[128,512]{1,0:T(8,128)(2,1)S(1)}, bf16[128,512]{1,0:T(8,128)(2,1)S(1)}, u32[]{:S(2)}, u32[]{:S(2)}) collective-permute-start(bf16[128,512]{1,0:T(8,128)(2,1)S(1)} %get-tuple-element.74), channel_id=1, source_target_pairs={{0,4},{1,5},{2,6},{3,7},{4,0},{5,1},{6,2},{7,3},{8,12},{9,13},{10,... | collective-permute-start | bytes 393224 | tf_op jit(solution)/shard_map/ppermute | solution.py:315
  19.1 1.1 %collective-permute-start.8 = (bf16[128,512]{1,0:T(8,128)(2,1)S(1)}, bf16[128,512]{1,0:T(8,128)(2,1)S(1)}, u32[]{:S(2)}, u32[]{:S(2)}) collective-permute-start(bf16[128,512]{1,0:T(8,128)(2,1)S(1)} %get-tuple-element.75), channel_id=1, source_target_pairs={{0,6},{1,7},{2,4},{3,5},{4,2},{5,3},{6,0},{7,1},{8,14},{9,15},{10,... | collective-permute-start | bytes 393224 | tf_op jit(solution)/shard_map/ppermute | solution.py:315
  20.3 1.1 %collective-permute-start.9 = (bf16[128,512]{1,0:T(8,128)(2,1)S(1)}, bf16[128,512]{1,0:T(8,128)(2,1)S(1)}, u32[]{:S(2)}, u32[]{:S(2)}) collective-permute-start(bf16[128,512]{1,0:T(8,128)(2,1)S(1)} %get-tuple-element.76), channel_id=1, source_target_pairs={{0,2},{1,3},{2,0},{3,1},{4,6},{5,7},{6,4},{7,5},{8,10},{9,11},{10,... | collective-permute-start | bytes 393224 | tf_op jit(solution)/shard_map/ppermute | solution.py:315
  21.6 1.7 %collective-permute-start.12 = (bf16[128,512]{1,0:T(8,128)(2,1)S(1)}, bf16[128,512]{1,0:T(8,128)(2,1)S(1)}, u32[]{:S(2)}, u32[]{:S(2)}) collective-permute-start(bf16[128,512]{1,0:T(8,128)(2,1)S(1)} %get-tuple-element.79), channel_id=1, source_target_pairs={{0,3},{1,2},{2,1},{3,0},{4,7},{5,6},{6,5},{7,4},{8,11},{9,10},{10,... | collective-permute-start | bytes 393224 | tf_op jit(solution)/shard_map/ppermute | solution.py:315
  23.3 1.0 %copy-done.1 = bf16[1024,172]{0,1:T(8,128)(2,1)S(1)} copy-done((bf16[1024,172]{0,1:T(8,128)(2,1)S(1)}, bf16[1024,172]{0,1:T(8,128)(2,1)}, u32[]{:S(2)}) %copy-start.1) | copy-done | bytes 352280
  24.3 0.9 %copy-done.2 = bf16[128,1024]{1,0:T(8,128)(2,1)S(1)} copy-done((bf16[128,1024]{1,0:T(8,128)(2,1)S(1)}, bf16[128,1024]{1,0:T(8,128)(2,1)}, u32[]{:S(2)}) %copy-start.2) | copy-done | bytes 262168
  28.2 2.1 %collective-permute-done.7.refs_0_ = bf16[128,512]{1,0:T(8,128)(2,1)S(1)} collective-permute-done((bf16[128,512]{1,0:T(8,128)(2,1)S(1)}, bf16[128,512]{1,0:T(8,128)(2,1)S(1)}, u32[]{:S(2)}, u32[]{:S(2)}) %collective-permute-start.7) | collective-permute-done | bytes 131104 | tf_op jit(solution)/shard_map/ppermute | solution.py:315
  30.3 2.4 %collective-permute-start.11 = (bf16[128,512]{1,0:T(8,128)(2,1)S(1)}, bf16[128,512]{1,0:T(8,128)(2,1)S(1)}, u32[]{:S(2)}, u32[]{:S(2)}) collective-permute-start(bf16[128,512]{1,0:T(8,128)(2,1)S(1)} %get-tuple-element.78), channel_id=1, source_target_pairs={{0,7},{1,6},{2,5},{3,4},{4,3},{5,2},{6,1},{7,0},{8,15},{9,14},{10,... | collective-permute-start | bytes 393224 | tf_op jit(solution)/shard_map/ppermute | solution.py:315
  32.7 7.8 %collective-permute-done.10.refs_3_ = bf16[128,512]{1,0:T(8,128)(2,1)S(1)} collective-permute-done((bf16[128,512]{1,0:T(8,128)(2,1)S(1)}, bf16[128,512]{1,0:T(8,128)(2,1)S(1)}, u32[]{:S(2)}, u32[]{:S(2)}) %collective-permute-start.10) | collective-permute-done | bytes 131104 | tf_op jit(solution)/shard_map/ppermute | solution.py:315
  40.6 8.3 %shard_map.142 = (f32[4,312,128]{2,1,0:T(8,128)S(1)}, bf16[128,2048]{1,0:T(8,128)(2,1)S(1)}, bf16[2048,1024]{1,0:T(8,128)(2,1)S(1)}, bf16[176,2048]{1,0:T(8,128)...) custom-call(s32[11]{0:T(128)S(1)} %pad_add_fusion.info, ...), custom_call_target="tpu_custom_call" | custom-call | tf_op jit(solution)/shard_map/pallas_call | solution.py:25
  49.0 1.5 %shard_map.143.keep = f32[4,312,128]{2,1,0:T(8,128)S(1)} custom-call(s32[11]{0:T(128)S(1)} %pad_add_fusion.info, bf16[128,2048]{1,0:T(8,128)(2,1)S(1)} %get-tuple-element.81.x_t, bf16[2048,1024]{1,0:T(8,128)(2,1)S(1)} %get-tuple-element.82.act, bf16[176,2048]{1,0:T(8,128)(2,1)S(1)} %get-tuple-element.83.dl_t, bf16[2048,1024]{1,0:T(8,128)(2,1)S(1)} %get-tuple-element.84.dpre, ...), custom_call_target="tpu_custom_call" | custom-call | tf_op jit(solution)/shard_map/pallas_call | solution.py:25
  51.1 1.6 %collective-permute-start.15 = (s16[320,128]{1,0:T(8,128)(2,1)S(1)}, s16[320,128]{1,0:T(8,128)(2,1)S(1)}, u32[]{:S(2)}, u32[]{:S(2)}) collective-permute-start(s16[320,128]{1,0:T(8,128)(2,1)S(1)} %get-tuple-element.89), channel_id=1, source_target_pairs={{0,8},{8,0},{16,24},{24,16},{1,9},{9,1},{17,25},{25,17},{2,10},{10... | collective-permute-start | bytes 245768 | tf_op jit(solution)/shard_map/ppermute | solution.py:315
  52.7 1.5 %collective-permute-start.16 = (s16[320,128]{1,0:T(8,128)(2,1)S(1)}, s16[320,128]{1,0:T(8,128)(2,1)S(1)}, u32[]{:S(2)}, u32[]{:S(2)}) collective-permute-start(s16[320,128]{1,0:T(8,128)(2,1)S(1)} %get-tuple-element.90), channel_id=1, source_target_pairs={{0,16},{8,24},{16,0},{24,8},{1,17},{9,25},{17,1},{25,9},{2,18},{10... | collective-permute-start | bytes 245768 | tf_op jit(solution)/shard_map/ppermute | solution.py:315
  54.7 1.0 %collective-permute-done.15.refs_0_ = s16[320,128]{1,0:T(8,128)(2,1)S(1)} collective-permute-done((s16[320,128]{1,0:T(8,128)(2,1)S(1)}, s16[320,128]{1,0:T(8,128)(2,1)S(1)}, u32[]{:S(2)}, u32[]{:S(2)}) %collective-permute-start.15) | collective-permute-done | bytes 81952 | tf_op jit(solution)/shard_map/ppermute | solution.py:315
  55.7 2.3 %collective-permute-done.16.refs_1_ = s16[320,128]{1,0:T(8,128)(2,1)S(1)} collective-permute-done((s16[320,128]{1,0:T(8,128)(2,1)S(1)}, s16[320,128]{1,0:T(8,128)(2,1)S(1)}, u32[]{:S(2)}, u32[]{:S(2)}) %collective-permute-start.16) | collective-permute-done | bytes 81952 | tf_op jit(solution)/shard_map/ppermute | solution.py:315
  58.0 1.6 %collective-permute-done.17.refs_2_ = s16[320,128]{1,0:T(8,128)(2,1)S(1)} collective-permute-done((s16[320,128]{1,0:T(8,128)(2,1)S(1)}, s16[320,128]{1,0:T(8,128)(2,1)S(1)}, u32[]{:S(2)}, u32[]{:S(2)}) %collective-permute-start.17) | collective-permute-done | bytes 81952 | tf_op jit(solution)/shard_map/ppermute | solution.py:315
  59.7 3.8 %collective-permute-start.18 = (s16[320,128]{1,0:T(8,128)(2,1)S(1)}, s16[320,128]{1,0:T(8,128)(2,1)S(1)}, u32[]{:S(2)}, u32[]{:S(2)}) collective-permute-start(s16[320,128]{1,0:T(8,128)(2,1)S(1)} %get-tuple-element.92), channel_id=1, source_target_pairs={{0,4},{1,5},{2,6},{3,7},{4,0},{5,1},{6,2},{7,3},{8,12},{9,13},{10,... | collective-permute-start | bytes 245768 | tf_op jit(solution)/shard_map/ppermute | solution.py:315
  63.5 1.9 %collective-permute-start.20 = (s16[320,128]{1,0:T(8,128)(2,1)S(1)}, s16[320,128]{1,0:T(8,128)(2,1)S(1)}, u32[]{:S(2)}, u32[]{:S(2)}) collective-permute-start(s16[320,128]{1,0:T(8,128)(2,1)S(1)} %get-tuple-element.94), channel_id=1, source_target_pairs={{0,6},{1,7},{2,4},{3,5},{4,2},{5,3},{6,0},{7,1},{8,14},{9,15},{10,... | collective-permute-start | bytes 245768 | tf_op jit(solution)/shard_map/ppermute | solution.py:315
  65.5 3.3 %collective-permute-done.18.refs_0_ = s16[320,128]{1,0:T(8,128)(2,1)S(1)} collective-permute-done((s16[320,128]{1,0:T(8,128)(2,1)S(1)}, s16[320,128]{1,0:T(8,128)(2,1)S(1)}, u32[]{:S(2)}, u32[]{:S(2)}) %collective-permute-start.18) | collective-permute-done | bytes 81952 | tf_op jit(solution)/shard_map/ppermute | solution.py:315
  68.7 1.1 %collective-permute-done.20.refs_2_ = s16[320,128]{1,0:T(8,128)(2,1)S(1)} collective-permute-done((s16[320,128]{1,0:T(8,128)(2,1)S(1)}, s16[320,128]{1,0:T(8,128)(2,1)S(1)}, u32[]{:S(2)}, u32[]{:S(2)}) %collective-permute-start.20) | collective-permute-done | bytes 81952 | tf_op jit(solution)/shard_map/ppermute | solution.py:315
  71.0 1.5 %collective-permute-start.22 = (s16[320,128]{1,0:T(8,128)(2,1)S(1)}, s16[320,128]{1,0:T(8,128)(2,1)S(1)}, u32[]{:S(2)}, u32[]{:S(2)}) collective-permute-start(s16[320,128]{1,0:T(8,128)(2,1)S(1)} %get-tuple-element.98), channel_id=1, source_target_pairs={{0,8},{8,0},{16,24},{24,16},{1,9},{9,1},{17,25},{25,17},{2,10},{10... | collective-permute-start | bytes 245768 | tf_op jit(solution)/shard_map/ppermute | solution.py:315
  72.4 1.2 %collective-permute-start.23 = (s16[320,128]{1,0:T(8,128)(2,1)S(1)}, s16[320,128]{1,0:T(8,128)(2,1)S(1)}, u32[]{:S(2)}, u32[]{:S(2)}) collective-permute-start(s16[320,128]{1,0:T(8,128)(2,1)S(1)} %get-tuple-element.99), channel_id=1, source_target_pairs={{0,16},{8,24},{16,0},{24,8},{1,17},{9,25},{17,1},{25,9},{2,18},{10... | collective-permute-start | bytes 245768 | tf_op jit(solution)/shard_map/ppermute | solution.py:315
  73.6 1.8 %collective-permute-done.21.refs_1_ = s16[320,128]{1,0:T(8,128)(2,1)S(1)} collective-permute-done((s16[320,128]{1,0:T(8,128)(2,1)S(1)}, s16[320,128]{1,0:T(8,128)(2,1)S(1)}, u32[]{:S(2)}, u32[]{:S(2)}) %collective-permute-start.21) | collective-permute-done | bytes 81952 | tf_op jit(solution)/shard_map/ppermute | solution.py:315
  77.0 1.1 %collective-permute-done.27.refs_7_ = s16[320,128]{1,0:T(8,128)(2,1)S(1)} collective-permute-done((s16[320,128]{1,0:T(8,128)(2,1)S(1)}, s16[320,128]{1,0:T(8,128)(2,1)S(1)}, u32[]{:S(2)}, u32[]{:S(2)}) %collective-permute-start.27) | collective-permute-done | bytes 81952 | tf_op jit(solution)/shard_map/ppermute | solution.py:315
  78.2 1.8 %shard_map.147 = (f32[128,1024]{1,0:T(8,128)}, f32[1,1024]{1,0:T(1,128)}, f32[172,1024]{1,0:T(8,128)}, f32[1,256]{1,0:T(1,128)}) custom-call(s32[11]{0:T(128)S(1)} %pad_add_fusion.info, s16[320,128]{1,0:T(8,128)(2,1)S(1)} %get-tuple-element.96.refs_0_, s16[320,128]{1,0:T(8,128)(2,1)S(1)} %collective-permute-done.21.refs_1_, ...), custom_call_target="tpu_custom_call" | custom-call | tf_op jit(solution)/shard_map/pallas_call | solution.py:25
  (52 shorter events, 12.7 us)
Async XLA Ops:
  2.9 8.7 %collective-permute-start = (bf16[144,128]{1,0:T(8,128)(2,1)S(1)}, bf16[144,128]{1,0:T(8,128)(2,1)S(1)}, u32[]{:S(2)}, u32[]{:S(2)}) collective-permute-start(bf16[144,128]{1,0:T(8,128)(2,1)S(1)} %get-tuple-element.58), channel_id=1, source_target_pairs={{0,4},{1,5},{2,6},{3,7},{4,0},{5,1},{6,2},{7,3},{8,12},{9,13},{10,... | collective-permute-start | bytes 110600 | tf_op jit(solution)/shard_map/ppermute | solution.py:315
  7.0 5.8 %collective-permute-start.1 = (bf16[144,128]{1,0:T(8,128)(2,1)S(1)}, bf16[144,128]{1,0:T(8,128)(2,1)S(1)}, u32[]{:S(2)}, u32[]{:S(2)}) collective-permute-start(bf16[144,128]{1,0:T(8,128)(2,1)S(1)} %get-tuple-element.59), channel_id=1, source_target_pairs={{0,6},{1,7},{2,4},{3,5},{4,2},{5,3},{6,0},{7,1},{8,14},{9,15},{10,... | collective-permute-start | bytes 110600 | tf_op jit(solution)/shard_map/ppermute | solution.py:315
  8.3 6.5 %collective-permute-start.2 = (bf16[144,128]{1,0:T(8,128)(2,1)S(1)}, bf16[144,128]{1,0:T(8,128)(2,1)S(1)}, u32[]{:S(2)}, u32[]{:S(2)}) collective-permute-start(bf16[144,128]{1,0:T(8,128)(2,1)S(1)} %get-tuple-element.60), channel_id=1, source_target_pairs={{0,5},{1,4},{2,7},{3,6},{4,1},{5,0},{6,3},{7,2},{8,13},{9,12},{10,... | collective-permute-start | bytes 110600 | tf_op jit(solution)/shard_map/ppermute | solution.py:315
  8.9 6.0 %collective-permute-start.3 = (bf16[144,128]{1,0:T(8,128)(2,1)S(1)}, bf16[144,128]{1,0:T(8,128)(2,1)S(1)}, u32[]{:S(2)}, u32[]{:S(2)}) collective-permute-start(bf16[144,128]{1,0:T(8,128)(2,1)S(1)} %get-tuple-element.61), channel_id=1, source_target_pairs={{0,7},{1,6},{2,5},{3,4},{4,3},{5,2},{6,1},{7,0},{8,15},{9,14},{10,... | collective-permute-start | bytes 110600 | tf_op jit(solution)/shard_map/ppermute | solution.py:315
  10.6 4.5 %collective-permute-start.4 = (bf16[144,128]{1,0:T(8,128)(2,1)S(1)}, bf16[144,128]{1,0:T(8,128)(2,1)S(1)}, u32[]{:S(2)}, u32[]{:S(2)}) collective-permute-start(bf16[144,128]{1,0:T(8,128)(2,1)S(1)} %get-tuple-element.62), channel_id=1, source_target_pairs={{0,2},{1,3},{2,0},{3,1},{4,6},{5,7},{6,4},{7,5},{8,10},{9,11},{10,... | collective-permute-start | bytes 110600 | tf_op jit(solution)/shard_map/ppermute | solution.py:315
  11.5 4.7 %collective-permute-start.5 = (bf16[144,128]{1,0:T(8,128)(2,1)S(1)}, bf16[144,128]{1,0:T(8,128)(2,1)S(1)}, u32[]{:S(2)}, u32[]{:S(2)}) collective-permute-start(bf16[144,128]{1,0:T(8,128)(2,1)S(1)} %get-tuple-element.63), channel_id=1, source_target_pairs={{0,3},{1,2},{2,1},{3,0},{4,7},{5,6},{6,5},{7,4},{8,11},{9,10},{10,... | collective-permute-start | bytes 110600 | tf_op jit(solution)/shard_map/ppermute | solution.py:315
  12.8 3.5 %collective-permute-start.6 = (bf16[144,128]{1,0:T(8,128)(2,1)S(1)}, bf16[144,128]{1,0:T(8,128)(2,1)S(1)}, u32[]{:S(2)}, u32[]{:S(2)}) collective-permute-start(bf16[144,128]{1,0:T(8,128)(2,1)S(1)} %get-tuple-element.64), channel_id=1, source_target_pairs={{0,1},{1,0},{2,3},{3,2},{4,5},{5,4},{6,7},{7,6},{8,9},{9,8},{10,11... | collective-permute-start | bytes 110600 | tf_op jit(solution)/shard_map/ppermute | solution.py:315
  12.8 1.0 %copy-start = (bf16[1,4,4,128,128]{4,3,2,1,0:T(8,128)(2,1)S(1)}, bf16[1,4,4,128,128]{4,3,2,1,0:T(8,128)(2,1)}, u32[]{:S(2)}) copy-start(bf16[1,4,4,128,128]{4,3,2,1,0:T(8,128)(2,1)} %param.15) | copy-start | bytes 1572868
  17.8 12.5 %collective-permute-start.7 = (bf16[128,512]{1,0:T(8,128)(2,1)S(1)}, bf16[128,512]{1,0:T(8,128)(2,1)S(1)}, u32[]{:S(2)}, u32[]{:S(2)}) collective-permute-start(bf16[128,512]{1,0:T(8,128)(2,1)S(1)} %get-tuple-element.74), channel_id=1, source_target_pairs={{0,4},{1,5},{2,6},{3,7},{4,0},{5,1},{6,2},{7,3},{8,12},{9,13},{10,... | collective-permute-start | bytes 393224 | tf_op jit(solution)/shard_map/ppermute | solution.py:315
  19.1 11.2 %collective-permute-start.8 = (bf16[128,512]{1,0:T(8,128)(2,1)S(1)}, bf16[128,512]{1,0:T(8,128)(2,1)S(1)}, u32[]{:S(2)}, u32[]{:S(2)}) collective-permute-start(bf16[128,512]{1,0:T(8,128)(2,1)S(1)} %get-tuple-element.75), channel_id=1, source_target_pairs={{0,6},{1,7},{2,4},{3,5},{4,2},{5,3},{6,0},{7,1},{8,14},{9,15},{10,... | collective-permute-start | bytes 393224 | tf_op jit(solution)/shard_map/ppermute | solution.py:315
  20.3 12.5 %collective-permute-start.9 = (bf16[128,512]{1,0:T(8,128)(2,1)S(1)}, bf16[128,512]{1,0:T(8,128)(2,1)S(1)}, u32[]{:S(2)}, u32[]{:S(2)}) collective-permute-start(bf16[128,512]{1,0:T(8,128)(2,1)S(1)} %get-tuple-element.76), channel_id=1, source_target_pairs={{0,2},{1,3},{2,0},{3,1},{4,6},{5,7},{6,4},{7,5},{8,10},{9,11},{10,... | collective-permute-start | bytes 393224 | tf_op jit(solution)/shard_map/ppermute | solution.py:315
  21.3 19.2 %collective-permute-start.10 = (bf16[128,512]{1,0:T(8,128)(2,1)S(1)}, bf16[128,512]{1,0:T(8,128)(2,1)S(1)}, u32[]{:S(2)}, u32[]{:S(2)}) collective-permute-start(bf16[128,512]{1,0:T(8,128)(2,1)S(1)} %get-tuple-element.77), channel_id=1, source_target_pairs={{0,5},{1,4},{2,7},{3,6},{4,1},{5,0},{6,3},{7,2},{8,13},{9,12},{10,... | collective-permute-start | bytes 393224 | tf_op jit(solution)/shard_map/ppermute | solution.py:315
  21.6 18.9 %collective-permute-start.12 = (bf16[128,512]{1,0:T(8,128)(2,1)S(1)}, bf16[128,512]{1,0:T(8,128)(2,1)S(1)}, u32[]{:S(2)}, u32[]{:S(2)}) collective-permute-start(bf16[128,512]{1,0:T(8,128)(2,1)S(1)} %get-tuple-element.79), channel_id=1, source_target_pairs={{0,3},{1,2},{2,1},{3,0},{4,7},{5,6},{6,5},{7,4},{8,11},{9,10},{10,... | collective-permute-start | bytes 393224 | tf_op jit(solution)/shard_map/ppermute | solution.py:315
  23.3 1.0 %copy-start.1 = (bf16[1024,172]{0,1:T(8,128)(2,1)S(1)}, bf16[1024,172]{0,1:T(8,128)(2,1)}, u32[]{:S(2)}) copy-start(bf16[1024,172]{0,1:T(8,128)(2,1)} %param.20) | copy-start | bytes 1056772
  24.3 0.9 %copy-start.2 = (bf16[128,1024]{1,0:T(8,128)(2,1)S(1)}, bf16[128,1024]{1,0:T(8,128)(2,1)}, u32[]{:S(2)}) copy-start(bf16[128,1024]{1,0:T(8,128)(2,1)} %w_in.1) | copy-start | bytes 786436
  25.3 0.7 copy-start.3
  30.3 10.2 %collective-permute-start.13 = (bf16[128,512]{1,0:T(8,128)(2,1)S(1)}, bf16[128,512]{1,0:T(8,128)(2,1)S(1)}, u32[]{:S(2)}, u32[]{:S(2)}) collective-permute-start(bf16[128,512]{1,0:T(8,128)(2,1)S(1)} %get-tuple-element.80), channel_id=1, source_target_pairs={{0,1},{1,0},{2,3},{3,2},{4,5},{5,4},{6,7},{7,6},{8,9},{9,8},{10,11... | collective-permute-start | bytes 393224 | tf_op jit(solution)/shard_map/ppermute | solution.py:315
  30.3 10.2 %collective-permute-start.11 = (bf16[128,512]{1,0:T(8,128)(2,1)S(1)}, bf16[128,512]{1,0:T(8,128)(2,1)S(1)}, u32[]{:S(2)}, u32[]{:S(2)}) collective-permute-start(bf16[128,512]{1,0:T(8,128)(2,1)S(1)} %get-tuple-element.78), channel_id=1, source_target_pairs={{0,7},{1,6},{2,5},{3,4},{4,3},{5,2},{6,1},{7,0},{8,15},{9,14},{10,... | collective-permute-start | bytes 393224 | tf_op jit(solution)/shard_map/ppermute | solution.py:315
  48.8 2.1 %collective-permute-start.14 = (f32[4,312,128]{2,1,0:T(8,128)S(1)}, f32[4,312,128]{2,1,0:T(8,128)S(1)}, u32[]{:S(2)}, u32[]{:S(2)}) collective-permute-start(f32[4,312,128]{2,1,0:T(8,128)S(1)} %get-tuple-element.87), channel_id=1, source_target_pairs={{0,1},{1,0},{2,3},{3,2},{4,5},{5,4},{6,7},{7,6},{8,9},{9,8},{10,11... | collective-permute-start | bytes 1916936 | tf_op jit(solution)/shard_map/ppermute | solution.py:315
  51.1 4.6 %collective-permute-start.15 = (s16[320,128]{1,0:T(8,128)(2,1)S(1)}, s16[320,128]{1,0:T(8,128)(2,1)S(1)}, u32[]{:S(2)}, u32[]{:S(2)}) collective-permute-start(s16[320,128]{1,0:T(8,128)(2,1)S(1)} %get-tuple-element.89), channel_id=1, source_target_pairs={{0,8},{8,0},{16,24},{24,16},{1,9},{9,1},{17,25},{25,17},{2,10},{10... | collective-permute-start | bytes 245768 | tf_op jit(solution)/shard_map/ppermute | solution.py:315
  52.7 5.3 %collective-permute-start.16 = (s16[320,128]{1,0:T(8,128)(2,1)S(1)}, s16[320,128]{1,0:T(8,128)(2,1)S(1)}, u32[]{:S(2)}, u32[]{:S(2)}) collective-permute-start(s16[320,128]{1,0:T(8,128)(2,1)S(1)} %get-tuple-element.90), channel_id=1, source_target_pairs={{0,16},{8,24},{16,0},{24,8},{1,17},{9,25},{17,1},{25,9},{2,18},{10... | collective-permute-start | bytes 245768 | tf_op jit(solution)/shard_map/ppermute | solution.py:315
  54.2 5.3 %collective-permute-start.17 = (s16[320,128]{1,0:T(8,128)(2,1)S(1)}, s16[320,128]{1,0:T(8,128)(2,1)S(1)}, u32[]{:S(2)}, u32[]{:S(2)}) collective-permute-start(s16[320,128]{1,0:T(8,128)(2,1)S(1)} %get-tuple-element.91), channel_id=1, source_target_pairs={{0,24},{8,16},{16,8},{24,0},{1,25},{9,17},{17,9},{25,1},{2,26},{10... | collective-permute-start | bytes 245768 | tf_op jit(solution)/shard_map/ppermute | solution.py:315
  59.7 9.0 %collective-permute-start.18 = (s16[320,128]{1,0:T(8,128)(2,1)S(1)}, s16[320,128]{1,0:T(8,128)(2,1)S(1)}, u32[]{:S(2)}, u32[]{:S(2)}) collective-permute-start(s16[320,128]{1,0:T(8,128)(2,1)S(1)} %get-tuple-element.92), channel_id=1, source_target_pairs={{0,4},{1,5},{2,6},{3,7},{4,0},{5,1},{6,2},{7,3},{8,12},{9,13},{10,... | collective-permute-start | bytes 245768 | tf_op jit(solution)/shard_map/ppermute | solution.py:315
  63.5 5.2 %collective-permute-start.19 = (s16[320,128]{1,0:T(8,128)(2,1)S(1)}, s16[320,128]{1,0:T(8,128)(2,1)S(1)}, u32[]{:S(2)}, u32[]{:S(2)}) collective-permute-start(s16[320,128]{1,0:T(8,128)(2,1)S(1)} %get-tuple-element.93), channel_id=1, source_target_pairs={{0,2},{1,3},{2,0},{3,1},{4,6},{5,7},{6,4},{7,5},{8,10},{9,11},{10,... | collective-permute-start | bytes 245768 | tf_op jit(solution)/shard_map/ppermute | solution.py:315
  63.5 6.3 %collective-permute-start.20 = (s16[320,128]{1,0:T(8,128)(2,1)S(1)}, s16[320,128]{1,0:T(8,128)(2,1)S(1)}, u32[]{:S(2)}, u32[]{:S(2)}) collective-permute-start(s16[320,128]{1,0:T(8,128)(2,1)S(1)} %get-tuple-element.94), channel_id=1, source_target_pairs={{0,6},{1,7},{2,4},{3,5},{4,2},{5,3},{6,0},{7,1},{8,14},{9,15},{10,... | collective-permute-start | bytes 245768 | tf_op jit(solution)/shard_map/ppermute | solution.py:315
  70.0 5.4 %collective-permute-start.21 = (s16[320,128]{1,0:T(8,128)(2,1)S(1)}, s16[320,128]{1,0:T(8,128)(2,1)S(1)}, u32[]{:S(2)}, u32[]{:S(2)}) collective-permute-start(s16[320,128]{1,0:T(8,128)(2,1)S(1)} %get-tuple-element.97), channel_id=1, source_target_pairs={{0,24},{8,16},{16,8},{24,0},{1,25},{9,17},{17,9},{25,1},{2,26},{10... | collective-permute-start | bytes 245768 | tf_op jit(solution)/shard_map/ppermute | solution.py:315
  71.0 4.8 %collective-permute-start.22 = (s16[320,128]{1,0:T(8,128)(2,1)S(1)}, s16[320,128]{1,0:T(8,128)(2,1)S(1)}, u32[]{:S(2)}, u32[]{:S(2)}) collective-permute-start(s16[320,128]{1,0:T(8,128)(2,1)S(1)} %get-tuple-element.98), channel_id=1, source_target_pairs={{0,8},{8,0},{16,24},{24,16},{1,9},{9,1},{17,25},{25,17},{2,10},{10... | collective-permute-start | bytes 245768 | tf_op jit(solution)/shard_map/ppermute | solution.py:315
  72.4 4.4 %collective-permute-start.23 = (s16[320,128]{1,0:T(8,128)(2,1)S(1)}, s16[320,128]{1,0:T(8,128)(2,1)S(1)}, u32[]{:S(2)}, u32[]{:S(2)}) collective-permute-start(s16[320,128]{1,0:T(8,128)(2,1)S(1)} %get-tuple-element.99), channel_id=1, source_target_pairs={{0,16},{8,24},{16,0},{24,8},{1,17},{9,25},{17,1},{25,9},{2,18},{10... | collective-permute-start | bytes 245768 | tf_op jit(solution)/shard_map/ppermute | solution.py:315
  73.6 3.3 %collective-permute-start.24 = (s16[320,128]{1,0:T(8,128)(2,1)S(1)}, s16[320,128]{1,0:T(8,128)(2,1)S(1)}, u32[]{:S(2)}, u32[]{:S(2)}) collective-permute-start(s16[320,128]{1,0:T(8,128)(2,1)S(1)} %get-tuple-element.96.refs_0_), channel_id=1, source_target_pairs={{0,1},{1,0},{2,3},{3,2},{4,5},{5,4},{6,7},{7,6},{8,9},{9,8},{10,11... | collective-permute-start | bytes 245768 | tf_op jit(solution)/shard_map/ppermute | solution.py:315
  75.5 1.4 %collective-permute-start.25 = (s16[320,128]{1,0:T(8,128)(2,1)S(1)}, s16[320,128]{1,0:T(8,128)(2,1)S(1)}, u32[]{:S(2)}, u32[]{:S(2)}) collective-permute-start(s16[320,128]{1,0:T(8,128)(2,1)S(1)} %collective-permute-done.21.refs_1_), channel_id=1, source_target_pairs={{0,1},{1,0},{2,3},{3,2},{4,5},{5,4},{6,7},{7,6},{8,9},{9,8},{10,11... | collective-permute-start | bytes 245768 | tf_op jit(solution)/shard_map/ppermute | solution.py:315
  75.7 1.3 %collective-permute-start.26 = (s16[320,128]{1,0:T(8,128)(2,1)S(1)}, s16[320,128]{1,0:T(8,128)(2,1)S(1)}, u32[]{:S(2)}, u32[]{:S(2)}) collective-permute-start(s16[320,128]{1,0:T(8,128)(2,1)S(1)} %collective-permute-done.22.refs_2_), channel_id=1, source_target_pairs={{0,1},{1,0},{2,3},{3,2},{4,5},{5,4},{6,7},{7,6},{8,9},{9,8},{10,11... | collective-permute-start | bytes 245768 | tf_op jit(solution)/shard_map/ppermute | solution.py:315
  76.9 1.3 %collective-permute-start.27 = (s16[320,128]{1,0:T(8,128)(2,1)S(1)}, s16[320,128]{1,0:T(8,128)(2,1)S(1)}, u32[]{:S(2)}, u32[]{:S(2)}) collective-permute-start(s16[320,128]{1,0:T(8,128)(2,1)S(1)} %collective-permute-done.23.refs_3_), channel_id=1, source_target_pairs={{0,1},{1,0},{2,3},{3,2},{4,5},{5,4},{6,7},{7,6},{8,9},{9,8},{10,11... | collective-permute-start | bytes 245768 | tf_op jit(solution)/shard_map/ppermute | solution.py:315
  (4 other events, 2.7 us)

commit v8 on v7

--- a/solution.py
+++ b/solution.py
@@ -167,7 +167,9 @@
                 slope[here, cols] = up + silu * (1.0 - t)
             logits = jnp.dot(act[here, :], w_out[...], preferred_element_type=F32) + b_out[...]
             e = jnp.exp(logits)
-            prob[here, :] = e * (1.0 / jnp.sum(e, -1, keepdims=True))
+            norm = jnp.sum(e, -1, keepdims=True)
+            shrink = jnp.where(norm > 2.0**64, 2.0**-64, 1.0)
+            prob[here, :] = (e * shrink) * (1.0 / (norm * shrink))
 
     def backward(r):
         base = r * rows

time: 80.3 us -> 80.4 us (level)
  no operation moved by 1% of the time
where the time goes in v8:
time: 80.4 us; the launch traced here: 80.1 us
  starting transfers between devices  30.6 us (38%)
  waiting for transfers between devices  25.9 us (32%)
  Pallas kernels  14.8 us (18%)
  local copies, waits for them, and re-layouts  6.38 us (8%)
  other arithmetic  1.67 us (2%)
    ppermute x28, starting transfers between devices, xor_permute(): lax.ppermute(x, axis, [(i, i ^ mask) for i in range(lax.axis_size(axis))])  30.6 us
    ppermute x28, waiting for transfers between devices, xor_permute(): lax.ppermute(x, axis, [(i, i ^ mask) for i in range(lax.axis_size(axis))])  25.9 us
    pallas_call x10, Pallas kernels, call(): pl.pallas_call(kernel, out_shape=outs, in_specs=[SMEM] * n_smem + [VMEM]...  14.8 us
    unnamed x16, local copies, waits for them, and re-layouts  6.38 us
  transfers between devices with their start and end apart: 28, of which 16 were waited for; matrix products, arithmetic and copies ran while one was open for 0% of the time, Pallas kernels for 3%

profile of v8, /device:TPU:0, one launch (start us, length us, event | category | flops | bytes accessed | tf_op | source)
XLA Modules:
  0.0 80.1 jit_solution(286228775879850230)
XLA Ops:
  0.6 0.9 %fusion.1.tiles = bf16[4,144,128]{2,1,0:T(8,128)(2,1)S(1)} fusion(bf16[4,4,128]{2,1,0:T(4,128)(2,1)} %bitcast.27, bf16[4,128,128]{2,1,0:T(8,128)(2,1)} %bitcast.26), kind=kLoop, calls=%fused_computation.2 | loop fusion | flops 442368 | bytes 282624 | tf_op jit(solution)/shard_map/concatenate | solution.py:386
  2.9 4.1 %collective-permute-start = (bf16[144,128]{1,0:T(8,128)(2,1)S(1)}, bf16[144,128]{1,0:T(8,128)(2,1)S(1)}, u32[]{:S(2)}, u32[]{:S(2)}) collective-permute-start(bf16[144,128]{1,0:T(8,128)(2,1)S(1)} %get-tuple-element.58), channel_id=1, source_target_pairs={{0,4},{1,5},{2,6},{3,7},{4,0},{5,1},{6,2},{7,3},{8,12},{9,13},{10,... | collective-permute-start | bytes 110600 | tf_op jit(solution)/shard_map/ppermute | solution.py:317
  7.0 1.3 %collective-permute-start.1 = (bf16[144,128]{1,0:T(8,128)(2,1)S(1)}, bf16[144,128]{1,0:T(8,128)(2,1)S(1)}, u32[]{:S(2)}, u32[]{:S(2)}) collective-permute-start(bf16[144,128]{1,0:T(8,128)(2,1)S(1)} %get-tuple-element.59), channel_id=1, source_target_pairs={{0,6},{1,7},{2,4},{3,5},{4,2},{5,3},{6,0},{7,1},{8,14},{9,15},{10,... | collective-permute-start | bytes 110600 | tf_op jit(solution)/shard_map/ppermute | solution.py:317
  8.9 1.7 %collective-permute-start.3 = (bf16[144,128]{1,0:T(8,128)(2,1)S(1)}, bf16[144,128]{1,0:T(8,128)(2,1)S(1)}, u32[]{:S(2)}, u32[]{:S(2)}) collective-permute-start(bf16[144,128]{1,0:T(8,128)(2,1)S(1)} %get-tuple-element.61), channel_id=1, source_target_pairs={{0,7},{1,6},{2,5},{3,4},{4,3},{5,2},{6,1},{7,0},{8,15},{9,14},{10,... | collective-permute-start | bytes 110600 | tf_op jit(solution)/shard_map/ppermute | solution.py:317
  12.8 1.0 %copy-done = bf16[1,4,4,128,128]{4,3,2,1,0:T(8,128)(2,1)S(1)} copy-done((bf16[1,4,4,128,128]{4,3,2,1,0:T(8,128)(2,1)S(1)}, bf16[1,4,4,128,128]{4,3,2,1,0:T(8,128)(2,1)}, u32[]{:S(2)}) %copy-start) | copy-done | bytes 524312
  15.2 1.0 %collective-permute-done.5.refs_5_ = bf16[144,128]{1,0:T(8,128)(2,1)S(1)} collective-permute-done((bf16[144,128]{1,0:T(8,128)(2,1)S(1)}, bf16[144,128]{1,0:T(8,128)(2,1)S(1)}, u32[]{:S(2)}, u32[]{:S(2)}) %collective-permute-start.5) | collective-permute-done | bytes 36896 | tf_op jit(solution)/shard_map/ppermute | solution.py:317
  16.2 1.5 %shard_map.140 = (bf16[4,128,512]{2,1,0:T(8,128)(2,1)S(1)}, f32[4,128,512]{2,1,0:T(8,128)S(1)}, bf16[128,512]{1,0:T(8,128)(2,1)S(1)}, bf16[128,512]{1,0:T(8,128)...) custom-call(s32[11]{0:T(128)S(1)} %pad_add_fusion.info, ...), custom_call_target="tpu_custom_call" | custom-call | tf_op jit(solution)/shard_map/pallas_call | solution.py:25
  17.8 1.4 %collective-permute-start.7 = (bf16[128,512]{1,0:T(8,128)(2,1)S(1)}, bf16[128,512]{1,0:T(8,128)(2,1)S(1)}, u32[]{:S(2)}, u32[]{:S(2)}) collective-permute-start(bf16[128,512]{1,0:T(8,128)(2,1)S(1)} %get-tuple-element.74), channel_id=1, source_target_pairs={{0,4},{1,5},{2,6},{3,7},{4,0},{5,1},{6,2},{7,3},{8,12},{9,13},{10,... | collective-permute-start | bytes 393224 | tf_op jit(solution)/shard_map/ppermute | solution.py:317
  19.1 1.1 %collective-permute-start.8 = (bf16[128,512]{1,0:T(8,128)(2,1)S(1)}, bf16[128,512]{1,0:T(8,128)(2,1)S(1)}, u32[]{:S(2)}, u32[]{:S(2)}) collective-permute-start(bf16[128,512]{1,0:T(8,128)(2,1)S(1)} %get-tuple-element.75), channel_id=1, source_target_pairs={{0,6},{1,7},{2,4},{3,5},{4,2},{5,3},{6,0},{7,1},{8,14},{9,15},{10,... | collective-permute-start | bytes 393224 | tf_op jit(solution)/shard_map/ppermute | solution.py:317
  20.3 1.1 %collective-permute-start.9 = (bf16[128,512]{1,0:T(8,128)(2,1)S(1)}, bf16[128,512]{1,0:T(8,128)(2,1)S(1)}, u32[]{:S(2)}, u32[]{:S(2)}) collective-permute-start(bf16[128,512]{1,0:T(8,128)(2,1)S(1)} %get-tuple-element.76), channel_id=1, source_target_pairs={{0,2},{1,3},{2,0},{3,1},{4,6},{5,7},{6,4},{7,5},{8,10},{9,11},{10,... | collective-permute-start | bytes 393224 | tf_op jit(solution)/shard_map/ppermute | solution.py:317
  21.6 1.7 %collective-permute-start.12 = (bf16[128,512]{1,0:T(8,128)(2,1)S(1)}, bf16[128,512]{1,0:T(8,128)(2,1)S(1)}, u32[]{:S(2)}, u32[]{:S(2)}) collective-permute-start(bf16[128,512]{1,0:T(8,128)(2,1)S(1)} %get-tuple-element.79), channel_id=1, source_target_pairs={{0,3},{1,2},{2,1},{3,0},{4,7},{5,6},{6,5},{7,4},{8,11},{9,10},{10,... | collective-permute-start | bytes 393224 | tf_op jit(solution)/shard_map/ppermute | solution.py:317
  23.3 1.0 %copy-done.1 = bf16[1024,172]{0,1:T(8,128)(2,1)S(1)} copy-done((bf16[1024,172]{0,1:T(8,128)(2,1)S(1)}, bf16[1024,172]{0,1:T(8,128)(2,1)}, u32[]{:S(2)}) %copy-start.1) | copy-done | bytes 352280
  24.3 0.9 %copy-done.2 = bf16[128,1024]{1,0:T(8,128)(2,1)S(1)} copy-done((bf16[128,1024]{1,0:T(8,128)(2,1)S(1)}, bf16[128,1024]{1,0:T(8,128)(2,1)}, u32[]{:S(2)}) %copy-start.2) | copy-done | bytes 262168
  28.2 2.1 %collective-permute-done.7.refs_0_ = bf16[128,512]{1,0:T(8,128)(2,1)S(1)} collective-permute-done((bf16[128,512]{1,0:T(8,128)(2,1)S(1)}, bf16[128,512]{1,0:T(8,128)(2,1)S(1)}, u32[]{:S(2)}, u32[]{:S(2)}) %collective-permute-start.7) | collective-permute-done | bytes 131104 | tf_op jit(solution)/shard_map/ppermute | solution.py:317
  30.3 2.4 %collective-permute-start.11 = (bf16[128,512]{1,0:T(8,128)(2,1)S(1)}, bf16[128,512]{1,0:T(8,128)(2,1)S(1)}, u32[]{:S(2)}, u32[]{:S(2)}) collective-permute-start(bf16[128,512]{1,0:T(8,128)(2,1)S(1)} %get-tuple-element.78), channel_id=1, source_target_pairs={{0,7},{1,6},{2,5},{3,4},{4,3},{5,2},{6,1},{7,0},{8,15},{9,14},{10,... | collective-permute-start | bytes 393224 | tf_op jit(solution)/shard_map/ppermute | solution.py:317
  32.7 7.8 %collective-permute-done.10.refs_3_ = bf16[128,512]{1,0:T(8,128)(2,1)S(1)} collective-permute-done((bf16[128,512]{1,0:T(8,128)(2,1)S(1)}, bf16[128,512]{1,0:T(8,128)(2,1)S(1)}, u32[]{:S(2)}, u32[]{:S(2)}) %collective-permute-start.10) | collective-permute-done | bytes 131104 | tf_op jit(solution)/shard_map/ppermute | solution.py:317
  40.6 8.4 %shard_map.142 = (f32[4,312,128]{2,1,0:T(8,128)S(1)}, bf16[128,2048]{1,0:T(8,128)(2,1)S(1)}, bf16[2048,1024]{1,0:T(8,128)(2,1)S(1)}, bf16[176,2048]{1,0:T(8,128)...) custom-call(s32[11]{0:T(128)S(1)} %pad_add_fusion.info, ...), custom_call_target="tpu_custom_call" | custom-call | tf_op jit(solution)/shard_map/pallas_call | solution.py:25
  49.1 1.5 %shard_map.143.keep = f32[4,312,128]{2,1,0:T(8,128)S(1)} custom-call(s32[11]{0:T(128)S(1)} %pad_add_fusion.info, bf16[128,2048]{1,0:T(8,128)(2,1)S(1)} %get-tuple-element.81.x_t, bf16[2048,1024]{1,0:T(8,128)(2,1)S(1)} %get-tuple-element.82.act, bf16[176,2048]{1,0:T(8,128)(2,1)S(1)} %get-tuple-element.83.dl_t, bf16[2048,1024]{1,0:T(8,128)(2,1)S(1)} %get-tuple-element.84.dpre, ...), custom_call_target="tpu_custom_call" | custom-call | tf_op jit(solution)/shard_map/pallas_call | solution.py:25
  51.2 1.6 %collective-permute-start.15 = (s16[320,128]{1,0:T(8,128)(2,1)S(1)}, s16[320,128]{1,0:T(8,128)(2,1)S(1)}, u32[]{:S(2)}, u32[]{:S(2)}) collective-permute-start(s16[320,128]{1,0:T(8,128)(2,1)S(1)} %get-tuple-element.89), channel_id=1, source_target_pairs={{0,8},{8,0},{16,24},{24,16},{1,9},{9,1},{17,25},{25,17},{2,10},{10... | collective-permute-start | bytes 245768 | tf_op jit(solution)/shard_map/ppermute | solution.py:317
  52.8 1.5 %collective-permute-start.16 = (s16[320,128]{1,0:T(8,128)(2,1)S(1)}, s16[320,128]{1,0:T(8,128)(2,1)S(1)}, u32[]{:S(2)}, u32[]{:S(2)}) collective-permute-start(s16[320,128]{1,0:T(8,128)(2,1)S(1)} %get-tuple-element.90), channel_id=1, source_target_pairs={{0,16},{8,24},{16,0},{24,8},{1,17},{9,25},{17,1},{25,9},{2,18},{10... | collective-permute-start | bytes 245768 | tf_op jit(solution)/shard_map/ppermute | solution.py:317
  54.8 1.0 %collective-permute-done.15.refs_0_ = s16[320,128]{1,0:T(8,128)(2,1)S(1)} collective-permute-done((s16[320,128]{1,0:T(8,128)(2,1)S(1)}, s16[320,128]{1,0:T(8,128)(2,1)S(1)}, u32[]{:S(2)}, u32[]{:S(2)}) %collective-permute-start.15) | collective-permute-done | bytes 81952 | tf_op jit(solution)/shard_map/ppermute | solution.py:317
  55.8 2.3 %collective-permute-done.16.refs_1_ = s16[320,128]{1,0:T(8,128)(2,1)S(1)} collective-permute-done((s16[320,128]{1,0:T(8,128)(2,1)S(1)}, s16[320,128]{1,0:T(8,128)(2,1)S(1)}, u32[]{:S(2)}, u32[]{:S(2)}) %collective-permute-start.16) | collective-permute-done | bytes 81952 | tf_op jit(solution)/shard_map/ppermute | solution.py:317
  58.1 1.6 %collective-permute-done.17.refs_2_ = s16[320,128]{1,0:T(8,128)(2,1)S(1)} collective-permute-done((s16[320,128]{1,0:T(8,128)(2,1)S(1)}, s16[320,128]{1,0:T(8,128)(2,1)S(1)}, u32[]{:S(2)}, u32[]{:S(2)}) %collective-permute-start.17) | collective-permute-done | bytes 81952 | tf_op jit(solution)/shard_map/ppermute | solution.py:317
  59.8 3.8 %collective-permute-start.18 = (s16[320,128]{1,0:T(8,128)(2,1)S(1)}, s16[320,128]{1,0:T(8,128)(2,1)S(1)}, u32[]{:S(2)}, u32[]{:S(2)}) collective-permute-start(s16[320,128]{1,0:T(8,128)(2,1)S(1)} %get-tuple-element.92), channel_id=1, source_target_pairs={{0,4},{1,5},{2,6},{3,7},{4,0},{5,1},{6,2},{7,3},{8,12},{9,13},{10,... | collective-permute-start | bytes 245768 | tf_op jit(solution)/shard_map/ppermute | solution.py:317
  63.6 1.9 %collective-permute-start.20 = (s16[320,128]{1,0:T(8,128)(2,1)S(1)}, s16[320,128]{1,0:T(8,128)(2,1)S(1)}, u32[]{:S(2)}, u32[]{:S(2)}) collective-permute-start(s16[320,128]{1,0:T(8,128)(2,1)S(1)} %get-tuple-element.94), channel_id=1, source_target_pairs={{0,6},{1,7},{2,4},{3,5},{4,2},{5,3},{6,0},{7,1},{8,14},{9,15},{10,... | collective-permute-start | bytes 245768 | tf_op jit(solution)/shard_map/ppermute | solution.py:317
  65.6 3.3 %collective-permute-done.18.refs_0_ = s16[320,128]{1,0:T(8,128)(2,1)S(1)} collective-permute-done((s16[320,128]{1,0:T(8,128)(2,1)S(1)}, s16[320,128]{1,0:T(8,128)(2,1)S(1)}, u32[]{:S(2)}, u32[]{:S(2)}) %collective-permute-start.18) | collective-permute-done | bytes 81952 | tf_op jit(solution)/shard_map/ppermute | solution.py:317
  68.9 1.1 %collective-permute-done.20.refs_2_ = s16[320,128]{1,0:T(8,128)(2,1)S(1)} collective-permute-done((s16[320,128]{1,0:T(8,128)(2,1)S(1)}, s16[320,128]{1,0:T(8,128)(2,1)S(1)}, u32[]{:S(2)}, u32[]{:S(2)}) %collective-permute-start.20) | collective-permute-done | bytes 81952 | tf_op jit(solution)/shard_map/ppermute | solution.py:317
  71.1 1.5 %collective-permute-start.22 = (s16[320,128]{1,0:T(8,128)(2,1)S(1)}, s16[320,128]{1,0:T(8,128)(2,1)S(1)}, u32[]{:S(2)}, u32[]{:S(2)}) collective-permute-start(s16[320,128]{1,0:T(8,128)(2,1)S(1)} %get-tuple-element.98), channel_id=1, source_target_pairs={{0,8},{8,0},{16,24},{24,16},{1,9},{9,1},{17,25},{25,17},{2,10},{10... | collective-permute-start | bytes 245768 | tf_op jit(solution)/shard_map/ppermute | solution.py:317
  72.5 1.2 %collective-permute-start.23 = (s16[320,128]{1,0:T(8,128)(2,1)S(1)}, s16[320,128]{1,0:T(8,128)(2,1)S(1)}, u32[]{:S(2)}, u32[]{:S(2)}) collective-permute-start(s16[320,128]{1,0:T(8,128)(2,1)S(1)} %get-tuple-element.99), channel_id=1, source_target_pairs={{0,16},{8,24},{16,0},{24,8},{1,17},{9,25},{17,1},{25,9},{2,18},{10... | collective-permute-start | bytes 245768 | tf_op jit(solution)/shard_map/ppermute | solution.py:317
  73.7 1.8 %collective-permute-done.21.refs_1_ = s16[320,128]{1,0:T(8,128)(2,1)S(1)} collective-permute-done((s16[320,128]{1,0:T(8,128)(2,1)S(1)}, s16[320,128]{1,0:T(8,128)(2,1)S(1)}, u32[]{:S(2)}, u32[]{:S(2)}) %collective-permute-start.21) | collective-permute-done | bytes 81952 | tf_op jit(solution)/shard_map/ppermute | solution.py:317
  77.1 1.1 %collective-permute-done.27.refs_7_ = s16[320,128]{1,0:T(8,128)(2,1)S(1)} collective-permute-done((s16[320,128]{1,0:T(8,128)(2,1)S(1)}, s16[320,128]{1,0:T(8,128)(2,1)S(1)}, u32[]{:S(2)}, u32[]{:S(2)}) %collective-permute-start.27) | collective-permute-done | bytes 81952 | tf_op jit(solution)/shard_map/ppermute | solution.py:317
  78.3 1.8 %shard_map.147 = (f32[128,1024]{1,0:T(8,128)}, f32[1,1024]{1,0:T(1,128)}, f32[172,1024]{1,0:T(8,128)}, f32[1,256]{1,0:T(1,128)}) custom-call(s32[11]{0:T(128)S(1)} %pad_add_fusion.info, s16[320,128]{1,0:T(8,128)(2,1)S(1)} %get-tuple-element.96.refs_0_, s16[320,128]{1,0:T(8,128)(2,1)S(1)} %collective-permute-done.21.refs_1_, ...), custom_call_target="tpu_custom_call" | custom-call | tf_op jit(solution)/shard_map/pallas_call | solution.py:25
  (52 shorter events, 12.7 us)
Async XLA Ops:
  2.9 8.7 %collective-permute-start = (bf16[144,128]{1,0:T(8,128)(2,1)S(1)}, bf16[144,128]{1,0:T(8,128)(2,1)S(1)}, u32[]{:S(2)}, u32[]{:S(2)}) collective-permute-start(bf16[144,128]{1,0:T(8,128)(2,1)S(1)} %get-tuple-element.58), channel_id=1, source_target_pairs={{0,4},{1,5},{2,6},{3,7},{4,0},{5,1},{6,2},{7,3},{8,12},{9,13},{10,... | collective-permute-start | bytes 110600 | tf_op jit(solution)/shard_map/ppermute | solution.py:317
  7.0 5.8 %collective-permute-start.1 = (bf16[144,128]{1,0:T(8,128)(2,1)S(1)}, bf16[144,128]{1,0:T(8,128)(2,1)S(1)}, u32[]{:S(2)}, u32[]{:S(2)}) collective-permute-start(bf16[144,128]{1,0:T(8,128)(2,1)S(1)} %get-tuple-element.59), channel_id=1, source_target_pairs={{0,6},{1,7},{2,4},{3,5},{4,2},{5,3},{6,0},{7,1},{8,14},{9,15},{10,... | collective-permute-start | bytes 110600 | tf_op jit(solution)/shard_map/ppermute | solution.py:317
  8.3 6.5 %collective-permute-start.2 = (bf16[144,128]{1,0:T(8,128)(2,1)S(1)}, bf16[144,128]{1,0:T(8,128)(2,1)S(1)}, u32[]{:S(2)}, u32[]{:S(2)}) collective-permute-start(bf16[144,128]{1,0:T(8,128)(2,1)S(1)} %get-tuple-element.60), channel_id=1, source_target_pairs={{0,5},{1,4},{2,7},{3,6},{4,1},{5,0},{6,3},{7,2},{8,13},{9,12},{10,... | collective-permute-start | bytes 110600 | tf_op jit(solution)/shard_map/ppermute | solution.py:317
  8.9 6.0 %collective-permute-start.3 = (bf16[144,128]{1,0:T(8,128)(2,1)S(1)}, bf16[144,128]{1,0:T(8,128)(2,1)S(1)}, u32[]{:S(2)}, u32[]{:S(2)}) collective-permute-start(bf16[144,128]{1,0:T(8,128)(2,1)S(1)} %get-tuple-element.61), channel_id=1, source_target_pairs={{0,7},{1,6},{2,5},{3,4},{4,3},{5,2},{6,1},{7,0},{8,15},{9,14},{10,... | collective-permute-start | bytes 110600 | tf_op jit(solution)/shard_map/ppermute | solution.py:317
  10.6 4.5 %collective-permute-start.4 = (bf16[144,128]{1,0:T(8,128)(2,1)S(1)}, bf16[144,128]{1,0:T(8,128)(2,1)S(1)}, u32[]{:S(2)}, u32[]{:S(2)}) collective-permute-start(bf16[144,128]{1,0:T(8,128)(2,1)S(1)} %get-tuple-element.62), channel_id=1, source_target_pairs={{0,2},{1,3},{2,0},{3,1},{4,6},{5,7},{6,4},{7,5},{8,10},{9,11},{10,... | collective-permute-start | bytes 110600 | tf_op jit(solution)/shard_map/ppermute | solution.py:317
  11.5 4.7 %collective-permute-start.5 = (bf16[144,128]{1,0:T(8,128)(2,1)S(1)}, bf16[144,128]{1,0:T(8,128)(2,1)S(1)}, u32[]{:S(2)}, u32[]{:S(2)}) collective-permute-start(bf16[144,128]{1,0:T(8,128)(2,1)S(1)} %get-tuple-element.63), channel_id=1, source_target_pairs={{0,3},{1,2},{2,1},{3,0},{4,7},{5,6},{6,5},{7,4},{8,11},{9,10},{10,... | collective-permute-start | bytes 110600 | tf_op jit(solution)/shard_map/ppermute | solution.py:317
  12.8 3.5 %collective-permute-start.6 = (bf16[144,128]{1,0:T(8,128)(2,1)S(1)}, bf16[144,128]{1,0:T(8,128)(2,1)S(1)}, u32[]{:S(2)}, u32[]{:S(2)}) collective-permute-start(bf16[144,128]{1,0:T(8,128)(2,1)S(1)} %get-tuple-element.64), channel_id=1, source_target_pairs={{0,1},{1,0},{2,3},{3,2},{4,5},{5,4},{6,7},{7,6},{8,9},{9,8},{10,11... | collective-permute-start | bytes 110600 | tf_op jit(solution)/shard_map/ppermute | solution.py:317
  12.8 1.0 %copy-start = (bf16[1,4,4,128,128]{4,3,2,1,0:T(8,128)(2,1)S(1)}, bf16[1,4,4,128,128]{4,3,2,1,0:T(8,128)(2,1)}, u32[]{:S(2)}) copy-start(bf16[1,4,4,128,128]{4,3,2,1,0:T(8,128)(2,1)} %param.15) | copy-start | bytes 1572868
  17.8 12.5 %collective-permute-start.7 = (bf16[128,512]{1,0:T(8,128)(2,1)S(1)}, bf16[128,512]{1,0:T(8,128)(2,1)S(1)}, u32[]{:S(2)}, u32[]{:S(2)}) collective-permute-start(bf16[128,512]{1,0:T(8,128)(2,1)S(1)} %get-tuple-element.74), channel_id=1, source_target_pairs={{0,4},{1,5},{2,6},{3,7},{4,0},{5,1},{6,2},{7,3},{8,12},{9,13},{10,... | collective-permute-start | bytes 393224 | tf_op jit(solution)/shard_map/ppermute | solution.py:317
  19.1 11.2 %collective-permute-start.8 = (bf16[128,512]{1,0:T(8,128)(2,1)S(1)}, bf16[128,512]{1,0:T(8,128)(2,1)S(1)}, u32[]{:S(2)}, u32[]{:S(2)}) collective-permute-start(bf16[128,512]{1,0:T(8,128)(2,1)S(1)} %get-tuple-element.75), channel_id=1, source_target_pairs={{0,6},{1,7},{2,4},{3,5},{4,2},{5,3},{6,0},{7,1},{8,14},{9,15},{10,... | collective-permute-start | bytes 393224 | tf_op jit(solution)/shard_map/ppermute | solution.py:317
  20.3 12.5 %collective-permute-start.9 = (bf16[128,512]{1,0:T(8,128)(2,1)S(1)}, bf16[128,512]{1,0:T(8,128)(2,1)S(1)}, u32[]{:S(2)}, u32[]{:S(2)}) collective-permute-start(bf16[128,512]{1,0:T(8,128)(2,1)S(1)} %get-tuple-element.76), channel_id=1, source_target_pairs={{0,2},{1,3},{2,0},{3,1},{4,6},{5,7},{6,4},{7,5},{8,10},{9,11},{10,... | collective-permute-start | bytes 393224 | tf_op jit(solution)/shard_map/ppermute | solution.py:317
  21.3 19.2 %collective-permute-start.10 = (bf16[128,512]{1,0:T(8,128)(2,1)S(1)}, bf16[128,512]{1,0:T(8,128)(2,1)S(1)}, u32[]{:S(2)}, u32[]{:S(2)}) collective-permute-start(bf16[128,512]{1,0:T(8,128)(2,1)S(1)} %get-tuple-element.77), channel_id=1, source_target_pairs={{0,5},{1,4},{2,7},{3,6},{4,1},{5,0},{6,3},{7,2},{8,13},{9,12},{10,... | collective-permute-start | bytes 393224 | tf_op jit(solution)/shard_map/ppermute | solution.py:317
  21.6 18.9 %collective-permute-start.12 = (bf16[128,512]{1,0:T(8,128)(2,1)S(1)}, bf16[128,512]{1,0:T(8,128)(2,1)S(1)}, u32[]{:S(2)}, u32[]{:S(2)}) collective-permute-start(bf16[128,512]{1,0:T(8,128)(2,1)S(1)} %get-tuple-element.79), channel_id=1, source_target_pairs={{0,3},{1,2},{2,1},{3,0},{4,7},{5,6},{6,5},{7,4},{8,11},{9,10},{10,... | collective-permute-start | bytes 393224 | tf_op jit(solution)/shard_map/ppermute | solution.py:317
  23.3 1.0 %copy-start.1 = (bf16[1024,172]{0,1:T(8,128)(2,1)S(1)}, bf16[1024,172]{0,1:T(8,128)(2,1)}, u32[]{:S(2)}) copy-start(bf16[1024,172]{0,1:T(8,128)(2,1)} %param.20) | copy-start | bytes 1056772
  24.3 0.9 %copy-start.2 = (bf16[128,1024]{1,0:T(8,128)(2,1)S(1)}, bf16[128,1024]{1,0:T(8,128)(2,1)}, u32[]{:S(2)}) copy-start(bf16[128,1024]{1,0:T(8,128)(2,1)} %w_in.1) | copy-start | bytes 786436
  25.3 0.7 copy-start.3
  30.3 10.2 %collective-permute-start.13 = (bf16[128,512]{1,0:T(8,128)(2,1)S(1)}, bf16[128,512]{1,0:T(8,128)(2,1)S(1)}, u32[]{:S(2)}, u32[]{:S(2)}) collective-permute-start(bf16[128,512]{1,0:T(8,128)(2,1)S(1)} %get-tuple-element.80), channel_id=1, source_target_pairs={{0,1},{1,0},{2,3},{3,2},{4,5},{5,4},{6,7},{7,6},{8,9},{9,8},{10,11... | collective-permute-start | bytes 393224 | tf_op jit(solution)/shard_map/ppermute | solution.py:317
  30.3 10.2 %collective-permute-start.11 = (bf16[128,512]{1,0:T(8,128)(2,1)S(1)}, bf16[128,512]{1,0:T(8,128)(2,1)S(1)}, u32[]{:S(2)}, u32[]{:S(2)}) collective-permute-start(bf16[128,512]{1,0:T(8,128)(2,1)S(1)} %get-tuple-element.78), channel_id=1, source_target_pairs={{0,7},{1,6},{2,5},{3,4},{4,3},{5,2},{6,1},{7,0},{8,15},{9,14},{10,... | collective-permute-start | bytes 393224 | tf_op jit(solution)/shard_map/ppermute | solution.py:317
  48.9 2.1 %collective-permute-start.14 = (f32[4,312,128]{2,1,0:T(8,128)S(1)}, f32[4,312,128]{2,1,0:T(8,128)S(1)}, u32[]{:S(2)}, u32[]{:S(2)}) collective-permute-start(f32[4,312,128]{2,1,0:T(8,128)S(1)} %get-tuple-element.87), channel_id=1, source_target_pairs={{0,1},{1,0},{2,3},{3,2},{4,5},{5,4},{6,7},{7,6},{8,9},{9,8},{10,11... | collective-permute-start | bytes 1916936 | tf_op jit(solution)/shard_map/ppermute | solution.py:317
  51.2 4.6 %collective-permute-start.15 = (s16[320,128]{1,0:T(8,128)(2,1)S(1)}, s16[320,128]{1,0:T(8,128)(2,1)S(1)}, u32[]{:S(2)}, u32[]{:S(2)}) collective-permute-start(s16[320,128]{1,0:T(8,128)(2,1)S(1)} %get-tuple-element.89), channel_id=1, source_target_pairs={{0,8},{8,0},{16,24},{24,16},{1,9},{9,1},{17,25},{25,17},{2,10},{10... | collective-permute-start | bytes 245768 | tf_op jit(solution)/shard_map/ppermute | solution.py:317
  52.8 5.3 %collective-permute-start.16 = (s16[320,128]{1,0:T(8,128)(2,1)S(1)}, s16[320,128]{1,0:T(8,128)(2,1)S(1)}, u32[]{:S(2)}, u32[]{:S(2)}) collective-permute-start(s16[320,128]{1,0:T(8,128)(2,1)S(1)} %get-tuple-element.90), channel_id=1, source_target_pairs={{0,16},{8,24},{16,0},{24,8},{1,17},{9,25},{17,1},{25,9},{2,18},{10... | collective-permute-start | bytes 245768 | tf_op jit(solution)/shard_map/ppermute | solution.py:317
  54.3 5.3 %collective-permute-start.17 = (s16[320,128]{1,0:T(8,128)(2,1)S(1)}, s16[320,128]{1,0:T(8,128)(2,1)S(1)}, u32[]{:S(2)}, u32[]{:S(2)}) collective-permute-start(s16[320,128]{1,0:T(8,128)(2,1)S(1)} %get-tuple-element.91), channel_id=1, source_target_pairs={{0,24},{8,16},{16,8},{24,0},{1,25},{9,17},{17,9},{25,1},{2,26},{10... | collective-permute-start | bytes 245768 | tf_op jit(solution)/shard_map/ppermute | solution.py:317
  59.8 9.1 %collective-permute-start.18 = (s16[320,128]{1,0:T(8,128)(2,1)S(1)}, s16[320,128]{1,0:T(8,128)(2,1)S(1)}, u32[]{:S(2)}, u32[]{:S(2)}) collective-permute-start(s16[320,128]{1,0:T(8,128)(2,1)S(1)} %get-tuple-element.92), channel_id=1, source_target_pairs={{0,4},{1,5},{2,6},{3,7},{4,0},{5,1},{6,2},{7,3},{8,12},{9,13},{10,... | collective-permute-start | bytes 245768 | tf_op jit(solution)/shard_map/ppermute | solution.py:317
  63.6 5.2 %collective-permute-start.19 = (s16[320,128]{1,0:T(8,128)(2,1)S(1)}, s16[320,128]{1,0:T(8,128)(2,1)S(1)}, u32[]{:S(2)}, u32[]{:S(2)}) collective-permute-start(s16[320,128]{1,0:T(8,128)(2,1)S(1)} %get-tuple-element.93), channel_id=1, source_target_pairs={{0,2},{1,3},{2,0},{3,1},{4,6},{5,7},{6,4},{7,5},{8,10},{9,11},{10,... | collective-permute-start | bytes 245768 | tf_op jit(solution)/shard_map/ppermute | solution.py:317
  63.6 6.4 %collective-permute-start.20 = (s16[320,128]{1,0:T(8,128)(2,1)S(1)}, s16[320,128]{1,0:T(8,128)(2,1)S(1)}, u32[]{:S(2)}, u32[]{:S(2)}) collective-permute-start(s16[320,128]{1,0:T(8,128)(2,1)S(1)} %get-tuple-element.94), channel_id=1, source_target_pairs={{0,6},{1,7},{2,4},{3,5},{4,2},{5,3},{6,0},{7,1},{8,14},{9,15},{10,... | collective-permute-start | bytes 245768 | tf_op jit(solution)/shard_map/ppermute | solution.py:317
  70.2 5.4 %collective-permute-start.21 = (s16[320,128]{1,0:T(8,128)(2,1)S(1)}, s16[320,128]{1,0:T(8,128)(2,1)S(1)}, u32[]{:S(2)}, u32[]{:S(2)}) collective-permute-start(s16[320,128]{1,0:T(8,128)(2,1)S(1)} %get-tuple-element.97), channel_id=1, source_target_pairs={{0,24},{8,16},{16,8},{24,0},{1,25},{9,17},{17,9},{25,1},{2,26},{10... | collective-permute-start | bytes 245768 | tf_op jit(solution)/shard_map/ppermute | solution.py:317
  71.1 4.8 %collective-permute-start.22 = (s16[320,128]{1,0:T(8,128)(2,1)S(1)}, s16[320,128]{1,0:T(8,128)(2,1)S(1)}, u32[]{:S(2)}, u32[]{:S(2)}) collective-permute-start(s16[320,128]{1,0:T(8,128)(2,1)S(1)} %get-tuple-element.98), channel_id=1, source_target_pairs={{0,8},{8,0},{16,24},{24,16},{1,9},{9,1},{17,25},{25,17},{2,10},{10... | collective-permute-start | bytes 245768 | tf_op jit(solution)/shard_map/ppermute | solution.py:317
  72.5 4.4 %collective-permute-start.23 = (s16[320,128]{1,0:T(8,128)(2,1)S(1)}, s16[320,128]{1,0:T(8,128)(2,1)S(1)}, u32[]{:S(2)}, u32[]{:S(2)}) collective-permute-start(s16[320,128]{1,0:T(8,128)(2,1)S(1)} %get-tuple-element.99), channel_id=1, source_target_pairs={{0,16},{8,24},{16,0},{24,8},{1,17},{9,25},{17,1},{25,9},{2,18},{10... | collective-permute-start | bytes 245768 | tf_op jit(solution)/shard_map/ppermute | solution.py:317
  73.7 3.3 %collective-permute-start.24 = (s16[320,128]{1,0:T(8,128)(2,1)S(1)}, s16[320,128]{1,0:T(8,128)(2,1)S(1)}, u32[]{:S(2)}, u32[]{:S(2)}) collective-permute-start(s16[320,128]{1,0:T(8,128)(2,1)S(1)} %get-tuple-element.96.refs_0_), channel_id=1, source_target_pairs={{0,1},{1,0},{2,3},{3,2},{4,5},{5,4},{6,7},{7,6},{8,9},{9,8},{10,11... | collective-permute-start | bytes 245768 | tf_op jit(solution)/shard_map/ppermute | solution.py:317
  75.6 1.4 %collective-permute-start.25 = (s16[320,128]{1,0:T(8,128)(2,1)S(1)}, s16[320,128]{1,0:T(8,128)(2,1)S(1)}, u32[]{:S(2)}, u32[]{:S(2)}) collective-permute-start(s16[320,128]{1,0:T(8,128)(2,1)S(1)} %collective-permute-done.21.refs_1_), channel_id=1, source_target_pairs={{0,1},{1,0},{2,3},{3,2},{4,5},{5,4},{6,7},{7,6},{8,9},{9,8},{10,11... | collective-permute-start | bytes 245768 | tf_op jit(solution)/shard_map/ppermute | solution.py:317
  75.8 1.3 %collective-permute-start.26 = (s16[320,128]{1,0:T(8,128)(2,1)S(1)}, s16[320,128]{1,0:T(8,128)(2,1)S(1)}, u32[]{:S(2)}, u32[]{:S(2)}) collective-permute-start(s16[320,128]{1,0:T(8,128)(2,1)S(1)} %collective-permute-done.22.refs_2_), channel_id=1, source_target_pairs={{0,1},{1,0},{2,3},{3,2},{4,5},{5,4},{6,7},{7,6},{8,9},{9,8},{10,11... | collective-permute-start | bytes 245768 | tf_op jit(solution)/shard_map/ppermute | solution.py:317
  77.0 1.3 %collective-permute-start.27 = (s16[320,128]{1,0:T(8,128)(2,1)S(1)}, s16[320,128]{1,0:T(8,128)(2,1)S(1)}, u32[]{:S(2)}, u32[]{:S(2)}) collective-permute-start(s16[320,128]{1,0:T(8,128)(2,1)S(1)} %collective-permute-done.23.refs_3_), channel_id=1, source_target_pairs={{0,1},{1,0},{2,3},{3,2},{4,5},{5,4},{6,7},{7,6},{8,9},{9,8},{10,11... | collective-permute-start | bytes 245768 | tf_op jit(solution)/shard_map/ppermute | solution.py:317
  (4 other events, 2.7 us)

commit v9 on v8

--- a/solution.py
+++ b/solution.py
@@ -41,7 +41,13 @@
 
 
 def partners(dom):
-    return [k for odd in (0, 1) for top in tops(dom) for k in range(top, 2 * top) if k % 2 == odd]
+    masks = []
+    for odd in (0, 1):
+        far = [k for k in range(dom // 2, dom) if k % 2 == odd]
+        near = [k for k in range(dom // 2 - 1, 0, -1) if k % 2 == odd]
+        for i in range(len(far)):
+            masks += far[i : i + 1] + near[i : i + 1]
+    return masks
 
 
 def partners_1(dom):

time: 80.4 us -> 80.5 us (level)
  starting transfers between devices: 30.6 us -> 27.4 us
  waiting for transfers between devices: 25.9 us -> 29.1 us
    ppermute x28, waiting for transfers between devices: 25.9 us -> 29.1 us  [xor_permute(): lax.ppermute(x, axis, [(i, i ^ mask) for i in range(lax.axis_size(axis))])]
    ppermute x28, starting transfers between devices: 30.6 us -> 27.4 us  [xor_permute(): lax.ppermute(x, axis, [(i, i ^ mask) for i in range(lax.axis_size(axis))])]
  transfers between devices with their start and end apart: 28 -> 28, of which waited for: 16 -> 17; matrix products, arithmetic and copies ran while one was open for 0% -> 0% of each run, Pallas kernels for 3% -> 3%
where the time goes in v9:
time: 80.5 us; the launch traced here: 80.1 us
  waiting for transfers between devices  29.1 us (36%)
  starting transfers between devices  27.4 us (34%)
  Pallas kernels  14.7 us (18%)
  local copies, waits for them, and re-layouts  6.38 us (8%)
  other arithmetic  1.67 us (2%)
    ppermute x28, waiting for transfers between devices, xor_permute(): lax.ppermute(x, axis, [(i, i ^ mask) for i in range(lax.axis_size(axis))])  29.1 us
    ppermute x28, starting transfers between devices, xor_permute(): lax.ppermute(x, axis, [(i, i ^ mask) for i in range(lax.axis_size(axis))])  27.4 us
    pallas_call x10, Pallas kernels, call(): pl.pallas_call(kernel, out_shape=outs, in_specs=[SMEM] * n_smem + [VMEM]...  14.7 us
    unnamed x16, local copies, waits for them, and re-layouts  6.38 us
  transfers between devices with their start and end apart: 28, of which 17 were waited for; matrix products, arithmetic and copies ran while one was open for 0% of the time, Pallas kernels for 3%

profile of v9, /device:TPU:0, one launch (start us, length us, event | category | flops | bytes accessed | tf_op | source)
XLA Modules:
  0.0 80.1 jit_solution(7159356901280583684)
XLA Ops:
  0.6 0.9 %fusion.1.tiles = bf16[4,144,128]{2,1,0:T(8,128)(2,1)S(1)} fusion(bf16[4,4,128]{2,1,0:T(4,128)(2,1)} %bitcast.27, bf16[4,128,128]{2,1,0:T(8,128)(2,1)} %bitcast.26), kind=kLoop, calls=%fused_computation.2 | loop fusion | flops 442368 | bytes 282624 | tf_op jit(solution)/shard_map/concatenate | solution.py:392
  2.9 4.1 %collective-permute-start = (bf16[144,128]{1,0:T(8,128)(2,1)S(1)}, bf16[144,128]{1,0:T(8,128)(2,1)S(1)}, u32[]{:S(2)}, u32[]{:S(2)}) collective-permute-start(bf16[144,128]{1,0:T(8,128)(2,1)S(1)} %get-tuple-element.58), channel_id=1, source_target_pairs={{0,4},{1,5},{2,6},{3,7},{4,0},{5,1},{6,2},{7,3},{8,12},{9,13},{10,... | collective-permute-start | bytes 110600 | tf_op jit(solution)/shard_map/ppermute | solution.py:323
  7.0 1.3 %collective-permute-start.1 = (bf16[144,128]{1,0:T(8,128)(2,1)S(1)}, bf16[144,128]{1,0:T(8,128)(2,1)S(1)}, u32[]{:S(2)}, u32[]{:S(2)}) collective-permute-start(bf16[144,128]{1,0:T(8,128)(2,1)S(1)} %get-tuple-element.59), channel_id=1, source_target_pairs={{0,6},{1,7},{2,4},{3,5},{4,2},{5,3},{6,0},{7,1},{8,14},{9,15},{10,... | collective-permute-start | bytes 110600 | tf_op jit(solution)/shard_map/ppermute | solution.py:323
  8.9 1.7 %collective-permute-start.3 = (bf16[144,128]{1,0:T(8,128)(2,1)S(1)}, bf16[144,128]{1,0:T(8,128)(2,1)S(1)}, u32[]{:S(2)}, u32[]{:S(2)}) collective-permute-start(bf16[144,128]{1,0:T(8,128)(2,1)S(1)} %get-tuple-element.61), channel_id=1, source_target_pairs={{0,7},{1,6},{2,5},{3,4},{4,3},{5,2},{6,1},{7,0},{8,15},{9,14},{10,... | collective-permute-start | bytes 110600 | tf_op jit(solution)/shard_map/ppermute | solution.py:323
  12.8 1.0 %copy-done = bf16[1,4,4,128,128]{4,3,2,1,0:T(8,128)(2,1)S(1)} copy-done((bf16[1,4,4,128,128]{4,3,2,1,0:T(8,128)(2,1)S(1)}, bf16[1,4,4,128,128]{4,3,2,1,0:T(8,128)(2,1)}, u32[]{:S(2)}) %copy-start) | copy-done | bytes 524312
  15.2 1.0 %collective-permute-done.5.refs_5_ = bf16[144,128]{1,0:T(8,128)(2,1)S(1)} collective-permute-done((bf16[144,128]{1,0:T(8,128)(2,1)S(1)}, bf16[144,128]{1,0:T(8,128)(2,1)S(1)}, u32[]{:S(2)}, u32[]{:S(2)}) %collective-permute-start.5) | collective-permute-done | bytes 36896 | tf_op jit(solution)/shard_map/ppermute | solution.py:323
  16.2 1.5 %shard_map.140 = (bf16[4,128,512]{2,1,0:T(8,128)(2,1)S(1)}, f32[4,128,512]{2,1,0:T(8,128)S(1)}, bf16[128,512]{1,0:T(8,128)(2,1)S(1)}, bf16[128,512]{1,0:T(8,128)...) custom-call(s32[11]{0:T(128)S(1)} %pad_add_fusion.info, ...), custom_call_target="tpu_custom_call" | custom-call | tf_op jit(solution)/shard_map/pallas_call | solution.py:25
  17.8 1.4 %collective-permute-start.7 = (bf16[128,512]{1,0:T(8,128)(2,1)S(1)}, bf16[128,512]{1,0:T(8,128)(2,1)S(1)}, u32[]{:S(2)}, u32[]{:S(2)}) collective-permute-start(bf16[128,512]{1,0:T(8,128)(2,1)S(1)} %get-tuple-element.74), channel_id=1, source_target_pairs={{0,4},{1,5},{2,6},{3,7},{4,0},{5,1},{6,2},{7,3},{8,12},{9,13},{10,... | collective-permute-start | bytes 393224 | tf_op jit(solution)/shard_map/ppermute | solution.py:323
  19.1 1.0 %collective-permute-start.8 = (bf16[128,512]{1,0:T(8,128)(2,1)S(1)}, bf16[128,512]{1,0:T(8,128)(2,1)S(1)}, u32[]{:S(2)}, u32[]{:S(2)}) collective-permute-start(bf16[128,512]{1,0:T(8,128)(2,1)S(1)} %get-tuple-element.75), channel_id=1, source_target_pairs={{0,2},{1,3},{2,0},{3,1},{4,6},{5,7},{6,4},{7,5},{8,10},{9,11},{10,... | collective-permute-start | bytes 393224 | tf_op jit(solution)/shard_map/ppermute | solution.py:323
  20.1 2.1 %collective-permute-start.9 = (bf16[128,512]{1,0:T(8,128)(2,1)S(1)}, bf16[128,512]{1,0:T(8,128)(2,1)S(1)}, u32[]{:S(2)}, u32[]{:S(2)}) collective-permute-start(bf16[128,512]{1,0:T(8,128)(2,1)S(1)} %get-tuple-element.76), channel_id=1, source_target_pairs={{0,6},{1,7},{2,4},{3,5},{4,2},{5,3},{6,0},{7,1},{8,14},{9,15},{10,... | collective-permute-start | bytes 393224 | tf_op jit(solution)/shard_map/ppermute | solution.py:323
  22.2 1.2 %collective-permute-start.12 = (bf16[128,512]{1,0:T(8,128)(2,1)S(1)}, bf16[128,512]{1,0:T(8,128)(2,1)S(1)}, u32[]{:S(2)}, u32[]{:S(2)}) collective-permute-start(bf16[128,512]{1,0:T(8,128)(2,1)S(1)} %get-tuple-element.79), channel_id=1, source_target_pairs={{0,7},{1,6},{2,5},{3,4},{4,3},{5,2},{6,1},{7,0},{8,15},{9,14},{10,... | collective-permute-start | bytes 393224 | tf_op jit(solution)/shard_map/ppermute | solution.py:323
  23.5 1.0 %copy-done.1 = bf16[1024,172]{0,1:T(8,128)(2,1)S(1)} copy-done((bf16[1024,172]{0,1:T(8,128)(2,1)S(1)}, bf16[1024,172]{0,1:T(8,128)(2,1)}, u32[]{:S(2)}) %copy-start.1) | copy-done | bytes 352280
  24.5 0.9 %copy-done.2 = bf16[128,1024]{1,0:T(8,128)(2,1)S(1)} copy-done((bf16[128,1024]{1,0:T(8,128)(2,1)S(1)}, bf16[128,1024]{1,0:T(8,128)(2,1)}, u32[]{:S(2)}) %copy-start.2) | copy-done | bytes 262168
  28.4 6.0 %collective-permute-done.7.refs_0_ = bf16[128,512]{1,0:T(8,128)(2,1)S(1)} collective-permute-done((bf16[128,512]{1,0:T(8,128)(2,1)S(1)}, bf16[128,512]{1,0:T(8,128)(2,1)S(1)}, u32[]{:S(2)}, u32[]{:S(2)}) %collective-permute-start.7) | collective-permute-done | bytes 131104 | tf_op jit(solution)/shard_map/ppermute | solution.py:323
  34.4 6.3 %collective-permute-done.10.refs_3_ = bf16[128,512]{1,0:T(8,128)(2,1)S(1)} collective-permute-done((bf16[128,512]{1,0:T(8,128)(2,1)S(1)}, bf16[128,512]{1,0:T(8,128)(2,1)S(1)}, u32[]{:S(2)}, u32[]{:S(2)}) %collective-permute-start.10) | collective-permute-done | bytes 131104 | tf_op jit(solution)/shard_map/ppermute | solution.py:323
  40.7 1.7 %collective-permute-done.11.refs_4_ = bf16[128,512]{1,0:T(8,128)(2,1)S(1)} collective-permute-done((bf16[128,512]{1,0:T(8,128)(2,1)S(1)}, bf16[128,512]{1,0:T(8,128)(2,1)S(1)}, u32[]{:S(2)}, u32[]{:S(2)}) %collective-permute-start.11) | collective-permute-done | bytes 131104 | tf_op jit(solution)/shard_map/ppermute | solution.py:323
  42.4 8.3 %shard_map.142 = (f32[4,312,128]{2,1,0:T(8,128)S(1)}, bf16[128,2048]{1,0:T(8,128)(2,1)S(1)}, bf16[2048,1024]{1,0:T(8,128)(2,1)S(1)}, bf16[176,2048]{1,0:T(8,128)...) custom-call(s32[11]{0:T(128)S(1)} %pad_add_fusion.info, ...), custom_call_target="tpu_custom_call" | custom-call | tf_op jit(solution)/shard_map/pallas_call | solution.py:25
  51.2 1.5 %shard_map.143.keep = f32[4,312,128]{2,1,0:T(8,128)S(1)} custom-call(s32[11]{0:T(128)S(1)} %pad_add_fusion.info, bf16[128,2048]{1,0:T(8,128)(2,1)S(1)} %get-tuple-element.81.x_t, bf16[2048,1024]{1,0:T(8,128)(2,1)S(1)} %get-tuple-element.82.act, bf16[176,2048]{1,0:T(8,128)(2,1)S(1)} %get-tuple-element.83.dl_t, bf16[2048,1024]{1,0:T(8,128)(2,1)S(1)} %get-tuple-element.84.dpre, ...), custom_call_target="tpu_custom_call" | custom-call | tf_op jit(solution)/shard_map/pallas_call | solution.py:25
  53.1 1.6 %collective-permute-start.15 = (s16[320,128]{1,0:T(8,128)(2,1)S(1)}, s16[320,128]{1,0:T(8,128)(2,1)S(1)}, u32[]{:S(2)}, u32[]{:S(2)}) collective-permute-start(s16[320,128]{1,0:T(8,128)(2,1)S(1)} %get-tuple-element.89), channel_id=1, source_target_pairs={{0,8},{8,0},{16,24},{24,16},{1,9},{9,1},{17,25},{25,17},{2,10},{10... | collective-permute-start | bytes 245768 | tf_op jit(solution)/shard_map/ppermute | solution.py:323
  54.6 1.5 %collective-permute-start.16 = (s16[320,128]{1,0:T(8,128)(2,1)S(1)}, s16[320,128]{1,0:T(8,128)(2,1)S(1)}, u32[]{:S(2)}, u32[]{:S(2)}) collective-permute-start(s16[320,128]{1,0:T(8,128)(2,1)S(1)} %get-tuple-element.90), channel_id=1, source_target_pairs={{0,16},{8,24},{16,0},{24,8},{1,17},{9,25},{17,1},{25,9},{2,18},{10... | collective-permute-start | bytes 245768 | tf_op jit(solution)/shard_map/ppermute | solution.py:323
  56.6 1.2 %collective-permute-done.15.refs_0_ = s16[320,128]{1,0:T(8,128)(2,1)S(1)} collective-permute-done((s16[320,128]{1,0:T(8,128)(2,1)S(1)}, s16[320,128]{1,0:T(8,128)(2,1)S(1)}, u32[]{:S(2)}, u32[]{:S(2)}) %collective-permute-start.15) | collective-permute-done | bytes 81952 | tf_op jit(solution)/shard_map/ppermute | solution.py:323
  57.8 2.1 %collective-permute-done.16.refs_1_ = s16[320,128]{1,0:T(8,128)(2,1)S(1)} collective-permute-done((s16[320,128]{1,0:T(8,128)(2,1)S(1)}, s16[320,128]{1,0:T(8,128)(2,1)S(1)}, u32[]{:S(2)}, u32[]{:S(2)}) %collective-permute-start.16) | collective-permute-done | bytes 81952 | tf_op jit(solution)/shard_map/ppermute | solution.py:323
  59.9 1.6 %collective-permute-done.17.refs_2_ = s16[320,128]{1,0:T(8,128)(2,1)S(1)} collective-permute-done((s16[320,128]{1,0:T(8,128)(2,1)S(1)}, s16[320,128]{1,0:T(8,128)(2,1)S(1)}, u32[]{:S(2)}, u32[]{:S(2)}) %collective-permute-start.17) | collective-permute-done | bytes 81952 | tf_op jit(solution)/shard_map/ppermute | solution.py:323
  61.6 2.0 %collective-permute-start.18 = (s16[320,128]{1,0:T(8,128)(2,1)S(1)}, s16[320,128]{1,0:T(8,128)(2,1)S(1)}, u32[]{:S(2)}, u32[]{:S(2)}) collective-permute-start(s16[320,128]{1,0:T(8,128)(2,1)S(1)} %get-tuple-element.92), channel_id=1, source_target_pairs={{0,4},{1,5},{2,6},{3,7},{4,0},{5,1},{6,2},{7,3},{8,12},{9,13},{10,... | collective-permute-start | bytes 245768 | tf_op jit(solution)/shard_map/ppermute | solution.py:323
  63.7 2.4 %collective-permute-start.20 = (s16[320,128]{1,0:T(8,128)(2,1)S(1)}, s16[320,128]{1,0:T(8,128)(2,1)S(1)}, u32[]{:S(2)}, u32[]{:S(2)}) collective-permute-start(s16[320,128]{1,0:T(8,128)(2,1)S(1)} %get-tuple-element.94), channel_id=1, source_target_pairs={{0,6},{1,7},{2,4},{3,5},{4,2},{5,3},{6,0},{7,1},{8,14},{9,15},{10,... | collective-permute-start | bytes 245768 | tf_op jit(solution)/shard_map/ppermute | solution.py:323
  66.1 3.0 %collective-permute-done.18.refs_0_ = s16[320,128]{1,0:T(8,128)(2,1)S(1)} collective-permute-done((s16[320,128]{1,0:T(8,128)(2,1)S(1)}, s16[320,128]{1,0:T(8,128)(2,1)S(1)}, u32[]{:S(2)}, u32[]{:S(2)}) %collective-permute-start.18) | collective-permute-done | bytes 81952 | tf_op jit(solution)/shard_map/ppermute | solution.py:323
  69.1 0.9 %collective-permute-done.20.refs_2_ = s16[320,128]{1,0:T(8,128)(2,1)S(1)} collective-permute-done((s16[320,128]{1,0:T(8,128)(2,1)S(1)}, s16[320,128]{1,0:T(8,128)(2,1)S(1)}, u32[]{:S(2)}, u32[]{:S(2)}) %collective-permute-start.20) | collective-permute-done | bytes 81952 | tf_op jit(solution)/shard_map/ppermute | solution.py:323
  71.1 1.4 %collective-permute-start.22 = (s16[320,128]{1,0:T(8,128)(2,1)S(1)}, s16[320,128]{1,0:T(8,128)(2,1)S(1)}, u32[]{:S(2)}, u32[]{:S(2)}) collective-permute-start(s16[320,128]{1,0:T(8,128)(2,1)S(1)} %get-tuple-element.98), channel_id=1, source_target_pairs={{0,8},{8,0},{16,24},{24,16},{1,9},{9,1},{17,25},{25,17},{2,10},{10... | collective-permute-start | bytes 245768 | tf_op jit(solution)/shard_map/ppermute | solution.py:323
  72.5 1.2 %collective-permute-start.23 = (s16[320,128]{1,0:T(8,128)(2,1)S(1)}, s16[320,128]{1,0:T(8,128)(2,1)S(1)}, u32[]{:S(2)}, u32[]{:S(2)}) collective-permute-start(s16[320,128]{1,0:T(8,128)(2,1)S(1)} %get-tuple-element.99), channel_id=1, source_target_pairs={{0,16},{8,24},{16,0},{24,8},{1,17},{9,25},{17,1},{25,9},{2,18},{10... | collective-permute-start | bytes 245768 | tf_op jit(solution)/shard_map/ppermute | solution.py:323
  73.8 1.8 %collective-permute-done.21.refs_1_ = s16[320,128]{1,0:T(8,128)(2,1)S(1)} collective-permute-done((s16[320,128]{1,0:T(8,128)(2,1)S(1)}, s16[320,128]{1,0:T(8,128)(2,1)S(1)}, u32[]{:S(2)}, u32[]{:S(2)}) %collective-permute-start.21) | collective-permute-done | bytes 81952 | tf_op jit(solution)/shard_map/ppermute | solution.py:323
  77.1 1.1 %collective-permute-done.27.refs_7_ = s16[320,128]{1,0:T(8,128)(2,1)S(1)} collective-permute-done((s16[320,128]{1,0:T(8,128)(2,1)S(1)}, s16[320,128]{1,0:T(8,128)(2,1)S(1)}, u32[]{:S(2)}, u32[]{:S(2)}) %collective-permute-start.27) | collective-permute-done | bytes 81952 | tf_op jit(solution)/shard_map/ppermute | solution.py:323
  78.3 1.8 %shard_map.147 = (f32[128,1024]{1,0:T(8,128)}, f32[1,1024]{1,0:T(1,128)}, f32[172,1024]{1,0:T(8,128)}, f32[1,256]{1,0:T(1,128)}) custom-call(s32[11]{0:T(128)S(1)} %pad_add_fusion.info, s16[320,128]{1,0:T(8,128)(2,1)S(1)} %get-tuple-element.96.refs_0_, s16[320,128]{1,0:T(8,128)(2,1)S(1)} %collective-permute-done.21.refs_1_, ...), custom_call_target="tpu_custom_call" | custom-call | tf_op jit(solution)/shard_map/pallas_call | solution.py:25
  (52 shorter events, 12.4 us)
Async XLA Ops:
  2.9 8.7 %collective-permute-start = (bf16[144,128]{1,0:T(8,128)(2,1)S(1)}, bf16[144,128]{1,0:T(8,128)(2,1)S(1)}, u32[]{:S(2)}, u32[]{:S(2)}) collective-permute-start(bf16[144,128]{1,0:T(8,128)(2,1)S(1)} %get-tuple-element.58), channel_id=1, source_target_pairs={{0,4},{1,5},{2,6},{3,7},{4,0},{5,1},{6,2},{7,3},{8,12},{9,13},{10,... | collective-permute-start | bytes 110600 | tf_op jit(solution)/shard_map/ppermute | solution.py:323
  7.0 5.8 %collective-permute-start.1 = (bf16[144,128]{1,0:T(8,128)(2,1)S(1)}, bf16[144,128]{1,0:T(8,128)(2,1)S(1)}, u32[]{:S(2)}, u32[]{:S(2)}) collective-permute-start(bf16[144,128]{1,0:T(8,128)(2,1)S(1)} %get-tuple-element.59), channel_id=1, source_target_pairs={{0,6},{1,7},{2,4},{3,5},{4,2},{5,3},{6,0},{7,1},{8,14},{9,15},{10,... | collective-permute-start | bytes 110600 | tf_op jit(solution)/shard_map/ppermute | solution.py:323
  8.3 6.5 %collective-permute-start.2 = (bf16[144,128]{1,0:T(8,128)(2,1)S(1)}, bf16[144,128]{1,0:T(8,128)(2,1)S(1)}, u32[]{:S(2)}, u32[]{:S(2)}) collective-permute-start(bf16[144,128]{1,0:T(8,128)(2,1)S(1)} %get-tuple-element.60), channel_id=1, source_target_pairs={{0,5},{1,4},{2,7},{3,6},{4,1},{5,0},{6,3},{7,2},{8,13},{9,12},{10,... | collective-permute-start | bytes 110600 | tf_op jit(solution)/shard_map/ppermute | solution.py:323
  8.9 6.0 %collective-permute-start.3 = (bf16[144,128]{1,0:T(8,128)(2,1)S(1)}, bf16[144,128]{1,0:T(8,128)(2,1)S(1)}, u32[]{:S(2)}, u32[]{:S(2)}) collective-permute-start(bf16[144,128]{1,0:T(8,128)(2,1)S(1)} %get-tuple-element.61), channel_id=1, source_target_pairs={{0,7},{1,6},{2,5},{3,4},{4,3},{5,2},{6,1},{7,0},{8,15},{9,14},{10,... | collective-permute-start | bytes 110600 | tf_op jit(solution)/shard_map/ppermute | solution.py:323
  10.6 4.5 %collective-permute-start.4 = (bf16[144,128]{1,0:T(8,128)(2,1)S(1)}, bf16[144,128]{1,0:T(8,128)(2,1)S(1)}, u32[]{:S(2)}, u32[]{:S(2)}) collective-permute-start(bf16[144,128]{1,0:T(8,128)(2,1)S(1)} %get-tuple-element.62), channel_id=1, source_target_pairs={{0,2},{1,3},{2,0},{3,1},{4,6},{5,7},{6,4},{7,5},{8,10},{9,11},{10,... | collective-permute-start | bytes 110600 | tf_op jit(solution)/shard_map/ppermute | solution.py:323
  11.5 4.7 %collective-permute-start.5 = (bf16[144,128]{1,0:T(8,128)(2,1)S(1)}, bf16[144,128]{1,0:T(8,128)(2,1)S(1)}, u32[]{:S(2)}, u32[]{:S(2)}) collective-permute-start(bf16[144,128]{1,0:T(8,128)(2,1)S(1)} %get-tuple-element.63), channel_id=1, source_target_pairs={{0,3},{1,2},{2,1},{3,0},{4,7},{5,6},{6,5},{7,4},{8,11},{9,10},{10,... | collective-permute-start | bytes 110600 | tf_op jit(solution)/shard_map/ppermute | solution.py:323
  12.8 3.5 %collective-permute-start.6 = (bf16[144,128]{1,0:T(8,128)(2,1)S(1)}, bf16[144,128]{1,0:T(8,128)(2,1)S(1)}, u32[]{:S(2)}, u32[]{:S(2)}) collective-permute-start(bf16[144,128]{1,0:T(8,128)(2,1)S(1)} %get-tuple-element.64), channel_id=1, source_target_pairs={{0,1},{1,0},{2,3},{3,2},{4,5},{5,4},{6,7},{7,6},{8,9},{9,8},{10,11... | collective-permute-start | bytes 110600 | tf_op jit(solution)/shard_map/ppermute | solution.py:323
  12.8 1.0 %copy-start = (bf16[1,4,4,128,128]{4,3,2,1,0:T(8,128)(2,1)S(1)}, bf16[1,4,4,128,128]{4,3,2,1,0:T(8,128)(2,1)}, u32[]{:S(2)}) copy-start(bf16[1,4,4,128,128]{4,3,2,1,0:T(8,128)(2,1)} %param.15) | copy-start | bytes 1572868
  17.8 16.5 %collective-permute-start.7 = (bf16[128,512]{1,0:T(8,128)(2,1)S(1)}, bf16[128,512]{1,0:T(8,128)(2,1)S(1)}, u32[]{:S(2)}, u32[]{:S(2)}) collective-permute-start(bf16[128,512]{1,0:T(8,128)(2,1)S(1)} %get-tuple-element.74), channel_id=1, source_target_pairs={{0,4},{1,5},{2,6},{3,7},{4,0},{5,1},{6,2},{7,3},{8,12},{9,13},{10,... | collective-permute-start | bytes 393224 | tf_op jit(solution)/shard_map/ppermute | solution.py:323
  19.1 15.2 %collective-permute-start.8 = (bf16[128,512]{1,0:T(8,128)(2,1)S(1)}, bf16[128,512]{1,0:T(8,128)(2,1)S(1)}, u32[]{:S(2)}, u32[]{:S(2)}) collective-permute-start(bf16[128,512]{1,0:T(8,128)(2,1)S(1)} %get-tuple-element.75), channel_id=1, source_target_pairs={{0,2},{1,3},{2,0},{3,1},{4,6},{5,7},{6,4},{7,5},{8,10},{9,11},{10,... | collective-permute-start | bytes 393224 | tf_op jit(solution)/shard_map/ppermute | solution.py:323
  20.1 14.2 %collective-permute-start.9 = (bf16[128,512]{1,0:T(8,128)(2,1)S(1)}, bf16[128,512]{1,0:T(8,128)(2,1)S(1)}, u32[]{:S(2)}, u32[]{:S(2)}) collective-permute-start(bf16[128,512]{1,0:T(8,128)(2,1)S(1)} %get-tuple-element.76), channel_id=1, source_target_pairs={{0,6},{1,7},{2,4},{3,5},{4,2},{5,3},{6,0},{7,1},{8,14},{9,15},{10,... | collective-permute-start | bytes 393224 | tf_op jit(solution)/shard_map/ppermute | solution.py:323
  22.2 18.4 %collective-permute-start.10 = (bf16[128,512]{1,0:T(8,128)(2,1)S(1)}, bf16[128,512]{1,0:T(8,128)(2,1)S(1)}, u32[]{:S(2)}, u32[]{:S(2)}) collective-permute-start(bf16[128,512]{1,0:T(8,128)(2,1)S(1)} %get-tuple-element.77), channel_id=1, source_target_pairs={{0,5},{1,4},{2,7},{3,6},{4,1},{5,0},{6,3},{7,2},{8,13},{9,12},{10,... | collective-permute-start | bytes 393224 | tf_op jit(solution)/shard_map/ppermute | solution.py:323
  22.2 18.4 %collective-permute-start.12 = (bf16[128,512]{1,0:T(8,128)(2,1)S(1)}, bf16[128,512]{1,0:T(8,128)(2,1)S(1)}, u32[]{:S(2)}, u32[]{:S(2)}) collective-permute-start(bf16[128,512]{1,0:T(8,128)(2,1)S(1)} %get-tuple-element.79), channel_id=1, source_target_pairs={{0,7},{1,6},{2,5},{3,4},{4,3},{5,2},{6,1},{7,0},{8,15},{9,14},{10,... | collective-permute-start | bytes 393224 | tf_op jit(solution)/shard_map/ppermute | solution.py:323
  23.5 1.0 %copy-start.1 = (bf16[1024,172]{0,1:T(8,128)(2,1)S(1)}, bf16[1024,172]{0,1:T(8,128)(2,1)}, u32[]{:S(2)}) copy-start(bf16[1024,172]{0,1:T(8,128)(2,1)} %param.20) | copy-start | bytes 1056772
  24.4 0.9 %copy-start.2 = (bf16[128,1024]{1,0:T(8,128)(2,1)S(1)}, bf16[128,1024]{1,0:T(8,128)(2,1)}, u32[]{:S(2)}) copy-start(bf16[128,1024]{1,0:T(8,128)(2,1)} %w_in.1) | copy-start | bytes 786436
  25.4 0.7 copy-start.3
  34.3 6.3 %collective-permute-start.13 = (bf16[128,512]{1,0:T(8,128)(2,1)S(1)}, bf16[128,512]{1,0:T(8,128)(2,1)S(1)}, u32[]{:S(2)}, u32[]{:S(2)}) collective-permute-start(bf16[128,512]{1,0:T(8,128)(2,1)S(1)} %get-tuple-element.80), channel_id=1, source_target_pairs={{0,1},{1,0},{2,3},{3,2},{4,5},{5,4},{6,7},{7,6},{8,9},{9,8},{10,11... | collective-permute-start | bytes 393224 | tf_op jit(solution)/shard_map/ppermute | solution.py:323
  34.3 8.1 %collective-permute-start.11 = (bf16[128,512]{1,0:T(8,128)(2,1)S(1)}, bf16[128,512]{1,0:T(8,128)(2,1)S(1)}, u32[]{:S(2)}, u32[]{:S(2)}) collective-permute-start(bf16[128,512]{1,0:T(8,128)(2,1)S(1)} %get-tuple-element.78), channel_id=1, source_target_pairs={{0,3},{1,2},{2,1},{3,0},{4,7},{5,6},{6,5},{7,4},{8,11},{9,10},{10,... | collective-permute-start | bytes 393224 | tf_op jit(solution)/shard_map/ppermute | solution.py:323
  50.7 2.1 %collective-permute-start.14 = (f32[4,312,128]{2,1,0:T(8,128)S(1)}, f32[4,312,128]{2,1,0:T(8,128)S(1)}, u32[]{:S(2)}, u32[]{:S(2)}) collective-permute-start(f32[4,312,128]{2,1,0:T(8,128)S(1)} %get-tuple-element.87), channel_id=1, source_target_pairs={{0,1},{1,0},{2,3},{3,2},{4,5},{5,4},{6,7},{7,6},{8,9},{9,8},{10,11... | collective-permute-start | bytes 1916936 | tf_op jit(solution)/shard_map/ppermute | solution.py:323
  53.1 4.8 %collective-permute-start.15 = (s16[320,128]{1,0:T(8,128)(2,1)S(1)}, s16[320,128]{1,0:T(8,128)(2,1)S(1)}, u32[]{:S(2)}, u32[]{:S(2)}) collective-permute-start(s16[320,128]{1,0:T(8,128)(2,1)S(1)} %get-tuple-element.89), channel_id=1, source_target_pairs={{0,8},{8,0},{16,24},{24,16},{1,9},{9,1},{17,25},{25,17},{2,10},{10... | collective-permute-start | bytes 245768 | tf_op jit(solution)/shard_map/ppermute | solution.py:323
  54.6 5.3 %collective-permute-start.16 = (s16[320,128]{1,0:T(8,128)(2,1)S(1)}, s16[320,128]{1,0:T(8,128)(2,1)S(1)}, u32[]{:S(2)}, u32[]{:S(2)}) collective-permute-start(s16[320,128]{1,0:T(8,128)(2,1)S(1)} %get-tuple-element.90), channel_id=1, source_target_pairs={{0,16},{8,24},{16,0},{24,8},{1,17},{9,25},{17,1},{25,9},{2,18},{10... | collective-permute-start | bytes 245768 | tf_op jit(solution)/shard_map/ppermute | solution.py:323
  56.1 5.3 %collective-permute-start.17 = (s16[320,128]{1,0:T(8,128)(2,1)S(1)}, s16[320,128]{1,0:T(8,128)(2,1)S(1)}, u32[]{:S(2)}, u32[]{:S(2)}) collective-permute-start(s16[320,128]{1,0:T(8,128)(2,1)S(1)} %get-tuple-element.91), channel_id=1, source_target_pairs={{0,24},{8,16},{16,8},{24,0},{1,25},{9,17},{17,9},{25,1},{2,26},{10... | collective-permute-start | bytes 245768 | tf_op jit(solution)/shard_map/ppermute | solution.py:323
  61.6 7.5 %collective-permute-start.18 = (s16[320,128]{1,0:T(8,128)(2,1)S(1)}, s16[320,128]{1,0:T(8,128)(2,1)S(1)}, u32[]{:S(2)}, u32[]{:S(2)}) collective-permute-start(s16[320,128]{1,0:T(8,128)(2,1)S(1)} %get-tuple-element.92), channel_id=1, source_target_pairs={{0,4},{1,5},{2,6},{3,7},{4,0},{5,1},{6,2},{7,3},{8,12},{9,13},{10,... | collective-permute-start | bytes 245768 | tf_op jit(solution)/shard_map/ppermute | solution.py:323
  63.6 5.5 %collective-permute-start.19 = (s16[320,128]{1,0:T(8,128)(2,1)S(1)}, s16[320,128]{1,0:T(8,128)(2,1)S(1)}, u32[]{:S(2)}, u32[]{:S(2)}) collective-permute-start(s16[320,128]{1,0:T(8,128)(2,1)S(1)} %get-tuple-element.93), channel_id=1, source_target_pairs={{0,2},{1,3},{2,0},{3,1},{4,6},{5,7},{6,4},{7,5},{8,10},{9,11},{10,... | collective-permute-start | bytes 245768 | tf_op jit(solution)/shard_map/ppermute | solution.py:323
  63.7 6.4 %collective-permute-start.20 = (s16[320,128]{1,0:T(8,128)(2,1)S(1)}, s16[320,128]{1,0:T(8,128)(2,1)S(1)}, u32[]{:S(2)}, u32[]{:S(2)}) collective-permute-start(s16[320,128]{1,0:T(8,128)(2,1)S(1)} %get-tuple-element.94), channel_id=1, source_target_pairs={{0,6},{1,7},{2,4},{3,5},{4,2},{5,3},{6,0},{7,1},{8,14},{9,15},{10,... | collective-permute-start | bytes 245768 | tf_op jit(solution)/shard_map/ppermute | solution.py:323
  70.2 5.4 %collective-permute-start.21 = (s16[320,128]{1,0:T(8,128)(2,1)S(1)}, s16[320,128]{1,0:T(8,128)(2,1)S(1)}, u32[]{:S(2)}, u32[]{:S(2)}) collective-permute-start(s16[320,128]{1,0:T(8,128)(2,1)S(1)} %get-tuple-element.97), channel_id=1, source_target_pairs={{0,24},{8,16},{16,8},{24,0},{1,25},{9,17},{17,9},{25,1},{2,26},{10... | collective-permute-start | bytes 245768 | tf_op jit(solution)/shard_map/ppermute | solution.py:323
  71.1 4.7 %collective-permute-start.22 = (s16[320,128]{1,0:T(8,128)(2,1)S(1)}, s16[320,128]{1,0:T(8,128)(2,1)S(1)}, u32[]{:S(2)}, u32[]{:S(2)}) collective-permute-start(s16[320,128]{1,0:T(8,128)(2,1)S(1)} %get-tuple-element.98), channel_id=1, source_target_pairs={{0,8},{8,0},{16,24},{24,16},{1,9},{9,1},{17,25},{25,17},{2,10},{10... | collective-permute-start | bytes 245768 | tf_op jit(solution)/shard_map/ppermute | solution.py:323
  72.5 4.4 %collective-permute-start.23 = (s16[320,128]{1,0:T(8,128)(2,1)S(1)}, s16[320,128]{1,0:T(8,128)(2,1)S(1)}, u32[]{:S(2)}, u32[]{:S(2)}) collective-permute-start(s16[320,128]{1,0:T(8,128)(2,1)S(1)} %get-tuple-element.99), channel_id=1, source_target_pairs={{0,16},{8,24},{16,0},{24,8},{1,17},{9,25},{17,1},{25,9},{2,18},{10... | collective-permute-start | bytes 245768 | tf_op jit(solution)/shard_map/ppermute | solution.py:323
  73.8 3.2 %collective-permute-start.24 = (s16[320,128]{1,0:T(8,128)(2,1)S(1)}, s16[320,128]{1,0:T(8,128)(2,1)S(1)}, u32[]{:S(2)}, u32[]{:S(2)}) collective-permute-start(s16[320,128]{1,0:T(8,128)(2,1)S(1)} %get-tuple-element.96.refs_0_), channel_id=1, source_target_pairs={{0,1},{1,0},{2,3},{3,2},{4,5},{5,4},{6,7},{7,6},{8,9},{9,8},{10,11... | collective-permute-start | bytes 245768 | tf_op jit(solution)/shard_map/ppermute | solution.py:323
  75.6 1.4 %collective-permute-start.25 = (s16[320,128]{1,0:T(8,128)(2,1)S(1)}, s16[320,128]{1,0:T(8,128)(2,1)S(1)}, u32[]{:S(2)}, u32[]{:S(2)}) collective-permute-start(s16[320,128]{1,0:T(8,128)(2,1)S(1)} %collective-permute-done.21.refs_1_), channel_id=1, source_target_pairs={{0,1},{1,0},{2,3},{3,2},{4,5},{5,4},{6,7},{7,6},{8,9},{9,8},{10,11... | collective-permute-start | bytes 245768 | tf_op jit(solution)/shard_map/ppermute | solution.py:323
  75.8 1.3 %collective-permute-start.26 = (s16[320,128]{1,0:T(8,128)(2,1)S(1)}, s16[320,128]{1,0:T(8,128)(2,1)S(1)}, u32[]{:S(2)}, u32[]{:S(2)}) collective-permute-start(s16[320,128]{1,0:T(8,128)(2,1)S(1)} %collective-permute-done.22.refs_2_), channel_id=1, source_target_pairs={{0,1},{1,0},{2,3},{3,2},{4,5},{5,4},{6,7},{7,6},{8,9},{9,8},{10,11... | collective-permute-start | bytes 245768 | tf_op jit(solution)/shard_map/ppermute | solution.py:323
  77.0 1.3 %collective-permute-start.27 = (s16[320,128]{1,0:T(8,128)(2,1)S(1)}, s16[320,128]{1,0:T(8,128)(2,1)S(1)}, u32[]{:S(2)}, u32[]{:S(2)}) collective-permute-start(s16[320,128]{1,0:T(8,128)(2,1)S(1)} %collective-permute-done.23.refs_3_), channel_id=1, source_target_pairs={{0,1},{1,0},{2,3},{3,2},{4,5},{5,4},{6,7},{7,6},{8,9},{9,8},{10,11... | collective-permute-start | bytes 245768 | tf_op jit(solution)/shard_map/ppermute | solution.py:323
  (4 other events, 2.7 us)
